TPU v7x, 32 devices: a whole 2x2x4 slice. The times are simulated.
32 devices in a mesh: group: 2 (over x), gx: 16 (over z, y, core).
Axes of the slice: x: 2, y: 2, z: 4, core: 2. Of those that a mesh axis runs over, the one named last changes fastest.
Arguments:
- initial: float32 [4, 64, 64, 256], P('group', 'gx'), parts along dimension 0, may hold values from -1.25 to 1.25
- observed: float32 [4, 64, 64, 256], P('group', 'gx'), parts along dimension 0, may hold values from -6 to 6
- mobility: float32 [128, 64, 256], P(('group', 'gx')), parts along dimension 0, may hold values from 0.25 to 2
Outputs:
- mobility_sensitivity: float32 [128, 64, 256], P(('group', 'gx')), parts along dimension 0
- misfit: float32 [2], P('group'), parts along dimension 0
There are 2 independent parts, one for each index of `group`. A program takes and returns all parts, laid end to end along the dimension named above; each array names one. Nothing has to cross between parts.
All inputs are finite; a program needn't handle non-finite values.
Results may differ from a plain program's by a relative error of at most 0.00002.
Values sent between devices are 32-bit elements; how exact they have to be, the bound alone decides.
No kernel may reach another device: no remote copies, remote signals or barrier semaphores. Data moves between devices by JAX's collectives and lax.ppermute only.
A program may use at most 64 MiB of HBM per device.

v0:
```python
import jax
import jax.numpy as jnp
from jax import lax
from jax.sharding import PartitionSpec as P

stiffness = 0.5
time_step = 0.005


def padded_2(block, sides, width):
    for axis, dim in sides:
        count = lax.axis_size(axis)
        forward = [(i, i + 1) for i in range(count - 1)]
        forward.append((count - 1, 0))
        backward = [(target, source) for source, target in forward]
        low = lax.ppermute(
            lax.slice_in_dim(block, block.shape[dim] - width, None, axis=dim), axis, forward
        )
        high = lax.ppermute(lax.slice_in_dim(block, 0, width, axis=dim), axis, backward)
        block = jnp.concatenate([low, block, high], axis=dim)
    return block


def laplace(field):
    inner = field[:, 1:-1]
    beside_all = field[:, 2:] + field[:, :-2]
    beside_all = beside_all + jnp.roll(inner, 1, 2) + jnp.roll(inner, -1, 2)
    beside_all = beside_all + jnp.roll(inner, 1, 3) + jnp.roll(inner, -1, 3)
    return beside_all - 6.0 * inner


def potential(conc):
    inner = conc[:, 1:-1]
    return inner * inner * inner - inner - stiffness * laplace(conc)


def transport(mob, field):
    m_mid = mob[:, 1:-1]
    f_mid = field[:, 1:-1]
    total = (mob[:, 2:] + m_mid) * (field[:, 2:] - f_mid)
    total = total + (mob[:, :-2] + m_mid) * (field[:, :-2] - f_mid)
    for axis_num in (2, 3):
        for offset in (1, -1):
            total = total + (jnp.roll(m_mid, offset, axis_num) + m_mid) * (
                jnp.roll(f_mid, offset, axis_num) - f_mid
            )
    return 0.5 * total


def sensitivity(adjoint, chem):
    a_mid = adjoint[:, 1:-1]
    c_mid = chem[:, 1:-1]
    total = (adjoint[:, 2:] - a_mid) * (chem[:, 2:] - c_mid)
    total = total + (adjoint[:, :-2] - a_mid) * (chem[:, :-2] - c_mid)
    for axis_num in (2, 3):
        for offset in (1, -1):
            total = total + (jnp.roll(a_mid, offset, axis_num) - a_mid) * (
                jnp.roll(c_mid, offset, axis_num) - c_mid
            )
    return -0.5 * jnp.sum(total, axis=0)


def advance_rim(conc, mob):
    padded = padded_2(conc, (("gx", 1),), 2)
    chem = potential(padded)
    return (conc + time_step * transport(mob[:, 3:-3], chem), chem)


def on_device(initial, observed, mobility):
    runs_here = initial.shape[0]
    mob = padded_2(mobility[None], (("gx", 1),), 4)
    state1, chem0 = advance_rim(initial, mob)
    state2, chem1 = advance_rim(state1, mob)
    miss = state2 - observed
    misfit = lax.psum(0.5 / runs_here * jnp.sum(miss * miss), "gx")
    adjoint2 = padded_2(miss / runs_here, (("gx", 1),), 2)
    flow = transport(mob[:, 2:-2], adjoint2)
    adjoint1 = adjoint2[:, 2:-2] + time_step * (
        (3.0 * state1 * state1 - 1.0) * flow[:, 1:-1] - stiffness * laplace(flow)
    )
    adjoint1_wide = padded_2(adjoint1, (("gx", 1),), 1)
    result = sensitivity(adjoint2[:, 1:-1], chem1) + sensitivity(adjoint1_wide, chem0)
    return (result, jnp.reshape(misfit, (1,)))


def solution(mesh):
    placed = (
        P("group", "gx", None, None),
        P("group", "gx", None, None),
        P(("group", "gx"), None, None),
    )
    return jax.shard_map(
        on_device,
        mesh=mesh,
        in_specs=placed,
        out_specs=(P(("group", "gx"), None, None), P("group")),
        check_vma=False,
    )
```

profile of v0, /device:TPU:0, one launch (start us, length us, event | category | flops | bytes accessed | tf_op | source)
XLA Modules:
  0.0 93.1 jit_solution(14704669566015931531)
XLA Ops:
  0.6 5.5 %collective-permute-start = (f32[1,4,64,256]{3,2,1,0:T(8,128)}, f32[1,4,64,256]{3,2,1,0:T(8,128)S(1)}, u32[]{:S(2)}, u32[]{:S(2)}) collective-permute-start(f32[1,4,64,256]{3,2,1,0:T(8,128)} %bitcast.34), channel_id=1, source_target_pairs={{1,0},{2,1},{3,2},{4,3},{5,4},{6,5},{7,6},{8,7},{9,8},{10,9},{11,1... | collective-permute-start | bytes 786440 | tf_op jit(solution)/shard_map/ppermute | solution.py:19
  6.1 1.1 %fusion.129 = (f32[2,2,64,256]{3,2,1,0:T(8,128)S(1)}, f32[2,2,64,256]{3,2,1,0:T(8,128)S(1)}) fusion(f32[2,4,64,256]{3,2,1,0:T(8,128)} %param.3), kind=kLoop, calls=%fused_computation.208 | loop fusion | bytes 1048576 | tf_op jit(solution)/shard_map/slice | solution.py:17
  7.3 4.5 %collective-permute-start.2 = (f32[2,2,64,256]{3,2,1,0:T(8,128)S(1)}, f32[2,2,64,256]{3,2,1,0:T(8,128)S(1)}, u32[]{:S(2)}, u32[]{:S(2)}) collective-permute-start(f32[2,2,64,256]{3,2,1,0:T(8,128)S(1)} %get-tuple-element.82), channel_id=1, source_target_pairs={{1,0},{2,1},{3,2},{4,3},{5,4},{6,5},{7,6},{8,7},{9,8},{10,9},{11,1... | collective-permute-start | bytes 786440 | tf_op jit(solution)/shard_map/ppermute | solution.py:19
  12.1 0.2 maximum_add_fusion.4
  12.3 8.0 %collective-permute-done.1 = f32[2,2,64,256]{3,2,1,0:T(8,128)S(1)} collective-permute-done((f32[2,2,64,256]{3,2,1,0:T(8,128)S(1)}, f32[2,2,64,256]{3,2,1,0:T(8,128)S(1)}, u32[]{:S(2)}, u32[]{:S(2)}) %collective-permute-start.1) | collective-permute-done | bytes 262176 | tf_op jit(solution)/shard_map/ppermute | solution.py:16
  20.5 0.3 fusion.99
  20.8 0.2 fusion.100
  21.0 0.6 fusion.10
  21.9 0.2 fusion.115
  22.3 0.2 fusion.109
  23.0 0.2 copy-done.14
  23.1 0.1 copy-done.16
  23.3 0.6 multiply_add_fusion
  24.0 0.5 collective-permute-start.4
  24.5 1.6 %fusion.80 = (f32[6,64,256]{2,1,0:T(8,128)}, f32[6,64,256]{2,1,0:T(8,128)}, f32[6,64,256]{2,1,0:T(8,128)}, f32[6,64,256]{2,1,0:T(8,128)}, f32[6,64,256]{2,1,0:T(8,128)}) fusion(f32[1,4,64,256]{3,2,1,0:T(8,128)S(1)} %collective-permute-done, f32[1,4,64,256]{3,2,1,0:T(8,128)S(1)} %bitcast.42, f32[1,4,64,256]{3,2,1,0:T(8,128)S(1)} %collective-permute-done.3, ...), kind=kLoop, calls=%fused_computation.137 | loop fusion | flops 1376256 | bytes 4313088 | tf_op jit(solution)/shard_map/mul | solution.py:44
  26.1 0.9 fusion.86
  27.0 0.9 %collective-permute-done.5 = f32[2,2,64,256]{3,2,1,0:T(8,128)S(1)} collective-permute-done((f32[2,2,64,256]{3,2,1,0:T(8,128)S(1)}, f32[2,2,64,256]{3,2,1,0:T(8,128)S(1)}, u32[]{:S(2)}, u32[]{:S(2)}) %collective-permute-start.5) | collective-permute-done | bytes 262176 | tf_op jit(solution)/shard_map/ppermute | solution.py:19
  27.9 4.7 %collective-permute-done.4 = f32[2,2,64,256]{3,2,1,0:T(8,128)S(1)} collective-permute-done((f32[2,2,64,256]{3,2,1,0:T(8,128)S(1)}, f32[2,2,64,256]{3,2,1,0:T(8,128)S(1)}, u32[]{:S(2)}, u32[]{:S(2)}) %collective-permute-start.4) | collective-permute-done | bytes 262176 | tf_op jit(solution)/shard_map/ppermute | solution.py:16
  32.8 0.3 fusion.96
  33.1 0.2 fusion.97
  33.2 0.6 fusion.11
  34.0 0.2 fusion.113
  34.4 0.3 copy-done.22
  34.8 0.2 copy-done.2
  35.1 0.7 copy-done.36
  35.7 1.3 %multiply_reduce_fusion = (f32[]{:T(128)}, f32[2,4,64,256]{3,2,1,0:T(8,128)S(1)}) fusion(f32[2,4,64,256]{3,2,1,0:T(8,128)S(1)} %copy-done.36, f32[2,4,64,256]{3,2,1,0:T(8,128)S(1)} %multiply_add_fusion, f32[2,4,64,1]{3,2,1,0:T(8,128)S(1)} %get-tuple-element.48, f32[2,4,64,255]{3,2,1,0:T(8,128)S(1)} %get-tuple-element.50, ...), kind=kLoop, calls=%fused_computation.126 | loop fusion | flops 3407871 | bytes 6815748 | tf_op jit(solution)/shard_map/reduce_sum | solution.py:75
  37.0 0.8 copy-done.8
  37.8 0.9 fusion.127
  38.7 1.1 %fusion.125 = (f32[2,4,63,256]{3,2,1,0:T(8,128)}, f32[2,4,63,256]{3,2,1,0:T(8,128)}) fusion(f32[2,4,64,256]{3,2,1,0:T(8,128)S(1)} %broadcast_multiply_fusion), kind=kLoop, calls=%fused_computation.204 | loop fusion | bytes 2064384 | tf_op jit(solution)/shard_map/jit(_roll_static)/slice | solution.py:57
  39.7 0.9 fusion.124
  40.6 4.4 %collective-permute-start.6 = (f32[2,2,64,256]{3,2,1,0:T(8,128)}, f32[2,2,64,256]{3,2,1,0:T(8,128)}, u32[]{:S(2)}, u32[]{:S(2)}) collective-permute-start(f32[2,2,64,256]{3,2,1,0:T(8,128)} %get-tuple-element.77), channel_id=1, source_target_pairs={{1,0},{2,1},{3,2},{4,3},{5,4},{6,5},{7,6},{8,7},{9,8},{10,9},{11,1... | collective-permute-start | bytes 786440 | tf_op jit(solution)/shard_map/ppermute | solution.py:19
  45.7 31.2 %psum.7 = f32[1]{0:T(128)} all-reduce(f32[1]{0:T(128)} %bitcast.17), channel_id=1, replica_groups=mesh['group'=2,'gx'=16] {'gx'}, use_global_device_ids=true, to_apply=%region_3.4 | all-reduce | flops 1 | bytes 8 | tf_op jit(solution)/shard_map/psum | solution.py:75
  76.9 0.2 fusion.123
  77.1 1.0 %pad_maximum_fusion.1 = f32[2,8,64,256]{3,2,1,0:T(8,128)S(1)} fusion(f32[2,2,64,256]{3,2,1,0:T(8,128)} %collective-permute-done.6, f32[2,4,64,256]{3,2,1,0:T(8,128)S(1)} %broadcast_multiply_fusion, f32[2,2,64,256]{3,2,1,0:T(8,128)S(1)} %collective-permute-done.7), kind=kLoop, calls=%fused_computation.3 | loop fusion | flops 524288 | bytes 2097152 | tf_op jit(solution)/shard_map/concatenate | solution.py:20
  78.3 0.3 fusion.93
  78.6 0.2 fusion.94
  78.8 0.5 copy-done.32
  79.4 0.2 copy-done.28
  80.0 1.9 %fusion.7 = f32[2,6,64,256]{3,2,1,0:T(8,128)S(1)} fusion(f32[2,4,64,256]{3,2,1,0:T(8,128)S(1)} %broadcast_multiply_fusion, f32[2,2,64,256]{3,2,1,0:T(8,128)S(1)} %collective-permute-done.7, f32[2,2,64,256]{3,2,1,0:T(8,128)} %collective-permute-done.6, f32[2,6,63,256]{3,2,1,0:T(8,128)S(1)} %get-tuple-element.13, f32[2,6,63,256]{3,2,1,0:T(8,128)S(1)} %get-tuple-element.12, ...), kind=kLoop, calls=%fused_computation.17 | loop fusion | flops 5505024 | bytes 8101888 | tf_op jit(solution)/shard_map/mul | solution.py:47
  82.0 0.2 fusion.103
  82.3 0.9 copy-done.9
  83.3 0.5 fusion.38
  84.0 0.2 fusion.118
  84.4 4.4 %collective-permute-start.8 = (f32[2,1,64,256]{3,2,1,0:T(8,128)S(1)}, f32[2,1,64,256]{3,2,1,0:T(8,128)S(1)}, u32[]{:S(2)}, u32[]{:S(2)}) collective-permute-start(f32[2,1,64,256]{3,2,1,0:T(8,128)S(1)} %get-tuple-element.67), channel_id=1, source_target_pairs={{1,0},{2,1},{3,2},{4,3},{5,4},{6,5},{7,6},{8,7},{9,8},{10,9},{11,1... | collective-permute-start | bytes 393224 | tf_op jit(solution)/shard_map/ppermute | solution.py:19
  89.0 2.0 %fusion.47 = f32[4,64,256]{2,1,0:T(8,128)S(1)} fusion(f32[2,4,64,256]{3,2,1,0:T(8,128)S(1)} %broadcast_multiply_fusion, f32[2,2,64,256]{3,2,1,0:T(8,128)S(1)} %collective-permute-done.7, f32[2,2,64,256]{3,2,1,0:T(8,128)} %collective-permute-done.6, f32[2,4,63,256]{3,2,1,0:T(8,128)S(1)} %copy-done.27, f32[2,4,1,256]{3,2,1,0:T(1,128)S(1)} %get-tuple-element.76, ...), kind=kLoop, calls=%fused_computation.71 | loop fusion | flops 4390912 | bytes 7077888 | tf_op jit(solution)/shard_map/reduce_sum | solution.py:60
  90.9 0.5 collective-permute-done.9
  91.5 0.8 fusion.58
  92.3 0.7 add_multiply_fusion
  (108 shorter events, 3.3 us)
Async XLA Ops:
  0.6 21.5 %collective-permute-start = (f32[1,4,64,256]{3,2,1,0:T(8,128)}, f32[1,4,64,256]{3,2,1,0:T(8,128)S(1)}, u32[]{:S(2)}, u32[]{:S(2)}) collective-permute-start(f32[1,4,64,256]{3,2,1,0:T(8,128)} %bitcast.34), channel_id=1, source_target_pairs={{1,0},{2,1},{3,2},{4,3},{5,4},{6,5},{7,6},{8,7},{9,8},{10,9},{11,1... | collective-permute-start | bytes 786440 | tf_op jit(solution)/shard_map/ppermute | solution.py:19
  6.1 16.0 %collective-permute-start.3 = (f32[1,4,64,256]{3,2,1,0:T(8,128)}, f32[1,4,64,256]{3,2,1,0:T(8,128)S(1)}, u32[]{:S(2)}, u32[]{:S(2)}) collective-permute-start(f32[1,4,64,256]{3,2,1,0:T(8,128)} %bitcast.35), channel_id=1, source_target_pairs={{0,1},{1,2},{2,3},{3,4},{4,5},{5,6},{6,7},{7,8},{8,9},{9,10},{10,1... | collective-permute-start | bytes 786440 | tf_op jit(solution)/shard_map/ppermute | solution.py:16
  6.1 5.6 %copy-start = (f32[4,64,256]{2,1,0:T(8,128)S(1)}, f32[4,64,256]{2,1,0:T(8,128)}, u32[]{:S(2)}) copy-start(f32[4,64,256]{2,1,0:T(8,128)} %param.5) | copy-start | bytes 786436
  7.3 13.1 %collective-permute-start.2 = (f32[2,2,64,256]{3,2,1,0:T(8,128)S(1)}, f32[2,2,64,256]{3,2,1,0:T(8,128)S(1)}, u32[]{:S(2)}, u32[]{:S(2)}) collective-permute-start(f32[2,2,64,256]{3,2,1,0:T(8,128)S(1)} %get-tuple-element.82), channel_id=1, source_target_pairs={{1,0},{2,1},{3,2},{4,3},{5,4},{6,5},{7,6},{8,7},{9,8},{10,9},{11,1... | collective-permute-start | bytes 786440 | tf_op jit(solution)/shard_map/ppermute | solution.py:19
  11.7 8.5 %collective-permute-start.1 = (f32[2,2,64,256]{3,2,1,0:T(8,128)S(1)}, f32[2,2,64,256]{3,2,1,0:T(8,128)S(1)}, u32[]{:S(2)}, u32[]{:S(2)}) collective-permute-start(f32[2,2,64,256]{3,2,1,0:T(8,128)S(1)} %get-tuple-element.81), channel_id=1, source_target_pairs={{0,1},{1,2},{2,3},{3,4},{4,5},{5,6},{6,7},{7,8},{8,9},{9,10},{10,1... | collective-permute-start | bytes 786440 | tf_op jit(solution)/shard_map/ppermute | solution.py:16
  12.2 8.0 %copy-start.1 = (f32[2,4,64,256]{3,2,1,0:T(8,128)S(1)}, f32[2,4,64,256]{3,2,1,0:T(8,128)}, u32[]{:S(2)}) copy-start(f32[2,4,64,256]{3,2,1,0:T(8,128)} %param.3) | copy-start | bytes 1572868
  21.7 0.9 copy-start.10
  21.8 1.0 %copy-start.12 = (f32[2,4,63,256]{3,2,1,0:T(8,128)}, f32[2,4,63,256]{3,2,1,0:T(8,128)S(1)}, u32[]{:S(2)}) copy-start(f32[2,4,63,256]{3,2,1,0:T(8,128)S(1)} %get-tuple-element.58) | copy-start | bytes 1548292
  21.9 1.0 %copy-start.18 = (f32[2,4,64,1]{3,2,1,0:T(8,128)}, f32[2,4,64,1]{3,2,1,0:T(8,128)S(1)}, u32[]{:S(2)}) copy-start(f32[2,4,64,1]{3,2,1,0:T(8,128)S(1)} %get-tuple-element.51) | copy-start | bytes 6148
  21.9 1.1 %copy-start.20 = (f32[2,4,64,1]{3,2,1,0:T(8,128)}, f32[2,4,64,1]{3,2,1,0:T(8,128)S(1)}, u32[]{:S(2)}) copy-start(f32[2,4,64,1]{3,2,1,0:T(8,128)S(1)} %get-tuple-element.52) | copy-start | bytes 6148
  22.1 1.0 %copy-start.14 = (f32[2,4,64,255]{3,2,1,0:T(8,128)}, f32[2,4,64,255]{3,2,1,0:T(8,128)S(1)}, u32[]{:S(2)}) copy-start(f32[2,4,64,255]{3,2,1,0:T(8,128)S(1)} %get-tuple-element.53) | copy-start | bytes 1566724
  22.1 1.1 %copy-start.16 = (f32[2,4,64,255]{3,2,1,0:T(8,128)}, f32[2,4,64,255]{3,2,1,0:T(8,128)S(1)}, u32[]{:S(2)}) copy-start(f32[2,4,64,255]{3,2,1,0:T(8,128)S(1)} %get-tuple-element.54) | copy-start | bytes 1566724
  23.9 4.0 %collective-permute-start.5 = (f32[2,2,64,256]{3,2,1,0:T(8,128)S(1)}, f32[2,2,64,256]{3,2,1,0:T(8,128)S(1)}, u32[]{:S(2)}, u32[]{:S(2)}) collective-permute-start(f32[2,2,64,256]{3,2,1,0:T(8,128)S(1)} %get-tuple-element.80), channel_id=1, source_target_pairs={{1,0},{2,1},{3,2},{4,3},{5,4},{6,5},{7,6},{8,7},{9,8},{10,9},{11,1... | collective-permute-start | bytes 786440 | tf_op jit(solution)/shard_map/ppermute | solution.py:19
  24.0 8.5 %collective-permute-start.4 = (f32[2,2,64,256]{3,2,1,0:T(8,128)S(1)}, f32[2,2,64,256]{3,2,1,0:T(8,128)S(1)}, u32[]{:S(2)}, u32[]{:S(2)}) collective-permute-start(f32[2,2,64,256]{3,2,1,0:T(8,128)S(1)} %get-tuple-element.79), channel_id=1, source_target_pairs={{0,1},{1,2},{2,3},{3,4},{4,5},{5,6},{6,7},{7,8},{8,9},{9,10},{10,1... | collective-permute-start | bytes 786440 | tf_op jit(solution)/shard_map/ppermute | solution.py:16
  34.0 0.7 copy-start.22
  34.0 0.8 copy-start.24
  34.2 0.8 copy-start.2
  34.3 1.4 %copy-start.36 = (f32[2,4,64,256]{3,2,1,0:T(8,128)S(1)}, f32[2,4,64,256]{3,2,1,0:T(8,128)}, u32[]{:S(2)}) copy-start(f32[2,4,64,256]{3,2,1,0:T(8,128)} %param.4) | copy-start | bytes 1572868
  34.4 2.6 %copy-start.4 = (f32[2,4,63,256]{3,2,1,0:T(8,128)}, f32[2,4,63,256]{3,2,1,0:T(8,128)S(1)}, u32[]{:S(2)}) copy-start(f32[2,4,63,256]{3,2,1,0:T(8,128)S(1)} %get-tuple-element.45) | copy-start | bytes 1548292
  34.4 2.6 %copy-start.6 = (f32[2,4,63,256]{3,2,1,0:T(8,128)}, f32[2,4,63,256]{3,2,1,0:T(8,128)S(1)}, u32[]{:S(2)}) copy-start(f32[2,4,63,256]{3,2,1,0:T(8,128)S(1)} %get-tuple-element.46) | copy-start | bytes 1548292
  37.0 0.8 copy-start.8
  40.6 36.5 %collective-permute-start.7 = (f32[2,2,64,256]{3,2,1,0:T(8,128)}, f32[2,2,64,256]{3,2,1,0:T(8,128)S(1)}, u32[]{:S(2)}, u32[]{:S(2)}) collective-permute-start(f32[2,2,64,256]{3,2,1,0:T(8,128)} %get-tuple-element.78), channel_id=1, source_target_pairs={{0,1},{1,2},{2,3},{3,4},{4,5},{5,6},{6,7},{7,8},{8,9},{9,10},{10,1... | collective-permute-start | bytes 786440 | tf_op jit(solution)/shard_map/ppermute | solution.py:16
  40.6 36.5 %collective-permute-start.6 = (f32[2,2,64,256]{3,2,1,0:T(8,128)}, f32[2,2,64,256]{3,2,1,0:T(8,128)}, u32[]{:S(2)}, u32[]{:S(2)}) collective-permute-start(f32[2,2,64,256]{3,2,1,0:T(8,128)} %get-tuple-element.77), channel_id=1, source_target_pairs={{1,0},{2,1},{3,2},{4,3},{5,4},{6,5},{7,6},{8,7},{9,8},{10,9},{11,1... | collective-permute-start | bytes 786440 | tf_op jit(solution)/shard_map/ppermute | solution.py:19
  78.3 1.0 %copy-start.32 = (f32[6,64,256]{2,1,0:T(8,128)S(1)}, f32[6,64,256]{2,1,0:T(8,128)}, u32[]{:S(2)}) copy-start(f32[6,64,256]{2,1,0:T(8,128)} %get-tuple-element.28) | copy-start | bytes 1179652
  78.3 1.1 %copy-start.33 = (f32[6,64,256]{2,1,0:T(8,128)S(1)}, f32[6,64,256]{2,1,0:T(8,128)}, u32[]{:S(2)}) copy-start(f32[6,64,256]{2,1,0:T(8,128)} %fusion.86) | copy-start | bytes 1179652
  78.6 1.1 %copy-start.28 = (f32[6,64,256]{2,1,0:T(8,128)S(1)}, f32[6,64,256]{2,1,0:T(8,128)}, u32[]{:S(2)}) copy-start(f32[6,64,256]{2,1,0:T(8,128)} %get-tuple-element.4) | copy-start | bytes 1179652
  78.6 1.2 %copy-start.29 = (f32[6,64,256]{2,1,0:T(8,128)S(1)}, f32[6,64,256]{2,1,0:T(8,128)}, u32[]{:S(2)}) copy-start(f32[6,64,256]{2,1,0:T(8,128)} %get-tuple-element.5) | copy-start | bytes 1179652
  78.6 1.3 %copy-start.30 = (f32[6,64,256]{2,1,0:T(8,128)S(1)}, f32[6,64,256]{2,1,0:T(8,128)}, u32[]{:S(2)}) copy-start(f32[6,64,256]{2,1,0:T(8,128)} %get-tuple-element.6) | copy-start | bytes 1179652
  78.6 1.4 %copy-start.31 = (f32[6,64,256]{2,1,0:T(8,128)S(1)}, f32[6,64,256]{2,1,0:T(8,128)}, u32[]{:S(2)}) copy-start(f32[6,64,256]{2,1,0:T(8,128)} %get-tuple-element.7) | copy-start | bytes 1179652
  82.2 1.0 %copy-start.9 = (f32[2,4,64,256]{3,2,1,0:T(8,128)S(1)}, f32[2,4,64,256]{3,2,1,0:T(8,128)}, u32[]{:S(2)}) copy-start(f32[2,4,64,256]{3,2,1,0:T(8,128)} %copy-done.8) | copy-start | bytes 1572868
  83.8 5.0 %copy-start.34 = (f32[2,4,64,1]{3,2,1,0:T(8,128)S(1)}, f32[2,4,64,1]{3,2,1,0:T(8,128)}, u32[]{:S(2)}) copy-start(f32[2,4,64,1]{3,2,1,0:T(8,128)} %get-tuple-element.71) | copy-start | bytes 6148
  83.8 5.0 %copy-start.35 = (f32[2,4,64,1]{3,2,1,0:T(8,128)S(1)}, f32[2,4,64,1]{3,2,1,0:T(8,128)}, u32[]{:S(2)}) copy-start(f32[2,4,64,1]{3,2,1,0:T(8,128)} %get-tuple-element.72) | copy-start | bytes 6148
  83.9 4.9 %copy-start.7 = (f32[2,4,63,256]{3,2,1,0:T(8,128)S(1)}, f32[2,4,63,256]{3,2,1,0:T(8,128)}, u32[]{:S(2)}) copy-start(f32[2,4,63,256]{3,2,1,0:T(8,128)} %copy-done.6) | copy-start | bytes 1548292
  83.9 4.9 %copy-start.23 = (f32[2,4,64,1]{3,2,1,0:T(8,128)S(1)}, f32[2,4,64,1]{3,2,1,0:T(8,128)}, u32[]{:S(2)}) copy-start(f32[2,4,64,1]{3,2,1,0:T(8,128)} %copy-done.22) | copy-start | bytes 6148
  83.9 4.9 %copy-start.25 = (f32[2,4,64,1]{3,2,1,0:T(8,128)S(1)}, f32[2,4,64,1]{3,2,1,0:T(8,128)}, u32[]{:S(2)}) copy-start(f32[2,4,64,1]{3,2,1,0:T(8,128)} %copy-done.24) | copy-start | bytes 6148
  84.0 4.9 %copy-start.26 = (f32[2,4,63,256]{3,2,1,0:T(8,128)S(1)}, f32[2,4,63,256]{3,2,1,0:T(8,128)}, u32[]{:S(2)}) copy-start(f32[2,4,63,256]{3,2,1,0:T(8,128)} %get-tuple-element.73) | copy-start | bytes 1548292
  84.0 4.9 %copy-start.27 = (f32[2,4,63,256]{3,2,1,0:T(8,128)S(1)}, f32[2,4,63,256]{3,2,1,0:T(8,128)}, u32[]{:S(2)}) copy-start(f32[2,4,63,256]{3,2,1,0:T(8,128)} %get-tuple-element.74) | copy-start | bytes 1548292
  84.2 4.7 %copy-start.3 = (f32[2,4,64,255]{3,2,1,0:T(8,128)S(1)}, f32[2,4,64,255]{3,2,1,0:T(8,128)}, u32[]{:S(2)}) copy-start(f32[2,4,64,255]{3,2,1,0:T(8,128)} %copy-done.2) | copy-start | bytes 1566724
  84.2 4.7 %copy-start.5 = (f32[2,4,63,256]{3,2,1,0:T(8,128)S(1)}, f32[2,4,63,256]{3,2,1,0:T(8,128)}, u32[]{:S(2)}) copy-start(f32[2,4,63,256]{3,2,1,0:T(8,128)} %copy-done.4) | copy-start | bytes 1548292
  84.3 7.1 %collective-permute-start.9 = (f32[2,1,64,256]{3,2,1,0:T(8,128)S(1)}, f32[2,1,64,256]{3,2,1,0:T(8,128)S(1)}, u32[]{:S(2)}, u32[]{:S(2)}) collective-permute-start(f32[2,1,64,256]{3,2,1,0:T(8,128)S(1)} %get-tuple-element.68), channel_id=1, source_target_pairs={{0,1},{1,2},{2,3},{3,4},{4,5},{5,6},{6,7},{7,8},{8,9},{9,10},{10,1... | collective-permute-start | bytes 393224 | tf_op jit(solution)/shard_map/ppermute | solution.py:16
  84.4 7.1 %collective-permute-start.8 = (f32[2,1,64,256]{3,2,1,0:T(8,128)S(1)}, f32[2,1,64,256]{3,2,1,0:T(8,128)S(1)}, u32[]{:S(2)}, u32[]{:S(2)}) collective-permute-start(f32[2,1,64,256]{3,2,1,0:T(8,128)S(1)} %get-tuple-element.67), channel_id=1, source_target_pairs={{1,0},{2,1},{3,2},{4,3},{5,4},{6,5},{7,6},{8,7},{9,8},{10,9},{11,1... | collective-permute-start | bytes 393224 | tf_op jit(solution)/shard_map/ppermute | solution.py:19
  88.9 2.6 %copy-start.11 = (f32[2,4,63,256]{3,2,1,0:T(8,128)S(1)}, f32[2,4,63,256]{3,2,1,0:T(8,128)}, u32[]{:S(2)}) copy-start(f32[2,4,63,256]{3,2,1,0:T(8,128)} %copy-done.10) | copy-start | bytes 1548292
  88.9 2.6 %copy-start.13 = (f32[2,4,63,256]{3,2,1,0:T(8,128)S(1)}, f32[2,4,63,256]{3,2,1,0:T(8,128)}, u32[]{:S(2)}) copy-start(f32[2,4,63,256]{3,2,1,0:T(8,128)} %copy-done.12) | copy-start | bytes 1548292
  88.9 2.6 %copy-start.15 = (f32[2,4,64,255]{3,2,1,0:T(8,128)S(1)}, f32[2,4,64,255]{3,2,1,0:T(8,128)}, u32[]{:S(2)}) copy-start(f32[2,4,64,255]{3,2,1,0:T(8,128)} %copy-done.14) | copy-start | bytes 1566724
  88.9 2.6 %copy-start.17 = (f32[2,4,64,255]{3,2,1,0:T(8,128)S(1)}, f32[2,4,64,255]{3,2,1,0:T(8,128)}, u32[]{:S(2)}) copy-start(f32[2,4,64,255]{3,2,1,0:T(8,128)} %copy-done.16) | copy-start | bytes 1566724
  88.9 2.6 %copy-start.19 = (f32[2,4,64,1]{3,2,1,0:T(8,128)S(1)}, f32[2,4,64,1]{3,2,1,0:T(8,128)}, u32[]{:S(2)}) copy-start(f32[2,4,64,1]{3,2,1,0:T(8,128)} %copy-done.18) | copy-start | bytes 6148
  88.9 2.6 %copy-start.21 = (f32[2,4,64,1]{3,2,1,0:T(8,128)S(1)}, f32[2,4,64,1]{3,2,1,0:T(8,128)}, u32[]{:S(2)}) copy-start(f32[2,4,64,1]{3,2,1,0:T(8,128)} %copy-done.20) | copy-start | bytes 6148
where the time goes:
time: 93.4 us; the launch traced here: 93.1 us
  blocking collectives  31.2 us (33%)
  starting transfers between devices  19.5 us (21%)
  waiting for transfers between devices  14.1 us (15%)
  local copies, waits for them, and re-layouts  13.4 us (14%)
  other arithmetic  12.9 us (14%)
  between operations  2 us (2%)
    psum x1, blocking collectives, on_device(): misfit = lax.psum(0.5 / runs_here * jnp.sum(miss * miss), 'gx')  31.2 us
    ppermute x5, starting transfers between devices, padded_2(): lax.ppermute(lax.slice_in_dim(block, 0, width, axis=dim), axis, backward)  18.9 us
    ppermute x5, waiting for transfers between devices, padded_2(): lax.ppermute(lax.slice_in_dim(block, block.shape[dim] - width, None, axis...  13.2 us
    unnamed x76, local copies, waits for them, and re-layouts  4.98 us
    reduce_sum x2, other arithmetic, sensitivity(): return -0.5 * jnp.sum(total, axis=0)  2.76 us
    slice x8, local copies, waits for them, and re-layouts, sensitivity(): jnp.roll(a_mid, offset, axis_num) - a_mid  2.61 us
    mul x2, other arithmetic, transport(): (jnp.roll(m_mid, offset, axis_num) + m_mid) * (jnp.roll(f_mid, offset, ax...  2.46 us
  transfers between devices with their start and end apart: 10, of which 4 were waited for; matrix products, arithmetic and copies ran while one was open for 9% of the time, Pallas kernels for 0%

commit v1 on v0

v1 whole, which is shorter than its diff:
```python
import functools

import jax
import jax.numpy as jnp
from jax import lax
from jax.experimental import pallas as pl
from jax.experimental.pallas import tpu as pltpu
from jax.sharding import PartitionSpec as P

stiffness = 0.5
time_step = 0.005
VMEM = pl.BlockSpec(memory_space=pltpu.VMEM)


def before(field, axis):
    return pltpu.roll(field, 1, axis)


def after(field, axis):
    return pltpu.roll(field, field.shape[axis] - 1, axis)


def in_plane(field):
    return before(field, 0) + after(field, 0) + (before(field, 1) + after(field, 1))


def planes(count, body):
    lax.fori_loop(0, count, lambda at, carry: (body(at), carry)[1], 0)


def copy_planes(pieces, target):
    start = 0
    for piece in pieces:
        target[start : start + piece.shape[0]] = piece[...]
        start += piece.shape[0]


def transport(mx, my, mz, m_at, field, at, want_steps=False):
    mid = field[at]
    step_y = after(mid, 0) - mid
    step_z = after(mid, 1) - mid
    flux_y = my[m_at] * step_y
    flux_z = mz[m_at] * step_z
    total = mx[m_at + 1] * (field[at + 1] - mid) - mx[m_at] * (mid - field[at - 1])
    total = total + (flux_y - before(flux_y, 0)) + (flux_z - before(flux_z, 1))
    return (total, step_y, step_z) if want_steps else total


def mobility_kernel(low, own, high, mx, my, mz, mob):
    copy_planes((low, own, high), mob)

    def faces(at):
        mx[at] = 0.5 * (mob[at] + mob[at + 1])

    planes(mx.shape[0], faces)

    def sides(at):
        mid = mob[at + 1]
        my[at] = 0.5 * (mid + after(mid, 0))
        mz[at] = 0.5 * (mid + after(mid, 1))

    planes(my.shape[0], sides)


def forward_kernel(
    runs, low, own, high, observed, mx, my, mz, miss_in, sum_y_in, sum_z_in,
    adjoint2, first, last, state1, chem0, chem1, step_y0, step_z0, miss_sum, sum_y, sum_z,
    conc, wide0, wide1,
):
    n = own.shape[0]
    copy_planes((low, own, high), conc)

    def potential(field, at):
        mid = field[at]
        beside = field[at - 1] + field[at + 1] + in_plane(mid)
        return mid * (mid * mid + (6.0 * stiffness - 1.0)) - stiffness * beside

    def potential0(at):
        wide0[at] = potential(conc, at + 1)

    planes(n + 6, potential0)

    def step0(at):
        wide1[at] = conc[at + 2] + time_step * transport(mx, my, mz, at, wide0, at + 1)

    planes(n + 4, step0)

    def potential1(at):
        state1[at] = wide1[at + 1]
        chem0[at] = wide0[at + 2]
        chem1[at] = potential(wide1, at + 1)

    planes(n + 2, potential1)
    miss_sum[...] = miss_in[...]

    def step1(at):
        flow, step_y1, step_z1 = transport(mx, my, mz, at + 2, chem1, at + 1, True)
        miss = state1[at + 1] + time_step * flow - observed[at]
        squares = miss * miss
        rows, columns = miss_sum.shape
        part = jnp.zeros((rows, columns), jnp.float32)
        for row in range(0, squares.shape[0], rows):
            for column in range(0, squares.shape[1], columns):
                part = part + squares[row : row + rows, column : column + columns]
        miss_sum[...] += part
        adj = miss * (1.0 / runs)
        adjoint2[at] = adj
        sum_y[at] = sum_y_in[at] + (after(adj, 0) - adj) * step_y1
        sum_z[at] = sum_z_in[at] + (after(adj, 1) - adj) * step_z1
        mid = chem0[at + 1]
        step_y0[at] = after(mid, 0) - mid
        step_z0[at] = after(mid, 1) - mid

    planes(n, step1)
    first[...] = adjoint2[: first.shape[0]]
    last[...] = adjoint2[n - last.shape[0] :]


def backward_kernel(
    final, low, own, high, mx, my, mz, state1, chem0, chem1, step_y0, step_z0, sum_y_in, sum_z_in,
    *rest,
):
    if final:
        sum_x_in, result, adj2, flow, adj1, sum_y, sum_z, sum_x = rest
    else:
        sum_x_in, sum_y, sum_z, sum_x, adj2, flow, adj1 = rest
    n = own.shape[0]
    copy_planes((low, own, high), adj2)

    def flows(at):
        flow[at] = transport(mx, my, mz, at, adj2, at + 1)

    planes(n + 4, flows)

    def adjoint(at):
        mid = flow[at + 1]
        beside = flow[at] + flow[at + 2] + in_plane(mid)
        conc = state1[at]
        slope = 3.0 * conc * conc + (6.0 * stiffness - 1.0)
        adj1[at] = adj2[at + 2] + time_step * (slope * mid - stiffness * beside)

    planes(n + 2, adjoint)

    def products(at):
        mid = adj1[at + 1]
        total_y = sum_y_in[at] + (after(mid, 0) - mid) * step_y0[at]
        total_z = sum_z_in[at] + (after(mid, 1) - mid) * step_z0[at]
        total_x = sum_x_in[at]
        for side in (0, 2):
            total_x = total_x + (adj1[at + side] - mid) * (chem0[at + side] - chem0[at + 1])
            total_x = total_x + (adj2[at + 2 + side] - adj2[at + 3]) * (
                chem1[at + side] - chem1[at + 1]
            )
        if final:
            total = total_x + (total_y + before(total_y, 0)) + (total_z + before(total_z, 1))
            result[at] = -0.5 * total
        else:
            sum_y[at] = total_y
            sum_z[at] = total_z
            sum_x[at] = total_x

    planes(n, products)


def call(kernel, outs, scratch, args, flops):
    moved = sum(a.size * 4 for a in args) + sum(4 * functools.reduce(lambda a, b: a * b, o) for o in outs)
    return pl.pallas_call(
        kernel,
        out_shape=tuple(jax.ShapeDtypeStruct(o, jnp.float32) for o in outs),
        in_specs=[VMEM] * len(args),
        out_specs=tuple([VMEM] * len(outs)),
        scratch_shapes=[pltpu.VMEM(s, jnp.float32) for s in scratch],
        compiler_params=pltpu.CompilerParams(vmem_limit_bytes=24 * 1024 * 1024),
        cost_estimate=pl.CostEstimate(flops=flops, bytes_accessed=moved, transcendentals=0),
    )(*args)


def sum_over(value, axis):
    count = lax.axis_size(axis)
    if count & (count - 1):
        return lax.psum(value, axis)
    hop = 1
    while hop < count:
        value = value + lax.ppermute(value, axis, [(i, i ^ hop) for i in range(count)])
        hop *= 2
    return value


def on_device(initial, observed, mobility):
    runs, n, ny, nz = initial.shape
    count = lax.axis_size("gx")
    forward = [(i, (i + 1) % count) for i in range(count)]
    backward = [(i, (i - 1) % count) for i in range(count)]

    def beside(first, last):
        return lax.ppermute(last, "gx", forward), lax.ppermute(first, "gx", backward)

    def size(count):
        return (count, ny, nz)

    cell = ny * nz
    low, high = beside(mobility[:3], mobility[n - 3 :])
    initial_sides = [beside(initial[r, :4], initial[r, n - 4 :]) for r in range(runs)]
    mx, my, mz = call(
        mobility_kernel,
        (size(n + 5), size(n + 4), size(n + 4)),
        (size(n + 6),),
        (low, mobility, high),
        30 * (n + 4) * cell,
    )
    sum_y = sum_z = sum_x = jnp.zeros(size(n), jnp.float32)
    miss_sum = jnp.zeros((8, 128), jnp.float32)
    kept = []
    for r in range(runs):
        low, high = initial_sides[r]
        (adj, first, last, state1, chem0, chem1, step_y0, step_z0, miss_sum, sum_y, sum_z) = call(
            functools.partial(forward_kernel, runs),
            (size(n), size(3), size(3), size(n + 2), size(n + 2), size(n + 2), size(n), size(n), (8, 128), size(n), size(n)),
            (size(n + 8), size(n + 6), size(n + 4)),
            (low, initial[r], high, observed[r], mx, my, mz, miss_sum, sum_y, sum_z),
            200 * (n + 4) * cell,
        )
        kept.append((adj, beside(first, last), state1, chem0, chem1, step_y0, step_z0))
    misfit = sum_over(0.5 / runs * jnp.sum(miss_sum), "gx")
    for r in range(runs):
        adj, (low, high), state1, chem0, chem1, step_y0, step_z0 = kept[r]
        args = (low, adj, high, mx, my, mz, state1, chem0, chem1, step_y0, step_z0, sum_y, sum_z, sum_x)
        scratch = (size(n + 6), size(n + 4), size(n + 2))
        final = r == runs - 1
        outs = (size(n),) if final else (size(n),) * 3
        if final:
            scratch = scratch + (size(n),) * 3
        out = call(functools.partial(backward_kernel, final), outs, scratch, args, 150 * (n + 4) * cell)
        if final:
            (result,) = out
        else:
            sum_y, sum_z, sum_x = out
    return (result, jnp.reshape(misfit, (1,)))


def solution(mesh):
    placed = (
        P("group", "gx", None, None),
        P("group", "gx", None, None),
        P(("group", "gx"), None, None),
    )
    return jax.shard_map(
        on_device,
        mesh=mesh,
        in_specs=placed,
        out_specs=(P(("group", "gx"), None, None), P("group")),
        check_vma=False,
    )
```

time: 93.4 us -> 80.9 us (0.87)
  blocking collectives: 31.2 us -> 0 us
  Pallas kernels: 0 us -> 19.3 us
  other arithmetic: 12.9 us -> 0.6 us
  starting transfers between devices: 19.5 us -> 24.7 us
  waiting for transfers between devices: 14.1 us -> 18.7 us
  between operations: 2 us -> 4.85 us
  local copies, waits for them, and re-layouts: 13.4 us -> 12.4 us
    psum x1 -> x0, blocking collectives: 31.2 us -> none  [on_device(): misfit = lax.psum(0.5 / runs_here * jnp.sum(miss * miss), 'gx')]
    pallas_call x0 -> x5, Pallas kernels: none -> 19.3 us  [call(): pl.pallas_call(kernel, out_shape=tuple((jax.ShapeDtypeStruct(o, jnp.float...]
    slice x37 -> x1, local copies, waits for them, and re-layouts: 8.1 us -> 1.11 us  [on_device(): low, high = beside(mobility[:3], mobility[n - 3:])]
    unnamed x76 -> x46, local copies, waits for them, and re-layouts: 4.98 us -> 11.2 us
    ppermute x10 -> x14, starting transfers between devices: 19.5 us -> 24.7 us  [the longest x5 19.5 us: beside(): lax.ppermute(first, 'gx', backward)]
    ppermute x10 -> x14, waiting for transfers between devices: 14.1 us -> 18.7 us  [the longest x5 10.5 us: beside(): lax.ppermute(last, 'gx', forward)]
    mul x4 -> x0, other arithmetic: 4.37 us -> none  [the longest x2 2.46 us: transport(): (jnp.roll(m_mid, offset, axis_num) + m_mid) * (jnp.roll(f_mid, offset, ax...]
    reduce_sum x3 -> x1, other arithmetic: 4.02 us -> 0.6 us  [on_device(): misfit = sum_over(0.5 / runs * jnp.sum(miss_sum), 'gx')]
  transfers between devices with their start and end apart: 10 -> 14, of which waited for: 4 -> 5; matrix products, arithmetic and copies ran while one was open for 9% -> 1% of each run, Pallas kernels for 0% -> 18%
where the time goes in v1:
time: 80.9 us; the launch traced here: 80.6 us
  starting transfers between devices  24.7 us (31%)
  Pallas kernels  19.3 us (24%)
  waiting for transfers between devices  18.7 us (23%)
  local copies, waits for them, and re-layouts  12.4 us (15%)
  between operations  4.85 us (6%)
    ppermute x5, starting transfers between devices, beside(): lax.ppermute(first, 'gx', backward)  19.5 us
    pallas_call x5, Pallas kernels, call(): pl.pallas_call(kernel, out_shape=tuple((jax.ShapeDtypeStruct(o, jnp.float...  19.3 us
    unnamed x46, local copies, waits for them, and re-layouts  11.2 us
    ppermute x5, waiting for transfers between devices, beside(): lax.ppermute(last, 'gx', forward)  10.5 us
    ppermute x4, waiting for transfers between devices, sum_over(): lax.ppermute(value, axis, [(i, i ^ hop) for i in range(count)])  8.22 us
    ppermute x4, starting transfers between devices, sum_over(): lax.ppermute(value, axis, [(i, i ^ hop) for i in range(count)])  5.13 us
  transfers between devices with their start and end apart: 14, of which 5 were waited for; matrix products, arithmetic and copies ran while one was open for 1% of the time, Pallas kernels for 18%

profile of v1, /device:TPU:0, one launch (start us, length us, event | category | flops | bytes accessed | tf_op | source)
XLA Modules:
  0.0 80.6 jit_solution(985979838898390327)
XLA Ops:
  0.6 1.1 %fusion = (f32[3,64,256]{2,1,0:T(8,128)S(1)}, f32[3,64,256]{2,1,0:T(8,128)S(1)}) fusion(f32[4,64,256]{2,1,0:T(8,128)} %own.1), kind=kLoop, calls=%fused_computation.4 | loop fusion | bytes 786432 | tf_op jit(solution)/shard_map/slice | solution.py:202
  1.8 0.0 copy-start.22
  1.8 5.5 %collective-permute-start.3 = (f32[3,64,256]{2,1,0:T(8,128)S(1)}, f32[3,64,256]{2,1,0:T(8,128)S(1)}, u32[]{:S(2)}, u32[]{:S(2)}) collective-permute-start(f32[3,64,256]{2,1,0:T(8,128)S(1)} %get-tuple-element.62), channel_id=1, source_target_pairs={{0,15},{1,0},{2,1},{3,2},{4,3},{5,4},{6,5},{7,6},{8,7},{9,8},{10,9... | collective-permute-start | bytes 589832 | tf_op jit(solution)/shard_map/ppermute | solution.py:196
  7.3 0.7 collective-permute-start.5
  8.0 0.0 collective-permute-start.4
  8.0 4.4 %collective-permute-start.1 = (f32[4,64,256]{2,1,0:T(8,128)S(1)}, f32[4,64,256]{2,1,0:T(8,128)S(1)}, u32[]{:S(2)}, u32[]{:S(2)}) collective-permute-start(f32[4,64,256]{2,1,0:T(8,128)S(1)} %get-tuple-element.61.own), channel_id=1, source_target_pairs={{0,15},{1,0},{2,1},{3,2},{4,3},{5,4},{6,5},{7,6},{8,7},{9,8},{10,9... | collective-permute-start | bytes 786440 | tf_op jit(solution)/shard_map/ppermute | solution.py:196
  12.5 0.0 collective-permute-start
  12.5 0.0 collective-permute-done.3.high
  12.5 0.1 collective-permute-start.2
  12.6 10.5 %collective-permute-done.2.low = f32[3,64,256]{2,1,0:T(8,128)S(1)} collective-permute-done((f32[3,64,256]{2,1,0:T(8,128)S(1)}, f32[3,64,256]{2,1,0:T(8,128)S(1)}, u32[]{:S(2)}, u32[]{:S(2)}) %collective-permute-start.2) | collective-permute-done | bytes 196640 | tf_op jit(solution)/shard_map/ppermute | solution.py:196
  23.1 0.8 %shard_map.50 = (f32[9,64,256]{2,1,0:T(8,128)S(1)}, f32[8,64,256]{2,1,0:T(8,128)S(1)}, f32[8,64,256]{2,1,0:T(8,128)S(1)}) custom-call(f32[3,64,256]{2,1,0:T(8,128)S(1)} %collective-permute-done.2.low, f32[4,64,256]{2,1,0:T(8,128)S(1)} %copy-done, f32[3,64,256]{2,1,0:T(8,128)S(1)} %collective-permute-done.3.high), custom_call_target="tpu_custom_call" | custom-call | flops 3932160 | bytes 2293760 | tf_op jit(solution)/shard_map/pallas_call | solution.py:167
  23.9 0.0 collective-permute-done.5.high
  23.9 0.0 collective-permute-done.4.low
  24.0 5.1 %shard_map.51 = (f32[4,64,256]{2,1,0:T(8,128)S(1)}, f32[3,64,256]{2,1,0:T(8,128)}, f32[3,64,256]{2,1,0:T(8,128)}, f32[6,64,256]{2,1,0:T(8,128)S(1)}, f32[6,64,25...) custom-call(f32[4,64,256]{2,1,0:T(8,128)S(1)} %collective-permute-do, ...), custom_call_target="tpu_custom_call" | custom-call | flops 26214400 | bytes 6103040 | tf_op jit(solution)/shard_map/pallas_call | solution.py:167
  29.1 0.7 copy-done.5
  29.8 0.7 copy-done.9
  30.5 0.0 collective-permute-start.8
  30.5 4.4 %collective-permute-start.9 = (f32[3,64,256]{2,1,0:T(8,128)}, f32[3,64,256]{2,1,0:T(8,128)}, u32[]{:S(2)}, u32[]{:S(2)}) collective-permute-start(f32[3,64,256]{2,1,0:T(8,128)} %get-tuple-element.46), channel_id=1, source_target_pairs={{0,15},{1,0},{2,1},{3,2},{4,3},{5,4},{6,5},{7,6},{8,7},{9,8},{10,9... | collective-permute-start | bytes 589832 | tf_op jit(solution)/shard_map/ppermute | solution.py:196
  34.9 0.0 collective-permute-done.1.high
  34.9 0.0 collective-permute-done.low
  34.9 5.1 %shard_map.52 = (f32[4,64,256]{2,1,0:T(8,128)S(1)}, f32[3,64,256]{2,1,0:T(8,128)}, f32[3,64,256]{2,1,0:T(8,128)}, f32[6,64,256]{2,1,0:T(8,128)S(1)}, f32[6,64,25...) custom-call(f32[4,64,256]{2,1,0:T(8,128)S(1)} %collective-permute-do, ...), custom_call_target="tpu_custom_call" | custom-call | flops 26214400 | bytes 6103040 | tf_op jit(solution)/shard_map/pallas_call | solution.py:167
  40.0 0.7 copy-done.1
  40.8 0.8 copy-done.3
  41.5 0.7 copy-done.11
  42.2 0.7 copy-done.13
  42.9 0.7 copy-done.15
  43.6 0.7 copy-done.17
  44.3 0.7 copy-done.19
  45.0 0.0 collective-permute-start.6
  45.0 4.4 %collective-permute-start.7 = (f32[3,64,256]{2,1,0:T(8,128)}, f32[3,64,256]{2,1,0:T(8,128)}, u32[]{:S(2)}, u32[]{:S(2)}) collective-permute-start(f32[3,64,256]{2,1,0:T(8,128)} %get-tuple-element.38), channel_id=1, source_target_pairs={{0,15},{1,0},{2,1},{3,2},{4,3},{5,4},{6,5},{7,6},{8,7},{9,8},{10,9... | collective-permute-start | bytes 589832 | tf_op jit(solution)/shard_map/ppermute | solution.py:196
  49.5 0.6 reduce_sum.9
  50.7 1.0 %collective-permute-start.10 = (f32[]{:T(128)}, f32[]{:T(128)}, u32[]{:S(2)}, u32[]{:S(2)}) collective-permute-start(f32[]{:T(128)} %mul_shard_map.3), channel_id=1, source_target_pairs={{0,1},{1,0},{2,3},{3,2},{4,5},{5,4},{6,7},{7,6},{8,9},{9,8},{10,11... | collective-permute-start | bytes 20 | tf_op jit(solution)/shard_map/ppermute | solution.py:184
  51.7 0.3 collective-permute-done.10
  52.6 1.4 %collective-permute-start.11 = (f32[]{:T(128)}, f32[]{:T(128)}, u32[]{:S(2)}, u32[]{:S(2)}) collective-permute-start(f32[]{:T(128)} %add.12), channel_id=1, source_target_pairs={{0,2},{1,3},{2,0},{3,1},{4,6},{5,7},{6,4},{7,5},{8,10},{9,11},{10,... | collective-permute-start | bytes 20 | tf_op jit(solution)/shard_map/ppermute | solution.py:184
  54.0 2.3 %collective-permute-done.11 = f32[]{:T(128)} collective-permute-done((f32[]{:T(128)}, f32[]{:T(128)}, u32[]{:S(2)}, u32[]{:S(2)}) %collective-permute-start.11) | collective-permute-done | bytes 36 | tf_op jit(solution)/shard_map/ppermute | solution.py:184
  56.8 1.4 %collective-permute-start.12 = (f32[]{:T(128)}, f32[]{:T(128)}, u32[]{:S(2)}, u32[]{:S(2)}) collective-permute-start(f32[]{:T(128)} %add.13), channel_id=1, source_target_pairs={{0,4},{1,5},{2,6},{3,7},{4,0},{5,1},{6,2},{7,3},{8,12},{9,13},{10,... | collective-permute-start | bytes 20 | tf_op jit(solution)/shard_map/ppermute | solution.py:184
  58.2 2.3 %collective-permute-done.12 = f32[]{:T(128)} collective-permute-done((f32[]{:T(128)}, f32[]{:T(128)}, u32[]{:S(2)}, u32[]{:S(2)}) %collective-permute-start.12) | collective-permute-done | bytes 36 | tf_op jit(solution)/shard_map/ppermute | solution.py:184
  61.1 1.4 %collective-permute-start.13 = (f32[]{:T(128)}, f32[]{:T(128)}, u32[]{:S(2)}, u32[]{:S(2)}) collective-permute-start(f32[]{:T(128)} %add.14), channel_id=1, source_target_pairs={{0,8},{1,9},{2,10},{3,11},{4,12},{5,13},{6,14},{7,15},{8,0},{9,1},... | collective-permute-start | bytes 20 | tf_op jit(solution)/shard_map/ppermute | solution.py:184
  62.5 3.2 %collective-permute-done.13 = f32[]{:T(128)} collective-permute-done((f32[]{:T(128)}, f32[]{:T(128)}, u32[]{:S(2)}, u32[]{:S(2)}) %collective-permute-start.13) | collective-permute-done | bytes 36 | tf_op jit(solution)/shard_map/ppermute | solution.py:184
  66.3 0.0 collective-permute-done.8.low
  66.3 0.9 %copy-done.6 = f32[4,64,256]{2,1,0:T(8,128)S(1)} copy-done((f32[4,64,256]{2,1,0:T(8,128)S(1)}, f32[4,64,256]{2,1,0:T(8,128)}, u32[]{:S(2)}) %copy-start.6) | copy-done | bytes 262168
  67.3 0.9 %copy-done.8 = f32[4,64,256]{2,1,0:T(8,128)S(1)} copy-done((f32[4,64,256]{2,1,0:T(8,128)S(1)}, f32[4,64,256]{2,1,0:T(8,128)}, u32[]{:S(2)}) %copy-start.8) | copy-done | bytes 262168
  68.2 0.9 %copy-done.10 = f32[4,64,256]{2,1,0:T(8,128)S(1)} copy-done((f32[4,64,256]{2,1,0:T(8,128)S(1)}, f32[4,64,256]{2,1,0:T(8,128)}, u32[]{:S(2)}) %copy-start.10) | copy-done | bytes 262168
  69.2 0.9 %copy-done.18 = f32[4,64,256]{2,1,0:T(8,128)S(1)} copy-done((f32[4,64,256]{2,1,0:T(8,128)S(1)}, f32[4,64,256]{2,1,0:T(8,128)}, u32[]{:S(2)}) %copy-start.18) | copy-done | bytes 262168
  70.1 0.9 %copy-done.20 = f32[4,64,256]{2,1,0:T(8,128)S(1)} copy-done((f32[4,64,256]{2,1,0:T(8,128)S(1)}, f32[4,64,256]{2,1,0:T(8,128)}, u32[]{:S(2)}) %copy-start.20) | copy-done | bytes 262168
  71.1 3.8 %shard_map.53 = (f32[4,64,256]{2,1,0:T(8,128)S(1)}, f32[4,64,256]{2,1,0:T(8,128)S(1)}, f32[4,64,256]{2,1,0:T(8,128)S(1)}) custom-call(f32[3,64,256]{2,1,0:T(8,128)} %collective-permute-done.8.low, f32[4,64,256]{2,1,0:T(8,128)S(1)} %copy-done.6, f32[3,64,256]{2,1,0:T(8,128)} %collective-permute-done.9.high, f32[9,64,256]{2,1,0:T(8,128)S(1)} %get-tuple-element.30.mx, ...), custom_call_target="tpu_custom_call" | custom-call | flops 19660800 | bytes 5570560 | tf_op jit(solution)/shard_map/pallas_call | solution.py:167
  74.8 0.0 collective-permute-done.6.low
  74.9 4.5 %shard_map.54 = f32[4,64,256]{2,1,0:T(8,128)} custom-call(f32[3,64,256]{2,1,0:T(8,128)} %collective-permute-done.6.low, f32[4,64,256]{2,1,0:T(8,128)S(1)} %copy-done.12, f32[3,64,256]{2,1,0:T(8,128)} %collective-permute-done.7.high, f32[9,64,256]{2,1,0:T(8,128)S(1)} %get-tuple-element.30.mx, f32[8,64,256]{2,1,0:T(8,128)S(1)} %get-tuple-element.31.my, ...), custom_call_target="tpu_custom_call" | custom-call | flops 19660800 | bytes 5046272 | tf_op jit(solution)/shard_map/pallas_call | solution.py:167
  (37 shorter events, 0.2 us)
Async XLA Ops:
  0.6 6.6 %copy-start.21 = (f32[2,4,64,256]{3,2,1,0:T(8,128)S(1)}, f32[2,4,64,256]{3,2,1,0:T(8,128)}, u32[]{:S(2)}) copy-start(f32[2,4,64,256]{3,2,1,0:T(8,128)} %param.3) | copy-start | bytes 1572868
  1.8 10.8 %copy-start.22 = (f32[2,4,64,256]{3,2,1,0:T(8,128)S(1)}, f32[2,4,64,256]{3,2,1,0:T(8,128)}, u32[]{:S(2)}) copy-start(f32[2,4,64,256]{3,2,1,0:T(8,128)} %param.4) | copy-start | bytes 1572868
  1.8 10.7 %collective-permute-start.3 = (f32[3,64,256]{2,1,0:T(8,128)S(1)}, f32[3,64,256]{2,1,0:T(8,128)S(1)}, u32[]{:S(2)}, u32[]{:S(2)}) collective-permute-start(f32[3,64,256]{2,1,0:T(8,128)S(1)} %get-tuple-element.62), channel_id=1, source_target_pairs={{0,15},{1,0},{2,1},{3,2},{4,3},{5,4},{6,5},{7,6},{8,7},{9,8},{10,9... | collective-permute-start | bytes 589832 | tf_op jit(solution)/shard_map/ppermute | solution.py:196
  7.3 16.6 %collective-permute-start.5 = (f32[4,64,256]{2,1,0:T(8,128)S(1)}, f32[4,64,256]{2,1,0:T(8,128)S(1)}, u32[]{:S(2)}, u32[]{:S(2)}) collective-permute-start(f32[4,64,256]{2,1,0:T(8,128)S(1)} %get-tuple-element.60.own), channel_id=1, source_target_pairs={{0,15},{1,0},{2,1},{3,2},{4,3},{5,4},{6,5},{7,6},{8,7},{9,8},{10,9... | collective-permute-start | bytes 786440 | tf_op jit(solution)/shard_map/ppermute | solution.py:196
  8.0 15.9 %collective-permute-start.4 = (f32[4,64,256]{2,1,0:T(8,128)S(1)}, f32[4,64,256]{2,1,0:T(8,128)S(1)}, u32[]{:S(2)}, u32[]{:S(2)}) collective-permute-start(f32[4,64,256]{2,1,0:T(8,128)S(1)} %get-tuple-element.60.own), channel_id=1, source_target_pairs={{0,1},{1,2},{2,3},{3,4},{4,5},{5,6},{6,7},{7,8},{8,9},{9,10},{10,1... | collective-permute-start | bytes 786440 | tf_op jit(solution)/shard_map/ppermute | solution.py:196
  8.0 26.9 %collective-permute-start.1 = (f32[4,64,256]{2,1,0:T(8,128)S(1)}, f32[4,64,256]{2,1,0:T(8,128)S(1)}, u32[]{:S(2)}, u32[]{:S(2)}) collective-permute-start(f32[4,64,256]{2,1,0:T(8,128)S(1)} %get-tuple-element.61.own), channel_id=1, source_target_pairs={{0,15},{1,0},{2,1},{3,2},{4,3},{5,4},{6,5},{7,6},{8,7},{9,8},{10,9... | collective-permute-start | bytes 786440 | tf_op jit(solution)/shard_map/ppermute | solution.py:196
  12.5 22.4 %collective-permute-start = (f32[4,64,256]{2,1,0:T(8,128)S(1)}, f32[4,64,256]{2,1,0:T(8,128)S(1)}, u32[]{:S(2)}, u32[]{:S(2)}) collective-permute-start(f32[4,64,256]{2,1,0:T(8,128)S(1)} %get-tuple-element.61.own), channel_id=1, source_target_pairs={{0,1},{1,2},{2,3},{3,4},{4,5},{5,6},{6,7},{7,8},{8,9},{9,10},{10,1... | collective-permute-start | bytes 786440 | tf_op jit(solution)/shard_map/ppermute | solution.py:196
  12.5 10.6 %copy-start = (f32[4,64,256]{2,1,0:T(8,128)S(1)}, f32[4,64,256]{2,1,0:T(8,128)}, u32[]{:S(2)}) copy-start(f32[4,64,256]{2,1,0:T(8,128)} %own.1) | copy-start | bytes 786436
  12.5 10.6 %collective-permute-start.2 = (f32[3,64,256]{2,1,0:T(8,128)S(1)}, f32[3,64,256]{2,1,0:T(8,128)S(1)}, u32[]{:S(2)}, u32[]{:S(2)}) collective-permute-start(f32[3,64,256]{2,1,0:T(8,128)S(1)} %get-tuple-element.63), channel_id=1, source_target_pairs={{0,1},{1,2},{2,3},{3,4},{4,5},{5,6},{6,7},{7,8},{8,9},{9,10},{10,1... | collective-permute-start | bytes 589832 | tf_op jit(solution)/shard_map/ppermute | solution.py:196
  29.1 0.7 copy-start.5
  29.8 0.7 copy-start.9
  30.5 9.5 %copy-start.7 = (f32[4,64,256]{2,1,0:T(8,128)}, f32[4,64,256]{2,1,0:T(8,128)S(1)}, u32[]{:S(2)}) copy-start(f32[4,64,256]{2,1,0:T(8,128)S(1)} %get-tuple-element.50.step_y0) | copy-start | bytes 786436
  30.5 35.8 %collective-permute-start.8 = (f32[3,64,256]{2,1,0:T(8,128)}, f32[3,64,256]{2,1,0:T(8,128)}, u32[]{:S(2)}, u32[]{:S(2)}) collective-permute-start(f32[3,64,256]{2,1,0:T(8,128)} %get-tuple-element.44), channel_id=1, source_target_pairs={{0,1},{1,2},{2,3},{3,4},{4,5},{5,6},{6,7},{7,8},{8,9},{9,10},{10,1... | collective-permute-start | bytes 589832 | tf_op jit(solution)/shard_map/ppermute | solution.py:196
  30.5 35.8 %collective-permute-start.9 = (f32[3,64,256]{2,1,0:T(8,128)}, f32[3,64,256]{2,1,0:T(8,128)}, u32[]{:S(2)}, u32[]{:S(2)}) collective-permute-start(f32[3,64,256]{2,1,0:T(8,128)} %get-tuple-element.46), channel_id=1, source_target_pairs={{0,15},{1,0},{2,1},{3,2},{4,3},{5,4},{6,5},{7,6},{8,7},{9,8},{10,9... | collective-permute-start | bytes 589832 | tf_op jit(solution)/shard_map/ppermute | solution.py:196
  40.0 0.7 copy-start.1
  40.8 0.8 copy-start.3
  41.5 0.7 copy-start.11
  42.2 0.7 copy-start.13
  42.9 0.7 copy-start.15
  43.6 0.7 copy-start.17
  44.3 0.7 copy-start.19
  45.0 29.8 %collective-permute-start.6 = (f32[3,64,256]{2,1,0:T(8,128)}, f32[3,64,256]{2,1,0:T(8,128)}, u32[]{:S(2)}, u32[]{:S(2)}) collective-permute-start(f32[3,64,256]{2,1,0:T(8,128)} %get-tuple-element.36), channel_id=1, source_target_pairs={{0,1},{1,2},{2,3},{3,4},{4,5},{5,6},{6,7},{7,8},{8,9},{9,10},{10,1... | collective-permute-start | bytes 589832 | tf_op jit(solution)/shard_map/ppermute | solution.py:196
  45.0 29.8 %collective-permute-start.7 = (f32[3,64,256]{2,1,0:T(8,128)}, f32[3,64,256]{2,1,0:T(8,128)}, u32[]{:S(2)}, u32[]{:S(2)}) collective-permute-start(f32[3,64,256]{2,1,0:T(8,128)} %get-tuple-element.38), channel_id=1, source_target_pairs={{0,15},{1,0},{2,1},{3,2},{4,3},{5,4},{6,5},{7,6},{8,7},{9,8},{10,9... | collective-permute-start | bytes 589832 | tf_op jit(solution)/shard_map/ppermute | solution.py:196
  50.7 1.3 %collective-permute-start.10 = (f32[]{:T(128)}, f32[]{:T(128)}, u32[]{:S(2)}, u32[]{:S(2)}) collective-permute-start(f32[]{:T(128)} %mul_shard_map.3), channel_id=1, source_target_pairs={{0,1},{1,0},{2,3},{3,2},{4,5},{5,4},{6,7},{7,6},{8,9},{9,8},{10,11... | collective-permute-start | bytes 20 | tf_op jit(solution)/shard_map/ppermute | solution.py:184
  52.6 3.7 %collective-permute-start.11 = (f32[]{:T(128)}, f32[]{:T(128)}, u32[]{:S(2)}, u32[]{:S(2)}) collective-permute-start(f32[]{:T(128)} %add.12), channel_id=1, source_target_pairs={{0,2},{1,3},{2,0},{3,1},{4,6},{5,7},{6,4},{7,5},{8,10},{9,11},{10,... | collective-permute-start | bytes 20 | tf_op jit(solution)/shard_map/ppermute | solution.py:184
  56.8 3.7 %collective-permute-start.12 = (f32[]{:T(128)}, f32[]{:T(128)}, u32[]{:S(2)}, u32[]{:S(2)}) collective-permute-start(f32[]{:T(128)} %add.13), channel_id=1, source_target_pairs={{0,4},{1,5},{2,6},{3,7},{4,0},{5,1},{6,2},{7,3},{8,12},{9,13},{10,... | collective-permute-start | bytes 20 | tf_op jit(solution)/shard_map/ppermute | solution.py:184
  61.1 4.6 %collective-permute-start.13 = (f32[]{:T(128)}, f32[]{:T(128)}, u32[]{:S(2)}, u32[]{:S(2)}) collective-permute-start(f32[]{:T(128)} %add.14), channel_id=1, source_target_pairs={{0,8},{1,9},{2,10},{3,11},{4,12},{5,13},{6,14},{7,15},{8,0},{9,1},... | collective-permute-start | bytes 20 | tf_op jit(solution)/shard_map/ppermute | solution.py:184
  66.3 1.0 %copy-start.6 = (f32[4,64,256]{2,1,0:T(8,128)S(1)}, f32[4,64,256]{2,1,0:T(8,128)}, u32[]{:S(2)}) copy-start(f32[4,64,256]{2,1,0:T(8,128)} %copy-done.5) | copy-start | bytes 786436
  67.2 0.9 %copy-start.8 = (f32[4,64,256]{2,1,0:T(8,128)S(1)}, f32[4,64,256]{2,1,0:T(8,128)}, u32[]{:S(2)}) copy-start(f32[4,64,256]{2,1,0:T(8,128)} %copy-done.7) | copy-start | bytes 786436
  68.2 0.9 %copy-start.10 = (f32[4,64,256]{2,1,0:T(8,128)S(1)}, f32[4,64,256]{2,1,0:T(8,128)}, u32[]{:S(2)}) copy-start(f32[4,64,256]{2,1,0:T(8,128)} %copy-done.9) | copy-start | bytes 786436
  69.2 0.9 %copy-start.18 = (f32[4,64,256]{2,1,0:T(8,128)S(1)}, f32[4,64,256]{2,1,0:T(8,128)}, u32[]{:S(2)}) copy-start(f32[4,64,256]{2,1,0:T(8,128)} %copy-done.17) | copy-start | bytes 786436
  70.1 0.9 %copy-start.20 = (f32[4,64,256]{2,1,0:T(8,128)S(1)}, f32[4,64,256]{2,1,0:T(8,128)}, u32[]{:S(2)}) copy-start(f32[4,64,256]{2,1,0:T(8,128)} %copy-done.19) | copy-start | bytes 786436
  71.1 3.8 %copy-start.2 = (f32[6,64,256]{2,1,0:T(8,128)S(1)}, f32[6,64,256]{2,1,0:T(8,128)}, u32[]{:S(2)}) copy-start(f32[6,64,256]{2,1,0:T(8,128)} %copy-done.1) | copy-start | bytes 1179652
  71.1 3.8 %copy-start.4 = (f32[6,64,256]{2,1,0:T(8,128)S(1)}, f32[6,64,256]{2,1,0:T(8,128)}, u32[]{:S(2)}) copy-start(f32[6,64,256]{2,1,0:T(8,128)} %copy-done.3) | copy-start | bytes 1179652
  71.1 3.8 %copy-start.12 = (f32[4,64,256]{2,1,0:T(8,128)S(1)}, f32[4,64,256]{2,1,0:T(8,128)}, u32[]{:S(2)}) copy-start(f32[4,64,256]{2,1,0:T(8,128)} %copy-done.11) | copy-start | bytes 786436
  71.1 3.8 %copy-start.14 = (f32[4,64,256]{2,1,0:T(8,128)S(1)}, f32[4,64,256]{2,1,0:T(8,128)}, u32[]{:S(2)}) copy-start(f32[4,64,256]{2,1,0:T(8,128)} %copy-done.13) | copy-start | bytes 786436
  71.1 3.8 %copy-start.16 = (f32[4,64,256]{2,1,0:T(8,128)S(1)}, f32[4,64,256]{2,1,0:T(8,128)}, u32[]{:S(2)}) copy-start(f32[4,64,256]{2,1,0:T(8,128)} %copy-done.15) | copy-start | bytes 786436

commit v2 on v0

v2 whole, which is shorter than its diff:
```python
import functools
import math

import jax
import jax.numpy as jnp
from jax import lax
from jax.experimental import pallas as pl
from jax.experimental.pallas import tpu as pltpu
from jax.sharding import PartitionSpec as P

stiffness = 0.5
time_step = 0.005
VMEM = pl.BlockSpec(memory_space=pltpu.VMEM)
LANES = 128
PAD = 8
CHUNK = 16


def chunks(ny):
    return range(0, ny, CHUNK)


def plain(ref, lead, row):
    return [
        ref[(*lead, pl.ds(row, CHUNK), pl.ds(at, LANES))] for at in range(0, ref.shape[-1], LANES)
    ]


def put_plain(ref, lead, row, value):
    for block, part in enumerate(value):
        ref[(*lead, pl.ds(row, CHUNK), pl.ds(block * LANES, LANES))] = part


def flat(ref, lead, row):
    return [ref[(*lead, block, pl.ds(row, CHUNK))] for block in range(ref.shape[-3])]


def put_flat(ref, lead, row, value):
    for block, part in enumerate(value):
        ref[(*lead, block, pl.ds(row, CHUNK))] = part


def padded(ref, lead, row, shift=0):
    return [ref[(*lead, block, pl.ds(PAD + row + shift, CHUNK))] for block in range(ref.shape[-3])]


def put_padded(ref, lead, row, value):
    ny = ref.shape[-2] - 2 * PAD
    for block, part in enumerate(value):
        ref[(*lead, block, pl.ds(PAD + row, CHUNK))] = part
        if row == 0:
            ref[(*lead, block, pl.ds(PAD + ny, 1))] = part[:1]
        if row + CHUNK == ny:
            ref[(*lead, block, pl.ds(PAD - 1, 1))] = part[CHUNK - 1 :]


def lane():
    return lax.broadcasted_iota(jnp.int32, (CHUNK, LANES), 1)


def after_z(value):
    turned = [pltpu.roll(part, LANES - 1, 1) for part in value]
    turned.append(turned[0])
    edge = lane() == LANES - 1
    return [jnp.where(edge, turned[at + 1], turned[at]) for at in range(len(value))]


def before_z(value):
    turned = [pltpu.roll(part, 1, 1) for part in value]
    edge = lane() == 0
    return [jnp.where(edge, turned[at - 1], turned[at]) for at in range(len(value))]


def each(function, *values):
    return [function(*parts) for parts in zip(*values)]


def beside(low, high, up, down, mid):
    return each(
        lambda a, b, c, d, e, f: (a + b) + (c + d) + (e + f),
        low, high, up, down, after_z(mid), before_z(mid),
    )


def potential(low, mid, high, up, down):
    return each(
        lambda c, total: c * (c * c + (6.0 * stiffness - 1.0)) - stiffness * total,
        mid, beside(low, high, up, down, mid),
    )


def flow_in_plane(faces, row, at, mid, up, down):
    _, my, mz, mz_low, m_all = faces
    return each(
        lambda a, b, c, d, e, u, v, w, x, y: (a * u + b * v) + (c * w + d * x) - e * y,
        padded(my, (at,), row), padded(my, (at,), row, -1), flat(mz, (at,), row),
        flat(mz_low, (at,), row), flat(m_all, (at,), row), up, down, after_z(mid), before_z(mid), mid,
    )


def add_product(total, a, b):
    return each(lambda t, x, y: t + x * y, total, a, b)


def sub(a, b):
    return each(lambda x, y: x - y, a, b)


def chem_kernel(low, own, high, chem0, conc):
    runs, n, ny, _ = own.shape

    def source(at):
        if at < 0:
            return low, at + low.shape[1]
        return (own, at) if at < n else (high, at - n)

    def one_run(run, carry):
        for row in chunks(ny):
            for at in range(-4, n + 4):
                ref, place = source(at)
                put_padded(conc, (at + 4,), row, plain(ref, (run, place), row))
        for row in chunks(ny):
            mids = [padded(conc, (at,), row) for at in range(n + 8)]
            for at in range(1, n + 7):
                value = potential(
                    mids[at - 1], mids[at], mids[at + 1],
                    padded(conc, (at,), row, 1), padded(conc, (at,), row, -1),
                )
                put_padded(chem0, (run, at - 1), row, value)
        return carry

    lax.fori_loop(0, runs, one_run, 0)


def forward_kernel(
    m_low, m_own, m_high, low, own, high, observed, chem0,
    mx, my, mz, mz_low, m_all, state1, chem1, adjoint2, first, last, miss_sum,
    mob, total,
):
    runs, n, ny, _ = own.shape
    pieces = [(m_low, at) for at in range(3)] + [(m_own, at) for at in range(n)] + [(m_high, at) for at in range(3)]
    for row in chunks(ny):
        for at, (ref, place) in enumerate(pieces):
            put_padded(mob, (at,), row, plain(ref, (place,), row))
    mean = lambda a, b: 0.5 * (a + b)
    for row in chunks(ny):
        face = None
        for at in range(n + 5):
            mid = padded(mob, (at,), row)
            face_low, face = face, each(mean, mid, padded(mob, (at + 1,), row))
            put_flat(mx, (at,), row, face)
            if at == 0:
                continue
            side_y = each(mean, mid, padded(mob, (at,), row, 1))
            side_y_low = each(mean, mid, padded(mob, (at,), row, -1))
            side_z = each(mean, mid, after_z(mid))
            side_z_low = each(mean, mid, before_z(mid))
            put_padded(my, (at - 1,), row, side_y)
            put_flat(mz, (at - 1,), row, side_z)
            put_flat(mz_low, (at - 1,), row, side_z_low)
            put_flat(m_all, (at - 1,), row, each(
                lambda a, b, c, d, e, f: (a + b) + (c + d) + (e + f),
                face, face_low, side_y, side_y_low, side_z, side_z_low,
            ))
    faces = (mx, my, mz, mz_low, m_all)
    total[...] = jnp.zeros_like(total)

    def source(at):
        if at < 0:
            return low, at + low.shape[1]
        return (own, at) if at < n else (high, at - n)

    def one_run(run, carry):
        for row in chunks(ny):
            mids = [padded(chem0, (run, at), row) for at in range(n + 6)]
            for at in range(n + 4):
                flow = flow_in_plane(
                    faces, row, at, mids[at + 1],
                    padded(chem0, (run, at + 1), row, 1), padded(chem0, (run, at + 1), row, -1),
                )
                flow = add_product(flow, flat(mx, (at,), row), mids[at])
                flow = add_product(flow, flat(mx, (at + 1,), row), mids[at + 2])
                ref, place = source(at - 2)
                value = each(lambda a, b: a + time_step * b, plain(ref, (run, place), row), flow)
                put_padded(state1, (run, at), row, value)
        for row in chunks(ny):
            mids = [padded(state1, (run, at), row) for at in range(n + 4)]
            for at in range(1, n + 3):
                value = potential(
                    mids[at - 1], mids[at], mids[at + 1],
                    padded(state1, (run, at), row, 1), padded(state1, (run, at), row, -1),
                )
                put_padded(chem1, (run, at - 1), row, value)
        squares = None
        for row in chunks(ny):
            mids = [padded(chem1, (run, at), row) for at in range(n + 2)]
            for at in range(n):
                flow = flow_in_plane(
                    faces, row, at + 2, mids[at + 1],
                    padded(chem1, (run, at + 1), row, 1), padded(chem1, (run, at + 1), row, -1),
                )
                flow = add_product(flow, flat(mx, (at + 2,), row), mids[at])
                flow = add_product(flow, flat(mx, (at + 3,), row), mids[at + 2])
                miss = each(
                    lambda a, b, c: a + time_step * b - c,
                    padded(state1, (run, at + 2), row), flow, plain(observed, (run, at), row),
                )
                for part in miss:
                    square = part * part
                    squares = square if squares is None else squares + square
                value = each(lambda a: a * (1.0 / runs), miss)
                put_padded(adjoint2, (run, at), row, value)
                if at < 3:
                    put_plain(first, (run, at), row, value)
                if at >= n - 3:
                    put_plain(last, (run, at - (n - 3)), row, value)
        total[...] += squares
        return carry

    lax.fori_loop(0, runs, one_run, 0)
    miss_sum[...] = (0.5 / runs) * jnp.sum(total[...], axis=0, keepdims=True)


def middle_kernel(
    mx, my, mz, mz_low, m_all, state1, chem0, chem1, adjoint2,
    flow_own, weight, step_z0, sum_x, sum_y, sum_z,
):
    runs, n = adjoint2.shape[:2]
    ny = flow_own.shape[-2] - 2 * PAD
    faces = (mx, my, mz, mz_low, m_all)
    sum_x[...] = jnp.zeros_like(sum_x)
    sum_y[...] = jnp.zeros_like(sum_y)
    sum_z[...] = jnp.zeros_like(sum_z)

    def one_run(run, carry):
        for row in chunks(ny):
            mids = [padded(adjoint2, (run, at), row) for at in range(n)]
            chems = [padded(chem1, (run, at + 1), row) for at in range(n)]
            for at in range(n):
                up = padded(adjoint2, (run, at), row, 1)
                flow = flow_in_plane(faces, row, at + 2, mids[at], up, padded(adjoint2, (run, at), row, -1))
                if at > 0:
                    flow = add_product(flow, flat(mx, (at + 2,), row), mids[at - 1])
                if at < n - 1:
                    flow = add_product(flow, flat(mx, (at + 3,), row), mids[at + 1])
                    face = add_product(
                        flat(sum_x, (at + 1,), row), sub(mids[at + 1], mids[at]), sub(chems[at + 1], chems[at])
                    )
                    put_flat(sum_x, (at + 1,), row, face)
                put_padded(flow_own, (run, at), row, flow)
                put_flat(sum_y, (at,), row, add_product(
                    flat(sum_y, (at,), row), sub(up, mids[at]),
                    sub(padded(chem1, (run, at + 1), row, 1), chems[at]),
                ))
                put_flat(sum_z, (at,), row, add_product(
                    flat(sum_z, (at,), row), sub(after_z(mids[at]), mids[at]),
                    sub(after_z(chems[at]), chems[at]),
                ))
                mid = padded(chem0, (run, at + 3), row)
                put_flat(step_z0, (run, at), row, sub(after_z(mid), mid))
            for at in range(n + 2):
                value = each(
                    lambda c: time_step * (3.0 * c * c + (6.0 * stiffness - 1.0)),
                    padded(state1, (run, at + 1), row),
                )
                put_flat(weight, (run, at), row, value)
        return carry

    lax.fori_loop(0, runs, one_run, 0)


def backward_kernel(
    low, high, mx, my, mz, mz_low, m_all, chem0, chem1, adjoint2, flow_own, weight, step_z0,
    sum_x_in, sum_y_in, sum_z_in, result, wide, flow_rim, adjoint1, sum_x, sum_y, sum_z,
):
    runs, n = adjoint2.shape[:2]
    ny = flow_own.shape[-2] - 2 * PAD
    faces = (mx, my, mz, mz_low, m_all)
    sum_x[...] = sum_x_in[...]
    sum_z[...] = sum_z_in[...]
    for row in chunks(ny):
        for at in range(n):
            put_padded(sum_y, (at,), row, flat(sum_y_in, (at,), row))

    def adj2(run, at):
        if at < 0:
            return wide, (at + 3,)
        return (adjoint2, (run, at)) if at < n else (wide, (at - n + 3,))

    def flow(run, at):
        if at <= 0:
            return flow_rim, (at + 2,)
        return (flow_own, (run, at)) if at < n - 1 else (flow_rim, (at - (n - 1) + 3,))

    def one_run(run, carry):
        for row in chunks(ny):
            for at in range(3):
                put_padded(wide, (at,), row, plain(low, (run, at), row))
                put_padded(wide, (at + 3,), row, plain(high, (run, at), row))
        for row in chunks(ny):
            mids = {at: padded(*adj2(run, at), row) for at in range(-3, n + 3)}
            for at in (-2, -1, n, n + 1):
                ref, lead = adj2(run, at)
                value = flow_in_plane(
                    faces, row, at + 2, mids[at], padded(ref, lead, row, 1), padded(ref, lead, row, -1)
                )
                value = add_product(value, flat(mx, (at + 2,), row), mids[at - 1])
                value = add_product(value, flat(mx, (at + 3,), row), mids[at + 1])
                put_padded(*flow(run, at), row, value)
            for at, side, face in ((0, -1, 2), (n - 1, n, n + 2)):
                value = add_product(
                    padded(flow_own, (run, at), row), flat(mx, (face,), row), mids[side]
                )
                put_padded(*flow(run, at), row, value)
        for row in chunks(ny):
            mids = {at: padded(*flow(run, at), row) for at in range(-2, n + 2)}
            for at in range(-1, n + 1):
                ref, lead = flow(run, at)
                total = beside(
                    mids[at - 1], mids[at + 1], padded(ref, lead, row, 1), padded(ref, lead, row, -1), mids[at]
                )
                value = each(
                    lambda a, w, f, t: a + w * f - (time_step * stiffness) * t,
                    padded(*adj2(run, at), row), flat(weight, (run, at + 1), row), mids[at], total,
                )
                put_padded(adjoint1, (at + 1,), row, value)
        for row in chunks(ny):
            mids = [padded(adjoint1, (at,), row) for at in range(n + 2)]
            chems = [padded(chem0, (run, at + 2), row) for at in range(n + 2)]
            for at in range(n + 1):
                face = add_product(
                    flat(sum_x, (at,), row), sub(mids[at + 1], mids[at]), sub(chems[at + 1], chems[at])
                )
                if at in (0, n):
                    face = add_product(
                        face, sub(padded(*adj2(run, at), row), padded(*adj2(run, at - 1), row)),
                        sub(padded(chem1, (run, at + 1), row), padded(chem1, (run, at), row)),
                    )
                put_flat(sum_x, (at,), row, face)
            for at in range(n):
                mid = mids[at + 1]
                put_padded(sum_y, (at,), row, add_product(
                    padded(sum_y, (at,), row), sub(padded(adjoint1, (at + 1,), row, 1), mid),
                    sub(padded(chem0, (run, at + 3), row, 1), chems[at + 1]),
                ))
                put_flat(sum_z, (at,), row, add_product(
                    flat(sum_z, (at,), row), sub(after_z(mid), mid), flat(step_z0, (run, at), row)
                ))
        return carry

    lax.fori_loop(0, runs, one_run, 0)
    for row in chunks(ny):
        for at in range(n):
            sides = flat(sum_z, (at,), row)
            value = each(
                lambda a, b, c, d, e, f: -0.5 * ((a + b) + (c + d) + (e + f)),
                flat(sum_x, (at,), row), flat(sum_x, (at + 1,), row),
                padded(sum_y, (at,), row), padded(sum_y, (at,), row, -1), sides, before_z(sides),
            )
            put_plain(result, (at,), row, value)


def misfit_kernel(parts, misfit):
    misfit[0] = jnp.sum(parts[...])


def call(kernel, outs, scratch, args, flops, out_space=None):
    moved = 4 * (sum(a.size for a in args) + sum(math.prod(o) for o in outs))
    return pl.pallas_call(
        kernel,
        out_shape=tuple(jax.ShapeDtypeStruct(o, jnp.float32) for o in outs),
        in_specs=[VMEM] * len(args),
        out_specs=tuple([out_space or VMEM] * len(outs)),
        scratch_shapes=[pltpu.VMEM(s, jnp.float32) for s in scratch],
        compiler_params=pltpu.CompilerParams(vmem_limit_bytes=16 * 1024 * 1024),
        cost_estimate=pl.CostEstimate(flops=flops, bytes_accessed=moved, transcendentals=0),
    )(*args)


def on_device(initial, observed, mobility):
    runs, n, ny, nz = initial.shape
    blocks = nz // LANES
    count = lax.axis_size("gx")
    forward = [(i, (i + 1) % count) for i in range(count)]
    backward = [(i, (i - 1) % count) for i in range(count)]
    cell = ny * nz

    def neighbours(first, last):
        return lax.ppermute(last, "gx", forward), lax.ppermute(first, "gx", backward)

    def lies(*lead):
        return (*lead, blocks, ny, LANES)

    def lies_padded(*lead):
        return (*lead, blocks, ny + 2 * PAD, LANES)

    low, high = neighbours(initial[:, :4], initial[:, n - 4 :])
    m_low, m_high = neighbours(mobility[:3], mobility[n - 3 :])
    (chem0,) = call(
        chem_kernel, (lies_padded(runs, n + 6),), (lies_padded(n + 8),), (low, initial, high),
        20 * runs * (n + 6) * cell,
    )
    *faces, state1, chem1, adjoint2, first, last, miss_sum = call(
        forward_kernel,
        (
            lies(n + 5), lies_padded(n + 4), lies(n + 4), lies(n + 4), lies(n + 4),
            lies_padded(runs, n + 4), lies_padded(runs, n + 2), lies_padded(runs, n),
            (runs, 3, ny, nz), (runs, 3, ny, nz), (1, LANES),
        ),
        (lies_padded(n + 6), (CHUNK, LANES)),
        (m_low, mobility, m_high, low, initial, high, observed, chem0),
        60 * runs * (n + 4) * cell,
    )
    low, high = neighbours(first, last)
    parts = lax.all_gather(miss_sum, "gx")
    flow_own, weight, step_z0, sum_x, sum_y, sum_z = call(
        middle_kernel,
        (
            lies_padded(runs, n), lies(runs, n + 2), lies(runs, n),
            lies(n + 1), lies(n), lies(n),
        ),
        (),
        (*faces, state1, chem0, chem1, adjoint2),
        40 * runs * n * cell,
    )
    (result,) = call(
        backward_kernel,
        ((n, ny, nz),),
        (
            lies_padded(6), lies_padded(6), lies_padded(n + 2),
            lies(n + 1), lies_padded(n), lies(n),
        ),
        (low, high, *faces, chem0, chem1, adjoint2, flow_own, weight, step_z0, sum_x, sum_y, sum_z),
        40 * runs * (n + 2) * cell,
    )
    (misfit,) = call(
        misfit_kernel, ((1,),), (), (parts,), parts.size, pl.BlockSpec(memory_space=pltpu.SMEM)
    )
    return (result, misfit)


def solution(mesh):
    placed = (
        P("group", "gx", None, None),
        P("group", "gx", None, None),
        P(("group", "gx"), None, None),
    )
    return jax.shard_map(
        on_device,
        mesh=mesh,
        in_specs=placed,
        out_specs=(P(("group", "gx"), None, None), P("group")),
        check_vma=False,
    )
```

time: 93.4 us -> 51.6 us (0.55)
  other arithmetic: 12.9 us -> 0 us
  local copies, waits for them, and re-layouts: 13.4 us -> 2.17 us
  blocking collectives: 31.2 us -> 20.7 us
  waiting for transfers between devices: 14.1 us -> 6.23 us
  Pallas kernels: 0 us -> 7.12 us
  starting transfers between devices: 19.5 us -> 14.5 us
  between operations: 2 us -> 0.69 us
    psum x1 -> x0, blocking collectives: 31.2 us -> none  [on_device(): misfit = lax.psum(0.5 / runs_here * jnp.sum(miss * miss), 'gx')]
    all_gather x0 -> x1, blocking collectives: none -> 20.7 us  [on_device(): parts = lax.all_gather(miss_sum, 'gx')]
    ppermute x10 -> x6, waiting for transfers between devices: 14.1 us -> 6.23 us  [the longest x3 4.84 us: neighbours(): lax.ppermute(last, 'gx', forward)]
    pallas_call x0 -> x5, Pallas kernels: none -> 7.12 us  [call(): pl.pallas_call(kernel, out_shape=tuple((jax.ShapeDtypeStruct(o, jnp.float...]
    slice x37 -> x1, local copies, waits for them, and re-layouts: 8.1 us -> 1.12 us  [on_device(): m_low, m_high = neighbours(mobility[:3], mobility[n - 3:])]
    ppermute x10 -> x6, starting transfers between devices: 19.5 us -> 14.5 us  [the longest x3 13.6 us: neighbours(): lax.ppermute(first, 'gx', backward)]
    mul x4 -> x0, other arithmetic: 4.37 us -> none  [the longest x2 2.46 us: transport(): (jnp.roll(m_mid, offset, axis_num) + m_mid) * (jnp.roll(f_mid, offset, ax...]
    reduce_sum x3 -> x0, other arithmetic: 4.02 us -> none  [the longest x2 2.76 us: sensitivity(): return -0.5 * jnp.sum(total, axis=0)]
  transfers between devices with their start and end apart: 10 -> 6, of which waited for: 4 -> 3; matrix products, arithmetic and copies ran while one was open for 9% -> 2% of each run, Pallas kernels for 0% -> 5%
where the time goes in v2:
time: 51.6 us; the launch traced here: 51.4 us
  blocking collectives  20.7 us (40%)
  starting transfers between devices  14.5 us (28%)
  Pallas kernels  7.12 us (14%)
  waiting for transfers between devices  6.23 us (12%)
  local copies, waits for them, and re-layouts  2.17 us (4%)
  between operations  0.69 us (1%)
    all_gather x1, blocking collectives, on_device(): parts = lax.all_gather(miss_sum, 'gx')  20.7 us
    ppermute x3, starting transfers between devices, neighbours(): lax.ppermute(first, 'gx', backward)  13.6 us
    pallas_call x5, Pallas kernels, call(): pl.pallas_call(kernel, out_shape=tuple((jax.ShapeDtypeStruct(o, jnp.float...  7.12 us
    ppermute x3, waiting for transfers between devices, neighbours(): lax.ppermute(last, 'gx', forward)  4.84 us
    ppermute x3, waiting for transfers between devices, neighbours(): lax.ppermute(first, 'gx', backward)  1.39 us
    slice x1, local copies, waits for them, and re-layouts, on_device(): m_low, m_high = neighbours(mobility[:3], mobility[n - 3:])  1.12 us
    unnamed x6, local copies, waits for them, and re-layouts  1.05 us
  transfers between devices with their start and end apart: 6, of which 3 were waited for; matrix products, arithmetic and copies ran while one was open for 2% of the time, Pallas kernels for 5%

profile of v2, /device:TPU:0, one launch (start us, length us, event | category | flops | bytes accessed | tf_op | source)
XLA Modules:
  0.0 51.4 jit_solution(14396788466417112557)
XLA Ops:
  0.6 5.5 %collective-permute-start.3 = (f32[2,4,64,256]{3,2,1,0:T(8,128)}, f32[2,4,64,256]{3,2,1,0:T(8,128)S(1)}, u32[]{:S(2)}, u32[]{:S(2)}) collective-permute-start(f32[2,4,64,256]{3,2,1,0:T(8,128)} %own.3), channel_id=1, source_target_pairs={{0,15},{1,0},{2,1},{3,2},{4,3},{5,4},{6,5},{7,6},{8,7},{9,8},{10,9... | collective-permute-start | bytes 1572872 | tf_op jit(solution)/shard_map/ppermute | solution.py:389
  6.1 0.0 collective-permute-start.2
  6.1 0.0 copy-start.1
  6.1 0.0 copy-start.2
  6.1 1.1 %fusion = (f32[3,64,256]{2,1,0:T(8,128)S(1)}, f32[3,64,256]{2,1,0:T(8,128)S(1)}) fusion(f32[4,64,256]{2,1,0:T(8,128)} %m_own.1), kind=kLoop, calls=%fused_computation | loop fusion | bytes 786432 | tf_op jit(solution)/shard_map/slice | solution.py:398
  7.3 4.5 %collective-permute-start.1 = (f32[3,64,256]{2,1,0:T(8,128)S(1)}, f32[3,64,256]{2,1,0:T(8,128)S(1)}, u32[]{:S(2)}, u32[]{:S(2)}) collective-permute-start(f32[3,64,256]{2,1,0:T(8,128)S(1)} %get-tuple-element.36), channel_id=1, source_target_pairs={{0,15},{1,0},{2,1},{3,2},{4,3},{5,4},{6,5},{7,6},{8,7},{9,8},{10,9... | collective-permute-start | bytes 589832 | tf_op jit(solution)/shard_map/ppermute | solution.py:389
  11.8 0.0 collective-permute-start
  11.8 1.4 %collective-permute-done.3.high = f32[2,4,64,256]{3,2,1,0:T(8,128)S(1)} collective-permute-done((f32[2,4,64,256]{3,2,1,0:T(8,128)}, f32[2,4,64,256]{3,2,1,0:T(8,128)S(1)}, u32[]{:S(2)}, u32[]{:S(2)}) %collective-permute-start.3) | collective-permute-done | bytes 524320 | tf_op jit(solution)/shard_map/ppermute | solution.py:389
  13.1 4.6 %collective-permute-done.2.low = f32[2,4,64,256]{3,2,1,0:T(8,128)S(1)} collective-permute-done((f32[2,4,64,256]{3,2,1,0:T(8,128)}, f32[2,4,64,256]{3,2,1,0:T(8,128)S(1)}, u32[]{:S(2)}, u32[]{:S(2)}) %collective-permute-start.2) | collective-permute-done | bytes 524320 | tf_op jit(solution)/shard_map/ppermute | solution.py:389
  17.7 0.0 copy-start
  17.7 1.0 %copy-done = f32[2,4,64,256]{3,2,1,0:T(8,128)S(1)} copy-done((f32[2,4,64,256]{3,2,1,0:T(8,128)S(1)}, f32[2,4,64,256]{3,2,1,0:T(8,128)}, u32[]{:S(2)}) %copy-start) | copy-done | bytes 524312
  18.8 0.8 %shard_map.50.chem0 = f32[2,10,2,80,128]{4,3,2,1,0:T(8,128)S(1)} custom-call(f32[2,4,64,256]{3,2,1,0:T(8,128)S(1)} %collective-permute-done.2.low, f32[2,4,64,256]{3,2,1,0:T(8,128)S(1)} %copy-done, f32[2,4,64,256]{3,2,1,0:T(8,128)S(1)} %collective-permute-done.3.high), custom_call_target="tpu_custom_call" | custom-call | flops 6553600 | bytes 3211264 | tf_op jit(solution)/shard_map/pallas_call | solution.py:369
  19.6 0.0 collective-permute-done.1.m_high
  19.6 0.2 collective-permute-done.m_low
  19.9 0.0 copy-done.1
  19.9 0.0 copy-done.2
  19.9 2.2 %shard_map.51 = (f32[9,2,64,128]{3,2,1,0:T(8,128)S(1)}, f32[8,2,80,128]{3,2,1,0:T(8,128)S(1)}, f32[8,2,64,128]{3,2,1,0:T(8,128)S(1)}, f32[8,2,64,128]{3,2,1,0:T(...) custom-call(f32[3,64,256]{2,1,0:T(8,128)S(1)} %collective-permute-do, ...), custom_call_target="tpu_custom_call" | custom-call | flops 15728640 | bytes 10945024 | tf_op jit(solution)/shard_map/pallas_call | solution.py:369
  22.1 0.9 %collective-permute-start.4 = (f32[2,3,64,256]{3,2,1,0:T(8,128)S(1)}, f32[2,3,64,256]{3,2,1,0:T(8,128)S(1)}, u32[]{:S(2)}, u32[]{:S(2)}) collective-permute-start(f32[2,3,64,256]{3,2,1,0:T(8,128)S(1)} %get-tuple-element.19), channel_id=1, source_target_pairs={{0,1},{1,2},{2,3},{3,4},{4,5},{5,6},{6,7},{7,8},{8,9},{9,10},{10,1... | collective-permute-start | bytes 1179656 | tf_op jit(solution)/shard_map/ppermute | solution.py:389
  22.9 3.6 %collective-permute-start.5 = (f32[2,3,64,256]{3,2,1,0:T(8,128)S(1)}, f32[2,3,64,256]{3,2,1,0:T(8,128)S(1)}, u32[]{:S(2)}, u32[]{:S(2)}) collective-permute-start(f32[2,3,64,256]{3,2,1,0:T(8,128)S(1)} %get-tuple-element.20), channel_id=1, source_target_pairs={{0,15},{1,0},{2,1},{3,2},{4,3},{5,4},{6,5},{7,6},{8,7},{9,8},{10,9... | collective-permute-start | bytes 1179656 | tf_op jit(solution)/shard_map/ppermute | solution.py:389
  26.6 20.7 %all-gather.1.parts = f32[16,1,128]{2,1,0:T(1,128)S(1)} all-gather(f32[1,1,128]{2,1,0:T(1,128)S(1)} %bitcast.1), channel_id=2, replica_groups=mesh['group'=2,'gx'=16] {'gx'}, dimensions={0}, use_global_device_ids=true | all-gather | bytes 8704 | tf_op jit(solution)/shard_map/all_gather | solution.py:415
  47.3 0.6 %shard_map.54 = f32[1]{0:T(128)} custom-call(f32[16,1,128]{2,1,0:T(1,128)S(1)} %all-gather.1.parts), custom_call_target="tpu_custom_call" | custom-call | flops 2048 | bytes 8196 | tf_op jit(solution)/shard_map/pallas_call | solution.py:369
  47.9 1.0 %shard_map.52 = (f32[2,4,2,80,128]{4,3,2,1,0:T(8,128)S(1)}, f32[2,6,2,64,128]{4,3,2,1,0:T(8,128)S(1)}, f32[2,4,2,64,128]{4,3,2,1,0:T(8,128)S(1)}, f32[5,2,64,128...) custom-call(f32[9,2,64,128]{3,2,1,0:T(8,128)S(1)} %get-tuple-element.21.mx, ...), custom_call_target="tpu_custom_call" | custom-call | flops 5242880 | bytes 10223616 | tf_op jit(solution)/shard_map/pallas_call | solution.py:369
  49.0 0.0 collective-permute-done.4.low
  49.0 0.0 collective-permute-done.5.high
  49.0 2.4 %shard_map.53 = f32[4,64,256]{2,1,0:T(8,128)} custom-call(f32[2,3,64,256]{3,2,1,0:T(8,128)S(1)} %collective-permute-done.4.low, f32[2,3,64,256]{3,2,1,0:T(8,128)S(1)} %collective-permute-done.5.high, f32[9,2,64,128]{3,2,1,0:T(8,128)S(1)} %get-tuple-element.21.mx, f32[8,2,80,128]{3,2,1,0:T(8,128)S(1)} %get-tuple-element.22.my, ...), custom_call_target="tpu_custom_call" | custom-call | flops 7864320 | bytes 9961472 | tf_op jit(solution)/shard_map/pallas_call | solution.py:369
Async XLA Ops:
  0.6 12.5 %collective-permute-start.3 = (f32[2,4,64,256]{3,2,1,0:T(8,128)}, f32[2,4,64,256]{3,2,1,0:T(8,128)S(1)}, u32[]{:S(2)}, u32[]{:S(2)}) collective-permute-start(f32[2,4,64,256]{3,2,1,0:T(8,128)} %own.3), channel_id=1, source_target_pairs={{0,15},{1,0},{2,1},{3,2},{4,3},{5,4},{6,5},{7,6},{8,7},{9,8},{10,9... | collective-permute-start | bytes 1572872 | tf_op jit(solution)/shard_map/ppermute | solution.py:389
  6.1 11.6 %collective-permute-start.2 = (f32[2,4,64,256]{3,2,1,0:T(8,128)}, f32[2,4,64,256]{3,2,1,0:T(8,128)S(1)}, u32[]{:S(2)}, u32[]{:S(2)}) collective-permute-start(f32[2,4,64,256]{3,2,1,0:T(8,128)} %own.3), channel_id=1, source_target_pairs={{0,1},{1,2},{2,3},{3,4},{4,5},{5,6},{6,7},{7,8},{8,9},{9,10},{10,1... | collective-permute-start | bytes 1572872 | tf_op jit(solution)/shard_map/ppermute | solution.py:389
  6.1 13.7 %copy-start.1 = (f32[4,64,256]{2,1,0:T(8,128)S(1)}, f32[4,64,256]{2,1,0:T(8,128)}, u32[]{:S(2)}) copy-start(f32[4,64,256]{2,1,0:T(8,128)} %m_own.1) | copy-start | bytes 786436
  6.1 13.7 %copy-start.2 = (f32[2,4,64,256]{3,2,1,0:T(8,128)S(1)}, f32[2,4,64,256]{3,2,1,0:T(8,128)}, u32[]{:S(2)}) copy-start(f32[2,4,64,256]{3,2,1,0:T(8,128)} %observed.1) | copy-start | bytes 1572868
  7.3 12.3 %collective-permute-start.1 = (f32[3,64,256]{2,1,0:T(8,128)S(1)}, f32[3,64,256]{2,1,0:T(8,128)S(1)}, u32[]{:S(2)}, u32[]{:S(2)}) collective-permute-start(f32[3,64,256]{2,1,0:T(8,128)S(1)} %get-tuple-element.36), channel_id=1, source_target_pairs={{0,15},{1,0},{2,1},{3,2},{4,3},{5,4},{6,5},{7,6},{8,7},{9,8},{10,9... | collective-permute-start | bytes 589832 | tf_op jit(solution)/shard_map/ppermute | solution.py:389
  11.8 8.1 %collective-permute-start = (f32[3,64,256]{2,1,0:T(8,128)S(1)}, f32[3,64,256]{2,1,0:T(8,128)S(1)}, u32[]{:S(2)}, u32[]{:S(2)}) collective-permute-start(f32[3,64,256]{2,1,0:T(8,128)S(1)} %get-tuple-element.37), channel_id=1, source_target_pairs={{0,1},{1,2},{2,3},{3,4},{4,5},{5,6},{6,7},{7,8},{8,9},{9,10},{10,1... | collective-permute-start | bytes 589832 | tf_op jit(solution)/shard_map/ppermute | solution.py:389
  17.7 1.0 %copy-start = (f32[2,4,64,256]{3,2,1,0:T(8,128)S(1)}, f32[2,4,64,256]{3,2,1,0:T(8,128)}, u32[]{:S(2)}) copy-start(f32[2,4,64,256]{3,2,1,0:T(8,128)} %own.3) | copy-start | bytes 1572868
  22.1 26.9 %collective-permute-start.4 = (f32[2,3,64,256]{3,2,1,0:T(8,128)S(1)}, f32[2,3,64,256]{3,2,1,0:T(8,128)S(1)}, u32[]{:S(2)}, u32[]{:S(2)}) collective-permute-start(f32[2,3,64,256]{3,2,1,0:T(8,128)S(1)} %get-tuple-element.19), channel_id=1, source_target_pairs={{0,1},{1,2},{2,3},{3,4},{4,5},{5,6},{6,7},{7,8},{8,9},{9,10},{10,1... | collective-permute-start | bytes 1179656 | tf_op jit(solution)/shard_map/ppermute | solution.py:389
  22.9 26.0 %collective-permute-start.5 = (f32[2,3,64,256]{3,2,1,0:T(8,128)S(1)}, f32[2,3,64,256]{3,2,1,0:T(8,128)S(1)}, u32[]{:S(2)}, u32[]{:S(2)}) collective-permute-start(f32[2,3,64,256]{3,2,1,0:T(8,128)S(1)} %get-tuple-element.20), channel_id=1, source_target_pairs={{0,15},{1,0},{2,1},{3,2},{4,3},{5,4},{6,5},{7,6},{8,7},{9,8},{10,9... | collective-permute-start | bytes 1179656 | tf_op jit(solution)/shard_map/ppermute | solution.py:389

commit v3 on v2

--- a/solution.py
+++ b/solution.py
@@ -11,6 +11,7 @@
 stiffness = 0.5
 time_step = 0.005
 VMEM = pl.BlockSpec(memory_space=pltpu.VMEM)
+SMEM = pl.BlockSpec(memory_space=pltpu.SMEM)
 LANES = 128
 PAD = 8
 CHUNK = 16
@@ -106,27 +107,45 @@
     return each(lambda x, y: x - y, a, b)
 
 
-def chem_kernel(low, own, high, chem0, conc):
-    runs, n, ny, _ = own.shape
-
-    def source(at):
+def own_kernel(initial, mobility, conc, mob, first, last):
+    runs, n, ny, _ = initial.shape
+
+    def one_run(run, carry):
+        for row in chunks(ny):
+            for at in range(n):
+                put_padded(conc, (run, at), row, plain(initial, (run, at), row))
+        return carry
+
+    lax.fori_loop(0, runs, one_run, 0)
+    for row in chunks(ny):
+        for at in range(n):
+            put_padded(mob, (at,), row, plain(mobility, (at,), row))
+    first[...] = mobility[:3]
+    last[...] = mobility[n - 3 :]
+
+
+def chem_kernel(low, own, high, chem0, rim):
+    runs, n = own.shape[:2]
+    ny = low.shape[2]
+
+    def conc(run, at):
         if at < 0:
-            return low, at + low.shape[1]
-        return (own, at) if at < n else (high, at - n)
+            return rim, (at + 4,)
+        return (own, (run, at)) if at < n else (rim, (at - n + 4,))
 
     def one_run(run, carry):
         for row in chunks(ny):
-            for at in range(-4, n + 4):
-                ref, place = source(at)
-                put_padded(conc, (at + 4,), row, plain(ref, (run, place), row))
-        for row in chunks(ny):
-            mids = [padded(conc, (at,), row) for at in range(n + 8)]
-            for at in range(1, n + 7):
+            for at in range(4):
+                put_padded(rim, (at,), row, plain(low, (run, at), row))
+                put_padded(rim, (at + 4,), row, plain(high, (run, at), row))
+        for row in chunks(ny):
+            mids = {at: padded(*conc(run, at), row) for at in range(-4, n + 4)}
+            for at in range(-3, n + 3):
+                ref, lead = conc(run, at)
                 value = potential(
-                    mids[at - 1], mids[at], mids[at + 1],
-                    padded(conc, (at,), row, 1), padded(conc, (at,), row, -1),
-                )
-                put_padded(chem0, (run, at - 1), row, value)
+                    mids[at - 1], mids[at], mids[at + 1], padded(ref, lead, row, 1), padded(ref, lead, row, -1)
+                )
+                put_padded(chem0, (run, at + 3), row, value)
         return carry
 
     lax.fori_loop(0, runs, one_run, 0)
@@ -135,24 +154,30 @@
 def forward_kernel(
     m_low, m_own, m_high, low, own, high, observed, chem0,
     mx, my, mz, mz_low, m_all, state1, chem1, adjoint2, first, last, miss_sum,
-    mob, total,
+    rim, total,
 ):
-    runs, n, ny, _ = own.shape
-    pieces = [(m_low, at) for at in range(3)] + [(m_own, at) for at in range(n)] + [(m_high, at) for at in range(3)]
+    runs, n, ny, _ = observed.shape
     for row in chunks(ny):
-        for at, (ref, place) in enumerate(pieces):
-            put_padded(mob, (at,), row, plain(ref, (place,), row))
+        for at in range(3):
+            put_padded(rim, (at,), row, plain(m_low, (at,), row))
+            put_padded(rim, (at + 3,), row, plain(m_high, (at,), row))
+
+    def mob(at):
+        if at < 3:
+            return rim, (at,)
+        return (m_own, (at - 3,)) if at < n + 3 else (rim, (at - n,))
+
     mean = lambda a, b: 0.5 * (a + b)
     for row in chunks(ny):
         face = None
         for at in range(n + 5):
-            mid = padded(mob, (at,), row)
-            face_low, face = face, each(mean, mid, padded(mob, (at + 1,), row))
+            mid = padded(*mob(at), row)
+            face_low, face = face, each(mean, mid, padded(*mob(at + 1), row))
             put_flat(mx, (at,), row, face)
             if at == 0:
                 continue
-            side_y = each(mean, mid, padded(mob, (at,), row, 1))
-            side_y_low = each(mean, mid, padded(mob, (at,), row, -1))
+            side_y = each(mean, mid, padded(*mob(at), row, 1))
+            side_y_low = each(mean, mid, padded(*mob(at), row, -1))
             side_z = each(mean, mid, after_z(mid))
             side_z_low = each(mean, mid, before_z(mid))
             put_padded(my, (at - 1,), row, side_y)
@@ -165,10 +190,10 @@
     faces = (mx, my, mz, mz_low, m_all)
     total[...] = jnp.zeros_like(total)
 
-    def source(at):
-        if at < 0:
-            return low, at + low.shape[1]
-        return (own, at) if at < n else (high, at - n)
+    def conc(run, at, row):
+        if 0 <= at < n:
+            return padded(own, (run, at), row)
+        return plain(low, (run, at + 4), row) if at < 0 else plain(high, (run, at - n), row)
 
     def one_run(run, carry):
         for row in chunks(ny):
@@ -180,8 +205,7 @@
                 )
                 flow = add_product(flow, flat(mx, (at,), row), mids[at])
                 flow = add_product(flow, flat(mx, (at + 1,), row), mids[at + 2])
-                ref, place = source(at - 2)
-                value = each(lambda a, b: a + time_step * b, plain(ref, (run, place), row), flow)
+                value = each(lambda a, b: a + time_step * b, conc(run, at - 2, row), flow)
                 put_padded(state1, (run, at), row, value)
         for row in chunks(ny):
             mids = [padded(state1, (run, at), row) for at in range(n + 4)]
@@ -222,12 +246,13 @@
 
 
 def middle_kernel(
-    mx, my, mz, mz_low, m_all, state1, chem0, chem1, adjoint2,
-    flow_own, weight, step_z0, sum_x, sum_y, sum_z,
+    mx, my, mz, mz_low, m_all, state1, chem0, chem1, adjoint2, miss_sum,
+    shares, flow_own, weight, step_z0, sum_x, sum_y, sum_z,
 ):
     runs, n = adjoint2.shape[:2]
     ny = flow_own.shape[-2] - 2 * PAD
     faces = (mx, my, mz, mz_low, m_all)
+    shares[...] = jnp.broadcast_to(miss_sum[...][None], shares.shape)
     sum_x[...] = jnp.zeros_like(sum_x)
     sum_y[...] = jnp.zeros_like(sum_y)
     sum_z[...] = jnp.zeros_like(sum_z)
@@ -271,11 +296,12 @@
 
 def backward_kernel(
     low, high, mx, my, mz, mz_low, m_all, chem0, chem1, adjoint2, flow_own, weight, step_z0,
-    sum_x_in, sum_y_in, sum_z_in, result, wide, flow_rim, adjoint1, sum_x, sum_y, sum_z,
+    sum_x_in, sum_y_in, sum_z_in, shares, result, misfit, wide, flow_rim, adjoint1, sum_x, sum_y, sum_z,
 ):
     runs, n = adjoint2.shape[:2]
     ny = flow_own.shape[-2] - 2 * PAD
     faces = (mx, my, mz, mz_low, m_all)
+    misfit[0] = jnp.sum(shares[...])
     sum_x[...] = sum_x_in[...]
     sum_z[...] = sum_z_in[...]
     for row in chunks(ny):
@@ -360,17 +386,13 @@
             put_plain(result, (at,), row, value)
 
 
-def misfit_kernel(parts, misfit):
-    misfit[0] = jnp.sum(parts[...])
-
-
-def call(kernel, outs, scratch, args, flops, out_space=None):
+def call(kernel, outs, scratch, args, flops, scalar=None):
     moved = 4 * (sum(a.size for a in args) + sum(math.prod(o) for o in outs))
     return pl.pallas_call(
         kernel,
         out_shape=tuple(jax.ShapeDtypeStruct(o, jnp.float32) for o in outs),
         in_specs=[VMEM] * len(args),
-        out_specs=tuple([out_space or VMEM] * len(outs)),
+        out_specs=tuple(SMEM if at == scalar else VMEM for at in range(len(outs))),
         scratch_shapes=[pltpu.VMEM(s, jnp.float32) for s in scratch],
         compiler_params=pltpu.CompilerParams(vmem_limit_bytes=16 * 1024 * 1024),
         cost_estimate=pl.CostEstimate(flops=flops, bytes_accessed=moved, transcendentals=0),
@@ -395,9 +417,16 @@
         return (*lead, blocks, ny + 2 * PAD, LANES)
 
     low, high = neighbours(initial[:, :4], initial[:, n - 4 :])
-    m_low, m_high = neighbours(mobility[:3], mobility[n - 3 :])
+    conc, mob, first, last = call(
+        own_kernel,
+        (lies_padded(runs, n), lies_padded(n), (3, ny, nz), (3, ny, nz)),
+        (),
+        (initial, mobility),
+        runs * n * cell,
+    )
+    m_low, m_high = neighbours(first, last)
     (chem0,) = call(
-        chem_kernel, (lies_padded(runs, n + 6),), (lies_padded(n + 8),), (low, initial, high),
+        chem_kernel, (lies_padded(runs, n + 6),), (lies_padded(8),), (low, conc, high),
         20 * runs * (n + 6) * cell,
     )
     *faces, state1, chem1, adjoint2, first, last, miss_sum = call(
@@ -407,36 +436,36 @@
             lies_padded(runs, n + 4), lies_padded(runs, n + 2), lies_padded(runs, n),
             (runs, 3, ny, nz), (runs, 3, ny, nz), (1, LANES),
         ),
-        (lies_padded(n + 6), (CHUNK, LANES)),
-        (m_low, mobility, m_high, low, initial, high, observed, chem0),
+        (lies_padded(6), (CHUNK, LANES)),
+        (m_low, mob, m_high, low, conc, high, observed, chem0),
         60 * runs * (n + 4) * cell,
     )
     low, high = neighbours(first, last)
-    parts = lax.all_gather(miss_sum, "gx")
-    flow_own, weight, step_z0, sum_x, sum_y, sum_z = call(
+    shares, flow_own, weight, step_z0, sum_x, sum_y, sum_z = call(
         middle_kernel,
         (
-            lies_padded(runs, n), lies(runs, n + 2), lies(runs, n),
+            (count, 1, LANES), lies_padded(runs, n), lies(runs, n + 2), lies(runs, n),
             lies(n + 1), lies(n), lies(n),
         ),
         (),
-        (*faces, state1, chem0, chem1, adjoint2),
+        (*faces, state1, chem0, chem1, adjoint2, miss_sum),
         40 * runs * n * cell,
     )
-    (result,) = call(
+    shares = lax.all_to_all(shares, "gx", 0, 0)
+    return call(
         backward_kernel,
-        ((n, ny, nz),),
+        ((n, ny, nz), (1,)),
         (
             lies_padded(6), lies_padded(6), lies_padded(n + 2),
             lies(n + 1), lies_padded(n), lies(n),
         ),
-        (low, high, *faces, chem0, chem1, adjoint2, flow_own, weight, step_z0, sum_x, sum_y, sum_z),
+        (
+            low, high, *faces, chem0, chem1, adjoint2, flow_own, weight, step_z0,
+            sum_x, sum_y, sum_z, shares,
+        ),
         40 * runs * (n + 2) * cell,
-    )
-    (misfit,) = call(
-        misfit_kernel, ((1,),), (), (parts,), parts.size, pl.BlockSpec(memory_space=pltpu.SMEM)
-    )
-    return (result, misfit)
+        scalar=1,
+    )
 
 
 def solution(mesh):

time: 51.6 us -> 41 us (0.79)
  blocking collectives: 20.7 us -> 10.4 us
    all_gather x1 -> x0, blocking collectives: 20.7 us -> none  [on_device(): parts = lax.all_gather(miss_sum, 'gx')]
    all_to_all x0 -> x1, blocking collectives: none -> 10.4 us  [on_device(): shares = lax.all_to_all(shares, 'gx', 0, 0)]
    slice x1 -> x0, local copies, waits for them, and re-layouts: 1.12 us -> none  [on_device(): m_low, m_high = neighbours(mobility[:3], mobility[n - 3:])]
    ppermute x3, waiting for transfers between devices: 1.39 us -> 0.34 us  [neighbours(): lax.ppermute(first, 'gx', backward)]
    ppermute x3, waiting for transfers between devices: 4.84 us -> 5.89 us  [neighbours(): lax.ppermute(last, 'gx', forward)]
    unnamed x6, local copies, waits for them, and re-layouts: 1.05 us -> 2.02 us
  transfers between devices with their start and end apart: 6 -> 6, of which waited for: 3 -> 3; matrix products, arithmetic and copies ran while one was open for 2% -> 0% of each run, Pallas kernels for 5% -> 5%
where the time goes in v3:
time: 41 us; the launch traced here: 40.7 us
  starting transfers between devices  14.5 us (35%)
  blocking collectives  10.4 us (25%)
  Pallas kernels  6.82 us (17%)
  waiting for transfers between devices  6.23 us (15%)
  local copies, waits for them, and re-layouts  2.02 us (5%)
  between operations  0.66 us (2%)
    ppermute x3, starting transfers between devices, neighbours(): lax.ppermute(first, 'gx', backward)  13.6 us
    all_to_all x1, blocking collectives, on_device(): shares = lax.all_to_all(shares, 'gx', 0, 0)  10.4 us
    pallas_call x5, Pallas kernels, call(): pl.pallas_call(kernel, out_shape=tuple((jax.ShapeDtypeStruct(o, jnp.float...  6.82 us
    ppermute x3, waiting for transfers between devices, neighbours(): lax.ppermute(last, 'gx', forward)  5.89 us
    unnamed x6, local copies, waits for them, and re-layouts  2.02 us
    ppermute x3, starting transfers between devices, neighbours(): lax.ppermute(last, 'gx', forward)  0.92 us
  transfers between devices with their start and end apart: 6, of which 3 were waited for; matrix products, arithmetic and copies ran while one was open for 0% of the time, Pallas kernels for 5%

profile of v3, /device:TPU:0, one launch (start us, length us, event | category | flops | bytes accessed | tf_op | source)
XLA Modules:
  0.0 40.7 jit_solution(14081762943982316198)
XLA Ops:
  0.6 5.5 %collective-permute-start.3 = (f32[2,4,64,256]{3,2,1,0:T(8,128)}, f32[2,4,64,256]{3,2,1,0:T(8,128)S(1)}, u32[]{:S(2)}, u32[]{:S(2)}) collective-permute-start(f32[2,4,64,256]{3,2,1,0:T(8,128)} %initial.1), channel_id=1, source_target_pairs={{0,15},{1,0},{2,1},{3,2},{4,3},{5,4},{6,5},{7,6},{8,7},{9,8},{10,9... | collective-permute-start | bytes 1572872 | tf_op jit(solution)/shard_map/ppermute | solution.py:411
  6.1 0.0 collective-permute-start.2
  6.1 0.0 copy-start.1
  6.1 1.1 %copy-done.1 = f32[2,4,64,256]{3,2,1,0:T(8,128)S(1)} copy-done((f32[2,4,64,256]{3,2,1,0:T(8,128)S(1)}, f32[2,4,64,256]{3,2,1,0:T(8,128)}, u32[]{:S(2)}) %copy-start.1) | copy-done | bytes 524312
  7.2 0.0 copy-start.2
  7.2 0.9 %copy-done.2 = f32[4,64,256]{2,1,0:T(8,128)S(1)} copy-done((f32[4,64,256]{2,1,0:T(8,128)S(1)}, f32[4,64,256]{2,1,0:T(8,128)}, u32[]{:S(2)}) %copy-start.2) | copy-done | bytes 262168
  8.2 0.1 shard_map.50
  8.2 0.1 collective-permute-start
  8.3 4.5 %collective-permute-start.1 = (f32[3,64,256]{2,1,0:T(8,128)S(1)}, f32[3,64,256]{2,1,0:T(8,128)S(1)}, u32[]{:S(2)}, u32[]{:S(2)}) collective-permute-start(f32[3,64,256]{2,1,0:T(8,128)S(1)} %get-tuple-element.26), channel_id=1, source_target_pairs={{0,15},{1,0},{2,1},{3,2},{4,3},{5,4},{6,5},{7,6},{8,7},{9,8},{10,9... | collective-permute-start | bytes 589832 | tf_op jit(solution)/shard_map/ppermute | solution.py:411
  12.8 0.3 collective-permute-done.3.high
  13.1 4.6 %collective-permute-done.2.low = f32[2,4,64,256]{3,2,1,0:T(8,128)S(1)} collective-permute-done((f32[2,4,64,256]{3,2,1,0:T(8,128)}, f32[2,4,64,256]{3,2,1,0:T(8,128)S(1)}, u32[]{:S(2)}, u32[]{:S(2)}) %collective-permute-start.2) | collective-permute-done | bytes 524320 | tf_op jit(solution)/shard_map/ppermute | solution.py:411
  17.7 0.0 copy-start
  17.7 0.8 %shard_map.51.chem0 = f32[2,10,2,80,128]{4,3,2,1,0:T(8,128)S(1)} custom-call(f32[2,4,64,256]{3,2,1,0:T(8,128)S(1)} %collective-permute-done.2.low, f32[2,4,2,80,128]{4,3,2,1,0:T(8,128)S(1)} %get-tuple-element.27.own, f32[2,4,64,256]{3,2,1,0:T(8,128)S(1)} %collective-permute-done.3.high), custom_call_target="tpu_custom_call" | custom-call | flops 6553600 | bytes 3342336 | tf_op jit(solution)/shard_map/pallas_call | solution.py:391
  18.6 1.3 %collective-permute-done.m_low = f32[3,64,256]{2,1,0:T(8,128)S(1)} collective-permute-done((f32[3,64,256]{2,1,0:T(8,128)S(1)}, f32[3,64,256]{2,1,0:T(8,128)S(1)}, u32[]{:S(2)}, u32[]{:S(2)}) %collective-permute-start) | collective-permute-done | bytes 196640 | tf_op jit(solution)/shard_map/ppermute | solution.py:411
  19.9 0.0 collective-permute-done.1.m_high
  19.9 0.0 copy-done
  19.9 2.3 %shard_map.52 = (f32[9,2,64,128]{3,2,1,0:T(8,128)S(1)}, f32[8,2,80,128]{3,2,1,0:T(8,128)S(1)}, f32[8,2,64,128]{3,2,1,0:T(8,128)S(1)}, f32[8,2,64,128]{3,2,1,0:T(...) custom-call(f32[3,64,256]{2,1,0:T(8,128)S(1)} %collective-permute-do, ...), custom_call_target="tpu_custom_call" | custom-call | flops 15728640 | bytes 11141632 | tf_op jit(solution)/shard_map/pallas_call | solution.py:391
  22.2 0.9 %collective-permute-start.4 = (f32[2,3,64,256]{3,2,1,0:T(8,128)S(1)}, f32[2,3,64,256]{3,2,1,0:T(8,128)S(1)}, u32[]{:S(2)}, u32[]{:S(2)}) collective-permute-start(f32[2,3,64,256]{3,2,1,0:T(8,128)S(1)} %get-tuple-element.28), channel_id=1, source_target_pairs={{0,1},{1,2},{2,3},{3,4},{4,5},{5,6},{6,7},{7,8},{8,9},{9,10},{10,1... | collective-permute-start | bytes 1179656 | tf_op jit(solution)/shard_map/ppermute | solution.py:411
  23.0 3.6 %collective-permute-start.5 = (f32[2,3,64,256]{3,2,1,0:T(8,128)S(1)}, f32[2,3,64,256]{3,2,1,0:T(8,128)S(1)}, u32[]{:S(2)}, u32[]{:S(2)}) collective-permute-start(f32[2,3,64,256]{3,2,1,0:T(8,128)S(1)} %get-tuple-element.29), channel_id=1, source_target_pairs={{0,15},{1,0},{2,1},{3,2},{4,3},{5,4},{6,5},{7,6},{8,7},{9,8},{10,9... | collective-permute-start | bytes 1179656 | tf_op jit(solution)/shard_map/ppermute | solution.py:411
  26.7 1.0 %shard_map.53 = (f32[16,1,128]{2,1,0:T(1,128)S(1)}, f32[2,4,2,80,128]{4,3,2,1,0:T(8,128)S(1)}, f32[2,6,2,64,128]{4,3,2,1,0:T(8,128)S(1)}, f32[2,4,2,64,128]{4,3,...) custom-call(f32[9,2,64,128]{3,2,1,0:T(8,128)S(1)} %get-tuple-element, ...), custom_call_target="tpu_custom_call" | custom-call | flops 5242880 | bytes 10232320 | tf_op jit(solution)/shard_map/pallas_call | solution.py:391
  27.7 10.4 %all_to_all.5.shares = f32[16,1,128]{2,1,0:T(1,128)S(1)} all-to-all(f32[16,1,128]{2,1,0:T(1,128)S(1)} %get-tuple-element.45), channel_id=1, replica_groups=mesh['group'=2,'gx'=16] {'gx'}, dimensions={0} | all-to-all | bytes 16384 | tf_op jit(solution)/shard_map/all_to_all | solution.py:454
  38.2 0.0 collective-permute-done.4.low
  38.2 0.0 collective-permute-done.5.high
  38.2 2.5 %shard_map.54 = (f32[4,64,256]{2,1,0:T(8,128)}, f32[1]{0:T(128)}) custom-call(f32[2,3,64,256]{3,2,1,0:T(8,128)S(1)} %collective-permute-done.4.low, f32[2,3,64,256]{3,2,1,0:T(8,128)S(1)} %collective-permute-done.5.high, f32[9,2,64,128]{3,2,1,0:T(8,128)S(1)} %get-tuple-element.30.mx, f32[8,2,80,128]{3,2,1,0:T(8,128)S(1)} %get-tuple-element.31.my, ...), custom_call_target="tpu_custom_call" | custom-call | flops 7864320 | bytes 9969668 | tf_op jit(solution)/shard_map/pallas_call | solution.py:391
Async XLA Ops:
  0.6 12.5 %collective-permute-start.3 = (f32[2,4,64,256]{3,2,1,0:T(8,128)}, f32[2,4,64,256]{3,2,1,0:T(8,128)S(1)}, u32[]{:S(2)}, u32[]{:S(2)}) collective-permute-start(f32[2,4,64,256]{3,2,1,0:T(8,128)} %initial.1), channel_id=1, source_target_pairs={{0,15},{1,0},{2,1},{3,2},{4,3},{5,4},{6,5},{7,6},{8,7},{9,8},{10,9... | collective-permute-start | bytes 1572872 | tf_op jit(solution)/shard_map/ppermute | solution.py:411
  6.1 11.6 %collective-permute-start.2 = (f32[2,4,64,256]{3,2,1,0:T(8,128)}, f32[2,4,64,256]{3,2,1,0:T(8,128)S(1)}, u32[]{:S(2)}, u32[]{:S(2)}) collective-permute-start(f32[2,4,64,256]{3,2,1,0:T(8,128)} %initial.1), channel_id=1, source_target_pairs={{0,1},{1,2},{2,3},{3,4},{4,5},{5,6},{6,7},{7,8},{8,9},{9,10},{10,1... | collective-permute-start | bytes 1572872 | tf_op jit(solution)/shard_map/ppermute | solution.py:411
  6.1 1.1 %copy-start.1 = (f32[2,4,64,256]{3,2,1,0:T(8,128)S(1)}, f32[2,4,64,256]{3,2,1,0:T(8,128)}, u32[]{:S(2)}) copy-start(f32[2,4,64,256]{3,2,1,0:T(8,128)} %initial.1) | copy-start | bytes 1572868
  7.2 0.9 %copy-start.2 = (f32[4,64,256]{2,1,0:T(8,128)S(1)}, f32[4,64,256]{2,1,0:T(8,128)}, u32[]{:S(2)}) copy-start(f32[4,64,256]{2,1,0:T(8,128)} %mobility.1) | copy-start | bytes 786436
  8.2 11.6 %collective-permute-start = (f32[3,64,256]{2,1,0:T(8,128)S(1)}, f32[3,64,256]{2,1,0:T(8,128)S(1)}, u32[]{:S(2)}, u32[]{:S(2)}) collective-permute-start(f32[3,64,256]{2,1,0:T(8,128)S(1)} %get-tuple-element.24), channel_id=1, source_target_pairs={{0,1},{1,2},{2,3},{3,4},{4,5},{5,6},{6,7},{7,8},{8,9},{9,10},{10,1... | collective-permute-start | bytes 589832 | tf_op jit(solution)/shard_map/ppermute | solution.py:411
  8.3 11.5 %collective-permute-start.1 = (f32[3,64,256]{2,1,0:T(8,128)S(1)}, f32[3,64,256]{2,1,0:T(8,128)S(1)}, u32[]{:S(2)}, u32[]{:S(2)}) collective-permute-start(f32[3,64,256]{2,1,0:T(8,128)S(1)} %get-tuple-element.26), channel_id=1, source_target_pairs={{0,15},{1,0},{2,1},{3,2},{4,3},{5,4},{6,5},{7,6},{8,7},{9,8},{10,9... | collective-permute-start | bytes 589832 | tf_op jit(solution)/shard_map/ppermute | solution.py:411
  17.7 2.1 %copy-start = (f32[2,4,64,256]{3,2,1,0:T(8,128)S(1)}, f32[2,4,64,256]{3,2,1,0:T(8,128)}, u32[]{:S(2)}) copy-start(f32[2,4,64,256]{3,2,1,0:T(8,128)} %observed.1) | copy-start | bytes 1572868
  22.2 16.0 %collective-permute-start.4 = (f32[2,3,64,256]{3,2,1,0:T(8,128)S(1)}, f32[2,3,64,256]{3,2,1,0:T(8,128)S(1)}, u32[]{:S(2)}, u32[]{:S(2)}) collective-permute-start(f32[2,3,64,256]{3,2,1,0:T(8,128)S(1)} %get-tuple-element.28), channel_id=1, source_target_pairs={{0,1},{1,2},{2,3},{3,4},{4,5},{5,6},{6,7},{7,8},{8,9},{9,10},{10,1... | collective-permute-start | bytes 1179656 | tf_op jit(solution)/shard_map/ppermute | solution.py:411
  23.0 15.1 %collective-permute-start.5 = (f32[2,3,64,256]{3,2,1,0:T(8,128)S(1)}, f32[2,3,64,256]{3,2,1,0:T(8,128)S(1)}, u32[]{:S(2)}, u32[]{:S(2)}) collective-permute-start(f32[2,3,64,256]{3,2,1,0:T(8,128)S(1)} %get-tuple-element.29), channel_id=1, source_target_pairs={{0,15},{1,0},{2,1},{3,2},{4,3},{5,4},{6,5},{7,6},{8,7},{9,8},{10,9... | collective-permute-start | bytes 1179656 | tf_op jit(solution)/shard_map/ppermute | solution.py:411

commit v4 on v0

v4 whole, which is shorter than its diff:
```python
import functools
import math

import jax
import jax.numpy as jnp
from jax import lax
from jax.experimental import pallas as pl
from jax.experimental.pallas import tpu as pltpu
from jax.sharding import PartitionSpec as P

stiffness = 0.5
time_step = 0.005
VMEM = pl.BlockSpec(memory_space=pltpu.VMEM)
LANES = 128
PAD = 8
CHUNK = 16


def chunks(ny):
    return range(0, ny, CHUNK)


def plain(ref, lead, row):
    return [
        ref[(*lead, pl.ds(row, CHUNK), pl.ds(at, LANES))] for at in range(0, ref.shape[-1], LANES)
    ]


def put_plain(ref, lead, row, value):
    for block, part in enumerate(value):
        ref[(*lead, pl.ds(row, CHUNK), pl.ds(block * LANES, LANES))] = part


def flat(ref, lead, row):
    return [ref[(*lead, block, pl.ds(row, CHUNK))] for block in range(ref.shape[-3])]


def put_flat(ref, lead, row, value):
    for block, part in enumerate(value):
        ref[(*lead, block, pl.ds(row, CHUNK))] = part


def padded(ref, lead, row, shift=0):
    return [ref[(*lead, block, pl.ds(PAD + row + shift, CHUNK))] for block in range(ref.shape[-3])]


def put_padded(ref, lead, row, value):
    ny = ref.shape[-2] - 2 * PAD
    for block, part in enumerate(value):
        ref[(*lead, block, pl.ds(PAD + row, CHUNK))] = part
        if row == 0:
            ref[(*lead, block, pl.ds(PAD + ny, 1))] = part[:1]
        if row + CHUNK == ny:
            ref[(*lead, block, pl.ds(PAD - 1, 1))] = part[CHUNK - 1 :]


def lane():
    return lax.broadcasted_iota(jnp.int32, (CHUNK, LANES), 1)


def after_z(value):
    turned = [pltpu.roll(part, LANES - 1, 1) for part in value]
    turned.append(turned[0])
    edge = lane() == LANES - 1
    return [jnp.where(edge, turned[at + 1], turned[at]) for at in range(len(value))]


def before_z(value):
    turned = [pltpu.roll(part, 1, 1) for part in value]
    edge = lane() == 0
    return [jnp.where(edge, turned[at - 1], turned[at]) for at in range(len(value))]


def each(function, *values):
    return [function(*parts) for parts in zip(*values)]


def beside(low, high, up, down, mid):
    return each(
        lambda a, b, c, d, e, f: (a + b) + (c + d) + (e + f),
        low, high, up, down, after_z(mid), before_z(mid),
    )


def potential(low, mid, high, up, down):
    return each(
        lambda c, total: c * (c * c + (6.0 * stiffness - 1.0)) - stiffness * total,
        mid, beside(low, high, up, down, mid),
    )


def flow_in_plane(faces, row, at, mid, up, down):
    _, my, mz, mz_low, m_all = faces
    return each(
        lambda a, b, c, d, e, u, v, w, x, y: (a * u + b * v) + (c * w + d * x) - e * y,
        padded(my, (at,), row), padded(my, (at,), row, -1), flat(mz, (at,), row),
        flat(mz_low, (at,), row), flat(m_all, (at,), row), up, down, after_z(mid), before_z(mid), mid,
    )


def add_product(total, a, b):
    return each(lambda t, x, y: t + x * y, total, a, b)


def sub(a, b):
    return each(lambda x, y: x - y, a, b)


def own_kernel(initial, mobility, conc, mob, *runs_out):
    runs, n, ny, _ = initial.shape

    def one_run(run, carry):
        for row in chunks(ny):
            for at in range(n):
                put_padded(conc, (run, at), row, plain(initial, (run, at), row))
        return carry

    lax.fori_loop(0, runs, one_run, 0)
    for row in chunks(ny):
        for at in range(n):
            put_padded(mob, (at,), row, plain(mobility, (at,), row))
    for run, out in enumerate(runs_out):
        out[...] = initial[run]


def faces_kernel(m_low, m_own, m_high, mx, my, mz, mz_low, m_all, rim):
    n = m_own.shape[0]
    ny = m_low.shape[1]
    for row in chunks(ny):
        for at in range(3):
            put_padded(rim, (at,), row, plain(m_low, (at + 1,), row))
            put_padded(rim, (at + 3,), row, plain(m_high, (at,), row))

    def mob(at):
        if at < 3:
            return rim, (at,)
        return (m_own, (at - 3,)) if at < n + 3 else (rim, (at - n,))

    mean = lambda a, b: 0.5 * (a + b)
    for row in chunks(ny):
        face = None
        for at in range(n + 5):
            mid = padded(*mob(at), row)
            face_low, face = face, each(mean, mid, padded(*mob(at + 1), row))
            put_flat(mx, (at,), row, face)
            if at == 0:
                continue
            side_y = each(mean, mid, padded(*mob(at), row, 1))
            side_y_low = each(mean, mid, padded(*mob(at), row, -1))
            side_z = each(mean, mid, after_z(mid))
            side_z_low = each(mean, mid, before_z(mid))
            put_padded(my, (at - 1,), row, side_y)
            put_flat(mz, (at - 1,), row, side_z)
            put_flat(mz_low, (at - 1,), row, side_z_low)
            put_flat(m_all, (at - 1,), row, each(
                lambda a, b, c, d, e, f: (a + b) + (c + d) + (e + f),
                face, face_low, side_y, side_y_low, side_z, side_z_low,
            ))


def forward_kernel(
    run, low, own, high, observed, mx, my, mz, mz_low, m_all, miss_in,
    chem0, state1, chem1, adjoint2, first, last, miss_sum, rim,
):
    runs, n, ny, _ = observed.shape
    faces = (mx, my, mz, mz_low, m_all)

    def conc(at):
        if at < 0:
            return rim, (at + 4,)
        return (own, (run, at)) if at < n else (rim, (at - n + 4,))

    for row in chunks(ny):
        for at in range(4):
            put_padded(rim, (at,), row, plain(low, (at,), row))
            put_padded(rim, (at + 4,), row, plain(high, (at,), row))
    for row in chunks(ny):
        mids = {at: padded(*conc(at), row) for at in range(-4, n + 4)}
        for at in range(-3, n + 3):
            ref, lead = conc(at)
            value = potential(
                mids[at - 1], mids[at], mids[at + 1], padded(ref, lead, row, 1), padded(ref, lead, row, -1)
            )
            put_padded(chem0, (at + 3,), row, value)
    for row in chunks(ny):
        mids = [padded(chem0, (at,), row) for at in range(n + 6)]
        for at in range(n + 4):
            flow = flow_in_plane(
                faces, row, at, mids[at + 1],
                padded(chem0, (at + 1,), row, 1), padded(chem0, (at + 1,), row, -1),
            )
            flow = add_product(flow, flat(mx, (at,), row), mids[at])
            flow = add_product(flow, flat(mx, (at + 1,), row), mids[at + 2])
            value = each(lambda a, b: a + time_step * b, padded(*conc(at - 2), row), flow)
            put_padded(state1, (at,), row, value)
    for row in chunks(ny):
        mids = [padded(state1, (at,), row) for at in range(n + 4)]
        for at in range(1, n + 3):
            value = potential(
                mids[at - 1], mids[at], mids[at + 1],
                padded(state1, (at,), row, 1), padded(state1, (at,), row, -1),
            )
            put_padded(chem1, (at - 1,), row, value)
    squares = None
    for row in chunks(ny):
        mids = [padded(chem1, (at,), row) for at in range(n + 2)]
        for at in range(n):
            flow = flow_in_plane(
                faces, row, at + 2, mids[at + 1],
                padded(chem1, (at + 1,), row, 1), padded(chem1, (at + 1,), row, -1),
            )
            flow = add_product(flow, flat(mx, (at + 2,), row), mids[at])
            flow = add_product(flow, flat(mx, (at + 3,), row), mids[at + 2])
            miss = each(
                lambda a, b, c: a + time_step * b - c,
                padded(state1, (at + 2,), row), flow, plain(observed, (run, at), row),
            )
            for part in miss:
                square = part * part
                squares = square if squares is None else squares + square
            value = each(lambda a: a * (1.0 / runs), miss)
            put_padded(adjoint2, (at,), row, value)
            if at < 3:
                put_plain(first, (at,), row, value)
            if at >= n - 3:
                put_plain(last, (at - (n - 3),), row, value)
    total = jnp.sum(squares, axis=0, keepdims=True)
    total = (0.5 / runs) * jnp.sum(total, axis=1, keepdims=True)
    miss_sum[...] = miss_in[...] + jnp.broadcast_to(total, miss_sum.shape)


def middle_kernel(
    run, mx, my, mz, mz_low, m_all, state1, chem0, chem1, adjoint2, share_in, sum_x_in, sum_y_in, sum_z_in,
    share, flow_own, weight, step_z0, sum_x, sum_y, sum_z,
):
    n = adjoint2.shape[0]
    ny = flow_own.shape[-2] - 2 * PAD
    faces = (mx, my, mz, mz_low, m_all)
    share[...] = share_in[...]

    def plus(sum_in, lead, row, a, b):
        if run == 0:
            return each(lambda x, y: x * y, a, b)
        return add_product(flat(sum_in, lead, row), a, b)

    for row in chunks(ny):
        mids = [padded(adjoint2, (at,), row) for at in range(n)]
        chems = [padded(chem1, (at + 1,), row) for at in range(n)]
        for at in range(n):
            up = padded(adjoint2, (at,), row, 1)
            flow = flow_in_plane(faces, row, at + 2, mids[at], up, padded(adjoint2, (at,), row, -1))
            if at > 0:
                flow = add_product(flow, flat(mx, (at + 2,), row), mids[at - 1])
            if at < n - 1:
                flow = add_product(flow, flat(mx, (at + 3,), row), mids[at + 1])
                face = plus(sum_x_in, (at + 1,), row, sub(mids[at + 1], mids[at]), sub(chems[at + 1], chems[at]))
                put_flat(sum_x, (at + 1,), row, face)
            put_padded(flow_own, (at,), row, flow)
            put_flat(sum_y, (at,), row, plus(
                sum_y_in, (at,), row, sub(up, mids[at]), sub(padded(chem1, (at + 1,), row, 1), chems[at])
            ))
            put_flat(sum_z, (at,), row, plus(
                sum_z_in, (at,), row, sub(after_z(mids[at]), mids[at]), sub(after_z(chems[at]), chems[at])
            ))
            mid = padded(chem0, (at + 3,), row)
            put_flat(step_z0, (at,), row, sub(after_z(mid), mid))
        for at in range(n + 2):
            value = each(
                lambda c: time_step * (3.0 * c * c + (6.0 * stiffness - 1.0)),
                padded(state1, (at + 1,), row),
            )
            put_flat(weight, (at,), row, value)
        for at in (0, n):
            chem = padded(chem1, (at,), row)
            put_flat(sum_x, (at,), row, each(jnp.zeros_like, chem) if run == 0 else flat(sum_x_in, (at,), row))


def backward_kernel(
    final, low, high, mx, my, mz, mz_low, m_all, chem0, chem1, adjoint2, flow_own, weight, step_z0,
    sum_x_in, sum_y_in, sum_z_in, *rest,
):
    n = adjoint2.shape[0]
    ny = flow_own.shape[-2] - 2 * PAD
    faces = (mx, my, mz, mz_low, m_all)
    if final:
        result, wide, flow_rim, adjoint1, sum_x, sum_y, sum_z = rest
    else:
        sum_x, sum_y, sum_z, wide, flow_rim, adjoint1 = rest

    def adj2(at):
        if at < 0:
            return wide, (at + 3,)
        return (adjoint2, (at,)) if at < n else (wide, (at - n + 3,))

    def flow(at):
        if at <= 0:
            return flow_rim, (at + 2,)
        return (flow_own, (at,)) if at < n - 1 else (flow_rim, (at - (n - 1) + 3,))

    for row in chunks(ny):
        for at in range(3):
            put_padded(wide, (at,), row, plain(low, (at,), row))
            put_padded(wide, (at + 3,), row, plain(high, (at,), row))
    for row in chunks(ny):
        mids = {at: padded(*adj2(at), row) for at in range(-3, n + 3)}
        for at in (-2, -1, n, n + 1):
            ref, lead = adj2(at)
            value = flow_in_plane(
                faces, row, at + 2, mids[at], padded(ref, lead, row, 1), padded(ref, lead, row, -1)
            )
            value = add_product(value, flat(mx, (at + 2,), row), mids[at - 1])
            value = add_product(value, flat(mx, (at + 3,), row), mids[at + 1])
            put_padded(*flow(at), row, value)
        for at, side, face in ((0, -1, 2), (n - 1, n, n + 2)):
            value = add_product(padded(flow_own, (at,), row), flat(mx, (face,), row), mids[side])
            put_padded(*flow(at), row, value)
    for row in chunks(ny):
        mids = {at: padded(*flow(at), row) for at in range(-2, n + 2)}
        for at in range(-1, n + 1):
            ref, lead = flow(at)
            total = beside(
                mids[at - 1], mids[at + 1], padded(ref, lead, row, 1), padded(ref, lead, row, -1), mids[at]
            )
            value = each(
                lambda a, w, f, t: a + w * f - (time_step * stiffness) * t,
                padded(*adj2(at), row), flat(weight, (at + 1,), row), mids[at], total,
            )
            put_padded(adjoint1, (at + 1,), row, value)
    for row in chunks(ny):
        mids = [padded(adjoint1, (at,), row) for at in range(n + 2)]
        chems = [padded(chem0, (at + 2,), row) for at in range(n + 2)]
        for at in range(n + 1):
            face = add_product(
                flat(sum_x_in, (at,), row), sub(mids[at + 1], mids[at]), sub(chems[at + 1], chems[at])
            )
            if at in (0, n):
                face = add_product(
                    face, sub(padded(*adj2(at), row), padded(*adj2(at - 1), row)),
                    sub(padded(chem1, (at + 1,), row), padded(chem1, (at,), row)),
                )
            put_flat(sum_x, (at,), row, face)
        for at in range(n):
            mid = mids[at + 1]
            total = add_product(
                flat(sum_y_in, (at,), row), sub(padded(adjoint1, (at + 1,), row, 1), mid),
                sub(padded(chem0, (at + 3,), row, 1), chems[at + 1]),
            )
            (put_padded if final else put_flat)(sum_y, (at,), row, total)
            put_flat(sum_z, (at,), row, add_product(
                flat(sum_z_in, (at,), row), sub(after_z(mid), mid), flat(step_z0, (at,), row)
            ))
    if not final:
        return
    for row in chunks(ny):
        for at in range(n):
            sides = flat(sum_z, (at,), row)
            value = each(
                lambda a, b, c, d, e, f: -0.5 * ((a + b) + (c + d) + (e + f)),
                flat(sum_x, (at,), row), flat(sum_x, (at + 1,), row),
                padded(sum_y, (at,), row), padded(sum_y, (at,), row, -1), sides, before_z(sides),
            )
            put_plain(result, (at,), row, value)


def call(kernel, outs, scratch, args, flops):
    moved = 4 * (sum(a.size for a in args) + sum(math.prod(o) for o in outs))
    return pl.pallas_call(
        kernel,
        out_shape=tuple(jax.ShapeDtypeStruct(o, jnp.float32) for o in outs),
        in_specs=[VMEM] * len(args),
        out_specs=tuple([VMEM] * len(outs)),
        scratch_shapes=[pltpu.VMEM(s, jnp.float32) for s in scratch],
        compiler_params=pltpu.CompilerParams(vmem_limit_bytes=16 * 1024 * 1024),
        cost_estimate=pl.CostEstimate(flops=flops, bytes_accessed=moved, transcendentals=0),
    )(*args)


def sum_over(value, axis, order):
    count = lax.axis_size(axis)
    if count & (count - 1):
        return lax.psum(value, axis)
    hops = [1 << bit for bit in range(count.bit_length() - 1)]
    hops = [hop for hop in order if hop in hops] + [hop for hop in hops if hop not in order]
    for hop in hops:
        value = value + lax.ppermute(value, axis, [(i, i ^ hop) for i in range(count)])
    return value


def on_device(initial, observed, mobility):
    runs, n, ny, nz = initial.shape
    blocks = nz // LANES
    count = lax.axis_size("gx")
    forward = [(i, (i + 1) % count) for i in range(count)]
    backward = [(i, (i - 1) % count) for i in range(count)]
    cell = ny * nz

    def neighbours(first, last):
        return lax.ppermute(last, "gx", forward), lax.ppermute(first, "gx", backward)

    def lies(*lead):
        return (*lead, blocks, ny, LANES)

    def lies_padded(*lead):
        return (*lead, blocks, ny + 2 * PAD, LANES)

    m_low, m_high = neighbours(mobility[:4], mobility[n - 4 :])
    conc, mob, *initials = call(
        own_kernel,
        (lies_padded(runs, n), lies_padded(n), *[(n, ny, nz)] * runs),
        (),
        (initial, mobility),
        runs * n * cell,
    )
    sides = [neighbours(part[:4], part[n - 4 :]) for part in initials]
    faces = call(
        faces_kernel,
        (lies(n + 5), lies_padded(n + 4), lies(n + 4), lies(n + 4), lies(n + 4)),
        (lies_padded(6),),
        (m_low, mob, m_high),
        15 * (n + 4) * cell,
    )
    share = jnp.zeros((1, LANES), jnp.float32)
    kept = []
    for run, (low, high) in enumerate(sides):
        chem0, state1, chem1, adjoint2, first, last, share = call(
            functools.partial(forward_kernel, run),
            (
                lies_padded(n + 6), lies_padded(n + 4), lies_padded(n + 2), lies_padded(n),
                (3, ny, nz), (3, ny, nz), (1, LANES),
            ),
            (lies_padded(8),),
            (low, conc, high, observed, *faces, share),
            80 * (n + 4) * cell,
        )
        kept.append((chem0, state1, chem1, adjoint2, neighbours(first, last)))
    sums = (jnp.zeros(lies(n + 1), jnp.float32), jnp.zeros(lies(n), jnp.float32), jnp.zeros(lies(n), jnp.float32))
    ready = []
    for run, (chem0, state1, chem1, adjoint2, (low, high)) in enumerate(kept):
        share, flow_own, weight, step_z0, *sums = call(
            functools.partial(middle_kernel, run),
            (
                (1, LANES), lies_padded(n), lies(n + 2), lies(n),
                lies(n + 1), lies(n), lies(n),
            ),
            (),
            (*faces, state1, chem0, chem1, adjoint2, share, *sums),
            40 * n * cell,
        )
        ready.append((low, high, *faces, chem0, chem1, adjoint2, flow_own, weight, step_z0))
    misfit = sum_over(share, "gx", (1, 4, 8, 2))
    for run, args in enumerate(ready):
        final = run == runs - 1
        scratch = (lies_padded(6), lies_padded(6), lies_padded(n + 2))
        if final:
            outs, scratch = ((n, ny, nz),), (*scratch, lies(n + 1), lies_padded(n), lies(n))
        else:
            outs = (lies(n + 1), lies(n), lies(n))
        sums = call(
            functools.partial(backward_kernel, final), outs, scratch, (*args, *sums), 40 * (n + 2) * cell
        )
    return (sums[0], misfit[0, :1])


def solution(mesh):
    placed = (
        P("group", "gx", None, None),
        P("group", "gx", None, None),
        P(("group", "gx"), None, None),
    )
    return jax.shard_map(
        on_device,
        mesh=mesh,
        in_specs=placed,
        out_specs=(P(("group", "gx"), None, None), P("group")),
        check_vma=False,
    )
```

time: 93.4 us -> 49.6 us (0.53)
  blocking collectives: 31.2 us -> 0 us
  other arithmetic: 12.9 us -> 0.52 us
  local copies, waits for them, and re-layouts: 13.4 us -> 2.04 us
  Pallas kernels: 0 us -> 6.46 us
  starting transfers between devices: 19.5 us -> 23.4 us
  waiting for transfers between devices: 14.1 us -> 16.3 us
  between operations: 2 us -> 0.73 us
    psum x1 -> x0, blocking collectives: 31.2 us -> none  [on_device(): misfit = lax.psum(0.5 / runs_here * jnp.sum(miss * miss), 'gx')]
    slice x37 -> x0, local copies, waits for them, and re-layouts: 8.1 us -> none  [the longest x8 2.61 us: sensitivity(): jnp.roll(a_mid, offset, axis_num) - a_mid]
    pallas_call x0 -> x8, Pallas kernels: none -> 6.46 us  [call(): pl.pallas_call(kernel, out_shape=tuple((jax.ShapeDtypeStruct(o, jnp.float...]
    mul x4 -> x0, other arithmetic: 4.37 us -> none  [the longest x2 2.46 us: transport(): (jnp.roll(m_mid, offset, axis_num) + m_mid) * (jnp.roll(f_mid, offset, ax...]
    reduce_sum x3 -> x0, other arithmetic: 4.02 us -> none  [the longest x2 2.76 us: sensitivity(): return -0.5 * jnp.sum(total, axis=0)]
    ppermute x10 -> x14, starting transfers between devices: 19.5 us -> 23.4 us  [the longest x5 23.3 us: neighbours(): lax.ppermute(first, 'gx', backward)]
    unnamed x76 -> x6, local copies, waits for them, and re-layouts: 4.98 us -> 2 us
    ppermute x10 -> x14, waiting for transfers between devices: 14.1 us -> 16.3 us  [the longest x4 12.6 us: sum_over(): lax.ppermute(value, axis, [(i, i ^ hop) for i in range(count)])]
  transfers between devices with their start and end apart: 10 -> 14, of which waited for: 4 -> 5; matrix products, arithmetic and copies ran while one was open for 9% -> 1% of each run, Pallas kernels for 0% -> 10%
where the time goes in v4:
time: 49.6 us; the launch traced here: 49.5 us
  starting transfers between devices  23.4 us (47%)
  waiting for transfers between devices  16.3 us (33%)
  Pallas kernels  6.46 us (13%)
  local copies, waits for them, and re-layouts  2.04 us (4%)
  between operations  0.73 us (1%)
  other arithmetic  0.52 us (1%)
    ppermute x5, starting transfers between devices, neighbours(): lax.ppermute(first, 'gx', backward)  23.3 us
    ppermute x4, waiting for transfers between devices, sum_over(): lax.ppermute(value, axis, [(i, i ^ hop) for i in range(count)])  12.6 us
    pallas_call x8, Pallas kernels, call(): pl.pallas_call(kernel, out_shape=tuple((jax.ShapeDtypeStruct(o, jnp.float...  6.46 us
    ppermute x5, waiting for transfers between devices, neighbours(): lax.ppermute(last, 'gx', forward)  3.65 us
    unnamed x6, local copies, waits for them, and re-layouts  2 us
  transfers between devices with their start and end apart: 14, of which 5 were waited for; matrix products, arithmetic and copies ran while one was open for 1% of the time, Pallas kernels for 10%

profile of v4, /device:TPU:0, one launch (start us, length us, event | category | flops | bytes accessed | tf_op | source)
XLA Modules:
  0.0 49.5 jit_solution(10197669903563729520)
XLA Ops:
  0.6 5.5 %collective-permute-start.3 = (f32[4,64,256]{2,1,0:T(8,128)}, f32[4,64,256]{2,1,0:T(8,128)S(1)}, u32[]{:S(2)}, u32[]{:S(2)}) collective-permute-start(f32[4,64,256]{2,1,0:T(8,128)} %mobility.1), channel_id=1, source_target_pairs={{0,15},{1,0},{2,1},{3,2},{4,3},{5,4},{6,5},{7,6},{8,7},{9,8},{10,9... | collective-permute-start | bytes 786440 | tf_op jit(solution)/shard_map/ppermute | solution.py:398
  6.1 0.0 collective-permute-start.2
  6.1 0.0 copy-start.1
  6.1 1.0 %copy-done.1 = f32[2,4,64,256]{3,2,1,0:T(8,128)S(1)} copy-done((f32[2,4,64,256]{3,2,1,0:T(8,128)S(1)}, f32[2,4,64,256]{3,2,1,0:T(8,128)}, u32[]{:S(2)}) %copy-start.1) | copy-done | bytes 524312
  7.2 0.0 copy-start.2
  7.2 0.9 %copy-done.2 = f32[4,64,256]{2,1,0:T(8,128)S(1)} copy-done((f32[4,64,256]{2,1,0:T(8,128)S(1)}, f32[4,64,256]{2,1,0:T(8,128)}, u32[]{:S(2)}) %copy-start.2) | copy-done | bytes 262168
  8.1 0.1 shard_map.50
  8.2 0.0 copy-start
  8.2 4.5 %collective-permute-start.5 = (f32[4,64,256]{2,1,0:T(8,128)S(1)}, f32[4,64,256]{2,1,0:T(8,128)S(1)}, u32[]{:S(2)}, u32[]{:S(2)}) collective-permute-start(f32[4,64,256]{2,1,0:T(8,128)S(1)} %get-tuple-element.50), channel_id=1, source_target_pairs={{0,15},{1,0},{2,1},{3,2},{4,3},{5,4},{6,5},{7,6},{8,7},{9,8},{10,9... | collective-permute-start | bytes 786440 | tf_op jit(solution)/shard_map/ppermute | solution.py:398
  12.7 0.0 collective-permute-start.4
  12.7 4.4 %collective-permute-start.1 = (f32[4,64,256]{2,1,0:T(8,128)S(1)}, f32[4,64,256]{2,1,0:T(8,128)S(1)}, u32[]{:S(2)}, u32[]{:S(2)}) collective-permute-start(f32[4,64,256]{2,1,0:T(8,128)S(1)} %get-tuple-element.42), channel_id=1, source_target_pairs={{0,15},{1,0},{2,1},{3,2},{4,3},{5,4},{6,5},{7,6},{8,7},{9,8},{10,9... | collective-permute-start | bytes 786440 | tf_op jit(solution)/shard_map/ppermute | solution.py:398
  17.2 0.0 collective-permute-done.3.m_high
  17.2 0.0 collective-permute-start
  17.2 0.0 collective-permute-done.2.m_low
  17.2 0.4 shard_map.51
  17.6 0.0 collective-permute-done.5.high
  17.6 3.6 %collective-permute-done.4.low = f32[4,64,256]{2,1,0:T(8,128)S(1)} collective-permute-done((f32[4,64,256]{2,1,0:T(8,128)S(1)}, f32[4,64,256]{2,1,0:T(8,128)S(1)}, u32[]{:S(2)}, u32[]{:S(2)}) %collective-permute-start.4) | collective-permute-done | bytes 262176 | tf_op jit(solution)/shard_map/ppermute | solution.py:398
  21.2 0.0 copy-done
  21.2 1.4 %shard_map.52 = (f32[10,2,80,128]{3,2,1,0:T(8,128)S(1)}, f32[8,2,80,128]{3,2,1,0:T(8,128)S(1)}, f32[6,2,80,128]{3,2,1,0:T(8,128)S(1)}, f32[4,2,80,128]{3,2,1,0:T...) custom-call(f32[4,64,256]{2,1,0:T(8,128)S(1)} %collective-permute-done.4.low, ...), custom_call_target="tpu_custom_call" | custom-call | flops 10485760 | bytes 7209984 | tf_op jit(solution)/shard_map/pallas_call | solution.py:367
  22.7 0.0 collective-permute-start.8
  22.7 4.4 %collective-permute-start.9 = (f32[3,64,256]{2,1,0:T(8,128)S(1)}, f32[3,64,256]{2,1,0:T(8,128)S(1)}, u32[]{:S(2)}, u32[]{:S(2)}) collective-permute-start(f32[3,64,256]{2,1,0:T(8,128)S(1)} %get-tuple-element.71), channel_id=1, source_target_pairs={{0,15},{1,0},{2,1},{3,2},{4,3},{5,4},{6,5},{7,6},{8,7},{9,8},{10,9... | collective-permute-start | bytes 589832 | tf_op jit(solution)/shard_map/ppermute | solution.py:398
  27.1 0.0 collective-permute-done.1.high
  27.1 0.0 collective-permute-done.low
  27.1 1.4 %shard_map.53 = (f32[10,2,80,128]{3,2,1,0:T(8,128)S(1)}, f32[8,2,80,128]{3,2,1,0:T(8,128)S(1)}, f32[6,2,80,128]{3,2,1,0:T(8,128)S(1)}, f32[4,2,80,128]{3,2,1,0:T...) custom-call(f32[4,64,256]{2,1,0:T(8,128)S(1)} %collective-permute-done.low, ...), custom_call_target="tpu_custom_call" | custom-call | flops 10485760 | bytes 7209984 | tf_op jit(solution)/shard_map/pallas_call | solution.py:367
  28.5 0.0 collective-permute-start.6
  28.5 4.4 %collective-permute-start.7 = (f32[3,64,256]{2,1,0:T(8,128)S(1)}, f32[3,64,256]{2,1,0:T(8,128)S(1)}, u32[]{:S(2)}, u32[]{:S(2)}) collective-permute-start(f32[3,64,256]{2,1,0:T(8,128)S(1)} %get-tuple-element.53), channel_id=1, source_target_pairs={{0,15},{1,0},{2,1},{3,2},{4,3},{5,4},{6,5},{7,6},{8,7},{9,8},{10,9... | collective-permute-start | bytes 589832 | tf_op jit(solution)/shard_map/ppermute | solution.py:398
  33.0 0.4 shard_map.54
  33.5 0.4 shard_map.55
  33.9 0.1 collective-permute-start.10
  34.0 1.1 %collective-permute-done.10 = f32[1,128]{1,0:T(1,128)S(1)} collective-permute-done((f32[1,128]{1,0:T(1,128)S(1)}, f32[1,128]{1,0:T(1,128)S(1)}, u32[]{:S(2)}, u32[]{:S(2)}) %collective-permute-start.10) | collective-permute-done | bytes 544 | tf_op jit(solution)/shard_map/ppermute | solution.py:385
  35.1 0.0 collective-permute-start.11
  35.1 3.5 %collective-permute-done.11 = f32[1,128]{1,0:T(1,128)S(1)} collective-permute-done((f32[1,128]{1,0:T(1,128)S(1)}, f32[1,128]{1,0:T(1,128)S(1)}, u32[]{:S(2)}, u32[]{:S(2)}) %collective-permute-start.11) | collective-permute-done | bytes 544 | tf_op jit(solution)/shard_map/ppermute | solution.py:385
  38.7 0.0 collective-permute-start.12
  38.7 4.4 %collective-permute-done.12 = f32[1,128]{1,0:T(1,128)S(1)} collective-permute-done((f32[1,128]{1,0:T(1,128)S(1)}, f32[1,128]{1,0:T(1,128)S(1)}, u32[]{:S(2)}, u32[]{:S(2)}) %collective-permute-start.12) | collective-permute-done | bytes 544 | tf_op jit(solution)/shard_map/ppermute | solution.py:385
  43.1 0.0 collective-permute-start.13
  43.1 3.5 %collective-permute-done.13 = f32[1,128]{1,0:T(1,128)S(1)} collective-permute-done((f32[1,128]{1,0:T(1,128)S(1)}, f32[1,128]{1,0:T(1,128)S(1)}, u32[]{:S(2)}, u32[]{:S(2)}) %collective-permute-start.13) | collective-permute-done | bytes 544 | tf_op jit(solution)/shard_map/ppermute | solution.py:385
  46.6 0.5 %add.15 = f32[1,128]{1,0:T(1,128)} add(f32[1,128]{1,0:T(1,128)S(1)} %add.14, f32[1,128]{1,0:T(1,128)S(1)} %collective-permute-done.13) | non-fusion elementwise | flops 128 | bytes 1536 | tf_op jit(solution)/shard_map/add | solution.py:385
  47.2 0.0 collective-permute-done.8.low
  47.2 0.0 collective-permute-done.9.high
  47.2 0.7 %shard_map.56 = (f32[5,2,64,128]{3,2,1,0:T(8,128)S(1)}, f32[4,2,64,128]{3,2,1,0:T(8,128)S(1)}, f32[4,2,64,128]{3,2,1,0:T(8,128)S(1)}) custom-call(f32[3,64,256]{2,1,0:T(8,128)S(1)} %collective-permute-done.8.low, f32[3,64,256]{2,1,0:T(8,128)S(1)} %collective-permute-done.9.high, f32[9,2,64,128]{3,2,1,0:T(8,128)S(1)} %get-tuple-element.45.mx, ...), custom_call_target="tpu_custom_call" | custom-call | flops 3932160 | bytes 7536640 | tf_op jit(solution)/shard_map/pallas_call | solution.py:367
  47.9 0.0 collective-permute-done.6.low
  47.9 0.0 collective-permute-done.7.high
  47.9 1.5 %shard_map.57 = f32[4,64,256]{2,1,0:T(8,128)} custom-call(f32[3,64,256]{2,1,0:T(8,128)S(1)} %collective-permute-done.6.low, f32[3,64,256]{2,1,0:T(8,128)S(1)} %collective-permute-done.7.high, f32[9,2,64,128]{3,2,1,0:T(8,128)S(1)} %get-tuple-element.45.mx, f32[8,2,80,128]{3,2,1,0:T(8,128)S(1)} %get-tuple-element.46.my, ...), custom_call_target="tpu_custom_call" | custom-call | flops 3932160 | bytes 6946816 | tf_op jit(solution)/shard_map/pallas_call | solution.py:367
  (6 shorter events, 0.1 us)
Async XLA Ops:
  0.6 16.5 %collective-permute-start.3 = (f32[4,64,256]{2,1,0:T(8,128)}, f32[4,64,256]{2,1,0:T(8,128)S(1)}, u32[]{:S(2)}, u32[]{:S(2)}) collective-permute-start(f32[4,64,256]{2,1,0:T(8,128)} %mobility.1), channel_id=1, source_target_pairs={{0,15},{1,0},{2,1},{3,2},{4,3},{5,4},{6,5},{7,6},{8,7},{9,8},{10,9... | collective-permute-start | bytes 786440 | tf_op jit(solution)/shard_map/ppermute | solution.py:398
  6.1 11.1 %collective-permute-start.2 = (f32[4,64,256]{2,1,0:T(8,128)}, f32[4,64,256]{2,1,0:T(8,128)S(1)}, u32[]{:S(2)}, u32[]{:S(2)}) collective-permute-start(f32[4,64,256]{2,1,0:T(8,128)} %mobility.1), channel_id=1, source_target_pairs={{0,1},{1,2},{2,3},{3,4},{4,5},{5,6},{6,7},{7,8},{8,9},{9,10},{10,1... | collective-permute-start | bytes 786440 | tf_op jit(solution)/shard_map/ppermute | solution.py:398
  6.1 1.0 %copy-start.1 = (f32[2,4,64,256]{3,2,1,0:T(8,128)S(1)}, f32[2,4,64,256]{3,2,1,0:T(8,128)}, u32[]{:S(2)}) copy-start(f32[2,4,64,256]{3,2,1,0:T(8,128)} %initial.1) | copy-start | bytes 1572868
  7.2 0.9 %copy-start.2 = (f32[4,64,256]{2,1,0:T(8,128)S(1)}, f32[4,64,256]{2,1,0:T(8,128)}, u32[]{:S(2)}) copy-start(f32[4,64,256]{2,1,0:T(8,128)} %mobility.1) | copy-start | bytes 786436
  8.2 13.0 %copy-start = (f32[2,4,64,256]{3,2,1,0:T(8,128)S(1)}, f32[2,4,64,256]{3,2,1,0:T(8,128)}, u32[]{:S(2)}) copy-start(f32[2,4,64,256]{3,2,1,0:T(8,128)} %observed.3) | copy-start | bytes 1572868
  8.2 9.3 %collective-permute-start.5 = (f32[4,64,256]{2,1,0:T(8,128)S(1)}, f32[4,64,256]{2,1,0:T(8,128)S(1)}, u32[]{:S(2)}, u32[]{:S(2)}) collective-permute-start(f32[4,64,256]{2,1,0:T(8,128)S(1)} %get-tuple-element.50), channel_id=1, source_target_pairs={{0,15},{1,0},{2,1},{3,2},{4,3},{5,4},{6,5},{7,6},{8,7},{9,8},{10,9... | collective-permute-start | bytes 786440 | tf_op jit(solution)/shard_map/ppermute | solution.py:398
  12.7 8.5 %collective-permute-start.4 = (f32[4,64,256]{2,1,0:T(8,128)S(1)}, f32[4,64,256]{2,1,0:T(8,128)S(1)}, u32[]{:S(2)}, u32[]{:S(2)}) collective-permute-start(f32[4,64,256]{2,1,0:T(8,128)S(1)} %get-tuple-element.50), channel_id=1, source_target_pairs={{0,1},{1,2},{2,3},{3,4},{4,5},{5,6},{6,7},{7,8},{8,9},{9,10},{10,1... | collective-permute-start | bytes 786440 | tf_op jit(solution)/shard_map/ppermute | solution.py:398
  12.7 14.4 %collective-permute-start.1 = (f32[4,64,256]{2,1,0:T(8,128)S(1)}, f32[4,64,256]{2,1,0:T(8,128)S(1)}, u32[]{:S(2)}, u32[]{:S(2)}) collective-permute-start(f32[4,64,256]{2,1,0:T(8,128)S(1)} %get-tuple-element.42), channel_id=1, source_target_pairs={{0,15},{1,0},{2,1},{3,2},{4,3},{5,4},{6,5},{7,6},{8,7},{9,8},{10,9... | collective-permute-start | bytes 786440 | tf_op jit(solution)/shard_map/ppermute | solution.py:398
  17.2 9.9 %collective-permute-start = (f32[4,64,256]{2,1,0:T(8,128)S(1)}, f32[4,64,256]{2,1,0:T(8,128)S(1)}, u32[]{:S(2)}, u32[]{:S(2)}) collective-permute-start(f32[4,64,256]{2,1,0:T(8,128)S(1)} %get-tuple-element.42), channel_id=1, source_target_pairs={{0,1},{1,2},{2,3},{3,4},{4,5},{5,6},{6,7},{7,8},{8,9},{9,10},{10,1... | collective-permute-start | bytes 786440 | tf_op jit(solution)/shard_map/ppermute | solution.py:398
  22.7 24.5 %collective-permute-start.8 = (f32[3,64,256]{2,1,0:T(8,128)S(1)}, f32[3,64,256]{2,1,0:T(8,128)S(1)}, u32[]{:S(2)}, u32[]{:S(2)}) collective-permute-start(f32[3,64,256]{2,1,0:T(8,128)S(1)} %get-tuple-element.70), channel_id=1, source_target_pairs={{0,1},{1,2},{2,3},{3,4},{4,5},{5,6},{6,7},{7,8},{8,9},{9,10},{10,1... | collective-permute-start | bytes 589832 | tf_op jit(solution)/shard_map/ppermute | solution.py:398
  22.7 24.5 %collective-permute-start.9 = (f32[3,64,256]{2,1,0:T(8,128)S(1)}, f32[3,64,256]{2,1,0:T(8,128)S(1)}, u32[]{:S(2)}, u32[]{:S(2)}) collective-permute-start(f32[3,64,256]{2,1,0:T(8,128)S(1)} %get-tuple-element.71), channel_id=1, source_target_pairs={{0,15},{1,0},{2,1},{3,2},{4,3},{5,4},{6,5},{7,6},{8,7},{9,8},{10,9... | collective-permute-start | bytes 589832 | tf_op jit(solution)/shard_map/ppermute | solution.py:398
  28.5 19.4 %collective-permute-start.6 = (f32[3,64,256]{2,1,0:T(8,128)S(1)}, f32[3,64,256]{2,1,0:T(8,128)S(1)}, u32[]{:S(2)}, u32[]{:S(2)}) collective-permute-start(f32[3,64,256]{2,1,0:T(8,128)S(1)} %get-tuple-element.52), channel_id=1, source_target_pairs={{0,1},{1,2},{2,3},{3,4},{4,5},{5,6},{6,7},{7,8},{8,9},{9,10},{10,1... | collective-permute-start | bytes 589832 | tf_op jit(solution)/shard_map/ppermute | solution.py:398
  28.5 19.4 %collective-permute-start.7 = (f32[3,64,256]{2,1,0:T(8,128)S(1)}, f32[3,64,256]{2,1,0:T(8,128)S(1)}, u32[]{:S(2)}, u32[]{:S(2)}) collective-permute-start(f32[3,64,256]{2,1,0:T(8,128)S(1)} %get-tuple-element.53), channel_id=1, source_target_pairs={{0,15},{1,0},{2,1},{3,2},{4,3},{5,4},{6,5},{7,6},{8,7},{9,8},{10,9... | collective-permute-start | bytes 589832 | tf_op jit(solution)/shard_map/ppermute | solution.py:398
  33.9 1.2 %collective-permute-start.10 = (f32[1,128]{1,0:T(1,128)S(1)}, f32[1,128]{1,0:T(1,128)S(1)}, u32[]{:S(2)}, u32[]{:S(2)}) collective-permute-start(f32[1,128]{1,0:T(1,128)S(1)} %get-tuple-element.81), channel_id=1, source_target_pairs={{0,1},{1,0},{2,3},{3,2},{4,5},{5,4},{6,7},{7,6},{8,9},{9,8},{10,11... | collective-permute-start | bytes 1544 | tf_op jit(solution)/shard_map/ppermute | solution.py:385
  35.1 3.5 %collective-permute-start.11 = (f32[1,128]{1,0:T(1,128)S(1)}, f32[1,128]{1,0:T(1,128)S(1)}, u32[]{:S(2)}, u32[]{:S(2)}) collective-permute-start(f32[1,128]{1,0:T(1,128)S(1)} %add.12), channel_id=1, source_target_pairs={{0,4},{1,5},{2,6},{3,7},{4,0},{5,1},{6,2},{7,3},{8,12},{9,13},{10,... | collective-permute-start | bytes 1544 | tf_op jit(solution)/shard_map/ppermute | solution.py:385
  38.7 4.4 %collective-permute-start.12 = (f32[1,128]{1,0:T(1,128)S(1)}, f32[1,128]{1,0:T(1,128)S(1)}, u32[]{:S(2)}, u32[]{:S(2)}) collective-permute-start(f32[1,128]{1,0:T(1,128)S(1)} %add.13), channel_id=1, source_target_pairs={{0,8},{1,9},{2,10},{3,11},{4,12},{5,13},{6,14},{7,15},{8,0},{9,1},... | collective-permute-start | bytes 1544 | tf_op jit(solution)/shard_map/ppermute | solution.py:385
  43.1 3.5 %collective-permute-start.13 = (f32[1,128]{1,0:T(1,128)S(1)}, f32[1,128]{1,0:T(1,128)S(1)}, u32[]{:S(2)}, u32[]{:S(2)}) collective-permute-start(f32[1,128]{1,0:T(1,128)S(1)} %add.14), channel_id=1, source_target_pairs={{0,2},{1,3},{2,0},{3,1},{4,6},{5,7},{6,4},{7,5},{8,10},{9,11},{10,... | collective-permute-start | bytes 1544 | tf_op jit(solution)/shard_map/ppermute | solution.py:385

commit v5 on v3

--- a/solution.py
+++ b/solution.py
@@ -72,6 +72,15 @@
     return [jnp.where(edge, turned[at - 1], turned[at]) for at in range(len(value))]
 
 
+def side():
+    return lax.rem(lax.axis_index("gx"), 2)
+
+
+def place(count):
+    at = side() * count
+    return at, count - at
+
+
 def each(function, *values):
     return [function(*parts) for parts in zip(*values)]
 
@@ -107,7 +116,7 @@
     return each(lambda x, y: x - y, a, b)
 
 
-def own_kernel(initial, mobility, conc, mob, first, last):
+def own_kernel(initial, mobility, conc, mob, to_chip, to_core):
     runs, n, ny, _ = initial.shape
 
     def one_run(run, carry):
@@ -120,24 +129,26 @@
     for row in chunks(ny):
         for at in range(n):
             put_padded(mob, (at,), row, plain(mobility, (at,), row))
-    first[...] = mobility[:3]
-    last[...] = mobility[n - 3 :]
-
-
-def chem_kernel(low, own, high, chem0, rim):
+    at_chip, at_core = place(n - 3)
+    to_chip[...] = mobility[pl.ds(at_chip, 3)]
+    to_core[...] = mobility[pl.ds(at_core, 3)]
+
+
+def chem_kernel(of_chip, of_core, own, chem0, rim):
     runs, n = own.shape[:2]
-    ny = low.shape[2]
+    ny = of_chip.shape[2]
+    at_chip, at_core = place(4)
 
     def conc(run, at):
         if at < 0:
-            return rim, (at + 4,)
-        return (own, (run, at)) if at < n else (rim, (at - n + 4,))
+            return rim, (run, at + 4)
+        return (own, (run, at)) if at < n else (rim, (run, at - n + 4))
 
     def one_run(run, carry):
         for row in chunks(ny):
             for at in range(4):
-                put_padded(rim, (at,), row, plain(low, (run, at), row))
-                put_padded(rim, (at + 4,), row, plain(high, (run, at), row))
+                put_padded(rim, (run, at_chip + at), row, plain(of_chip, (run, at), row))
+                put_padded(rim, (run, at_core + at), row, plain(of_core, (run, at), row))
         for row in chunks(ny):
             mids = {at: padded(*conc(run, at), row) for at in range(-4, n + 4)}
             for at in range(-3, n + 3):
@@ -152,15 +163,16 @@
 
 
 def forward_kernel(
-    m_low, m_own, m_high, low, own, high, observed, chem0,
-    mx, my, mz, mz_low, m_all, state1, chem1, adjoint2, first, last, miss_sum,
+    m_chip, m_core, m_own, own, conc_rim, observed, chem0,
+    mx, my, mz, mz_low, m_all, state1, chem1, adjoint2, to_chip, to_core, miss_sum,
     rim, total,
 ):
     runs, n, ny, _ = observed.shape
+    at_chip, at_core = place(3)
     for row in chunks(ny):
         for at in range(3):
-            put_padded(rim, (at,), row, plain(m_low, (at,), row))
-            put_padded(rim, (at + 3,), row, plain(m_high, (at,), row))
+            put_padded(rim, (at_chip + at,), row, plain(m_chip, (at,), row))
+            put_padded(rim, (at_core + at,), row, plain(m_core, (at,), row))
 
     def mob(at):
         if at < 3:
@@ -193,7 +205,7 @@
     def conc(run, at, row):
         if 0 <= at < n:
             return padded(own, (run, at), row)
-        return plain(low, (run, at + 4), row) if at < 0 else plain(high, (run, at - n), row)
+        return padded(conc_rim, (run, at + 4 if at < 0 else at - n + 4), row)
 
     def one_run(run, carry):
         for row in chunks(ny):
@@ -234,10 +246,11 @@
                     squares = square if squares is None else squares + square
                 value = each(lambda a: a * (1.0 / runs), miss)
                 put_padded(adjoint2, (run, at), row, value)
-                if at < 3:
-                    put_plain(first, (run, at), row, value)
-                if at >= n - 3:
-                    put_plain(last, (run, at - (n - 3)), row, value)
+        at_chip, at_core = place(n - 3)
+        for row in chunks(ny):
+            for at in range(3):
+                put_flat(to_chip, (run, at), row, padded(adjoint2, (run, at_chip + at), row))
+                put_flat(to_core, (run, at), row, padded(adjoint2, (run, at_core + at), row))
         total[...] += squares
         return carry
 
@@ -295,7 +308,7 @@
 
 
 def backward_kernel(
-    low, high, mx, my, mz, mz_low, m_all, chem0, chem1, adjoint2, flow_own, weight, step_z0,
+    of_chip, of_core, mx, my, mz, mz_low, m_all, chem0, chem1, adjoint2, flow_own, weight, step_z0,
     sum_x_in, sum_y_in, sum_z_in, shares, result, misfit, wide, flow_rim, adjoint1, sum_x, sum_y, sum_z,
 ):
     runs, n = adjoint2.shape[:2]
@@ -318,11 +331,13 @@
             return flow_rim, (at + 2,)
         return (flow_own, (run, at)) if at < n - 1 else (flow_rim, (at - (n - 1) + 3,))
 
+    at_chip, at_core = place(3)
+
     def one_run(run, carry):
         for row in chunks(ny):
             for at in range(3):
-                put_padded(wide, (at,), row, plain(low, (run, at), row))
-                put_padded(wide, (at + 3,), row, plain(high, (run, at), row))
+                put_padded(wide, (at_chip + at,), row, flat(of_chip, (run, at), row))
+                put_padded(wide, (at_core + at,), row, flat(of_core, (run, at), row))
         for row in chunks(ny):
             mids = {at: padded(*adj2(run, at), row) for at in range(-3, n + 3)}
             for at in (-2, -1, n, n + 1):
@@ -403,12 +418,12 @@
     runs, n, ny, nz = initial.shape
     blocks = nz // LANES
     count = lax.axis_size("gx")
-    forward = [(i, (i + 1) % count) for i in range(count)]
-    backward = [(i, (i - 1) % count) for i in range(count)]
+    over_chips = [(i, (i - 1 + 2 * (i % 2)) % count) for i in range(count)]
+    over_cores = [(i, i ^ 1) for i in range(count)]
     cell = ny * nz
 
-    def neighbours(first, last):
-        return lax.ppermute(last, "gx", forward), lax.ppermute(first, "gx", backward)
+    def neighbours(to_chip, to_core):
+        return lax.ppermute(to_chip, "gx", over_chips), lax.ppermute(to_core, "gx", over_cores)
 
     def lies(*lead):
         return (*lead, blocks, ny, LANES)
@@ -416,31 +431,35 @@
     def lies_padded(*lead):
         return (*lead, blocks, ny + 2 * PAD, LANES)
 
-    low, high = neighbours(initial[:, :4], initial[:, n - 4 :])
-    conc, mob, first, last = call(
+    if n == 4:
+        near = (initial, initial)
+    else:
+        near = [lax.dynamic_slice_in_dim(initial, at, 4, 1) for at in place(n - 4)]
+    of_chip, of_core = neighbours(*near)
+    conc, mob, to_chip, to_core = call(
         own_kernel,
         (lies_padded(runs, n), lies_padded(n), (3, ny, nz), (3, ny, nz)),
         (),
         (initial, mobility),
         runs * n * cell,
     )
-    m_low, m_high = neighbours(first, last)
-    (chem0,) = call(
-        chem_kernel, (lies_padded(runs, n + 6),), (lies_padded(8),), (low, conc, high),
+    m_chip, m_core = neighbours(to_chip, to_core)
+    chem0, conc_rim = call(
+        chem_kernel, (lies_padded(runs, n + 6), lies_padded(runs, 8)), (), (of_chip, of_core, conc),
         20 * runs * (n + 6) * cell,
     )
-    *faces, state1, chem1, adjoint2, first, last, miss_sum = call(
+    *faces, state1, chem1, adjoint2, to_chip, to_core, miss_sum = call(
         forward_kernel,
         (
             lies(n + 5), lies_padded(n + 4), lies(n + 4), lies(n + 4), lies(n + 4),
             lies_padded(runs, n + 4), lies_padded(runs, n + 2), lies_padded(runs, n),
-            (runs, 3, ny, nz), (runs, 3, ny, nz), (1, LANES),
+            lies(runs, 3), lies(runs, 3), (1, LANES),
         ),
         (lies_padded(6), (CHUNK, LANES)),
-        (m_low, mob, m_high, low, conc, high, observed, chem0),
+        (m_chip, m_core, mob, conc, conc_rim, observed, chem0),
         60 * runs * (n + 4) * cell,
     )
-    low, high = neighbours(first, last)
+    of_chip, of_core = neighbours(to_chip, to_core)
     shares, flow_own, weight, step_z0, sum_x, sum_y, sum_z = call(
         middle_kernel,
         (
@@ -460,7 +479,7 @@
             lies(n + 1), lies_padded(n), lies(n),
         ),
         (
-            low, high, *faces, chem0, chem1, adjoint2, flow_own, weight, step_z0,
+            of_chip, of_core, *faces, chem0, chem1, adjoint2, flow_own, weight, step_z0,
             sum_x, sum_y, sum_z, shares,
         ),
         40 * runs * (n + 2) * cell,

time: 41 us -> 44.2 us (1.078)
  blocking collectives: 10.4 us -> 15.4 us
  starting transfers between devices: 14.5 us -> 12 us
  waiting for transfers between devices: 6.23 us -> 6.89 us
    all_to_all x1, blocking collectives: 10.4 us -> 15.4 us  [on_device(): shares = lax.all_to_all(shares, 'gx', 0, 0)]
    ppermute x6, starting transfers between devices: 14.5 us -> 12 us  [the longest x3 9.45 us: neighbours(): lax.ppermute(to_chip, 'gx', over_chips)]
    ppermute x6, waiting for transfers between devices: 6.23 us -> 6.89 us  [the longest x3 6.88 us: neighbours(): lax.ppermute(to_chip, 'gx', over_chips)]
  transfers between devices with their start and end apart: 6 -> 6, of which waited for: 3 -> 2; matrix products, arithmetic and copies ran while one was open for 0% -> 0% of each run, Pallas kernels for 5% -> 5%
where the time goes in v5:
time: 44.2 us; the launch traced here: 44 us
  blocking collectives  15.4 us (35%)
  starting transfers between devices  12 us (27%)
  Pallas kernels  6.98 us (16%)
  waiting for transfers between devices  6.89 us (16%)
  local copies, waits for them, and re-layouts  2.03 us (5%)
  between operations  0.69 us (2%)
    all_to_all x1, blocking collectives, on_device(): shares = lax.all_to_all(shares, 'gx', 0, 0)  15.4 us
    ppermute x3, starting transfers between devices, neighbours(): lax.ppermute(to_chip, 'gx', over_chips)  9.45 us
    pallas_call x5, Pallas kernels, call(): pl.pallas_call(kernel, out_shape=tuple((jax.ShapeDtypeStruct(o, jnp.float...  6.98 us
    ppermute x3, waiting for transfers between devices, neighbours(): lax.ppermute(to_chip, 'gx', over_chips)  6.88 us
    ppermute x3, starting transfers between devices, neighbours(): lax.ppermute(to_core, 'gx', over_cores)  2.54 us
    unnamed x6, local copies, waits for them, and re-layouts  2.03 us
  transfers between devices with their start and end apart: 6, of which 2 were waited for; matrix products, arithmetic and copies ran while one was open for 0% of the time, Pallas kernels for 5%

profile of v5, /device:TPU:0, one launch (start us, length us, event | category | flops | bytes accessed | tf_op | source)
XLA Modules:
  0.0 44.0 jit_solution(10882694380747915062)
XLA Ops:
  0.6 0.0 copy-start
  0.6 0.5 %collective-permute-start.3 = (f32[2,4,64,256]{3,2,1,0:T(8,128)}, f32[2,4,64,256]{3,2,1,0:T(8,128)S(1)}, u32[]{:S(2)}, u32[]{:S(2)}) collective-permute-start(f32[2,4,64,256]{3,2,1,0:T(8,128)} %initial.1), channel_id=1, source_target_pairs={{0,1},{1,0},{2,3},{3,2},{4,5},{5,4},{6,7},{7,6},{8,9},{9,8},{10,11... | collective-permute-start | bytes 1572872 | tf_op jit(solution)/shard_map/ppermute | solution.py:426
  1.2 5.7 %collective-permute-start.2 = (f32[2,4,64,256]{3,2,1,0:T(8,128)}, f32[2,4,64,256]{3,2,1,0:T(8,128)S(1)}, u32[]{:S(2)}, u32[]{:S(2)}) collective-permute-start(f32[2,4,64,256]{3,2,1,0:T(8,128)} %initial.1), channel_id=1, source_target_pairs={{0,15},{1,2},{2,1},{3,4},{4,3},{5,6},{6,5},{7,8},{8,7},{9,10},{10,... | collective-permute-start | bytes 1572872 | tf_op jit(solution)/shard_map/ppermute | solution.py:426
  6.8 0.0 copy-start.1
  6.8 1.1 %copy-done.1 = f32[2,4,64,256]{3,2,1,0:T(8,128)S(1)} copy-done((f32[2,4,64,256]{3,2,1,0:T(8,128)S(1)}, f32[2,4,64,256]{3,2,1,0:T(8,128)}, u32[]{:S(2)}) %copy-start.1) | copy-done | bytes 524312
  7.9 0.0 copy-start.2
  7.9 0.9 %copy-done.2 = f32[4,64,256]{2,1,0:T(8,128)S(1)} copy-done((f32[4,64,256]{2,1,0:T(8,128)S(1)}, f32[4,64,256]{2,1,0:T(8,128)}, u32[]{:S(2)}) %copy-start.2) | copy-done | bytes 262168
  8.9 0.1 shard_map.50
  8.9 0.1 collective-permute-start
  9.0 0.1 collective-permute-start.1
  9.1 0.0 collective-permute-done.3.of_core
  9.1 4.9 %collective-permute-done.2.of_chip = f32[2,4,64,256]{3,2,1,0:T(8,128)S(1)} collective-permute-done((f32[2,4,64,256]{3,2,1,0:T(8,128)}, f32[2,4,64,256]{3,2,1,0:T(8,128)S(1)}, u32[]{:S(2)}, u32[]{:S(2)}) %collective-permute-start.2) | collective-permute-done | bytes 524320 | tf_op jit(solution)/shard_map/ppermute | solution.py:426
  14.0 0.9 %shard_map.51 = (f32[2,10,2,80,128]{4,3,2,1,0:T(8,128)S(1)}, f32[2,8,2,80,128]{4,3,2,1,0:T(8,128)S(1)}) custom-call(f32[2,4,64,256]{3,2,1,0:T(8,128)S(1)} %collective-permute-done.2.of_chip, f32[2,4,64,256]{3,2,1,0:T(8,128)S(1)} %collective-permute-done.3.of_core, f32[2,4,2,80,128]{4,3,2,1,0:T(8,128)S(1)} %get-tuple-element.29.own), custom_call_target="tpu_custom_call" | custom-call | flops 6553600 | bytes 4653056 | tf_op jit(solution)/shard_map/pallas_call | solution.py:406
  14.9 2.0 %collective-permute-done.m_chip = f32[3,64,256]{2,1,0:T(8,128)S(1)} collective-permute-done((f32[3,64,256]{2,1,0:T(8,128)S(1)}, f32[3,64,256]{2,1,0:T(8,128)S(1)}, u32[]{:S(2)}, u32[]{:S(2)}) %collective-permute-start) | collective-permute-done | bytes 196640 | tf_op jit(solution)/shard_map/ppermute | solution.py:426
  16.9 0.0 collective-permute-done.1.m_core
  16.9 0.0 copy-done
  16.9 2.4 %shard_map.52 = (f32[9,2,64,128]{3,2,1,0:T(8,128)S(1)}, f32[8,2,80,128]{3,2,1,0:T(8,128)S(1)}, f32[8,2,64,128]{3,2,1,0:T(8,128)S(1)}, f32[8,2,64,128]{3,2,1,0:T(...) custom-call(f32[3,64,256]{2,1,0:T(8,128)S(1)} %collective-permute-do, ...), custom_call_target="tpu_custom_call" | custom-call | flops 15728640 | bytes 11403776 | tf_op jit(solution)/shard_map/pallas_call | solution.py:406
  19.3 3.7 %collective-permute-start.4 = (f32[2,3,2,64,128]{4,3,2,1,0:T(8,128)S(1)}, f32[2,3,2,64,128]{4,3,2,1,0:T(8,128)S(1)}, u32[]{:S(2)}, u32[]{:S(2)}) collective-permute-start(f32[2,3,2,64,128]{4,3,2,1,0:T(8,128)S(1)} %get-tuple-element.32), channel_id=1, source_target_pairs={{0,15},{1,2},{2,1},{3,4},{4,3},{5,6},{6,5},{7,8},{8,7},{9,10},{10,... | collective-permute-start | bytes 1179656 | tf_op jit(solution)/shard_map/ppermute | solution.py:426
  23.0 2.0 %collective-permute-start.5 = (f32[2,3,2,64,128]{4,3,2,1,0:T(8,128)S(1)}, f32[2,3,2,64,128]{4,3,2,1,0:T(8,128)S(1)}, u32[]{:S(2)}, u32[]{:S(2)}) collective-permute-start(f32[2,3,2,64,128]{4,3,2,1,0:T(8,128)S(1)} %get-tuple-element.33), channel_id=1, source_target_pairs={{0,1},{1,0},{2,3},{3,2},{4,5},{5,4},{6,7},{7,6},{8,9},{9,8},{10,11... | collective-permute-start | bytes 1179656 | tf_op jit(solution)/shard_map/ppermute | solution.py:426
  24.9 1.0 %shard_map.53 = (f32[16,1,128]{2,1,0:T(1,128)S(1)}, f32[2,4,2,80,128]{4,3,2,1,0:T(8,128)S(1)}, f32[2,6,2,64,128]{4,3,2,1,0:T(8,128)S(1)}, f32[2,4,2,64,128]{4,3,...) custom-call(f32[9,2,64,128]{3,2,1,0:T(8,128)S(1)} %get-tuple-element, ...), custom_call_target="tpu_custom_call" | custom-call | flops 5242880 | bytes 10232320 | tf_op jit(solution)/shard_map/pallas_call | solution.py:406
  26.0 15.4 %all_to_all.5.shares = f32[16,1,128]{2,1,0:T(1,128)S(1)} all-to-all(f32[16,1,128]{2,1,0:T(1,128)S(1)} %get-tuple-element.49), channel_id=1, replica_groups=mesh['group'=2,'gx'=16] {'gx'}, dimensions={0} | all-to-all | bytes 16384 | tf_op jit(solution)/shard_map/all_to_all | solution.py:473
  41.4 0.0 collective-permute-done.4.of_chip
  41.4 0.0 collective-permute-done.5.of_core
  41.4 2.6 %shard_map.54 = (f32[4,64,256]{2,1,0:T(8,128)}, f32[1]{0:T(128)}) custom-call(f32[2,3,2,64,128]{4,3,2,1,0:T(8,128)S(1)} %collective-permute-done.4.of_chip, f32[2,3,2,64,128]{4,3,2,1,0:T(8,128)S(1)} %collective-permute-done.5.of_core, f32[9,2,64,128]{3,2,1,0:T(8,128)S(1)} %get-tuple-element.34.mx, f32[8,2,80,128]{3,2,1,0:T(8,128)S(1)} %get-tuple-element.35.my, ...), custom_call_target="tpu_custom_call" | custom-call | flops 7864320 | bytes 9969668 | tf_op jit(solution)/shard_map/pallas_call | solution.py:406
Async XLA Ops:
  0.6 16.3 %copy-start = (f32[2,4,64,256]{3,2,1,0:T(8,128)S(1)}, f32[2,4,64,256]{3,2,1,0:T(8,128)}, u32[]{:S(2)}) copy-start(f32[2,4,64,256]{3,2,1,0:T(8,128)} %observed.1) | copy-start | bytes 1572868
  0.6 8.5 %collective-permute-start.3 = (f32[2,4,64,256]{3,2,1,0:T(8,128)}, f32[2,4,64,256]{3,2,1,0:T(8,128)S(1)}, u32[]{:S(2)}, u32[]{:S(2)}) collective-permute-start(f32[2,4,64,256]{3,2,1,0:T(8,128)} %initial.1), channel_id=1, source_target_pairs={{0,1},{1,0},{2,3},{3,2},{4,5},{5,4},{6,7},{7,6},{8,9},{9,8},{10,11... | collective-permute-start | bytes 1572872 | tf_op jit(solution)/shard_map/ppermute | solution.py:426
  1.2 12.8 %collective-permute-start.2 = (f32[2,4,64,256]{3,2,1,0:T(8,128)}, f32[2,4,64,256]{3,2,1,0:T(8,128)S(1)}, u32[]{:S(2)}, u32[]{:S(2)}) collective-permute-start(f32[2,4,64,256]{3,2,1,0:T(8,128)} %initial.1), channel_id=1, source_target_pairs={{0,15},{1,2},{2,1},{3,4},{4,3},{5,6},{6,5},{7,8},{8,7},{9,10},{10,... | collective-permute-start | bytes 1572872 | tf_op jit(solution)/shard_map/ppermute | solution.py:426
  6.8 1.1 %copy-start.1 = (f32[2,4,64,256]{3,2,1,0:T(8,128)S(1)}, f32[2,4,64,256]{3,2,1,0:T(8,128)}, u32[]{:S(2)}) copy-start(f32[2,4,64,256]{3,2,1,0:T(8,128)} %initial.1) | copy-start | bytes 1572868
  7.9 0.9 %copy-start.2 = (f32[4,64,256]{2,1,0:T(8,128)S(1)}, f32[4,64,256]{2,1,0:T(8,128)}, u32[]{:S(2)}) copy-start(f32[4,64,256]{2,1,0:T(8,128)} %mobility.1) | copy-start | bytes 786436
  8.9 8.0 %collective-permute-start = (f32[3,64,256]{2,1,0:T(8,128)S(1)}, f32[3,64,256]{2,1,0:T(8,128)S(1)}, u32[]{:S(2)}, u32[]{:S(2)}) collective-permute-start(f32[3,64,256]{2,1,0:T(8,128)S(1)} %get-tuple-element.26), channel_id=1, source_target_pairs={{0,15},{1,2},{2,1},{3,4},{4,3},{5,6},{6,5},{7,8},{8,7},{9,10},{10,... | collective-permute-start | bytes 589832 | tf_op jit(solution)/shard_map/ppermute | solution.py:426
  9.0 7.9 %collective-permute-start.1 = (f32[3,64,256]{2,1,0:T(8,128)S(1)}, f32[3,64,256]{2,1,0:T(8,128)S(1)}, u32[]{:S(2)}, u32[]{:S(2)}) collective-permute-start(f32[3,64,256]{2,1,0:T(8,128)S(1)} %get-tuple-element.27), channel_id=1, source_target_pairs={{0,1},{1,0},{2,3},{3,2},{4,5},{5,4},{6,7},{7,6},{8,9},{9,8},{10,11... | collective-permute-start | bytes 589832 | tf_op jit(solution)/shard_map/ppermute | solution.py:426
  19.3 22.1 %collective-permute-start.4 = (f32[2,3,2,64,128]{4,3,2,1,0:T(8,128)S(1)}, f32[2,3,2,64,128]{4,3,2,1,0:T(8,128)S(1)}, u32[]{:S(2)}, u32[]{:S(2)}) collective-permute-start(f32[2,3,2,64,128]{4,3,2,1,0:T(8,128)S(1)} %get-tuple-element.32), channel_id=1, source_target_pairs={{0,15},{1,2},{2,1},{3,4},{4,3},{5,6},{6,5},{7,8},{8,7},{9,10},{10,... | collective-permute-start | bytes 1179656 | tf_op jit(solution)/shard_map/ppermute | solution.py:426
  23.0 18.4 %collective-permute-start.5 = (f32[2,3,2,64,128]{4,3,2,1,0:T(8,128)S(1)}, f32[2,3,2,64,128]{4,3,2,1,0:T(8,128)S(1)}, u32[]{:S(2)}, u32[]{:S(2)}) collective-permute-start(f32[2,3,2,64,128]{4,3,2,1,0:T(8,128)S(1)} %get-tuple-element.33), channel_id=1, source_target_pairs={{0,1},{1,0},{2,3},{3,2},{4,5},{5,4},{6,7},{7,6},{8,9},{9,8},{10,11... | collective-permute-start | bytes 1179656 | tf_op jit(solution)/shard_map/ppermute | solution.py:426

commit v6 on v5

--- a/solution.py
+++ b/solution.py
@@ -164,7 +164,7 @@
 
 def forward_kernel(
     m_chip, m_core, m_own, own, conc_rim, observed, chem0,
-    mx, my, mz, mz_low, m_all, state1, chem1, adjoint2, to_chip, to_core, miss_sum,
+    mx, my, mz, mz_low, m_all, state1, chem1, adjoint2, to_core, to_chip, miss_sum,
     rim, total,
 ):
     runs, n, ny, _ = observed.shape
@@ -308,7 +308,7 @@
 
 
 def backward_kernel(
-    of_chip, of_core, mx, my, mz, mz_low, m_all, chem0, chem1, adjoint2, flow_own, weight, step_z0,
+    of_core, of_chip, mx, my, mz, mz_low, m_all, chem0, chem1, adjoint2, flow_own, weight, step_z0,
     sum_x_in, sum_y_in, sum_z_in, shares, result, misfit, wide, flow_rim, adjoint1, sum_x, sum_y, sum_z,
 ):
     runs, n = adjoint2.shape[:2]
@@ -423,7 +423,8 @@
     cell = ny * nz
 
     def neighbours(to_chip, to_core):
-        return lax.ppermute(to_chip, "gx", over_chips), lax.ppermute(to_core, "gx", over_cores)
+        of_core = lax.ppermute(to_core, "gx", over_cores)
+        return lax.ppermute(to_chip, "gx", over_chips), of_core
 
     def lies(*lead):
         return (*lead, blocks, ny, LANES)
@@ -448,7 +449,7 @@
         chem_kernel, (lies_padded(runs, n + 6), lies_padded(runs, 8)), (), (of_chip, of_core, conc),
         20 * runs * (n + 6) * cell,
     )
-    *faces, state1, chem1, adjoint2, to_chip, to_core, miss_sum = call(
+    *faces, state1, chem1, adjoint2, to_core, to_chip, miss_sum = call(
         forward_kernel,
         (
             lies(n + 5), lies_padded(n + 4), lies(n + 4), lies(n + 4), lies(n + 4),
@@ -479,7 +480,7 @@
             lies(n + 1), lies_padded(n), lies(n),
         ),
         (
-            of_chip, of_core, *faces, chem0, chem1, adjoint2, flow_own, weight, step_z0,
+            of_core, of_chip, *faces, chem0, chem1, adjoint2, flow_own, weight, step_z0,
             sum_x, sum_y, sum_z, shares,
         ),
         40 * runs * (n + 2) * cell,

time: 44.2 us -> 40.8 us (0.923)
  blocking collectives: 15.4 us -> 8.98 us
  starting transfers between devices: 12 us -> 15 us
    all_to_all x1, blocking collectives: 15.4 us -> 8.98 us  [on_device(): shares = lax.all_to_all(shares, 'gx', 0, 0)]
    ppermute x6, starting transfers between devices: 12 us -> 15 us  [the longest x3 10.5 us: neighbours(): return (lax.ppermute(to_chip, 'gx', over_chips), of_core)]
where the time goes in v6:
time: 40.8 us; the launch traced here: 40.6 us
  starting transfers between devices  15 us (37%)
  blocking collectives  8.98 us (22%)
  Pallas kernels  6.99 us (17%)
  waiting for transfers between devices  6.89 us (17%)
  local copies, waits for them, and re-layouts  2.03 us (5%)
  between operations  0.69 us (2%)
    ppermute x3, starting transfers between devices, neighbours(): return (lax.ppermute(to_chip, 'gx', over_chips), of_core)  10.5 us
    all_to_all x1, blocking collectives, on_device(): shares = lax.all_to_all(shares, 'gx', 0, 0)  8.98 us
    pallas_call x5, Pallas kernels, call(): pl.pallas_call(kernel, out_shape=tuple((jax.ShapeDtypeStruct(o, jnp.float...  6.99 us
    ppermute x3, waiting for transfers between devices, neighbours(): return (lax.ppermute(to_chip, 'gx', over_chips), of_core)  6.88 us
    ppermute x3, starting transfers between devices, neighbours(): of_core = lax.ppermute(to_core, 'gx', over_cores)  4.52 us
    unnamed x6, local copies, waits for them, and re-layouts  2.03 us
  transfers between devices with their start and end apart: 6, of which 2 were waited for; matrix products, arithmetic and copies ran while one was open for 0% of the time, Pallas kernels for 5%

profile of v6, /device:TPU:0, one launch (start us, length us, event | category | flops | bytes accessed | tf_op | source)
XLA Modules:
  0.0 40.6 jit_solution(18427473433286736655)
XLA Ops:
  0.6 0.0 copy-start
  0.6 0.5 %collective-permute-start.3 = (f32[2,4,64,256]{3,2,1,0:T(8,128)}, f32[2,4,64,256]{3,2,1,0:T(8,128)S(1)}, u32[]{:S(2)}, u32[]{:S(2)}) collective-permute-start(f32[2,4,64,256]{3,2,1,0:T(8,128)} %initial.1), channel_id=1, source_target_pairs={{0,1},{1,0},{2,3},{3,2},{4,5},{5,4},{6,7},{7,6},{8,9},{9,8},{10,11... | collective-permute-start | bytes 1572872 | tf_op jit(solution)/shard_map/ppermute | solution.py:426
  1.2 5.7 %collective-permute-start.2 = (f32[2,4,64,256]{3,2,1,0:T(8,128)}, f32[2,4,64,256]{3,2,1,0:T(8,128)S(1)}, u32[]{:S(2)}, u32[]{:S(2)}) collective-permute-start(f32[2,4,64,256]{3,2,1,0:T(8,128)} %initial.1), channel_id=1, source_target_pairs={{0,15},{1,2},{2,1},{3,4},{4,3},{5,6},{6,5},{7,8},{8,7},{9,10},{10,... | collective-permute-start | bytes 1572872 | tf_op jit(solution)/shard_map/ppermute | solution.py:427
  6.8 0.0 copy-start.1
  6.8 1.1 %copy-done.1 = f32[2,4,64,256]{3,2,1,0:T(8,128)S(1)} copy-done((f32[2,4,64,256]{3,2,1,0:T(8,128)S(1)}, f32[2,4,64,256]{3,2,1,0:T(8,128)}, u32[]{:S(2)}) %copy-start.1) | copy-done | bytes 524312
  7.9 0.0 copy-start.2
  7.9 0.9 %copy-done.2 = f32[4,64,256]{2,1,0:T(8,128)S(1)} copy-done((f32[4,64,256]{2,1,0:T(8,128)S(1)}, f32[4,64,256]{2,1,0:T(8,128)}, u32[]{:S(2)}) %copy-start.2) | copy-done | bytes 262168
  8.9 0.1 shard_map.50
  8.9 0.1 collective-permute-start
  9.0 0.1 collective-permute-start.1
  9.1 0.0 collective-permute-done.3.of_core
  9.1 4.9 %collective-permute-done.2.of_chip = f32[2,4,64,256]{3,2,1,0:T(8,128)S(1)} collective-permute-done((f32[2,4,64,256]{3,2,1,0:T(8,128)}, f32[2,4,64,256]{3,2,1,0:T(8,128)S(1)}, u32[]{:S(2)}, u32[]{:S(2)}) %collective-permute-start.2) | collective-permute-done | bytes 524320 | tf_op jit(solution)/shard_map/ppermute | solution.py:427
  14.0 0.9 %shard_map.51 = (f32[2,10,2,80,128]{4,3,2,1,0:T(8,128)S(1)}, f32[2,8,2,80,128]{4,3,2,1,0:T(8,128)S(1)}) custom-call(f32[2,4,64,256]{3,2,1,0:T(8,128)S(1)} %collective-permute-done.2.of_chip, f32[2,4,64,256]{3,2,1,0:T(8,128)S(1)} %collective-permute-done.3.of_core, f32[2,4,2,80,128]{4,3,2,1,0:T(8,128)S(1)} %get-tuple-element.29.own), custom_call_target="tpu_custom_call" | custom-call | flops 6553600 | bytes 4653056 | tf_op jit(solution)/shard_map/pallas_call | solution.py:406
  14.9 2.0 %collective-permute-done.m_chip = f32[3,64,256]{2,1,0:T(8,128)S(1)} collective-permute-done((f32[3,64,256]{2,1,0:T(8,128)S(1)}, f32[3,64,256]{2,1,0:T(8,128)S(1)}, u32[]{:S(2)}, u32[]{:S(2)}) %collective-permute-start) | collective-permute-done | bytes 196640 | tf_op jit(solution)/shard_map/ppermute | solution.py:427
  16.9 0.0 collective-permute-done.1.m_core
  16.9 0.0 copy-done
  16.9 2.4 %shard_map.52 = (f32[9,2,64,128]{3,2,1,0:T(8,128)S(1)}, f32[8,2,80,128]{3,2,1,0:T(8,128)S(1)}, f32[8,2,64,128]{3,2,1,0:T(8,128)S(1)}, f32[8,2,64,128]{3,2,1,0:T(...) custom-call(f32[3,64,256]{2,1,0:T(8,128)S(1)} %collective-permute-do, ...), custom_call_target="tpu_custom_call" | custom-call | flops 15728640 | bytes 11403776 | tf_op jit(solution)/shard_map/pallas_call | solution.py:406
  19.3 3.9 %collective-permute-start.4 = (f32[2,3,2,64,128]{4,3,2,1,0:T(8,128)S(1)}, f32[2,3,2,64,128]{4,3,2,1,0:T(8,128)S(1)}, u32[]{:S(2)}, u32[]{:S(2)}) collective-permute-start(f32[2,3,2,64,128]{4,3,2,1,0:T(8,128)S(1)} %get-tuple-element.32), channel_id=1, source_target_pairs={{0,1},{1,0},{2,3},{3,2},{4,5},{5,4},{6,7},{7,6},{8,9},{9,8},{10,11... | collective-permute-start | bytes 1179656 | tf_op jit(solution)/shard_map/ppermute | solution.py:426
  23.2 4.8 %collective-permute-start.5 = (f32[2,3,2,64,128]{4,3,2,1,0:T(8,128)S(1)}, f32[2,3,2,64,128]{4,3,2,1,0:T(8,128)S(1)}, u32[]{:S(2)}, u32[]{:S(2)}) collective-permute-start(f32[2,3,2,64,128]{4,3,2,1,0:T(8,128)S(1)} %get-tuple-element.33), channel_id=1, source_target_pairs={{0,15},{1,2},{2,1},{3,4},{4,3},{5,6},{6,5},{7,8},{8,7},{9,10},{10,... | collective-permute-start | bytes 1179656 | tf_op jit(solution)/shard_map/ppermute | solution.py:427
  28.0 1.0 %shard_map.53 = (f32[16,1,128]{2,1,0:T(1,128)S(1)}, f32[2,4,2,80,128]{4,3,2,1,0:T(8,128)S(1)}, f32[2,6,2,64,128]{4,3,2,1,0:T(8,128)S(1)}, f32[2,4,2,64,128]{4,3,...) custom-call(f32[9,2,64,128]{3,2,1,0:T(8,128)S(1)} %get-tuple-element, ...), custom_call_target="tpu_custom_call" | custom-call | flops 5242880 | bytes 10232320 | tf_op jit(solution)/shard_map/pallas_call | solution.py:406
  29.0 9.0 %all_to_all.5.shares = f32[16,1,128]{2,1,0:T(1,128)S(1)} all-to-all(f32[16,1,128]{2,1,0:T(1,128)S(1)} %get-tuple-element.49), channel_id=1, replica_groups=mesh['group'=2,'gx'=16] {'gx'}, dimensions={0} | all-to-all | bytes 16384 | tf_op jit(solution)/shard_map/all_to_all | solution.py:474
  38.0 0.0 collective-permute-done.4.of_core
  38.0 0.0 collective-permute-done.5.of_chip
  38.0 2.6 %shard_map.54 = (f32[4,64,256]{2,1,0:T(8,128)}, f32[1]{0:T(128)}) custom-call(f32[2,3,2,64,128]{4,3,2,1,0:T(8,128)S(1)} %collective-permute-done.4.of_core, f32[2,3,2,64,128]{4,3,2,1,0:T(8,128)S(1)} %collective-permute-done.5.of_chip, f32[9,2,64,128]{3,2,1,0:T(8,128)S(1)} %get-tuple-element.34.mx, f32[8,2,80,128]{3,2,1,0:T(8,128)S(1)} %get-tuple-element.35.my, ...), custom_call_target="tpu_custom_call" | custom-call | flops 7864320 | bytes 9969668 | tf_op jit(solution)/shard_map/pallas_call | solution.py:406
Async XLA Ops:
  0.6 16.3 %copy-start = (f32[2,4,64,256]{3,2,1,0:T(8,128)S(1)}, f32[2,4,64,256]{3,2,1,0:T(8,128)}, u32[]{:S(2)}) copy-start(f32[2,4,64,256]{3,2,1,0:T(8,128)} %observed.1) | copy-start | bytes 1572868
  0.6 8.5 %collective-permute-start.3 = (f32[2,4,64,256]{3,2,1,0:T(8,128)}, f32[2,4,64,256]{3,2,1,0:T(8,128)S(1)}, u32[]{:S(2)}, u32[]{:S(2)}) collective-permute-start(f32[2,4,64,256]{3,2,1,0:T(8,128)} %initial.1), channel_id=1, source_target_pairs={{0,1},{1,0},{2,3},{3,2},{4,5},{5,4},{6,7},{7,6},{8,9},{9,8},{10,11... | collective-permute-start | bytes 1572872 | tf_op jit(solution)/shard_map/ppermute | solution.py:426
  1.2 12.8 %collective-permute-start.2 = (f32[2,4,64,256]{3,2,1,0:T(8,128)}, f32[2,4,64,256]{3,2,1,0:T(8,128)S(1)}, u32[]{:S(2)}, u32[]{:S(2)}) collective-permute-start(f32[2,4,64,256]{3,2,1,0:T(8,128)} %initial.1), channel_id=1, source_target_pairs={{0,15},{1,2},{2,1},{3,4},{4,3},{5,6},{6,5},{7,8},{8,7},{9,10},{10,... | collective-permute-start | bytes 1572872 | tf_op jit(solution)/shard_map/ppermute | solution.py:427
  6.8 1.1 %copy-start.1 = (f32[2,4,64,256]{3,2,1,0:T(8,128)S(1)}, f32[2,4,64,256]{3,2,1,0:T(8,128)}, u32[]{:S(2)}) copy-start(f32[2,4,64,256]{3,2,1,0:T(8,128)} %initial.1) | copy-start | bytes 1572868
  7.9 0.9 %copy-start.2 = (f32[4,64,256]{2,1,0:T(8,128)S(1)}, f32[4,64,256]{2,1,0:T(8,128)}, u32[]{:S(2)}) copy-start(f32[4,64,256]{2,1,0:T(8,128)} %mobility.1) | copy-start | bytes 786436
  8.9 8.0 %collective-permute-start = (f32[3,64,256]{2,1,0:T(8,128)S(1)}, f32[3,64,256]{2,1,0:T(8,128)S(1)}, u32[]{:S(2)}, u32[]{:S(2)}) collective-permute-start(f32[3,64,256]{2,1,0:T(8,128)S(1)} %get-tuple-element.26), channel_id=1, source_target_pairs={{0,15},{1,2},{2,1},{3,4},{4,3},{5,6},{6,5},{7,8},{8,7},{9,10},{10,... | collective-permute-start | bytes 589832 | tf_op jit(solution)/shard_map/ppermute | solution.py:427
  9.0 7.9 %collective-permute-start.1 = (f32[3,64,256]{2,1,0:T(8,128)S(1)}, f32[3,64,256]{2,1,0:T(8,128)S(1)}, u32[]{:S(2)}, u32[]{:S(2)}) collective-permute-start(f32[3,64,256]{2,1,0:T(8,128)S(1)} %get-tuple-element.27), channel_id=1, source_target_pairs={{0,1},{1,0},{2,3},{3,2},{4,5},{5,4},{6,7},{7,6},{8,9},{9,8},{10,11... | collective-permute-start | bytes 589832 | tf_op jit(solution)/shard_map/ppermute | solution.py:426
  19.3 18.7 %collective-permute-start.4 = (f32[2,3,2,64,128]{4,3,2,1,0:T(8,128)S(1)}, f32[2,3,2,64,128]{4,3,2,1,0:T(8,128)S(1)}, u32[]{:S(2)}, u32[]{:S(2)}) collective-permute-start(f32[2,3,2,64,128]{4,3,2,1,0:T(8,128)S(1)} %get-tuple-element.32), channel_id=1, source_target_pairs={{0,1},{1,0},{2,3},{3,2},{4,5},{5,4},{6,7},{7,6},{8,9},{9,8},{10,11... | collective-permute-start | bytes 1179656 | tf_op jit(solution)/shard_map/ppermute | solution.py:426
  23.2 14.8 %collective-permute-start.5 = (f32[2,3,2,64,128]{4,3,2,1,0:T(8,128)S(1)}, f32[2,3,2,64,128]{4,3,2,1,0:T(8,128)S(1)}, u32[]{:S(2)}, u32[]{:S(2)}) collective-permute-start(f32[2,3,2,64,128]{4,3,2,1,0:T(8,128)S(1)} %get-tuple-element.33), channel_id=1, source_target_pairs={{0,15},{1,2},{2,1},{3,4},{4,3},{5,6},{6,5},{7,8},{8,7},{9,10},{10,... | collective-permute-start | bytes 1179656 | tf_op jit(solution)/shard_map/ppermute | solution.py:427

commit v7 on v0

v7 whole, which is shorter than its diff:
```python
import functools
import math

import jax
import jax.numpy as jnp
from jax import lax
from jax.experimental import pallas as pl
from jax.experimental.pallas import tpu as pltpu
from jax.sharding import PartitionSpec as P

stiffness = 0.5
time_step = 0.005
VMEM = pl.BlockSpec(memory_space=pltpu.VMEM)
LANES = 128
ROWS = 8
PAD = ROWS
CHUNK = 16


def chunks(ny):
    return range(0, ny, CHUNK)


def plain(ref, lead, row):
    return [
        ref[(*lead, pl.ds(row, CHUNK), pl.ds(at, LANES))] for at in range(0, ref.shape[-1], LANES)
    ]


def put_plain(ref, lead, row, value):
    for block, part in enumerate(value):
        ref[(*lead, pl.ds(row, CHUNK), pl.ds(block * LANES, LANES))] = part


def flat(ref, lead, row):
    return [ref[(*lead, block, pl.ds(row, CHUNK))] for block in range(ref.shape[-3])]


def put_flat(ref, lead, row, value):
    for block, part in enumerate(value):
        ref[(*lead, block, pl.ds(row, CHUNK))] = part


def padded(ref, lead, row, shift=0):
    return [ref[(*lead, block, pl.ds(PAD + row + shift, CHUNK))] for block in range(ref.shape[-3])]


def put_padded(ref, lead, row, value):
    ny = ref.shape[-2] - 2 * PAD
    for block, part in enumerate(value):
        ref[(*lead, block, pl.ds(PAD + row, CHUNK))] = part
        if row == 0:
            ref[(*lead, block, pl.ds(PAD + ny, 1))] = part[:1]
        if row + CHUNK == ny:
            ref[(*lead, block, pl.ds(PAD - 1, 1))] = part[CHUNK - 1 :]


def lane():
    return lax.broadcasted_iota(jnp.int32, (CHUNK, LANES), 1)


def after_z(value):
    turned = [pltpu.roll(part, LANES - 1, 1) for part in value]
    turned.append(turned[0])
    edge = lane() == LANES - 1
    return [jnp.where(edge, turned[at + 1], turned[at]) for at in range(len(value))]


def before_z(value):
    turned = [pltpu.roll(part, 1, 1) for part in value]
    edge = lane() == 0
    return [jnp.where(edge, turned[at - 1], turned[at]) for at in range(len(value))]


def side():
    return lax.rem(lax.axis_index("gx"), 2)


def either(first, second):
    return first + side() * (second - first)


class Line:
    def __init__(self, *parts):
        self.parts = parts

    def __call__(self, at, *lead):
        for ref, first, last in self.parts:
            if first <= at <= last:
                return ref, (*lead, at - first)
        raise IndexError(at)


def each(function, *values):
    return [function(*parts) for parts in zip(*values)]


def beside(low, high, up, down, mid):
    return each(
        lambda a, b, c, d, e, f: (a + b) + (c + d) + (e + f),
        low, high, up, down, after_z(mid), before_z(mid),
    )


def potential(low, mid, high, up, down):
    return each(
        lambda c, total: c * (c * c + (6.0 * stiffness - 1.0)) - stiffness * total,
        mid, beside(low, high, up, down, mid),
    )


class Faces:
    def __init__(self, n, refs):
        mx_a, my_a, mz_a, mz_low_a, all_a, *late = refs
        two = lambda ref, first, last, at: ((ref, first, last), *(((late[at], last + 1, n + 1),) if late else ()))
        self.mx = Line(*two(mx_a, -3, n - 2, 0))
        self.my = Line(*two(my_a, -2, n - 1, 1))
        self.mz = Line(*two(mz_a, -2, n - 1, 2))
        self.mz_low = Line(*two(mz_low_a, -2, n - 1, 3))
        self.all = Line(*two(all_a, -2, n - 2, 4))

    def flow(self, row, at, mid, up, down, low=None, high=None):
        total = each(
            lambda a, b, c, d, e, u, v, w, x, y: (a * u + b * v) + (c * w + d * x) - e * y,
            padded(*self.my(at), row), padded(*self.my(at), row, -1), flat(*self.mz(at), row),
            flat(*self.mz_low(at), row), flat(*self.all(at), row), up, down, after_z(mid), before_z(mid), mid,
        )
        if low is not None:
            total = add_product(total, flat(*self.mx(at - 1), row), low)
        if high is not None:
            total = add_product(total, flat(*self.mx(at), row), high)
        return total


def add_product(total, a, b):
    return each(lambda t, x, y: t + x * y, total, a, b)


def sub(a, b):
    return each(lambda x, y: x - y, a, b)


def own_kernel(initial, mobility, conc, mob, to_chip, to_core):
    runs, n, ny, _ = initial.shape
    place = [either(n - 1 - at, at) for at in range(n)]

    def one_run(run, carry):
        for row in chunks(ny):
            for at in range(n):
                put_padded(conc, (run, at), row, plain(initial, (run, place[at]), row))
        return carry

    lax.fori_loop(0, runs, one_run, 0)
    for row in chunks(ny):
        for at in range(n):
            value = plain(mobility, (place[at],), row)
            put_padded(mob, (at,), row, value)
            if at < 3:
                put_flat(to_core, (at,), row, value)
            if at >= n - 3:
                put_flat(to_chip, (n - 1 - at,), row, value)


def mean(a, b):
    return 0.5 * (a + b)


def put_faces(row, mob, places, my, mz, mz_low):
    for at in places:
        mid = padded(*mob(at), row)
        put_padded(*my(at), row, each(mean, mid, padded(*mob(at), row, 1)))
        put_flat(*mz(at), row, each(mean, mid, after_z(mid)))
        put_flat(*mz_low(at), row, each(mean, mid, before_z(mid)))


def put_all(row, faces, places):
    for at in places:
        put_flat(*faces.all(at), row, each(
            lambda a, b, c, d, e, f: (a + b) + (c + d) + (e + f),
            flat(*faces.mx(at - 1), row), flat(*faces.mx(at), row), padded(*faces.my(at), row),
            padded(*faces.my(at), row, -1), flat(*faces.mz(at), row), flat(*faces.mz_low(at), row),
        ))


def put_potential(row, field, run, places, target):
    mids = {at: padded(*field(at, run), row) for at in range(places[0] - 1, places[-1] + 2)}
    for at in places:
        value = potential(
            mids[at - 1], mids[at], mids[at + 1],
            padded(*field(at, run), row, 1), padded(*field(at, run), row, -1),
        )
        put_padded(*target(at, run), row, value)


def put_step(row, faces, chem, state, run, places, target):
    mids = {at: padded(*chem(at, run), row) for at in range(places[0] - 1, places[-1] + 2)}
    for at in places:
        flow = faces.flow(
            row, at, mids[at], padded(*chem(at, run), row, 1), padded(*chem(at, run), row, -1),
            mids[at - 1], mids[at + 1],
        )
        value = each(lambda a, b: a + time_step * b, padded(*state(at, run), row), flow)
        target(at, value)


def put_miss(row, runs, observed, place, run, at, value, adjoint2):
    miss = sub(value, plain(observed, (run, place[at]), row))
    adjoint = each(lambda a: a * (1.0 / runs), miss)
    put_padded(*adjoint2(at, run), row, adjoint)
    return adjoint, sum(part * part for part in miss)


def core_kernel(of_core, m_core, conc_own, mob_own, conc_core, chem0, mx, my, mz, mz_low, m_all, rim):
    runs, n = conc_own.shape[:2]
    ny = of_core.shape[2]
    mob = Line((rim, -3, -1), (mob_own, 0, n - 1))
    faces = Faces(n, (mx, my, mz, mz_low, m_all))
    for row in chunks(ny):
        for at in range(3):
            put_padded(rim, (2 - at,), row, flat(m_core, (at,), row))
    for row in chunks(ny):
        mids = [padded(*mob(at), row) for at in range(-3, n)]
        for at in range(n + 2):
            put_flat(mx, (at,), row, each(mean, mids[at], mids[at + 1]))
        put_faces(row, mob, range(-2, n), faces.my, faces.mz, faces.mz_low)
    for row in chunks(ny):
        put_all(row, faces, range(-2, n - 1))
    place = [either(at, 3 - at) for at in range(4)]
    conc = Line((conc_core, -4, -1), (conc_own, 0, n - 1))

    def one_run(run, carry):
        for row in chunks(ny):
            for at in range(4):
                put_padded(conc_core, (run, 3 - at), row, plain(of_core, (run, place[at]), row))
        for row in chunks(ny):
            put_potential(row, conc, run, range(-3, n - 1), Line((chem0, -3, n - 2)))
        return carry

    lax.fori_loop(0, runs, one_run, 0)


def chip_kernel(
    of_chip, conc_own, conc_core, chem0_a, observed, mx, my, mz, mz_low, m_all,
    conc_chip, chem0_b, state1_a, chem1_a, adjoint2_a, squares,
):
    runs, n = conc_own.shape[:2]
    ny = observed.shape[2]
    faces = Faces(n, (mx, my, mz, mz_low, m_all))
    message = [either(3 - at, at) for at in range(4)]
    place = [either(n - 1 - at, at) for at in range(n)]
    conc = Line((conc_core, -4, -1), (conc_own, 0, n - 1), (conc_chip, n, n + 3))
    chem0 = Line((chem0_a, -3, n - 2), (chem0_b, n - 1, n + 2))
    state1 = Line((state1_a, -2, n - 2))
    chem1 = Line((chem1_a, -1, n - 3))
    adjoint2 = Line((adjoint2_a, 0, n - 4))
    squares[...] = jnp.zeros_like(squares)

    def one_run(run, carry):
        for row in chunks(ny):
            for at in range(4):
                put_padded(conc_chip, (run, at), row, plain(of_chip, (run, message[at]), row))
        for row in chunks(ny):
            put_potential(row, conc, run, range(n - 1, n + 3), chem0)
        for row in chunks(ny):
            put_step(
                row, faces, chem0, conc, run, range(-2, n - 1),
                lambda at, value: put_padded(*state1(at, run), row, value),
            )
        for row in chunks(ny):
            put_potential(row, state1, run, range(-1, n - 2), chem1)
        for row in chunks(ny):

            def target(at, value):
                squares[...] += put_miss(row, runs, observed, place, run, at, value, adjoint2)[1]

            put_step(row, faces, chem1, state1, run, range(0, n - 3), target)
        return carry

    lax.fori_loop(0, runs, one_run, 0)


def forward_kernel(
    m_chip, mob_own, conc_own, conc_chip, chem0_a, chem0_b, state1_a, chem1_a, adjoint2_a, squares, observed,
    mx_a, my_a, mz_a, mz_low_a, all_a,
    mx_b, my_b, mz_b, mz_low_b, all_b, state1_b, chem1_b, adjoint2_b, to_core, to_chip, share, rim, total,
):
    runs, n = conc_own.shape[:2]
    ny = observed.shape[2]
    faces = Faces(n, (mx_a, my_a, mz_a, mz_low_a, all_a, mx_b, my_b, mz_b, mz_low_b, all_b))
    mob = Line((mob_own, 0, n - 1), (rim, n, n + 2))
    place = [either(n - 1 - at, at) for at in range(n)]
    conc = Line((conc_own, 0, n - 1), (conc_chip, n, n + 3))
    chem0 = Line((chem0_a, -3, n - 2), (chem0_b, n - 1, n + 2))
    state1 = Line((state1_a, -2, n - 2), (state1_b, n - 1, n + 1))
    chem1 = Line((chem1_a, -1, n - 3), (chem1_b, n - 2, n))
    adjoint2 = Line((adjoint2_a, 0, n - 4), (adjoint2_b, n - 3, n - 1))
    for row in chunks(ny):
        for at in range(3):
            put_padded(rim, (at,), row, flat(m_chip, (at,), row))
    for row in chunks(ny):
        mids = [padded(*mob(at), row) for at in range(n - 1, n + 3)]
        for at in range(3):
            put_flat(mx_b, (at,), row, each(mean, mids[at], mids[at + 1]))
        put_faces(row, mob, range(n, n + 2), faces.my, faces.mz, faces.mz_low)
    for row in chunks(ny):
        put_all(row, faces, range(n - 1, n + 2))
    total[...] = squares[...]

    def one_run(run, carry):
        for row in chunks(ny):
            put_step(
                row, faces, chem0, conc, run, range(n - 1, n + 2),
                lambda at, value: put_padded(*state1(at, run), row, value),
            )
        for row in chunks(ny):
            put_potential(row, state1, run, range(n - 2, n + 1), chem1)
        for row in chunks(ny):

            def target(at, value):
                adjoint, square = put_miss(row, runs, observed, place, run, at, value, adjoint2)
                total[...] += square
                put_flat(to_chip, (run, n - 1 - at), row, adjoint)
                if at < 3:
                    put_flat(to_core, (run, at), row, adjoint)

            put_step(row, faces, chem1, state1, run, range(n - 3, n), target)
            for at in range(min(3, n - 3)):
                put_flat(to_core, (run, at), row, padded(*adjoint2(at, run), row))
        return carry

    lax.fori_loop(0, runs, one_run, 0)
    columns = (0.5 / runs) * jnp.sum(total[...], axis=0, keepdims=True)
    mine = jnp.broadcast_to(jnp.sum(columns, axis=1, keepdims=True), share.shape)
    share[...] = mine
    to_core[0, 0, 0, ny:] = mine


def put_adjoint1(row, flow, adjoint2, run, places, weight, target):
    mids = {at: padded(*flow(at, run), row) for at in range(places[0] - 1, places[-1] + 2)}
    for at in places:
        total = beside(
            mids[at - 1], mids[at + 1], padded(*flow(at, run), row, 1), padded(*flow(at, run), row, -1), mids[at]
        )
        value = each(
            lambda a, w, f, t: a + w * f - (time_step * stiffness) * t,
            padded(*adjoint2(at, run), row), weight(at), mids[at], total,
        )
        put_padded(*target(at, run), row, value)


def slope(state):
    return each(lambda c: time_step * (3.0 * c * c + (6.0 * stiffness - 1.0)), state)


def step_x(field, run, at, row):
    return sub(padded(*field(at + 1, run), row), padded(*field(at, run), row))


def step_y(field, run, at, row):
    return sub(padded(*field(at, run), row, 1), padded(*field(at, run), row))


def step_z(field, run, at, row):
    mid = padded(*field(at, run), row)
    return sub(after_z(mid), mid)


def early_kernel(
    of_core, mx_a, my_a, mz_a, mz_low_a, all_a, mx_b, my_b, mz_b, mz_low_b, all_b,
    chem0_a, chem0_b, state1_a, state1_b, chem1_a, chem1_b, adjoint2_a, adjoint2_b,
    share_in, flow_a, flow_part, adjoint1_a, weight_b, step_z_b, part, sum_x_b, sum_y_b, sum_z_b, share,
    rim, sum_x, sum_y, sum_z,
):
    share[...] = share_in[...]
    runs = of_core.shape[0]
    n = part.shape[0] + 2
    ny = part.shape[-2]
    faces = Faces(n, (mx_a, my_a, mz_a, mz_low_a, all_a, mx_b, my_b, mz_b, mz_low_b, all_b))
    chem0 = Line((chem0_a, -3, n - 2), (chem0_b, n - 1, n + 2))
    state1 = Line((state1_a, -2, n - 2), (state1_b, n - 1, n + 1))
    chem1 = Line((chem1_a, -1, n - 3), (chem1_b, n - 2, n))
    adjoint2 = Line((rim, -3, -1), (adjoint2_a, 0, n - 4), (adjoint2_b, n - 3, n - 1))
    flow = Line((flow_a, -2, n - 2), (flow_part, n - 1, n - 1))
    adjoint1 = Line((adjoint1_a, -1, n - 3))
    for sums in (sum_x, sum_y, sum_z):
        sums[...] = jnp.zeros_like(sums)

    def one_run(run, carry):
        for row in chunks(ny):
            for at in range(3):
                put_padded(rim, (run, 2 - at), row, flat(of_core, (run, at), row))
        for row in chunks(ny):
            mids = {at: padded(*adjoint2(at, run), row) for at in range(-3, n)}
            for at in range(-2, n):
                value = faces.flow(
                    row, at, mids[at], padded(*adjoint2(at, run), row, 1), padded(*adjoint2(at, run), row, -1),
                    mids[at - 1], mids.get(at + 1),
                )
                put_padded(*flow(at, run), row, value)
        for row in chunks(ny):
            put_adjoint1(
                row, flow, adjoint2, run, range(-1, n - 2),
                lambda at: slope(padded(*state1(at, run), row)), adjoint1,
            )
            for at in range(n - 2, n + 1):
                put_flat(weight_b, (run, at - (n - 2)), row, slope(padded(*state1(at, run), row)))
        for row in chunks(ny):
            for at in range(-1, n - 1):
                total = add_product(
                    flat(sum_x, (at + 1,), row), step_x(adjoint2, run, at, row), step_x(chem1, run, at, row)
                )
                if at < n - 3:
                    total = add_product(total, step_x(adjoint1, run, at, row), step_x(chem0, run, at, row))
                put_flat(sum_x, (at + 1,), row, total)
            for at in range(n):
                total_y = add_product(
                    padded(sum_y, (at,), row), step_y(adjoint2, run, at, row), step_y(chem1, run, at, row)
                )
                total_z = add_product(
                    flat(sum_z, (at,), row), step_z(adjoint2, run, at, row), step_z(chem1, run, at, row)
                )
                slant = step_z(chem0, run, at, row)
                if at < n - 2:
                    total_y = add_product(total_y, step_y(adjoint1, run, at, row), step_y(chem0, run, at, row))
                    total_z = add_product(total_z, step_z(adjoint1, run, at, row), slant)
                else:
                    put_flat(step_z_b, (run, at - (n - 2)), row, slant)
                put_padded(sum_y, (at,), row, total_y)
                put_flat(sum_z, (at,), row, total_z)
        return carry

    lax.fori_loop(0, runs, one_run, 0)
    for row in chunks(ny):
        for at in range(n - 2):
            sides = flat(sum_z, (at,), row)
            value = each(
                lambda a, b, c, d, e: -0.5 * ((a + b) + (c + d) + e),
                padded(sum_y, (at,), row), padded(sum_y, (at,), row, -1), sides, before_z(sides),
                flat(sum_x, (at,), row),
            )
            if at < n - 3:
                value = each(lambda a, b: a - 0.5 * b, value, flat(sum_x, (at + 1,), row))
            put_flat(part, (at,), row, value)
        for at in range(2):
            put_flat(sum_x_b, (at,), row, flat(sum_x, (n - 2 + at,), row))
            put_flat(sum_y_b, (at,), row, padded(sum_y, (n - 2 + at,), row))
            put_flat(sum_z_b, (at,), row, flat(sum_z, (n - 2 + at,), row))


def late_kernel(
    of_chip, mx_a, my_a, mz_a, mz_low_a, all_a, mx_b, my_b, mz_b, mz_low_b, all_b,
    chem0_a, chem0_b, chem1_b, adjoint2_b, flow_a, flow_part, adjoint1_a, weight_b, step_z_b,
    part, sum_x_b, sum_y_b, sum_z_b, share_in, result, share, rim, flow_b, adjoint1_b, sum_x, sum_y, sum_z,
):
    share[...] = share_in[...]
    runs = of_chip.shape[0]
    n, ny, _ = result.shape
    faces = Faces(n, (mx_a, my_a, mz_a, mz_low_a, all_a, mx_b, my_b, mz_b, mz_low_b, all_b))
    place = [either(n - 1 - at, at) for at in range(n)]
    chem0 = Line((chem0_a, -3, n - 2), (chem0_b, n - 1, n + 2))
    chem1 = Line((chem1_b, n - 2, n))
    adjoint2 = Line((adjoint2_b, n - 3, n - 1), (rim, n, n + 2))
    flow = Line((flow_a, -2, n - 2), (flow_b, n - 1, n + 1))
    adjoint1 = Line((adjoint1_a, -1, n - 3), (adjoint1_b, n - 2, n))
    for row in chunks(ny):
        for at in range(2):
            put_flat(sum_x, (at,), row, flat(sum_x_b, (at,), row))
            put_padded(sum_y, (at,), row, flat(sum_y_b, (at,), row))
            put_flat(sum_z, (at,), row, flat(sum_z_b, (at,), row))
    sum_x[2] = jnp.zeros_like(sum_x[2])

    def one_run(run, carry):
        for row in chunks(ny):
            for at in range(3):
                put_padded(rim, (run, at), row, flat(of_chip, (run, at), row))
        for row in chunks(ny):
            mids = {at: padded(*adjoint2(at, run), row) for at in range(n - 1, n + 3)}
            value = add_product(padded(flow_part, (run, 0), row), flat(*faces.mx(n - 1), row), mids[n])
            put_padded(*flow(n - 1, run), row, value)
            for at in range(n, n + 2):
                value = faces.flow(
                    row, at, mids[at], padded(*adjoint2(at, run), row, 1), padded(*adjoint2(at, run), row, -1),
                    mids[at - 1], mids[at + 1],
                )
                put_padded(*flow(at, run), row, value)
        for row in chunks(ny):
            put_adjoint1(
                row, flow, adjoint2, run, range(n - 2, n + 1),
                lambda at: flat(weight_b, (run, at - (n - 2)), row), adjoint1,
            )
        for row in chunks(ny):
            for at in range(n - 3, n):
                total = add_product(
                    flat(sum_x, (at - (n - 3),), row), step_x(adjoint1, run, at, row), step_x(chem0, run, at, row)
                )
                if at == n - 1:
                    total = add_product(total, step_x(adjoint2, run, at, row), step_x(chem1, run, at, row))
                put_flat(sum_x, (at - (n - 3),), row, total)
            for at in range(n - 2, n):
                to = (at - (n - 2),)
                put_padded(sum_y, to, row, add_product(
                    padded(sum_y, to, row), step_y(adjoint1, run, at, row), step_y(chem0, run, at, row)
                ))
                put_flat(sum_z, to, row, add_product(
                    flat(sum_z, to, row), step_z(adjoint1, run, at, row), flat(step_z_b, (run, *to), row)
                ))
        return carry

    lax.fori_loop(0, runs, one_run, 0)
    for row in chunks(ny):
        for at in range(n - 2):
            value = flat(part, (at,), row)
            if at == n - 3:
                value = each(lambda a, b: a - 0.5 * b, value, flat(sum_x, (0,), row))
            put_plain(result, (place[at],), row, value)
        for at in range(2):
            sides = flat(sum_z, (at,), row)
            value = each(
                lambda a, b, c, d, e, f: -0.5 * ((a + b) + (c + d) + (e + f)),
                flat(sum_x, (at,), row), flat(sum_x, (at + 1,), row),
                padded(sum_y, (at,), row), padded(sum_y, (at,), row, -1), sides, before_z(sides),
            )
            put_plain(result, (place[n - 2 + at],), row, value)


def call(kernel, outs, scratch, args, flops):
    moved = 4 * (sum(a.size for a in args) + sum(math.prod(o) for o in outs))
    return pl.pallas_call(
        kernel,
        out_shape=tuple(jax.ShapeDtypeStruct(o, jnp.float32) for o in outs),
        in_specs=[VMEM] * len(args),
        out_specs=tuple([VMEM] * len(outs)),
        scratch_shapes=[pltpu.VMEM(s, jnp.float32) for s in scratch],
        compiler_params=pltpu.CompilerParams(vmem_limit_bytes=16 * 1024 * 1024),
        cost_estimate=pl.CostEstimate(flops=flops, bytes_accessed=moved, transcendentals=0),
    )(*args)


def on_device(initial, observed, mobility):
    runs, n, ny, nz = initial.shape
    blocks = nz // LANES
    count = lax.axis_size("gx")
    over_chips = [(i, (i - 1 + 2 * (i % 2)) % count) for i in range(count)]
    over_cores = [(i, i ^ 1) for i in range(count)]
    cell = ny * nz

    def neighbours(to_chip, to_core):
        of_core = lax.ppermute(to_core, "gx", over_cores)
        return lax.ppermute(to_chip, "gx", over_chips), of_core

    def lies(*lead):
        return (*lead, blocks, ny, LANES)

    def lies_padded(*lead):
        return (*lead, blocks, ny + 2 * PAD, LANES)

    if n == 4:
        near = (initial, initial)
    else:
        near = [lax.dynamic_slice_in_dim(initial, at, 4, 1) for at in (either(0, n - 4), either(n - 4, 0))]
    of_chip, of_core = neighbours(*near)
    conc, mob, to_chip, to_core = call(
        own_kernel, (lies_padded(runs, n), lies_padded(n), lies(3), lies(3)), (), (initial, mobility),
        runs * n * cell,
    )
    m_chip, m_core = neighbours(to_chip, to_core)
    conc_core, chem0_a, *faces_a = call(
        core_kernel,
        (
            lies_padded(runs, 4), lies_padded(runs, n + 2),
            lies(n + 2), lies_padded(n + 2), lies(n + 2), lies(n + 2), lies(n + 1),
        ),
        (lies_padded(3),),
        (of_core, m_core, conc, mob),
        20 * runs * (n + 2) * cell,
    )
    conc_chip, chem0_b, state1_a, chem1_a, adjoint2_a, squares = call(
        chip_kernel,
        (
            lies_padded(runs, 4), lies_padded(runs, 4), lies_padded(runs, n + 1),
            lies_padded(runs, n - 1), lies_padded(runs, n - 3), (CHUNK, LANES),
        ),
        (),
        (of_chip, conc, conc_core, chem0_a, observed, *faces_a),
        60 * runs * (n - 1) * cell,
    )
    *faces_b, state1_b, chem1_b, adjoint2_b, to_core, to_chip, share = call(
        forward_kernel,
        (
            lies(3), lies_padded(2), lies(2), lies(2), lies(3),
            lies_padded(runs, 3), lies_padded(runs, 3), lies_padded(runs, 3),
            (runs, 3, blocks, ny + ROWS, LANES), lies(runs, 3), (ROWS, LANES),
        ),
        (lies_padded(3), (CHUNK, LANES)),
        (m_chip, mob, conc, conc_chip, chem0_a, chem0_b, state1_a, chem1_a, adjoint2_a, squares, observed, *faces_a),
        60 * runs * 3 * cell,
    )
    faces = (*faces_a, *faces_b)
    of_chip, of_core = neighbours(to_chip, to_core)
    hops = []
    if count & (count - 1):
        share = lax.psum(share, "gx")
    else:
        share = share + of_core[0, 0, 0, ny:]
        hops = [1 << bit for bit in range(count.bit_length() - 1, 0, -1) if 1 << bit < count]

    def hop_of(value, hop):
        return lax.ppermute(value, "gx", [(i, i ^ hop) for i in range(count)])

    far = hop_of(share, hops[0]) if hops else None
    flow_a, flow_part, adjoint1_a, weight_b, step_z_b, part, *sums_b, share = call(
        early_kernel,
        (
            lies_padded(runs, n + 1), lies_padded(runs, 1), lies_padded(runs, n - 1), lies(runs, 3), lies(runs, 2),
            lies(n - 2), lies(2), lies(2), lies(2), (ROWS, LANES),
        ),
        (lies_padded(runs, 3), lies(n), lies_padded(n), lies(n)),
        (of_core, *faces, chem0_a, chem0_b, state1_a, state1_b, chem1_a, chem1_b, adjoint2_a, adjoint2_b, share),
        60 * runs * n * cell,
    )
    for hop in hops[1:]:
        share = share + far
        far = hop_of(share, hop)
    result, share = call(
        late_kernel,
        ((n, ny, nz), (ROWS, LANES)),
        (
            lies_padded(runs, 3), lies_padded(runs, 3), lies_padded(runs, 3),
            lies(3), lies_padded(2), lies(2),
        ),
        (
            of_chip, *faces, chem0_a, chem0_b, chem1_b, adjoint2_b, flow_a, flow_part, adjoint1_a,
            weight_b, step_z_b, part, *sums_b, share,
        ),
        60 * runs * 3 * cell,
    )
    if hops:
        share = share + far
    return (result, share[0, :1])


def solution(mesh):
    placed = (
        P("group", "gx", None, None),
        P("group", "gx", None, None),
        P(("group", "gx"), None, None),
    )
    return jax.shard_map(
        on_device,
        mesh=mesh,
        in_specs=placed,
        out_specs=(P(("group", "gx"), None, None), P("group")),
        check_vma=False,
    )
```

time: 93.4 us -> 40.2 us (0.43)
  blocking collectives: 31.2 us -> 0 us
  other arithmetic: 12.9 us -> 0.01 us
  local copies, waits for them, and re-layouts: 13.4 us -> 2.54 us
  Pallas kernels: 0 us -> 7.23 us
  starting transfers between devices: 19.5 us -> 16.9 us
  waiting for transfers between devices: 14.1 us -> 12.6 us
  between operations: 2 us -> 0.69 us
    psum x1 -> x0, blocking collectives: 31.2 us -> none  [on_device(): misfit = lax.psum(0.5 / runs_here * jnp.sum(miss * miss), 'gx')]
    slice x37 -> x1, local copies, waits for them, and re-layouts: 8.1 us -> 0.51 us  [on_device(): return (result, share[0, :1])]
    pallas_call x0 -> x6, Pallas kernels: none -> 7.23 us  [call(): pl.pallas_call(kernel, out_shape=tuple((jax.ShapeDtypeStruct(o, jnp.float...]
    mul x4 -> x0, other arithmetic: 4.37 us -> none  [the longest x2 2.46 us: transport(): (jnp.roll(m_mid, offset, axis_num) + m_mid) * (jnp.roll(f_mid, offset, ax...]
    reduce_sum x3 -> x0, other arithmetic: 4.02 us -> none  [the longest x2 2.76 us: sensitivity(): return -0.5 * jnp.sum(total, axis=0)]
    unnamed x76 -> x6, local copies, waits for them, and re-layouts: 4.98 us -> 2.03 us
    ppermute x10 -> x9, starting transfers between devices: 19.5 us -> 16.9 us  [the longest x3 11.1 us: neighbours(): return (lax.ppermute(to_chip, 'gx', over_chips), of_core)]
    add x4, other arithmetic: 2.07 us -> 0.01 us  [the longest x3 0.01 us: on_device(): share = share + far]
  transfers between devices with their start and end apart: 10 -> 9, of which waited for: 4 -> 6; matrix products, arithmetic and copies ran while one was open for 9% -> 0% of each run, Pallas kernels for 0% -> 15%
where the time goes in v7:
time: 40.2 us; the launch traced here: 40 us
  starting transfers between devices  16.9 us (42%)
  waiting for transfers between devices  12.6 us (31%)
  Pallas kernels  7.23 us (18%)
  local copies, waits for them, and re-layouts  2.54 us (6%)
  between operations  0.69 us (2%)
    ppermute x3, starting transfers between devices, neighbours(): return (lax.ppermute(to_chip, 'gx', over_chips), of_core)  11.1 us
    ppermute x3, waiting for transfers between devices, hop_of(): return lax.ppermute(value, 'gx', [(i, i ^ hop) for i in range(count)])  7.42 us
    pallas_call x6, Pallas kernels, call(): pl.pallas_call(kernel, out_shape=tuple((jax.ShapeDtypeStruct(o, jnp.float...  7.23 us
    ppermute x3, starting transfers between devices, neighbours(): of_core = lax.ppermute(to_core, 'gx', over_cores)  4.37 us
    ppermute x3, waiting for transfers between devices, neighbours(): return (lax.ppermute(to_chip, 'gx', over_chips), of_core)  4.32 us
    unnamed x6, local copies, waits for them, and re-layouts  2.03 us
    ppermute x3, starting transfers between devices, hop_of(): return lax.ppermute(value, 'gx', [(i, i ^ hop) for i in range(count)])  1.52 us
    ppermute x3, waiting for transfers between devices, neighbours(): of_core = lax.ppermute(to_core, 'gx', over_cores)  0.83 us
  transfers between devices with their start and end apart: 9, of which 6 were waited for; matrix products, arithmetic and copies ran while one was open for 0% of the time, Pallas kernels for 15%

profile of v7, /device:TPU:0, one launch (start us, length us, event | category | flops | bytes accessed | tf_op | source)
XLA Modules:
  0.0 40.0 jit_solution(16726457472381012162)
XLA Ops:
  0.6 0.5 %collective-permute-start.2 = (f32[2,4,64,256]{3,2,1,0:T(8,128)}, f32[2,4,64,256]{3,2,1,0:T(8,128)S(1)}, u32[]{:S(2)}, u32[]{:S(2)}) collective-permute-start(f32[2,4,64,256]{3,2,1,0:T(8,128)} %initial.1), channel_id=1, source_target_pairs={{0,1},{1,0},{2,3},{3,2},{4,5},{5,4},{6,7},{7,6},{8,9},{9,8},{10,11... | collective-permute-start | bytes 1572872 | tf_op jit(solution)/shard_map/ppermute | solution.py:548
  1.1 5.7 %collective-permute-start.1 = (f32[2,4,64,256]{3,2,1,0:T(8,128)}, f32[2,4,64,256]{3,2,1,0:T(8,128)S(1)}, u32[]{:S(2)}, u32[]{:S(2)}) collective-permute-start(f32[2,4,64,256]{3,2,1,0:T(8,128)} %initial.1), channel_id=1, source_target_pairs={{0,15},{1,2},{2,1},{3,4},{4,3},{5,6},{6,5},{7,8},{8,7},{9,10},{10,... | collective-permute-start | bytes 1572872 | tf_op jit(solution)/shard_map/ppermute | solution.py:549
  6.8 0.0 copy-start.1
  6.8 1.1 %copy-done.1 = f32[2,4,64,256]{3,2,1,0:T(8,128)S(1)} copy-done((f32[2,4,64,256]{3,2,1,0:T(8,128)S(1)}, f32[2,4,64,256]{3,2,1,0:T(8,128)}, u32[]{:S(2)}) %copy-start.1) | copy-done | bytes 524312
  7.9 0.0 copy-start.2
  7.9 0.9 %copy-done.2 = f32[4,64,256]{2,1,0:T(8,128)S(1)} copy-done((f32[4,64,256]{2,1,0:T(8,128)S(1)}, f32[4,64,256]{2,1,0:T(8,128)}, u32[]{:S(2)}) %copy-start.2) | copy-done | bytes 262168
  8.8 0.1 shard_map.50
  8.9 0.1 collective-permute-start.3
  9.0 0.6 %collective-permute-start = (f32[3,2,64,128]{3,2,1,0:T(8,128)S(1)}, f32[3,2,64,128]{3,2,1,0:T(8,128)S(1)}, u32[]{:S(2)}, u32[]{:S(2)}) collective-permute-start(f32[3,2,64,128]{3,2,1,0:T(8,128)S(1)} %get-tuple-element.42), channel_id=1, source_target_pairs={{0,15},{1,2},{2,1},{3,4},{4,3},{5,6},{6,5},{7,8},{8,7},{9,10},{10,... | collective-permute-start | bytes 589832 | tf_op jit(solution)/shard_map/ppermute | solution.py:549
  9.6 0.8 %collective-permute-done.3.m_core = f32[3,2,64,128]{3,2,1,0:T(8,128)S(1)} collective-permute-done((f32[3,2,64,128]{3,2,1,0:T(8,128)S(1)}, f32[3,2,64,128]{3,2,1,0:T(8,128)S(1)}, u32[]{:S(2)}, u32[]{:S(2)}) %collective-permute-start.3) | collective-permute-done | bytes 196640 | tf_op jit(solution)/shard_map/ppermute | solution.py:548
  10.4 0.0 collective-permute-done.2.of_core
  10.4 0.0 copy-start
  10.5 0.9 %shard_map.51 = (f32[2,4,2,80,128]{4,3,2,1,0:T(8,128)S(1)}, f32[2,6,2,80,128]{4,3,2,1,0:T(8,128)S(1)}, f32[6,2,64,128]{3,2,1,0:T(8,128)S(1)}, f32[6,2,80,128]{3,...) custom-call(f32[2,4,64,256]{3,2,1,0:T(8,128)S(1)} %collective-permut, ...), custom_call_target="tpu_custom_call" | custom-call | flops 3932160 | bytes 5341184 | tf_op jit(solution)/shard_map/pallas_call | solution.py:528
  11.3 2.7 %collective-permute-done.1.of_chip = f32[2,4,64,256]{3,2,1,0:T(8,128)S(1)} collective-permute-done((f32[2,4,64,256]{3,2,1,0:T(8,128)}, f32[2,4,64,256]{3,2,1,0:T(8,128)S(1)}, u32[]{:S(2)}, u32[]{:S(2)}) %collective-permute-start.1) | collective-permute-done | bytes 524320 | tf_op jit(solution)/shard_map/ppermute | solution.py:549
  14.0 0.0 copy-done
  14.0 1.3 %shard_map.52 = (f32[2,4,2,80,128]{4,3,2,1,0:T(8,128)S(1)}, f32[2,4,2,80,128]{4,3,2,1,0:T(8,128)S(1)}, f32[2,5,2,80,128]{4,3,2,1,0:T(8,128)S(1)}, f32[2,3,2,80,1...) custom-call(f32[2,4,64,256]{3,2,1,0:T(8,128)S(1)} %collective-permute-done.1.of_chip, ...), custom_call_target="tpu_custom_call" | custom-call | flops 5898240 | bytes 8134656 | tf_op jit(solution)/shard_map/pallas_call | solution.py:528
  15.3 1.7 %collective-permute-done.m_chip = f32[3,2,64,128]{3,2,1,0:T(8,128)S(1)} collective-permute-done((f32[3,2,64,128]{3,2,1,0:T(8,128)S(1)}, f32[3,2,64,128]{3,2,1,0:T(8,128)S(1)}, u32[]{:S(2)}, u32[]{:S(2)}) %collective-permute-start) | collective-permute-done | bytes 196640 | tf_op jit(solution)/shard_map/ppermute | solution.py:549
  17.0 1.3 %shard_map.53 = (f32[3,2,64,128]{3,2,1,0:T(8,128)S(1)}, f32[2,2,80,128]{3,2,1,0:T(8,128)S(1)}, f32[2,2,64,128]{3,2,1,0:T(8,128)S(1)}, f32[2,2,64,128]{3,2,1,0:T(...) custom-call(f32[3,2,64,128]{3,2,1,0:T(8,128)S(1)} %collective-permut, ...), custom_call_target="tpu_custom_call" | custom-call | flops 5898240 | bytes 10612736 | tf_op jit(solution)/shard_map/pallas_call | solution.py:528
  18.3 3.8 %collective-permute-start.5 = (f32[2,3,2,72,128]{4,3,2,1,0:T(8,128)S(1)}, f32[2,3,2,72,128]{4,3,2,1,0:T(8,128)S(1)}, u32[]{:S(2)}, u32[]{:S(2)}) collective-permute-start(f32[2,3,2,72,128]{4,3,2,1,0:T(8,128)S(1)} %get-tuple-element.67), channel_id=1, source_target_pairs={{0,1},{1,0},{2,3},{3,2},{4,5},{5,4},{6,7},{7,6},{8,9},{9,8},{10,11... | collective-permute-start | bytes 1327112 | tf_op jit(solution)/shard_map/ppermute | solution.py:548
  22.1 4.8 %collective-permute-start.4 = (f32[2,3,2,64,128]{4,3,2,1,0:T(8,128)S(1)}, f32[2,3,2,64,128]{4,3,2,1,0:T(8,128)S(1)}, u32[]{:S(2)}, u32[]{:S(2)}) collective-permute-start(f32[2,3,2,64,128]{4,3,2,1,0:T(8,128)S(1)} %get-tuple-element.59), channel_id=1, source_target_pairs={{0,15},{1,2},{2,1},{3,4},{4,3},{5,6},{6,5},{7,8},{8,7},{9,10},{10,... | collective-permute-start | bytes 1179656 | tf_op jit(solution)/shard_map/ppermute | solution.py:549
  26.9 0.0 collective-permute-done.5.of_core
  26.9 0.0 collective-permute-start.6
  26.9 1.9 %shard_map.54 = (f32[2,5,2,80,128]{4,3,2,1,0:T(8,128)S(1)}, f32[2,1,2,80,128]{4,3,2,1,0:T(8,128)S(1)}, f32[2,3,2,80,128]{4,3,2,1,0:T(8,128)S(1)}, f32[2,3,2,64,1...) custom-call(f32[2,3,2,72,128]{4,3,2,1,0:T(8,128)S(1)} %collective-pe, ...), custom_call_target="tpu_custom_call" | custom-call | flops 7864320 | bytes 10510336 | tf_op jit(solution)/shard_map/pallas_call | solution.py:528
  28.8 3.4 %collective-permute-done.6 = f32[8,128]{1,0:T(8,128)S(1)} collective-permute-done((f32[8,128]{1,0:T(8,128)S(1)}, f32[8,128]{1,0:T(8,128)S(1)}, u32[]{:S(2)}, u32[]{:S(2)}) %collective-permute-start.6) | collective-permute-done | bytes 4128 | tf_op jit(solution)/shard_map/ppermute | solution.py:608
  32.3 1.5 %collective-permute-start.7 = (f32[8,128]{1,0:T(8,128)S(1)}, f32[8,128]{1,0:T(8,128)S(1)}, u32[]{:S(2)}, u32[]{:S(2)}) collective-permute-start(f32[8,128]{1,0:T(8,128)S(1)} %add.13), channel_id=1, source_target_pairs={{0,4},{1,5},{2,6},{3,7},{4,0},{5,1},{6,2},{7,3},{8,12},{9,13},{10,... | collective-permute-start | bytes 12296 | tf_op jit(solution)/shard_map/ppermute | solution.py:608
  33.8 2.1 %collective-permute-done.7 = f32[8,128]{1,0:T(8,128)S(1)} collective-permute-done((f32[8,128]{1,0:T(8,128)S(1)}, f32[8,128]{1,0:T(8,128)S(1)}, u32[]{:S(2)}, u32[]{:S(2)}) %collective-permute-start.7) | collective-permute-done | bytes 4128 | tf_op jit(solution)/shard_map/ppermute | solution.py:608
  35.9 0.0 collective-permute-start.8
  35.9 0.0 collective-permute-done.4.of_chip
  35.9 1.7 %shard_map.55 = (f32[4,64,256]{2,1,0:T(8,128)}, f32[8,128]{1,0:T(8,128)S(1)}) custom-call(f32[2,3,2,64,128]{4,3,2,1,0:T(8,128)S(1)} %collective-permute-done.4.of_chip, f32[6,2,64,128]{3,2,1,0:T(8,128)S(1)} %get-tuple-element.48.mx.mx_a, f32[6,2,80,128]{3,2,1,0:T(8,128)S(1)} %get-tuple-element.49.my.my_a, f32[6,2,64,128]{3,2,1,0:T(8,128)S(1)} %get-tuple-element.50.mz.mz_a, ...), custom_call_target="tpu_custom_call" | custom-call | flops 5898240 | bytes 8757248 | tf_op jit(solution)/shard_map/pallas_call | solution.py:528
  37.6 1.9 %collective-permute-done.8 = f32[8,128]{1,0:T(8,128)S(1)} collective-permute-done((f32[8,128]{1,0:T(8,128)S(1)}, f32[8,128]{1,0:T(8,128)S(1)}, u32[]{:S(2)}, u32[]{:S(2)}) %collective-permute-start.8) | collective-permute-done | bytes 4128 | tf_op jit(solution)/shard_map/ppermute | solution.py:608
  39.5 0.5 %slice.7 = f32[1,1]{1,0:T(1,128)} slice(f32[8,128]{1,0:T(8,128)S(1)} %add.15), slice={[0:1], [0:1]} | slice | bytes 8 | tf_op jit(solution)/shard_map/slice | solution.py:639
  (4 shorter events, 0.0 us)
Async XLA Ops:
  0.6 9.8 %collective-permute-start.2 = (f32[2,4,64,256]{3,2,1,0:T(8,128)}, f32[2,4,64,256]{3,2,1,0:T(8,128)S(1)}, u32[]{:S(2)}, u32[]{:S(2)}) collective-permute-start(f32[2,4,64,256]{3,2,1,0:T(8,128)} %initial.1), channel_id=1, source_target_pairs={{0,1},{1,0},{2,3},{3,2},{4,5},{5,4},{6,7},{7,6},{8,9},{9,8},{10,11... | collective-permute-start | bytes 1572872 | tf_op jit(solution)/shard_map/ppermute | solution.py:548
  1.1 12.8 %collective-permute-start.1 = (f32[2,4,64,256]{3,2,1,0:T(8,128)}, f32[2,4,64,256]{3,2,1,0:T(8,128)S(1)}, u32[]{:S(2)}, u32[]{:S(2)}) collective-permute-start(f32[2,4,64,256]{3,2,1,0:T(8,128)} %initial.1), channel_id=1, source_target_pairs={{0,15},{1,2},{2,1},{3,4},{4,3},{5,6},{6,5},{7,8},{8,7},{9,10},{10,... | collective-permute-start | bytes 1572872 | tf_op jit(solution)/shard_map/ppermute | solution.py:549
  6.8 1.1 %copy-start.1 = (f32[2,4,64,256]{3,2,1,0:T(8,128)S(1)}, f32[2,4,64,256]{3,2,1,0:T(8,128)}, u32[]{:S(2)}) copy-start(f32[2,4,64,256]{3,2,1,0:T(8,128)} %initial.1) | copy-start | bytes 1572868
  7.9 0.9 %copy-start.2 = (f32[4,64,256]{2,1,0:T(8,128)S(1)}, f32[4,64,256]{2,1,0:T(8,128)}, u32[]{:S(2)}) copy-start(f32[4,64,256]{2,1,0:T(8,128)} %mobility.1) | copy-start | bytes 786436
  8.9 1.5 %collective-permute-start.3 = (f32[3,2,64,128]{3,2,1,0:T(8,128)S(1)}, f32[3,2,64,128]{3,2,1,0:T(8,128)S(1)}, u32[]{:S(2)}, u32[]{:S(2)}) collective-permute-start(f32[3,2,64,128]{3,2,1,0:T(8,128)S(1)} %get-tuple-element.45), channel_id=1, source_target_pairs={{0,1},{1,0},{2,3},{3,2},{4,5},{5,4},{6,7},{7,6},{8,9},{9,8},{10,11... | collective-permute-start | bytes 589832 | tf_op jit(solution)/shard_map/ppermute | solution.py:548
  9.0 8.0 %collective-permute-start = (f32[3,2,64,128]{3,2,1,0:T(8,128)S(1)}, f32[3,2,64,128]{3,2,1,0:T(8,128)S(1)}, u32[]{:S(2)}, u32[]{:S(2)}) collective-permute-start(f32[3,2,64,128]{3,2,1,0:T(8,128)S(1)} %get-tuple-element.42), channel_id=1, source_target_pairs={{0,15},{1,2},{2,1},{3,4},{4,3},{5,6},{6,5},{7,8},{8,7},{9,10},{10,... | collective-permute-start | bytes 589832 | tf_op jit(solution)/shard_map/ppermute | solution.py:549
  10.4 3.6 %copy-start = (f32[2,4,64,256]{3,2,1,0:T(8,128)S(1)}, f32[2,4,64,256]{3,2,1,0:T(8,128)}, u32[]{:S(2)}) copy-start(f32[2,4,64,256]{3,2,1,0:T(8,128)} %observed.3) | copy-start | bytes 1572868
  18.3 8.6 %collective-permute-start.5 = (f32[2,3,2,72,128]{4,3,2,1,0:T(8,128)S(1)}, f32[2,3,2,72,128]{4,3,2,1,0:T(8,128)S(1)}, u32[]{:S(2)}, u32[]{:S(2)}) collective-permute-start(f32[2,3,2,72,128]{4,3,2,1,0:T(8,128)S(1)} %get-tuple-element.67), channel_id=1, source_target_pairs={{0,1},{1,0},{2,3},{3,2},{4,5},{5,4},{6,7},{7,6},{8,9},{9,8},{10,11... | collective-permute-start | bytes 1327112 | tf_op jit(solution)/shard_map/ppermute | solution.py:548
  22.1 13.8 %collective-permute-start.4 = (f32[2,3,2,64,128]{4,3,2,1,0:T(8,128)S(1)}, f32[2,3,2,64,128]{4,3,2,1,0:T(8,128)S(1)}, u32[]{:S(2)}, u32[]{:S(2)}) collective-permute-start(f32[2,3,2,64,128]{4,3,2,1,0:T(8,128)S(1)} %get-tuple-element.59), channel_id=1, source_target_pairs={{0,15},{1,2},{2,1},{3,4},{4,3},{5,6},{6,5},{7,8},{8,7},{9,10},{10,... | collective-permute-start | bytes 1179656 | tf_op jit(solution)/shard_map/ppermute | solution.py:549
  26.9 5.4 %collective-permute-start.6 = (f32[8,128]{1,0:T(8,128)S(1)}, f32[8,128]{1,0:T(8,128)S(1)}, u32[]{:S(2)}, u32[]{:S(2)}) collective-permute-start(f32[8,128]{1,0:T(8,128)S(1)} %fusion.share_in), channel_id=1, source_target_pairs={{0,8},{1,9},{2,10},{3,11},{4,12},{5,13},{6,14},{7,15},{8,0},{9,1},... | collective-permute-start | bytes 12296 | tf_op jit(solution)/shard_map/ppermute | solution.py:608
  32.3 3.6 %collective-permute-start.7 = (f32[8,128]{1,0:T(8,128)S(1)}, f32[8,128]{1,0:T(8,128)S(1)}, u32[]{:S(2)}, u32[]{:S(2)}) collective-permute-start(f32[8,128]{1,0:T(8,128)S(1)} %add.13), channel_id=1, source_target_pairs={{0,4},{1,5},{2,6},{3,7},{4,0},{5,1},{6,2},{7,3},{8,12},{9,13},{10,... | collective-permute-start | bytes 12296 | tf_op jit(solution)/shard_map/ppermute | solution.py:608
  35.9 3.6 %collective-permute-start.8 = (f32[8,128]{1,0:T(8,128)S(1)}, f32[8,128]{1,0:T(8,128)S(1)}, u32[]{:S(2)}, u32[]{:S(2)}) collective-permute-start(f32[8,128]{1,0:T(8,128)S(1)} %add.14.share_in), channel_id=1, source_target_pairs={{0,2},{1,3},{2,0},{3,1},{4,6},{5,7},{6,4},{7,5},{8,10},{9,11},{10,... | collective-permute-start | bytes 12296 | tf_op jit(solution)/shard_map/ppermute | solution.py:608

commit v8 on v7

--- a/solution.py
+++ b/solution.py
@@ -332,7 +332,6 @@
     columns = (0.5 / runs) * jnp.sum(total[...], axis=0, keepdims=True)
     mine = jnp.broadcast_to(jnp.sum(columns, axis=1, keepdims=True), share.shape)
     share[...] = mine
-    to_core[0, 0, 0, ny:] = mine
 
 
 def put_adjoint1(row, flow, adjoint2, run, places, weight, target):
@@ -368,10 +367,9 @@
 def early_kernel(
     of_core, mx_a, my_a, mz_a, mz_low_a, all_a, mx_b, my_b, mz_b, mz_low_b, all_b,
     chem0_a, chem0_b, state1_a, state1_b, chem1_a, chem1_b, adjoint2_a, adjoint2_b,
-    share_in, flow_a, flow_part, adjoint1_a, weight_b, step_z_b, part, sum_x_b, sum_y_b, sum_z_b, share,
+    flow_a, flow_part, adjoint1_a, weight_b, step_z_b, part, sum_x_b, sum_y_b, sum_z_b,
     rim, sum_x, sum_y, sum_z,
 ):
-    share[...] = share_in[...]
     runs = of_core.shape[0]
     n = part.shape[0] + 2
     ny = part.shape[-2]
@@ -450,9 +448,8 @@
 def late_kernel(
     of_chip, mx_a, my_a, mz_a, mz_low_a, all_a, mx_b, my_b, mz_b, mz_low_b, all_b,
     chem0_a, chem0_b, chem1_b, adjoint2_b, flow_a, flow_part, adjoint1_a, weight_b, step_z_b,
-    part, sum_x_b, sum_y_b, sum_z_b, share_in, result, share, rim, flow_b, adjoint1_b, sum_x, sum_y, sum_z,
+    part, sum_x_b, sum_y_b, sum_z_b, result, rim, flow_b, adjoint1_b, sum_x, sum_y, sum_z,
 ):
-    share[...] = share_in[...]
     runs = of_chip.shape[0]
     n, ny, _ = result.shape
     faces = Faces(n, (mx_a, my_a, mz_a, mz_low_a, all_a, mx_b, my_b, mz_b, mz_low_b, all_b))
@@ -523,6 +520,10 @@
             put_plain(result, (place[n - 2 + at],), row, value)
 
 
+def misfit_kernel(shares, misfit):
+    misfit[...] = jnp.sum(shares[...], axis=0)
+
+
 def call(kernel, outs, scratch, args, flops):
     moved = 4 * (sum(a.size for a in args) + sum(math.prod(o) for o in outs))
     return pl.pallas_call(
@@ -589,7 +590,7 @@
         (
             lies(3), lies_padded(2), lies(2), lies(2), lies(3),
             lies_padded(runs, 3), lies_padded(runs, 3), lies_padded(runs, 3),
-            (runs, 3, blocks, ny + ROWS, LANES), lies(runs, 3), (ROWS, LANES),
+            lies(runs, 3), lies(runs, 3), (LANES, LANES),
         ),
         (lies_padded(3), (CHUNK, LANES)),
         (m_chip, mob, conc, conc_chip, chem0_a, chem0_b, state1_a, chem1_a, adjoint2_a, squares, observed, *faces_a),
@@ -597,46 +598,32 @@
     )
     faces = (*faces_a, *faces_b)
     of_chip, of_core = neighbours(to_chip, to_core)
-    hops = []
-    if count & (count - 1):
-        share = lax.psum(share, "gx")
-    else:
-        share = share + of_core[0, 0, 0, ny:]
-        hops = [1 << bit for bit in range(count.bit_length() - 1, 0, -1) if 1 << bit < count]
-
-    def hop_of(value, hop):
-        return lax.ppermute(value, "gx", [(i, i ^ hop) for i in range(count)])
-
-    far = hop_of(share, hops[0]) if hops else None
-    flow_a, flow_part, adjoint1_a, weight_b, step_z_b, part, *sums_b, share = call(
+    shares = lax.all_gather(share, "gx")
+    flow_a, flow_part, adjoint1_a, weight_b, step_z_b, part, *sums_b = call(
         early_kernel,
         (
             lies_padded(runs, n + 1), lies_padded(runs, 1), lies_padded(runs, n - 1), lies(runs, 3), lies(runs, 2),
-            lies(n - 2), lies(2), lies(2), lies(2), (ROWS, LANES),
+            lies(n - 2), lies(2), lies(2), lies(2),
         ),
         (lies_padded(runs, 3), lies(n), lies_padded(n), lies(n)),
-        (of_core, *faces, chem0_a, chem0_b, state1_a, state1_b, chem1_a, chem1_b, adjoint2_a, adjoint2_b, share),
+        (of_core, *faces, chem0_a, chem0_b, state1_a, state1_b, chem1_a, chem1_b, adjoint2_a, adjoint2_b),
         60 * runs * n * cell,
     )
-    for hop in hops[1:]:
-        share = share + far
-        far = hop_of(share, hop)
-    result, share = call(
+    (result,) = call(
         late_kernel,
-        ((n, ny, nz), (ROWS, LANES)),
+        ((n, ny, nz),),
         (
             lies_padded(runs, 3), lies_padded(runs, 3), lies_padded(runs, 3),
             lies(3), lies_padded(2), lies(2),
         ),
         (
             of_chip, *faces, chem0_a, chem0_b, chem1_b, adjoint2_b, flow_a, flow_part, adjoint1_a,
-            weight_b, step_z_b, part, *sums_b, share,
+            weight_b, step_z_b, part, *sums_b,
         ),
         60 * runs * 3 * cell,
     )
-    if hops:
-        share = share + far
-    return (result, share[0, :1])
+    (misfit,) = call(misfit_kernel, ((1, LANES),), (), (shares[:, :1],), count)
+    return (result, misfit[0, :1])
 
 
 def solution(mesh):

time: 40.2 us -> 103 us (2.56)
  local copies, waits for them, and re-layouts: 2.54 us -> 42.6 us
  between operations: 0.69 us -> 14.2 us
  waiting for transfers between devices: 12.6 us -> 21.5 us
  starting transfers between devices: 16.9 us -> 15.5 us
    unnamed x6 -> x106, local copies, waits for them, and re-layouts: 2.03 us -> 41.8 us
    all_gather x0 -> x1, waiting for transfers between devices: none -> 16.1 us  [on_device(): shares = lax.all_gather(share, 'gx')]
    ppermute x3 -> x0, waiting for transfers between devices: 7.42 us -> none  [hop_of(): return lax.ppermute(value, 'gx', [(i, i ^ hop) for i in range(count)])]
    ppermute x3 -> x0, starting transfers between devices: 1.52 us -> none  [hop_of(): return lax.ppermute(value, 'gx', [(i, i ^ hop) for i in range(count)])]
    pallas_call x6 -> x7, Pallas kernels: 7.23 us -> 8.13 us  [call(): pl.pallas_call(kernel, out_shape=tuple((jax.ShapeDtypeStruct(o, jnp.float...]
  transfers between devices with their start and end apart: 9 -> 7, of which waited for: 6 -> 4; matrix products, arithmetic and copies ran while one was open for 0% -> 1% of each run, Pallas kernels for 15% -> 4%
where the time goes in v8:
time: 103 us; the launch traced here: 102 us
  local copies, waits for them, and re-layouts  42.6 us (41%)
  waiting for transfers between devices  21.5 us (21%)
  starting transfers between devices  15.5 us (15%)
  between operations  14.2 us (14%)
  Pallas kernels  8.13 us (8%)
    unnamed x106, local copies, waits for them, and re-layouts  41.8 us
    all_gather x1, waiting for transfers between devices, on_device(): shares = lax.all_gather(share, 'gx')  16.1 us
    ppermute x3, starting transfers between devices, neighbours(): return (lax.ppermute(to_chip, 'gx', over_chips), of_core)  11.1 us
    pallas_call x7, Pallas kernels, call(): pl.pallas_call(kernel, out_shape=tuple((jax.ShapeDtypeStruct(o, jnp.float...  8.13 us
    ppermute x3, waiting for transfers between devices, neighbours(): return (lax.ppermute(to_chip, 'gx', over_chips), of_core)  4.47 us
    ppermute x3, starting transfers between devices, neighbours(): of_core = lax.ppermute(to_core, 'gx', over_cores)  4.44 us
  transfers between devices with their start and end apart: 7, of which 4 were waited for; matrix products, arithmetic and copies ran while one was open for 1% of the time, Pallas kernels for 4%

profile of v8, /device:TPU:0, one launch (start us, length us, event | category | flops | bytes accessed | tf_op | source)
XLA Modules:
  0.0 101.9 jit_solution(10508318859974390205)
XLA Ops:
  7.7 5.7 %collective-permute-start.1 = (f32[2,4,64,256]{3,2,1,0:T(8,128)}, f32[2,4,64,256]{3,2,1,0:T(8,128)S(1)}, u32[]{:S(2)}, u32[]{:S(2)}) collective-permute-start(f32[2,4,64,256]{3,2,1,0:T(8,128)} %initial.1), channel_id=1, source_target_pairs={{0,15},{1,2},{2,1},{3,4},{4,3},{5,6},{6,5},{7,8},{8,7},{9,10},{10,... | collective-permute-start | bytes 1572872 | tf_op jit(solution)/shard_map/ppermute | solution.py:550
  13.4 1.1 %copy-done.30 = f32[2,4,64,256]{3,2,1,0:T(8,128)S(1)} copy-done((f32[2,4,64,256]{3,2,1,0:T(8,128)S(1)}, f32[2,4,64,256]{3,2,1,0:T(8,128)}, u32[]{:S(2)}) %copy-start.30) | copy-done | bytes 524312
  14.5 0.9 copy-done.37
  16.2 0.8 collective-permute-done.3.m_core
  17.0 0.8 shard_map.51
  17.9 2.7 %collective-permute-done.1.of_chip = f32[2,4,64,256]{3,2,1,0:T(8,128)S(1)} collective-permute-done((f32[2,4,64,256]{3,2,1,0:T(8,128)}, f32[2,4,64,256]{3,2,1,0:T(8,128)S(1)}, u32[]{:S(2)}, u32[]{:S(2)}) %collective-permute-start.1) | collective-permute-done | bytes 524320 | tf_op jit(solution)/shard_map/ppermute | solution.py:550
  20.6 1.2 %shard_map.52 = (f32[2,4,2,80,128]{4,3,2,1,0:T(8,128)S(1)}, f32[2,4,2,80,128]{4,3,2,1,0:T(8,128)S(1)}, f32[2,5,2,80,128]{4,3,2,1,0:T(8,128)S(1)}, f32[2,3,2,80,1...) custom-call(f32[2,4,64,256]{3,2,1,0:T(8,128)S(1)} %collective-permute-done.1.of_chip, ...), custom_call_target="tpu_custom_call" | custom-call | flops 5898240 | bytes 8134656 | tf_op jit(solution)/shard_map/pallas_call | solution.py:529
  21.8 1.8 %collective-permute-done.m_chip = f32[3,2,64,128]{3,2,1,0:T(8,128)S(1)} collective-permute-done((f32[3,2,64,128]{3,2,1,0:T(8,128)S(1)}, f32[3,2,64,128]{3,2,1,0:T(8,128)S(1)}, u32[]{:S(2)}, u32[]{:S(2)}) %collective-permute-start) | collective-permute-done | bytes 196640 | tf_op jit(solution)/shard_map/ppermute | solution.py:550
  23.6 1.2 %shard_map.53 = (f32[3,2,64,128]{3,2,1,0:T(8,128)S(1)}, f32[2,2,80,128]{3,2,1,0:T(8,128)S(1)}, f32[2,2,64,128]{3,2,1,0:T(8,128)S(1)}, f32[2,2,64,128]{3,2,1,0:T(...) custom-call(f32[3,2,64,128]{3,2,1,0:T(8,128)S(1)} %collective-permut, ...), custom_call_target="tpu_custom_call" | custom-call | flops 5898240 | bytes 10625024 | tf_op jit(solution)/shard_map/pallas_call | solution.py:529
  24.8 0.8 copy-done.6
  25.6 0.8 copy-done.9
  29.0 0.8 copy-done.33
  31.2 0.8 copy-done.52
  32.0 3.8 %collective-permute-start.5 = (f32[2,3,2,64,128]{4,3,2,1,0:T(8,128)}, f32[2,3,2,64,128]{4,3,2,1,0:T(8,128)S(1)}, u32[]{:S(2)}, u32[]{:S(2)}) collective-permute-start(f32[2,3,2,64,128]{4,3,2,1,0:T(8,128)} %copy-done.52), channel_id=1, source_target_pairs={{0,1},{1,0},{2,3},{3,2},{4,5},{5,4},{6,7},{7,6},{8,9},{9,8},{10,11... | collective-permute-start | bytes 1179656 | tf_op jit(solution)/shard_map/ppermute | solution.py:549
  35.8 4.8 %collective-permute-start.4 = (f32[2,3,2,64,128]{4,3,2,1,0:T(8,128)}, f32[2,3,2,64,128]{4,3,2,1,0:T(8,128)}, u32[]{:S(2)}, u32[]{:S(2)}) collective-permute-start(f32[2,3,2,64,128]{4,3,2,1,0:T(8,128)} %copy-done.51), channel_id=1, source_target_pairs={{0,15},{1,2},{2,1},{3,4},{4,3},{5,6},{6,5},{7,8},{8,7},{9,10},{10,... | collective-permute-start | bytes 1179656 | tf_op jit(solution)/shard_map/ppermute | solution.py:550
  40.6 1.0 copy-done.1
  41.6 1.1 %copy-done.4 = f32[2,5,2,80,128]{4,3,2,1,0:T(8,128)S(1)} copy-done((f32[2,5,2,80,128]{4,3,2,1,0:T(8,128)S(1)}, f32[2,5,2,80,128]{4,3,2,1,0:T(8,128)}, u32[]{:S(2)}) %copy-start.4) | copy-done | bytes 819224
  42.8 1.0 %copy-done.7 = f32[2,3,2,80,128]{4,3,2,1,0:T(8,128)S(1)} copy-done((f32[2,3,2,80,128]{4,3,2,1,0:T(8,128)S(1)}, f32[2,3,2,80,128]{4,3,2,1,0:T(8,128)}, u32[]{:S(2)}) %copy-start.7) | copy-done | bytes 491544
  43.8 1.0 %copy-done.10 = f32[2,3,2,80,128]{4,3,2,1,0:T(8,128)S(1)} copy-done((f32[2,3,2,80,128]{4,3,2,1,0:T(8,128)S(1)}, f32[2,3,2,80,128]{4,3,2,1,0:T(8,128)}, u32[]{:S(2)}) %copy-start.10) | copy-done | bytes 491544
  44.8 1.0 %copy-done.13 = f32[2,3,2,80,128]{4,3,2,1,0:T(8,128)S(1)} copy-done((f32[2,3,2,80,128]{4,3,2,1,0:T(8,128)S(1)}, f32[2,3,2,80,128]{4,3,2,1,0:T(8,128)}, u32[]{:S(2)}) %copy-start.13) | copy-done | bytes 491544
  45.8 0.9 copy-done.17
  46.8 0.9 copy-done.20
  47.7 0.9 copy-done.23
  48.6 0.9 copy-done.25
  49.5 0.9 copy-done.28
  50.4 1.0 %copy-done.34 = f32[2,3,2,80,128]{4,3,2,1,0:T(8,128)S(1)} copy-done((f32[2,3,2,80,128]{4,3,2,1,0:T(8,128)S(1)}, f32[2,3,2,80,128]{4,3,2,1,0:T(8,128)}, u32[]{:S(2)}) %copy-start.34) | copy-done | bytes 491544
  51.4 1.6 %shard_map.54 = (f32[2,5,2,80,128]{4,3,2,1,0:T(8,128)S(1)}, f32[2,1,2,80,128]{4,3,2,1,0:T(8,128)S(1)}, f32[2,3,2,80,128]{4,3,2,1,0:T(8,128)S(1)}, f32[2,3,2,64,1...) custom-call(f32[2,3,2,64,128]{4,3,2,1,0:T(8,128)S(1)} %collective-pe, ...), custom_call_target="tpu_custom_call" | custom-call | flops 7864320 | bytes 10452992 | tf_op jit(solution)/shard_map/pallas_call | solution.py:529
  53.0 0.9 copy-done.14
  54.0 0.8 copy-done.31
  59.5 16.1 %all-gather.3.cloned.1.call-done = f32[2048,128]{1,0:T(8,128)} async-done(((f32[128,128]{1,0:T(8,128)}), f32[2048,128]{1,0:T(8,128)}) %all-gather.3.cloned.1.call-update) | async-done | bytes 1048592 | tf_op jit(solution)/shard_map/all_gather | solution.py:601
  75.7 0.8 slice.8.shares
  76.5 1.0 copy-done.2
  77.5 1.0 %copy-done.8 = f32[2,3,2,80,128]{4,3,2,1,0:T(8,128)S(1)} copy-done((f32[2,3,2,80,128]{4,3,2,1,0:T(8,128)S(1)}, f32[2,3,2,80,128]{4,3,2,1,0:T(8,128)}, u32[]{:S(2)}) %copy-start.8) | copy-done | bytes 491544
  78.5 1.0 %copy-done.11 = f32[2,3,2,80,128]{4,3,2,1,0:T(8,128)S(1)} copy-done((f32[2,3,2,80,128]{4,3,2,1,0:T(8,128)S(1)}, f32[2,3,2,80,128]{4,3,2,1,0:T(8,128)}, u32[]{:S(2)}) %copy-start.11) | copy-done | bytes 491544
  79.5 1.1 %copy-done.15 = f32[2,5,2,80,128]{4,3,2,1,0:T(8,128)S(1)} copy-done((f32[2,5,2,80,128]{4,3,2,1,0:T(8,128)S(1)}, f32[2,5,2,80,128]{4,3,2,1,0:T(8,128)}, u32[]{:S(2)}) %copy-start.15) | copy-done | bytes 819224
  80.7 0.9 copy-done.18
  81.6 0.9 copy-done.21
  82.5 0.9 copy-done.26
  83.4 0.9 copy-done.29
  84.3 1.0 %copy-done.32 = f32[2,3,2,80,128]{4,3,2,1,0:T(8,128)S(1)} copy-done((f32[2,3,2,80,128]{4,3,2,1,0:T(8,128)S(1)}, f32[2,3,2,80,128]{4,3,2,1,0:T(8,128)}, u32[]{:S(2)}) %copy-start.32) | copy-done | bytes 491544
  85.4 1.0 copy-done.36
  86.4 0.9 copy-done.39
  87.3 0.9 copy-done.41
  88.2 0.9 copy-done.43
  89.1 0.9 copy-done.45
  90.0 0.9 copy-done.47
  90.9 0.9 copy-done.49
  91.8 2.7 %shard_map.55 = f32[4,64,256]{2,1,0:T(8,128)} custom-call(f32[2,3,2,64,128]{4,3,2,1,0:T(8,128)} %collective-permute-done.4.of_chip, f32[6,2,64,128]{3,2,1,0:T(8,128)S(1)} %get-tuple-element.45.mx.mx_a, f32[6,2,80,128]{3,2,1,0:T(8,128)S(1)} %get-tuple-element.46.my.my_a, f32[6,2,64,128]{3,2,1,0:T(8,128)S(1)} %get-tuple-element.47.mz.mz_a, ...), custom_call_target="tpu_custom_call" | custom-call | flops 5898240 | bytes 8749056 | tf_op jit(solution)/shard_map/pallas_call | solution.py:529
  (81 shorter events, 10.7 us)
Async XLA Ops:
  7.2 68.5 %all-gather.3.cloned.1.call-start = ((), (), s32[]{:S(2)}) async-start(), calls=%async_computation | async-start | bytes 1114112 | tf_op jit(solution)/shard_map/all_gather | solution.py:601
  7.2 9.8 %collective-permute-start.2 = (f32[2,4,64,256]{3,2,1,0:T(8,128)}, f32[2,4,64,256]{3,2,1,0:T(8,128)S(1)}, u32[]{:S(2)}, u32[]{:S(2)}) collective-permute-start(f32[2,4,64,256]{3,2,1,0:T(8,128)} %initial.1), channel_id=1, source_target_pairs={{0,1},{1,0},{2,3},{3,2},{4,5},{5,4},{6,7},{7,6},{8,9},{9,8},{10,11... | collective-permute-start | bytes 1572872 | tf_op jit(solution)/shard_map/ppermute | solution.py:549
  7.7 12.8 %collective-permute-start.1 = (f32[2,4,64,256]{3,2,1,0:T(8,128)}, f32[2,4,64,256]{3,2,1,0:T(8,128)S(1)}, u32[]{:S(2)}, u32[]{:S(2)}) collective-permute-start(f32[2,4,64,256]{3,2,1,0:T(8,128)} %initial.1), channel_id=1, source_target_pairs={{0,15},{1,2},{2,1},{3,4},{4,3},{5,6},{6,5},{7,8},{8,7},{9,10},{10,... | collective-permute-start | bytes 1572872 | tf_op jit(solution)/shard_map/ppermute | solution.py:550
  13.4 1.1 %copy-start.30 = (f32[2,4,64,256]{3,2,1,0:T(8,128)S(1)}, f32[2,4,64,256]{3,2,1,0:T(8,128)}, u32[]{:S(2)}) copy-start(f32[2,4,64,256]{3,2,1,0:T(8,128)} %initial.1) | copy-start | bytes 1572868
  14.5 0.9 copy-start.37
  15.5 1.5 %collective-permute-start.3 = (f32[3,2,64,128]{3,2,1,0:T(8,128)S(1)}, f32[3,2,64,128]{3,2,1,0:T(8,128)S(1)}, u32[]{:S(2)}, u32[]{:S(2)}) collective-permute-start(f32[3,2,64,128]{3,2,1,0:T(8,128)S(1)} %get-tuple-element.42), channel_id=1, source_target_pairs={{0,1},{1,0},{2,3},{3,2},{4,5},{5,4},{6,7},{7,6},{8,9},{9,8},{10,11... | collective-permute-start | bytes 589832 | tf_op jit(solution)/shard_map/ppermute | solution.py:549
  15.6 8.0 %collective-permute-start = (f32[3,2,64,128]{3,2,1,0:T(8,128)S(1)}, f32[3,2,64,128]{3,2,1,0:T(8,128)S(1)}, u32[]{:S(2)}, u32[]{:S(2)}) collective-permute-start(f32[3,2,64,128]{3,2,1,0:T(8,128)S(1)} %get-tuple-element.39), channel_id=1, source_target_pairs={{0,15},{1,2},{2,1},{3,4},{4,3},{5,6},{6,5},{7,8},{8,7},{9,10},{10,... | collective-permute-start | bytes 589832 | tf_op jit(solution)/shard_map/ppermute | solution.py:550
  17.0 3.6 %copy-start.5 = (f32[2,4,64,256]{3,2,1,0:T(8,128)S(1)}, f32[2,4,64,256]{3,2,1,0:T(8,128)}, u32[]{:S(2)}) copy-start(f32[2,4,64,256]{3,2,1,0:T(8,128)} %observed.3) | copy-start | bytes 1572868
  17.9 5.7 %copy-start = (f32[5,2,64,128]{3,2,1,0:T(8,128)}, f32[5,2,64,128]{3,2,1,0:T(8,128)S(1)}, u32[]{:S(2)}) copy-start(f32[5,2,64,128]{3,2,1,0:T(8,128)S(1)} %get-tuple-element.49.m_all.all_a) | copy-start | bytes 983044
  21.7 3.0 %copy-start.3 = (f32[2,5,2,80,128]{4,3,2,1,0:T(8,128)}, f32[2,5,2,80,128]{4,3,2,1,0:T(8,128)S(1)}, u32[]{:S(2)}) copy-start(f32[2,5,2,80,128]{4,3,2,1,0:T(8,128)S(1)} %get-tuple-element.52.state1_a) | copy-start | bytes 2457604
  21.8 3.0 %copy-start.12 = (f32[2,3,2,80,128]{4,3,2,1,0:T(8,128)}, f32[2,3,2,80,128]{4,3,2,1,0:T(8,128)S(1)}, u32[]{:S(2)}) copy-start(f32[2,3,2,80,128]{4,3,2,1,0:T(8,128)S(1)} %get-tuple-element.53.chem1_a) | copy-start | bytes 1474564
  21.8 3.0 %copy-start.22 = (f32[2,1,2,80,128]{4,3,2,1,0:T(8,128)}, f32[2,1,2,80,128]{4,3,2,1,0:T(8,128)S(1)}, u32[]{:S(2)}) copy-start(f32[2,1,2,80,128]{4,3,2,1,0:T(8,128)S(1)} %get-tuple-element.54.adjoint2_a) | copy-start | bytes 491524
  24.8 0.8 copy-start.6
  25.6 0.8 copy-start.9
  29.0 0.8 copy-start.33
  31.2 0.8 copy-start.52
  32.0 8.6 %collective-permute-start.5 = (f32[2,3,2,64,128]{4,3,2,1,0:T(8,128)}, f32[2,3,2,64,128]{4,3,2,1,0:T(8,128)S(1)}, u32[]{:S(2)}, u32[]{:S(2)}) collective-permute-start(f32[2,3,2,64,128]{4,3,2,1,0:T(8,128)} %copy-done.52), channel_id=1, source_target_pairs={{0,1},{1,0},{2,3},{3,2},{4,5},{5,4},{6,7},{7,6},{8,9},{9,8},{10,11... | collective-permute-start | bytes 1179656 | tf_op jit(solution)/shard_map/ppermute | solution.py:549
  35.8 40.6 %collective-permute-start.4 = (f32[2,3,2,64,128]{4,3,2,1,0:T(8,128)}, f32[2,3,2,64,128]{4,3,2,1,0:T(8,128)}, u32[]{:S(2)}, u32[]{:S(2)}) collective-permute-start(f32[2,3,2,64,128]{4,3,2,1,0:T(8,128)} %copy-done.51), channel_id=1, source_target_pairs={{0,15},{1,2},{2,1},{3,4},{4,3},{5,6},{6,5},{7,8},{8,7},{9,10},{10,... | collective-permute-start | bytes 1179656 | tf_op jit(solution)/shard_map/ppermute | solution.py:550
  40.6 1.0 copy-start.1
  41.6 1.1 %copy-start.4 = (f32[2,5,2,80,128]{4,3,2,1,0:T(8,128)S(1)}, f32[2,5,2,80,128]{4,3,2,1,0:T(8,128)}, u32[]{:S(2)}) copy-start(f32[2,5,2,80,128]{4,3,2,1,0:T(8,128)} %copy-done.3) | copy-start | bytes 2457604
  42.7 1.0 %copy-start.7 = (f32[2,3,2,80,128]{4,3,2,1,0:T(8,128)S(1)}, f32[2,3,2,80,128]{4,3,2,1,0:T(8,128)}, u32[]{:S(2)}) copy-start(f32[2,3,2,80,128]{4,3,2,1,0:T(8,128)} %copy-done.6) | copy-start | bytes 1474564
  43.8 1.0 %copy-start.10 = (f32[2,3,2,80,128]{4,3,2,1,0:T(8,128)S(1)}, f32[2,3,2,80,128]{4,3,2,1,0:T(8,128)}, u32[]{:S(2)}) copy-start(f32[2,3,2,80,128]{4,3,2,1,0:T(8,128)} %copy-done.9) | copy-start | bytes 1474564
  44.8 1.0 %copy-start.13 = (f32[2,3,2,80,128]{4,3,2,1,0:T(8,128)S(1)}, f32[2,3,2,80,128]{4,3,2,1,0:T(8,128)}, u32[]{:S(2)}) copy-start(f32[2,3,2,80,128]{4,3,2,1,0:T(8,128)} %copy-done.12) | copy-start | bytes 1474564
  45.8 0.9 copy-start.17
  46.8 0.9 copy-start.20
  47.7 0.9 copy-start.23
  48.6 0.9 copy-start.25
  49.5 0.9 copy-start.28
  50.4 1.0 %copy-start.34 = (f32[2,3,2,80,128]{4,3,2,1,0:T(8,128)S(1)}, f32[2,3,2,80,128]{4,3,2,1,0:T(8,128)}, u32[]{:S(2)}) copy-start(f32[2,3,2,80,128]{4,3,2,1,0:T(8,128)} %copy-done.33) | copy-start | bytes 1474564
  53.0 0.9 copy-start.14
  54.0 0.8 copy-start.31
  54.8 0.8 copy-start.35
  76.5 1.0 copy-start.2
  77.5 1.0 %copy-start.8 = (f32[2,3,2,80,128]{4,3,2,1,0:T(8,128)S(1)}, f32[2,3,2,80,128]{4,3,2,1,0:T(8,128)}, u32[]{:S(2)}) copy-start(f32[2,3,2,80,128]{4,3,2,1,0:T(8,128)} %copy-done.6) | copy-start | bytes 1474564
  78.5 1.0 %copy-start.11 = (f32[2,3,2,80,128]{4,3,2,1,0:T(8,128)S(1)}, f32[2,3,2,80,128]{4,3,2,1,0:T(8,128)}, u32[]{:S(2)}) copy-start(f32[2,3,2,80,128]{4,3,2,1,0:T(8,128)} %copy-done.9) | copy-start | bytes 1474564
  79.5 1.1 %copy-start.15 = (f32[2,5,2,80,128]{4,3,2,1,0:T(8,128)S(1)}, f32[2,5,2,80,128]{4,3,2,1,0:T(8,128)}, u32[]{:S(2)}) copy-start(f32[2,5,2,80,128]{4,3,2,1,0:T(8,128)} %copy-done.14) | copy-start | bytes 2457604
  80.7 0.9 copy-start.18
  81.6 0.9 copy-start.21
  82.5 0.9 copy-start.26
  83.4 0.9 copy-start.29
  84.3 1.0 %copy-start.32 = (f32[2,3,2,80,128]{4,3,2,1,0:T(8,128)S(1)}, f32[2,3,2,80,128]{4,3,2,1,0:T(8,128)}, u32[]{:S(2)}) copy-start(f32[2,3,2,80,128]{4,3,2,1,0:T(8,128)} %copy-done.31) | copy-start | bytes 1474564
  85.4 1.0 copy-start.36
  86.4 0.9 copy-start.39
  87.3 0.9 copy-start.41
  88.2 0.9 copy-start.43
  89.1 0.9 copy-start.45
  90.0 0.9 copy-start.47
  90.9 0.9 copy-start.49
  (12 other events, 8.0 us)
Sparse Core Ops, SparseCore 0:
  32.1 43.4 all-gather.2

commit v9 on v7

--- a/solution.py
+++ b/solution.py
@@ -11,6 +11,7 @@
 stiffness = 0.5
 time_step = 0.005
 VMEM = pl.BlockSpec(memory_space=pltpu.VMEM)
+SMEM = pl.BlockSpec(memory_space=pltpu.SMEM)
 LANES = 128
 ROWS = 8
 PAD = ROWS
@@ -450,9 +451,9 @@
 def late_kernel(
     of_chip, mx_a, my_a, mz_a, mz_low_a, all_a, mx_b, my_b, mz_b, mz_low_b, all_b,
     chem0_a, chem0_b, chem1_b, adjoint2_b, flow_a, flow_part, adjoint1_a, weight_b, step_z_b,
-    part, sum_x_b, sum_y_b, sum_z_b, share_in, result, share, rim, flow_b, adjoint1_b, sum_x, sum_y, sum_z,
+    part, sum_x_b, sum_y_b, sum_z_b, share, far, result, misfit, rim, flow_b, adjoint1_b, sum_x, sum_y, sum_z,
 ):
-    share[...] = share_in[...]
+    misfit[0] = (share[...] + far[...])[0, 0]
     runs = of_chip.shape[0]
     n, ny, _ = result.shape
     faces = Faces(n, (mx_a, my_a, mz_a, mz_low_a, all_a, mx_b, my_b, mz_b, mz_low_b, all_b))
@@ -523,13 +524,13 @@
             put_plain(result, (place[n - 2 + at],), row, value)
 
 
-def call(kernel, outs, scratch, args, flops):
+def call(kernel, outs, scratch, args, flops, scalar=None):
     moved = 4 * (sum(a.size for a in args) + sum(math.prod(o) for o in outs))
     return pl.pallas_call(
         kernel,
         out_shape=tuple(jax.ShapeDtypeStruct(o, jnp.float32) for o in outs),
         in_specs=[VMEM] * len(args),
-        out_specs=tuple([VMEM] * len(outs)),
+        out_specs=tuple(SMEM if at == scalar else VMEM for at in range(len(outs))),
         scratch_shapes=[pltpu.VMEM(s, jnp.float32) for s in scratch],
         compiler_params=pltpu.CompilerParams(vmem_limit_bytes=16 * 1024 * 1024),
         cost_estimate=pl.CostEstimate(flops=flops, bytes_accessed=moved, transcendentals=0),
@@ -597,17 +598,18 @@
     )
     faces = (*faces_a, *faces_b)
     of_chip, of_core = neighbours(to_chip, to_core)
-    hops = []
-    if count & (count - 1):
-        share = lax.psum(share, "gx")
-    else:
-        share = share + of_core[0, 0, 0, ny:]
-        hops = [1 << bit for bit in range(count.bit_length() - 1, 0, -1) if 1 << bit < count]
-
-    def hop_of(value, hop):
-        return lax.ppermute(value, "gx", [(i, i ^ hop) for i in range(count)])
-
-    far = hop_of(share, hops[0]) if hops else None
+    bits = range(count.bit_length() - 2)
+
+    def target(at, step):
+        apart = (at ^ at >> 1) & 1
+        bit = bits[-1 - step] if apart else bits[step]
+        return at ^ (3 if bit == 0 else 2 << bit)
+
+    def hop(value, step):
+        return lax.ppermute(value, "gx", [(at, target(at, step)) for at in range(count)])
+
+    share = share + of_core[0, 0, 0, ny:]
+    far = hop(share, 0)
     flow_a, flow_part, adjoint1_a, weight_b, step_z_b, part, *sums_b, share = call(
         early_kernel,
         (
@@ -618,25 +620,23 @@
         (of_core, *faces, chem0_a, chem0_b, state1_a, state1_b, chem1_a, chem1_b, adjoint2_a, adjoint2_b, share),
         60 * runs * n * cell,
     )
-    for hop in hops[1:]:
+    for step in bits[1:]:
         share = share + far
-        far = hop_of(share, hop)
-    result, share = call(
+        far = hop(share, step)
+    return call(
         late_kernel,
-        ((n, ny, nz), (ROWS, LANES)),
+        ((n, ny, nz), (1,)),
         (
             lies_padded(runs, 3), lies_padded(runs, 3), lies_padded(runs, 3),
             lies(3), lies_padded(2), lies(2),
         ),
         (
             of_chip, *faces, chem0_a, chem0_b, chem1_b, adjoint2_b, flow_a, flow_part, adjoint1_a,
-            weight_b, step_z_b, part, *sums_b, share,
+            weight_b, step_z_b, part, *sums_b, share, far,
         ),
         60 * runs * 3 * cell,
-    )
-    if hops:
-        share = share + far
-    return (result, share[0, :1])
+        scalar=1,
+    )
 
 
 def solution(mesh):

time: 40.2 us -> 42.6 us (1.060)
  waiting for transfers between devices: 12.6 us -> 16.1 us
  local copies, waits for them, and re-layouts: 2.54 us -> 2.03 us
  starting transfers between devices: 16.9 us -> 16.4 us
    ppermute x3, waiting for transfers between devices: 7.42 us -> 10.9 us  [hop(): lax.ppermute(value, 'gx', [(at, target(at, step)) for at in range(count)])]
    ppermute x3, starting transfers between devices: 1.52 us -> 0.93 us  [hop(): lax.ppermute(value, 'gx', [(at, target(at, step)) for at in range(count)])]
    slice x1 -> x0, local copies, waits for them, and re-layouts: 0.51 us -> none  [on_device(): return (result, share[0, :1])]
  transfers between devices with their start and end apart: 9 -> 9, of which waited for: 6 -> 6; matrix products, arithmetic and copies ran while one was open for 0% -> 0% of each run, Pallas kernels for 15% -> 10%
where the time goes in v9:
time: 42.6 us; the launch traced here: 42.4 us
  starting transfers between devices  16.4 us (38%)
  waiting for transfers between devices  16.1 us (38%)
  Pallas kernels  7.2 us (17%)
  local copies, waits for them, and re-layouts  2.03 us (5%)
  between operations  0.69 us (2%)
    ppermute x3, starting transfers between devices, neighbours(): return (lax.ppermute(to_chip, 'gx', over_chips), of_core)  11.1 us
    ppermute x3, waiting for transfers between devices, hop(): lax.ppermute(value, 'gx', [(at, target(at, step)) for at in range(count)])  10.9 us
    pallas_call x6, Pallas kernels, call(): pl.pallas_call(kernel, out_shape=tuple((jax.ShapeDtypeStruct(o, jnp.float...  7.2 us
    ppermute x3, starting transfers between devices, neighbours(): of_core = lax.ppermute(to_core, 'gx', over_cores)  4.37 us
    ppermute x3, waiting for transfers between devices, neighbours(): return (lax.ppermute(to_chip, 'gx', over_chips), of_core)  4.32 us
    unnamed x6, local copies, waits for them, and re-layouts  2.03 us
    ppermute x3, starting transfers between devices, hop(): lax.ppermute(value, 'gx', [(at, target(at, step)) for at in range(count)])  0.93 us
  transfers between devices with their start and end apart: 9, of which 6 were waited for; matrix products, arithmetic and copies ran while one was open for 0% of the time, Pallas kernels for 10%

profile of v9, /device:TPU:0, one launch (start us, length us, event | category | flops | bytes accessed | tf_op | source)
XLA Modules:
  0.0 42.4 jit_solution(9197231891142350549)
XLA Ops:
  0.6 0.5 %collective-permute-start.2 = (f32[2,4,64,256]{3,2,1,0:T(8,128)}, f32[2,4,64,256]{3,2,1,0:T(8,128)S(1)}, u32[]{:S(2)}, u32[]{:S(2)}) collective-permute-start(f32[2,4,64,256]{3,2,1,0:T(8,128)} %initial.1), channel_id=1, source_target_pairs={{0,1},{1,0},{2,3},{3,2},{4,5},{5,4},{6,7},{7,6},{8,9},{9,8},{10,11... | collective-permute-start | bytes 1572872 | tf_op jit(solution)/shard_map/ppermute | solution.py:549
  1.1 5.7 %collective-permute-start.1 = (f32[2,4,64,256]{3,2,1,0:T(8,128)}, f32[2,4,64,256]{3,2,1,0:T(8,128)S(1)}, u32[]{:S(2)}, u32[]{:S(2)}) collective-permute-start(f32[2,4,64,256]{3,2,1,0:T(8,128)} %initial.1), channel_id=1, source_target_pairs={{0,15},{1,2},{2,1},{3,4},{4,3},{5,6},{6,5},{7,8},{8,7},{9,10},{10,... | collective-permute-start | bytes 1572872 | tf_op jit(solution)/shard_map/ppermute | solution.py:550
  6.8 0.0 copy-start.1
  6.8 1.1 %copy-done.1 = f32[2,4,64,256]{3,2,1,0:T(8,128)S(1)} copy-done((f32[2,4,64,256]{3,2,1,0:T(8,128)S(1)}, f32[2,4,64,256]{3,2,1,0:T(8,128)}, u32[]{:S(2)}) %copy-start.1) | copy-done | bytes 524312
  7.9 0.0 copy-start.2
  7.9 0.9 %copy-done.2 = f32[4,64,256]{2,1,0:T(8,128)S(1)} copy-done((f32[4,64,256]{2,1,0:T(8,128)S(1)}, f32[4,64,256]{2,1,0:T(8,128)}, u32[]{:S(2)}) %copy-start.2) | copy-done | bytes 262168
  8.8 0.1 shard_map.50
  8.9 0.1 collective-permute-start.3
  9.0 0.6 %collective-permute-start = (f32[3,2,64,128]{3,2,1,0:T(8,128)S(1)}, f32[3,2,64,128]{3,2,1,0:T(8,128)S(1)}, u32[]{:S(2)}, u32[]{:S(2)}) collective-permute-start(f32[3,2,64,128]{3,2,1,0:T(8,128)S(1)} %get-tuple-element.40), channel_id=1, source_target_pairs={{0,15},{1,2},{2,1},{3,4},{4,3},{5,6},{6,5},{7,8},{8,7},{9,10},{10,... | collective-permute-start | bytes 589832 | tf_op jit(solution)/shard_map/ppermute | solution.py:550
  9.6 0.8 %collective-permute-done.3.m_core = f32[3,2,64,128]{3,2,1,0:T(8,128)S(1)} collective-permute-done((f32[3,2,64,128]{3,2,1,0:T(8,128)S(1)}, f32[3,2,64,128]{3,2,1,0:T(8,128)S(1)}, u32[]{:S(2)}, u32[]{:S(2)}) %collective-permute-start.3) | collective-permute-done | bytes 196640 | tf_op jit(solution)/shard_map/ppermute | solution.py:549
  10.4 0.0 collective-permute-done.2.of_core
  10.4 0.0 copy-start
  10.5 0.9 %shard_map.51 = (f32[2,4,2,80,128]{4,3,2,1,0:T(8,128)S(1)}, f32[2,6,2,80,128]{4,3,2,1,0:T(8,128)S(1)}, f32[6,2,64,128]{3,2,1,0:T(8,128)S(1)}, f32[6,2,80,128]{3,...) custom-call(f32[2,4,64,256]{3,2,1,0:T(8,128)S(1)} %collective-permut, ...), custom_call_target="tpu_custom_call" | custom-call | flops 3932160 | bytes 5341184 | tf_op jit(solution)/shard_map/pallas_call | solution.py:529
  11.3 2.7 %collective-permute-done.1.of_chip = f32[2,4,64,256]{3,2,1,0:T(8,128)S(1)} collective-permute-done((f32[2,4,64,256]{3,2,1,0:T(8,128)}, f32[2,4,64,256]{3,2,1,0:T(8,128)S(1)}, u32[]{:S(2)}, u32[]{:S(2)}) %collective-permute-start.1) | collective-permute-done | bytes 524320 | tf_op jit(solution)/shard_map/ppermute | solution.py:550
  14.0 0.0 copy-done
  14.0 1.3 %shard_map.52 = (f32[2,4,2,80,128]{4,3,2,1,0:T(8,128)S(1)}, f32[2,4,2,80,128]{4,3,2,1,0:T(8,128)S(1)}, f32[2,5,2,80,128]{4,3,2,1,0:T(8,128)S(1)}, f32[2,3,2,80,1...) custom-call(f32[2,4,64,256]{3,2,1,0:T(8,128)S(1)} %collective-permute-done.1.of_chip, ...), custom_call_target="tpu_custom_call" | custom-call | flops 5898240 | bytes 8134656 | tf_op jit(solution)/shard_map/pallas_call | solution.py:529
  15.3 1.7 %collective-permute-done.m_chip = f32[3,2,64,128]{3,2,1,0:T(8,128)S(1)} collective-permute-done((f32[3,2,64,128]{3,2,1,0:T(8,128)S(1)}, f32[3,2,64,128]{3,2,1,0:T(8,128)S(1)}, u32[]{:S(2)}, u32[]{:S(2)}) %collective-permute-start) | collective-permute-done | bytes 196640 | tf_op jit(solution)/shard_map/ppermute | solution.py:550
  17.0 1.3 %shard_map.53 = (f32[3,2,64,128]{3,2,1,0:T(8,128)S(1)}, f32[2,2,80,128]{3,2,1,0:T(8,128)S(1)}, f32[2,2,64,128]{3,2,1,0:T(8,128)S(1)}, f32[2,2,64,128]{3,2,1,0:T(...) custom-call(f32[3,2,64,128]{3,2,1,0:T(8,128)S(1)} %collective-permut, ...), custom_call_target="tpu_custom_call" | custom-call | flops 5898240 | bytes 10612736 | tf_op jit(solution)/shard_map/pallas_call | solution.py:529
  18.3 3.8 %collective-permute-start.5 = (f32[2,3,2,72,128]{4,3,2,1,0:T(8,128)S(1)}, f32[2,3,2,72,128]{4,3,2,1,0:T(8,128)S(1)}, u32[]{:S(2)}, u32[]{:S(2)}) collective-permute-start(f32[2,3,2,72,128]{4,3,2,1,0:T(8,128)S(1)} %get-tuple-element.65), channel_id=1, source_target_pairs={{0,1},{1,0},{2,3},{3,2},{4,5},{5,4},{6,7},{7,6},{8,9},{9,8},{10,11... | collective-permute-start | bytes 1327112 | tf_op jit(solution)/shard_map/ppermute | solution.py:549
  22.1 4.8 %collective-permute-start.4 = (f32[2,3,2,64,128]{4,3,2,1,0:T(8,128)S(1)}, f32[2,3,2,64,128]{4,3,2,1,0:T(8,128)S(1)}, u32[]{:S(2)}, u32[]{:S(2)}) collective-permute-start(f32[2,3,2,64,128]{4,3,2,1,0:T(8,128)S(1)} %get-tuple-element.57), channel_id=1, source_target_pairs={{0,15},{1,2},{2,1},{3,4},{4,3},{5,6},{6,5},{7,8},{8,7},{9,10},{10,... | collective-permute-start | bytes 1179656 | tf_op jit(solution)/shard_map/ppermute | solution.py:550
  26.8 0.0 collective-permute-done.5.of_core
  26.8 0.0 collective-permute-start.6
  26.9 2.0 %shard_map.54 = (f32[2,5,2,80,128]{4,3,2,1,0:T(8,128)S(1)}, f32[2,1,2,80,128]{4,3,2,1,0:T(8,128)S(1)}, f32[2,3,2,80,128]{4,3,2,1,0:T(8,128)S(1)}, f32[2,3,2,64,1...) custom-call(f32[2,3,2,72,128]{4,3,2,1,0:T(8,128)S(1)} %collective-pe, ...), custom_call_target="tpu_custom_call" | custom-call | flops 7864320 | bytes 10510336 | tf_op jit(solution)/shard_map/pallas_call | solution.py:529
  28.8 3.8 %collective-permute-done.6 = f32[8,128]{1,0:T(8,128)S(1)} collective-permute-done((f32[8,128]{1,0:T(8,128)S(1)}, f32[8,128]{1,0:T(8,128)S(1)}, u32[]{:S(2)}, u32[]{:S(2)}) %collective-permute-start.6) | collective-permute-done | bytes 4128 | tf_op jit(solution)/shard_map/ppermute | solution.py:609
  32.6 0.0 collective-permute-start.7
  32.6 3.6 %collective-permute-done.7 = f32[8,128]{1,0:T(8,128)S(1)} collective-permute-done((f32[8,128]{1,0:T(8,128)S(1)}, f32[8,128]{1,0:T(8,128)S(1)}, u32[]{:S(2)}, u32[]{:S(2)}) %collective-permute-start.7) | collective-permute-done | bytes 4128 | tf_op jit(solution)/shard_map/ppermute | solution.py:609
  36.2 0.9 %collective-permute-start.8 = (f32[8,128]{1,0:T(8,128)S(1)}, f32[8,128]{1,0:T(8,128)S(1)}, u32[]{:S(2)}, u32[]{:S(2)}) collective-permute-start(f32[8,128]{1,0:T(8,128)S(1)} %add.11.share), channel_id=1, source_target_pairs={{0,8},{1,2},{2,1},{3,11},{4,12},{5,6},{6,5},{7,15},{8,0},{9,10},{1... | collective-permute-start | bytes 12296 | tf_op jit(solution)/shard_map/ppermute | solution.py:609
  37.1 0.0 collective-permute-done.4.of_chip
  37.1 3.6 %collective-permute-done.8.far = f32[8,128]{1,0:T(8,128)S(1)} collective-permute-done((f32[8,128]{1,0:T(8,128)S(1)}, f32[8,128]{1,0:T(8,128)S(1)}, u32[]{:S(2)}, u32[]{:S(2)}) %collective-permute-start.8) | collective-permute-done | bytes 4128 | tf_op jit(solution)/shard_map/ppermute | solution.py:609
  40.7 1.7 %shard_map.55 = (f32[4,64,256]{2,1,0:T(8,128)}, f32[1]{0:T(128)}) custom-call(f32[2,3,2,64,128]{4,3,2,1,0:T(8,128)S(1)} %collective-permute-done.4.of_chip, f32[6,2,64,128]{3,2,1,0:T(8,128)S(1)} %get-tuple-element.46.mx.mx_a, f32[6,2,80,128]{3,2,1,0:T(8,128)S(1)} %get-tuple-element.47.my.my_a, f32[6,2,64,128]{3,2,1,0:T(8,128)S(1)} %get-tuple-element.48.mz.mz_a, ...), custom_call_target="tpu_custom_call" | custom-call | flops 5898240 | bytes 8757252 | tf_op jit(solution)/shard_map/pallas_call | solution.py:529
  (3 shorter events, 0.0 us)
Async XLA Ops:
  0.6 9.8 %collective-permute-start.2 = (f32[2,4,64,256]{3,2,1,0:T(8,128)}, f32[2,4,64,256]{3,2,1,0:T(8,128)S(1)}, u32[]{:S(2)}, u32[]{:S(2)}) collective-permute-start(f32[2,4,64,256]{3,2,1,0:T(8,128)} %initial.1), channel_id=1, source_target_pairs={{0,1},{1,0},{2,3},{3,2},{4,5},{5,4},{6,7},{7,6},{8,9},{9,8},{10,11... | collective-permute-start | bytes 1572872 | tf_op jit(solution)/shard_map/ppermute | solution.py:549
  1.1 12.8 %collective-permute-start.1 = (f32[2,4,64,256]{3,2,1,0:T(8,128)}, f32[2,4,64,256]{3,2,1,0:T(8,128)S(1)}, u32[]{:S(2)}, u32[]{:S(2)}) collective-permute-start(f32[2,4,64,256]{3,2,1,0:T(8,128)} %initial.1), channel_id=1, source_target_pairs={{0,15},{1,2},{2,1},{3,4},{4,3},{5,6},{6,5},{7,8},{8,7},{9,10},{10,... | collective-permute-start | bytes 1572872 | tf_op jit(solution)/shard_map/ppermute | solution.py:550
  6.8 1.1 %copy-start.1 = (f32[2,4,64,256]{3,2,1,0:T(8,128)S(1)}, f32[2,4,64,256]{3,2,1,0:T(8,128)}, u32[]{:S(2)}) copy-start(f32[2,4,64,256]{3,2,1,0:T(8,128)} %initial.1) | copy-start | bytes 1572868
  7.9 0.9 %copy-start.2 = (f32[4,64,256]{2,1,0:T(8,128)S(1)}, f32[4,64,256]{2,1,0:T(8,128)}, u32[]{:S(2)}) copy-start(f32[4,64,256]{2,1,0:T(8,128)} %mobility.1) | copy-start | bytes 786436
  8.9 1.5 %collective-permute-start.3 = (f32[3,2,64,128]{3,2,1,0:T(8,128)S(1)}, f32[3,2,64,128]{3,2,1,0:T(8,128)S(1)}, u32[]{:S(2)}, u32[]{:S(2)}) collective-permute-start(f32[3,2,64,128]{3,2,1,0:T(8,128)S(1)} %get-tuple-element.43), channel_id=1, source_target_pairs={{0,1},{1,0},{2,3},{3,2},{4,5},{5,4},{6,7},{7,6},{8,9},{9,8},{10,11... | collective-permute-start | bytes 589832 | tf_op jit(solution)/shard_map/ppermute | solution.py:549
  9.0 8.0 %collective-permute-start = (f32[3,2,64,128]{3,2,1,0:T(8,128)S(1)}, f32[3,2,64,128]{3,2,1,0:T(8,128)S(1)}, u32[]{:S(2)}, u32[]{:S(2)}) collective-permute-start(f32[3,2,64,128]{3,2,1,0:T(8,128)S(1)} %get-tuple-element.40), channel_id=1, source_target_pairs={{0,15},{1,2},{2,1},{3,4},{4,3},{5,6},{6,5},{7,8},{8,7},{9,10},{10,... | collective-permute-start | bytes 589832 | tf_op jit(solution)/shard_map/ppermute | solution.py:550
  10.4 3.6 %copy-start = (f32[2,4,64,256]{3,2,1,0:T(8,128)S(1)}, f32[2,4,64,256]{3,2,1,0:T(8,128)}, u32[]{:S(2)}) copy-start(f32[2,4,64,256]{3,2,1,0:T(8,128)} %observed.3) | copy-start | bytes 1572868
  18.3 8.6 %collective-permute-start.5 = (f32[2,3,2,72,128]{4,3,2,1,0:T(8,128)S(1)}, f32[2,3,2,72,128]{4,3,2,1,0:T(8,128)S(1)}, u32[]{:S(2)}, u32[]{:S(2)}) collective-permute-start(f32[2,3,2,72,128]{4,3,2,1,0:T(8,128)S(1)} %get-tuple-element.65), channel_id=1, source_target_pairs={{0,1},{1,0},{2,3},{3,2},{4,5},{5,4},{6,7},{7,6},{8,9},{9,8},{10,11... | collective-permute-start | bytes 1327112 | tf_op jit(solution)/shard_map/ppermute | solution.py:549
  22.1 15.1 %collective-permute-start.4 = (f32[2,3,2,64,128]{4,3,2,1,0:T(8,128)S(1)}, f32[2,3,2,64,128]{4,3,2,1,0:T(8,128)S(1)}, u32[]{:S(2)}, u32[]{:S(2)}) collective-permute-start(f32[2,3,2,64,128]{4,3,2,1,0:T(8,128)S(1)} %get-tuple-element.57), channel_id=1, source_target_pairs={{0,15},{1,2},{2,1},{3,4},{4,3},{5,6},{6,5},{7,8},{8,7},{9,10},{10,... | collective-permute-start | bytes 1179656 | tf_op jit(solution)/shard_map/ppermute | solution.py:550
  26.8 5.7 %collective-permute-start.6 = (f32[8,128]{1,0:T(8,128)S(1)}, f32[8,128]{1,0:T(8,128)S(1)}, u32[]{:S(2)}, u32[]{:S(2)}) collective-permute-start(f32[8,128]{1,0:T(8,128)S(1)} %fusion.share_in), channel_id=1, source_target_pairs={{0,3},{1,9},{2,10},{3,0},{4,7},{5,13},{6,14},{7,4},{8,11},{9,1},{1... | collective-permute-start | bytes 12296 | tf_op jit(solution)/shard_map/ppermute | solution.py:609
  32.6 3.6 %collective-permute-start.7 = (f32[8,128]{1,0:T(8,128)S(1)}, f32[8,128]{1,0:T(8,128)S(1)}, u32[]{:S(2)}, u32[]{:S(2)}) collective-permute-start(f32[8,128]{1,0:T(8,128)S(1)} %add.10), channel_id=1, source_target_pairs={{0,4},{1,5},{2,6},{3,7},{4,0},{5,1},{6,2},{7,3},{8,12},{9,13},{10,... | collective-permute-start | bytes 12296 | tf_op jit(solution)/shard_map/ppermute | solution.py:609
  36.2 4.5 %collective-permute-start.8 = (f32[8,128]{1,0:T(8,128)S(1)}, f32[8,128]{1,0:T(8,128)S(1)}, u32[]{:S(2)}, u32[]{:S(2)}) collective-permute-start(f32[8,128]{1,0:T(8,128)S(1)} %add.11.share), channel_id=1, source_target_pairs={{0,8},{1,2},{2,1},{3,11},{4,12},{5,6},{6,5},{7,15},{8,0},{9,10},{1... | collective-permute-start | bytes 12296 | tf_op jit(solution)/shard_map/ppermute | solution.py:609

commit v10 on v9

--- a/solution.py
+++ b/solution.py
@@ -369,10 +369,12 @@
 def early_kernel(
     of_core, mx_a, my_a, mz_a, mz_low_a, all_a, mx_b, my_b, mz_b, mz_low_b, all_b,
     chem0_a, chem0_b, state1_a, state1_b, chem1_a, chem1_b, adjoint2_a, adjoint2_b,
-    share_in, flow_a, flow_part, adjoint1_a, weight_b, step_z_b, part, sum_x_b, sum_y_b, sum_z_b, share,
+    share, flow_a, flow_part, adjoint1_a, weight_b, step_z_b, part, sum_x_b, sum_y_b, sum_z_b, shares,
     rim, sum_x, sum_y, sum_z,
 ):
-    share[...] = share_in[...]
+    ny = part.shape[-2]
+    chip = share[:1] + of_core[0, 0, 0, ny : ny + 1]
+    shares[...] = jnp.broadcast_to(chip[None], shares.shape)
     runs = of_core.shape[0]
     n = part.shape[0] + 2
     ny = part.shape[-2]
@@ -451,9 +453,9 @@
 def late_kernel(
     of_chip, mx_a, my_a, mz_a, mz_low_a, all_a, mx_b, my_b, mz_b, mz_low_b, all_b,
     chem0_a, chem0_b, chem1_b, adjoint2_b, flow_a, flow_part, adjoint1_a, weight_b, step_z_b,
-    part, sum_x_b, sum_y_b, sum_z_b, share, far, result, misfit, rim, flow_b, adjoint1_b, sum_x, sum_y, sum_z,
+    part, sum_x_b, sum_y_b, sum_z_b, shares, result, misfit, rim, flow_b, adjoint1_b, sum_x, sum_y, sum_z,
 ):
-    misfit[0] = (share[...] + far[...])[0, 0]
+    misfit[0] = jnp.sum(shares[...], axis=0)[0, 0]
     runs = of_chip.shape[0]
     n, ny, _ = result.shape
     faces = Faces(n, (mx_a, my_a, mz_a, mz_low_a, all_a, mx_b, my_b, mz_b, mz_low_b, all_b))
@@ -598,31 +600,18 @@
     )
     faces = (*faces_a, *faces_b)
     of_chip, of_core = neighbours(to_chip, to_core)
-    bits = range(count.bit_length() - 2)
-
-    def target(at, step):
-        apart = (at ^ at >> 1) & 1
-        bit = bits[-1 - step] if apart else bits[step]
-        return at ^ (3 if bit == 0 else 2 << bit)
-
-    def hop(value, step):
-        return lax.ppermute(value, "gx", [(at, target(at, step)) for at in range(count)])
-
-    share = share + of_core[0, 0, 0, ny:]
-    far = hop(share, 0)
-    flow_a, flow_part, adjoint1_a, weight_b, step_z_b, part, *sums_b, share = call(
+    sets = [[at for at in range(count) if (at ^ at >> 1) & 1 == which] for which in (0, 1)]
+    flow_a, flow_part, adjoint1_a, weight_b, step_z_b, part, *sums_b, shares = call(
         early_kernel,
         (
             lies_padded(runs, n + 1), lies_padded(runs, 1), lies_padded(runs, n - 1), lies(runs, 3), lies(runs, 2),
-            lies(n - 2), lies(2), lies(2), lies(2), (ROWS, LANES),
+            lies(n - 2), lies(2), lies(2), lies(2), (count // 2, 1, LANES),
         ),
         (lies_padded(runs, 3), lies(n), lies_padded(n), lies(n)),
         (of_core, *faces, chem0_a, chem0_b, state1_a, state1_b, chem1_a, chem1_b, adjoint2_a, adjoint2_b, share),
         60 * runs * n * cell,
     )
-    for step in bits[1:]:
-        share = share + far
-        far = hop(share, step)
+    shares = lax.all_to_all(shares, "gx", 0, 0, axis_index_groups=sets)
     return call(
         late_kernel,
         ((n, ny, nz), (1,)),
@@ -632,7 +621,7 @@
         ),
         (
             of_chip, *faces, chem0_a, chem0_b, chem1_b, adjoint2_b, flow_a, flow_part, adjoint1_a,
-            weight_b, step_z_b, part, *sums_b, share, far,
+            weight_b, step_z_b, part, *sums_b, shares,
         ),
         60 * runs * 3 * cell,
         scalar=1,

time: 42.6 us -> 63.9 us (1.50)
  local copies, waits for them, and re-layouts: 2.03 us -> 23.8 us
  waiting for transfers between devices: 16.1 us -> 11.1 us
  starting transfers between devices: 16.4 us -> 18.8 us
  Pallas kernels: 7.2 us -> 8.66 us
    unnamed x6 -> x70, local copies, waits for them, and re-layouts: 2.03 us -> 23.8 us
    ppermute x3 -> x0, waiting for transfers between devices: 10.9 us -> none  [hop(): lax.ppermute(value, 'gx', [(at, target(at, step)) for at in range(count)])]
    all_to_all x0 -> x1, waiting for transfers between devices: none -> 5.82 us  [on_device(): shares = lax.all_to_all(shares, 'gx', 0, 0, axis_index_groups=sets)]
    all_to_all x0 -> x1, starting transfers between devices: none -> 3.33 us  [on_device(): shares = lax.all_to_all(shares, 'gx', 0, 0, axis_index_groups=sets)]
    pallas_call x6, Pallas kernels: 7.2 us -> 8.66 us  [call(): pl.pallas_call(kernel, out_shape=tuple((jax.ShapeDtypeStruct(o, jnp.float...]
    ppermute x3 -> x0, starting transfers between devices: 0.93 us -> none  [hop(): lax.ppermute(value, 'gx', [(at, target(at, step)) for at in range(count)])]
  transfers between devices with their start and end apart: 9 -> 7, of which waited for: 6 -> 4; matrix products, arithmetic and copies ran while one was open for 0% -> 0% of each run, Pallas kernels for 10% -> 7%
where the time goes in v10:
time: 63.9 us; the launch traced here: 63.2 us
  local copies, waits for them, and re-layouts  23.8 us (37%)
  starting transfers between devices  18.8 us (29%)
  waiting for transfers between devices  11.1 us (17%)
  Pallas kernels  8.66 us (14%)
  between operations  0.77 us (1%)
    unnamed x70, local copies, waits for them, and re-layouts  23.8 us
    ppermute x3, starting transfers between devices, neighbours(): return (lax.ppermute(to_chip, 'gx', over_chips), of_core)  11.1 us
    pallas_call x6, Pallas kernels, call(): pl.pallas_call(kernel, out_shape=tuple((jax.ShapeDtypeStruct(o, jnp.float...  8.66 us
    all_to_all x1, waiting for transfers between devices, on_device(): shares = lax.all_to_all(shares, 'gx', 0, 0, axis_index_groups=sets)  5.82 us
    ppermute x3, waiting for transfers between devices, neighbours(): return (lax.ppermute(to_chip, 'gx', over_chips), of_core)  4.5 us
    ppermute x3, starting transfers between devices, neighbours(): of_core = lax.ppermute(to_core, 'gx', over_cores)  4.44 us
    all_to_all x1, starting transfers between devices, on_device(): shares = lax.all_to_all(shares, 'gx', 0, 0, axis_index_groups=sets)  3.33 us
  transfers between devices with their start and end apart: 7, of which 4 were waited for; matrix products, arithmetic and copies ran while one was open for 0% of the time, Pallas kernels for 7%

profile of v10, /device:TPU:0, one launch (start us, length us, event | category | flops | bytes accessed | tf_op | source)
XLA Modules:
  0.0 63.2 jit_solution(10279173624594239745)
XLA Ops:
  0.6 0.5 collective-permute-start.2
  1.1 5.7 %collective-permute-start.1 = (f32[2,4,64,256]{3,2,1,0:T(8,128)}, f32[2,4,64,256]{3,2,1,0:T(8,128)S(1)}, u32[]{:S(2)}, u32[]{:S(2)}) collective-permute-start(f32[2,4,64,256]{3,2,1,0:T(8,128)} %initial.1), channel_id=1, source_target_pairs={{0,15},{1,2},{2,1},{3,4},{4,3},{5,6},{6,5},{7,8},{8,7},{9,10},{10,... | collective-permute-start | bytes 1572872 | tf_op jit(solution)/shard_map/ppermute | solution.py:552
  6.8 1.1 %copy-done.17 = f32[2,4,64,256]{3,2,1,0:T(8,128)S(1)} copy-done((f32[2,4,64,256]{3,2,1,0:T(8,128)S(1)}, f32[2,4,64,256]{3,2,1,0:T(8,128)}, u32[]{:S(2)}) %copy-start.17) | copy-done | bytes 524312
  7.9 0.9 %copy-done.22 = f32[4,64,256]{2,1,0:T(8,128)S(1)} copy-done((f32[4,64,256]{2,1,0:T(8,128)S(1)}, f32[4,64,256]{2,1,0:T(8,128)}, u32[]{:S(2)}) %copy-start.22) | copy-done | bytes 262168
  8.8 0.1 shard_map.50
  8.9 0.1 collective-permute-start.3
  9.0 0.6 collective-permute-start
  9.6 0.8 %collective-permute-done.3.m_core = f32[3,2,64,128]{3,2,1,0:T(8,128)S(1)} collective-permute-done((f32[3,2,64,128]{3,2,1,0:T(8,128)S(1)}, f32[3,2,64,128]{3,2,1,0:T(8,128)S(1)}, u32[]{:S(2)}, u32[]{:S(2)}) %collective-permute-start.3) | collective-permute-done | bytes 196640 | tf_op jit(solution)/shard_map/ppermute | solution.py:551
  10.4 0.0 collective-permute-done.2.of_core
  10.5 0.8 %shard_map.51 = (f32[2,4,2,80,128]{4,3,2,1,0:T(8,128)S(1)}, f32[2,6,2,80,128]{4,3,2,1,0:T(8,128)S(1)}, f32[6,2,64,128]{3,2,1,0:T(8,128)S(1)}, f32[6,2,80,128]{3,...) custom-call(f32[2,4,64,256]{3,2,1,0:T(8,128)S(1)} %collective-permut, ...), custom_call_target="tpu_custom_call" | custom-call | flops 3932160 | bytes 5341184 | tf_op jit(solution)/shard_map/pallas_call | solution.py:531
  11.3 2.7 %collective-permute-done.1.of_chip = f32[2,4,64,256]{3,2,1,0:T(8,128)S(1)} collective-permute-done((f32[2,4,64,256]{3,2,1,0:T(8,128)}, f32[2,4,64,256]{3,2,1,0:T(8,128)S(1)}, u32[]{:S(2)}, u32[]{:S(2)}) %collective-permute-start.1) | collective-permute-done | bytes 524320 | tf_op jit(solution)/shard_map/ppermute | solution.py:552
  14.0 1.2 %shard_map.52 = (f32[2,4,2,80,128]{4,3,2,1,0:T(8,128)S(1)}, f32[2,4,2,80,128]{4,3,2,1,0:T(8,128)S(1)}, f32[2,5,2,80,128]{4,3,2,1,0:T(8,128)S(1)}, f32[2,3,2,80,1...) custom-call(f32[2,4,64,256]{3,2,1,0:T(8,128)S(1)} %collective-permute-done.1.of_chip, ...), custom_call_target="tpu_custom_call" | custom-call | flops 5898240 | bytes 8134656 | tf_op jit(solution)/shard_map/pallas_call | solution.py:531
  15.2 1.8 %collective-permute-done.m_chip = f32[3,2,64,128]{3,2,1,0:T(8,128)S(1)} collective-permute-done((f32[3,2,64,128]{3,2,1,0:T(8,128)S(1)}, f32[3,2,64,128]{3,2,1,0:T(8,128)S(1)}, u32[]{:S(2)}, u32[]{:S(2)}) %collective-permute-start) | collective-permute-done | bytes 196640 | tf_op jit(solution)/shard_map/ppermute | solution.py:552
  17.0 1.9 %shard_map.53 = (f32[3,2,64,128]{3,2,1,0:T(8,128)S(1)}, f32[2,2,80,128]{3,2,1,0:T(8,128)S(1)}, f32[2,2,64,128]{3,2,1,0:T(8,128)S(1)}, f32[2,2,64,128]{3,2,1,0:T(...) custom-call(f32[3,2,64,128]{3,2,1,0:T(8,128)S(1)} %collective-permut, ...), custom_call_target="tpu_custom_call" | custom-call | flops 5898240 | bytes 10612736 | tf_op jit(solution)/shard_map/pallas_call | solution.py:531
  18.9 3.8 %collective-permute-start.5 = (f32[2,3,2,72,128]{4,3,2,1,0:T(8,128)S(1)}, f32[2,3,2,72,128]{4,3,2,1,0:T(8,128)S(1)}, u32[]{:S(2)}, u32[]{:S(2)}) collective-permute-start(f32[2,3,2,72,128]{4,3,2,1,0:T(8,128)S(1)} %get-tuple-element.65), channel_id=1, source_target_pairs={{0,1},{1,0},{2,3},{3,2},{4,5},{5,4},{6,7},{7,6},{8,9},{9,8},{10,11... | collective-permute-start | bytes 1327112 | tf_op jit(solution)/shard_map/ppermute | solution.py:551
  22.7 4.8 %collective-permute-start.4 = (f32[2,3,2,64,128]{4,3,2,1,0:T(8,128)}, f32[2,3,2,64,128]{4,3,2,1,0:T(8,128)}, u32[]{:S(2)}, u32[]{:S(2)}) collective-permute-start(f32[2,3,2,64,128]{4,3,2,1,0:T(8,128)} %get-tuple-element.57), channel_id=1, source_target_pairs={{0,15},{1,2},{2,1},{3,4},{4,3},{5,6},{6,5},{7,8},{8,7},{9,10},{10,... | collective-permute-start | bytes 1179656 | tf_op jit(solution)/shard_map/ppermute | solution.py:552
  27.5 0.0 collective-permute-done.5.of_core
  27.5 2.1 %shard_map.54 = (f32[2,5,2,80,128]{4,3,2,1,0:T(8,128)S(1)}, f32[2,1,2,80,128]{4,3,2,1,0:T(8,128)S(1)}, f32[2,3,2,80,128]{4,3,2,1,0:T(8,128)S(1)}, f32[2,3,2,64,1...) custom-call(f32[2,3,2,72,128]{4,3,2,1,0:T(8,128)S(1)} %collective-pe, ...), custom_call_target="tpu_custom_call" | custom-call | flops 7864320 | bytes 10510336 | tf_op jit(solution)/shard_map/pallas_call | solution.py:531
  29.6 0.0 copy-done.5
  29.6 0.9 %copy-done.7 = f32[2,5,2,80,128]{4,3,2,1,0:T(8,128)} copy-done((f32[2,5,2,80,128]{4,3,2,1,0:T(8,128)}, f32[2,5,2,80,128]{4,3,2,1,0:T(8,128)S(1)}, u32[]{:S(2)}) %copy-start.7) | copy-done | bytes 819224
  30.5 0.8 %copy-done.18 = f32[2,3,2,80,128]{4,3,2,1,0:T(8,128)} copy-done((f32[2,3,2,80,128]{4,3,2,1,0:T(8,128)}, f32[2,3,2,80,128]{4,3,2,1,0:T(8,128)S(1)}, u32[]{:S(2)}) %copy-start.18) | copy-done | bytes 491544
  31.3 0.7 %copy-done.20 = f32[2,3,2,64,128]{4,3,2,1,0:T(8,128)} copy-done((f32[2,3,2,64,128]{4,3,2,1,0:T(8,128)}, f32[2,3,2,64,128]{4,3,2,1,0:T(8,128)S(1)}, u32[]{:S(2)}) %copy-start.20) | copy-done | bytes 393240
  32.1 0.7 %copy-done.23 = f32[2,2,2,64,128]{4,3,2,1,0:T(8,128)} copy-done((f32[2,2,2,64,128]{4,3,2,1,0:T(8,128)}, f32[2,2,2,64,128]{4,3,2,1,0:T(8,128)S(1)}, u32[]{:S(2)}) %copy-start.23) | copy-done | bytes 262168
  32.8 0.7 %copy-done.25 = f32[2,1,2,80,128]{4,3,2,1,0:T(8,128)} copy-done((f32[2,1,2,80,128]{4,3,2,1,0:T(8,128)}, f32[2,1,2,80,128]{4,3,2,1,0:T(8,128)S(1)}, u32[]{:S(2)}) %copy-start.25) | copy-done | bytes 163864
  33.5 0.6 %copy-done.27 = f32[2,2,64,128]{3,2,1,0:T(8,128)} copy-done((f32[2,2,64,128]{3,2,1,0:T(8,128)}, f32[2,2,64,128]{3,2,1,0:T(8,128)S(1)}, u32[]{:S(2)}) %copy-start.27) | copy-done | bytes 131096
  34.1 0.7 %copy-done.29 = f32[2,2,64,128]{3,2,1,0:T(8,128)} copy-done((f32[2,2,64,128]{3,2,1,0:T(8,128)}, f32[2,2,64,128]{3,2,1,0:T(8,128)S(1)}, u32[]{:S(2)}) %copy-start.29) | copy-done | bytes 131096
  34.8 0.6 %copy-done.31 = f32[2,2,64,128]{3,2,1,0:T(8,128)} copy-done((f32[2,2,64,128]{3,2,1,0:T(8,128)}, f32[2,2,64,128]{3,2,1,0:T(8,128)S(1)}, u32[]{:S(2)}) %copy-start.31) | copy-done | bytes 131096
  35.4 0.7 %copy-done.33 = f32[2,2,64,128]{3,2,1,0:T(8,128)} copy-done((f32[2,2,64,128]{3,2,1,0:T(8,128)}, f32[2,2,64,128]{3,2,1,0:T(8,128)S(1)}, u32[]{:S(2)}) %copy-start.33) | copy-done | bytes 131096
  36.1 3.3 %all-to-all-start = ((f32[8,1,128]{2,1,0:T(1,128)}), f32[8,1,128]{2,1,0:T(1,128)S(1)}, u32[]{:S(2)}, u32[]{:S(2)}) async-start(f32[8,1,128]{2,1,0:T(1,128)} %get-tuple-element.77), calls=%async_computation | async-start | bytes 8192 | tf_op jit(solution)/shard_map/all_to_all | solution.py:614
  39.4 0.0 collective-permute-done.4.of_chip
  39.4 5.8 %all-to-all-done.shares = f32[8,1,128]{2,1,0:T(1,128)S(1)} async-done(((f32[8,1,128]{2,1,0:T(1,128)}), f32[8,1,128]{2,1,0:T(1,128)S(1)}, u32[]{:S(2)}, u32[]{:S(2)}) %all-to-all-start) | async-done | bytes 4128 | tf_op jit(solution)/shard_map/all_to_all | solution.py:614
  45.2 1.0 %copy-done.1 = f32[5,2,64,128]{3,2,1,0:T(8,128)S(1)} copy-done((f32[5,2,64,128]{3,2,1,0:T(8,128)S(1)}, f32[5,2,64,128]{3,2,1,0:T(8,128)}, u32[]{:S(2)}) %copy-start.1) | copy-done | bytes 327704
  46.2 1.0 %copy-done.4 = f32[2,3,2,80,128]{4,3,2,1,0:T(8,128)S(1)} copy-done((f32[2,3,2,80,128]{4,3,2,1,0:T(8,128)S(1)}, f32[2,3,2,80,128]{4,3,2,1,0:T(8,128)}, u32[]{:S(2)}) %copy-start.4) | copy-done | bytes 491544
  47.2 1.0 %copy-done.6 = f32[2,3,2,80,128]{4,3,2,1,0:T(8,128)S(1)} copy-done((f32[2,3,2,80,128]{4,3,2,1,0:T(8,128)S(1)}, f32[2,3,2,80,128]{4,3,2,1,0:T(8,128)}, u32[]{:S(2)}) %copy-start.6) | copy-done | bytes 491544
  48.3 1.1 %copy-done.8 = f32[2,5,2,80,128]{4,3,2,1,0:T(8,128)S(1)} copy-done((f32[2,5,2,80,128]{4,3,2,1,0:T(8,128)S(1)}, f32[2,5,2,80,128]{4,3,2,1,0:T(8,128)}, u32[]{:S(2)}) %copy-start.8) | copy-done | bytes 819224
  49.4 0.9 %copy-done.10 = f32[3,2,64,128]{3,2,1,0:T(8,128)S(1)} copy-done((f32[3,2,64,128]{3,2,1,0:T(8,128)S(1)}, f32[3,2,64,128]{3,2,1,0:T(8,128)}, u32[]{:S(2)}) %copy-start.10) | copy-done | bytes 196632
  50.3 0.9 %copy-done.12 = f32[2,2,80,128]{3,2,1,0:T(8,128)S(1)} copy-done((f32[2,2,80,128]{3,2,1,0:T(8,128)S(1)}, f32[2,2,80,128]{3,2,1,0:T(8,128)}, u32[]{:S(2)}) %copy-start.12) | copy-done | bytes 163864
  51.3 0.9 %copy-done.14 = f32[2,2,64,128]{3,2,1,0:T(8,128)S(1)} copy-done((f32[2,2,64,128]{3,2,1,0:T(8,128)S(1)}, f32[2,2,64,128]{3,2,1,0:T(8,128)}, u32[]{:S(2)}) %copy-start.14) | copy-done | bytes 131096
  52.2 0.9 %copy-done.16 = f32[2,2,64,128]{3,2,1,0:T(8,128)S(1)} copy-done((f32[2,2,64,128]{3,2,1,0:T(8,128)S(1)}, f32[2,2,64,128]{3,2,1,0:T(8,128)}, u32[]{:S(2)}) %copy-start.16) | copy-done | bytes 131096
  53.1 1.0 %copy-done.19 = f32[2,3,2,80,128]{4,3,2,1,0:T(8,128)S(1)} copy-done((f32[2,3,2,80,128]{4,3,2,1,0:T(8,128)S(1)}, f32[2,3,2,80,128]{4,3,2,1,0:T(8,128)}, u32[]{:S(2)}) %copy-start.19) | copy-done | bytes 491544
  54.1 1.0 %copy-done.21 = f32[2,3,2,64,128]{4,3,2,1,0:T(8,128)S(1)} copy-done((f32[2,3,2,64,128]{4,3,2,1,0:T(8,128)S(1)}, f32[2,3,2,64,128]{4,3,2,1,0:T(8,128)}, u32[]{:S(2)}) %copy-start.21) | copy-done | bytes 393240
  55.1 0.9 %copy-done.24 = f32[2,2,2,64,128]{4,3,2,1,0:T(8,128)S(1)} copy-done((f32[2,2,2,64,128]{4,3,2,1,0:T(8,128)S(1)}, f32[2,2,2,64,128]{4,3,2,1,0:T(8,128)}, u32[]{:S(2)}) %copy-start.24) | copy-done | bytes 262168
  56.1 0.9 %copy-done.26 = f32[2,1,2,80,128]{4,3,2,1,0:T(8,128)S(1)} copy-done((f32[2,1,2,80,128]{4,3,2,1,0:T(8,128)S(1)}, f32[2,1,2,80,128]{4,3,2,1,0:T(8,128)}, u32[]{:S(2)}) %copy-start.26) | copy-done | bytes 163864
  57.0 0.9 %copy-done.28 = f32[2,2,64,128]{3,2,1,0:T(8,128)S(1)} copy-done((f32[2,2,64,128]{3,2,1,0:T(8,128)S(1)}, f32[2,2,64,128]{3,2,1,0:T(8,128)}, u32[]{:S(2)}) %copy-start.28) | copy-done | bytes 131096
  57.9 0.9 %copy-done.30 = f32[2,2,64,128]{3,2,1,0:T(8,128)S(1)} copy-done((f32[2,2,64,128]{3,2,1,0:T(8,128)S(1)}, f32[2,2,64,128]{3,2,1,0:T(8,128)}, u32[]{:S(2)}) %copy-start.30) | copy-done | bytes 131096
  58.8 0.9 %copy-done.32 = f32[2,2,64,128]{3,2,1,0:T(8,128)S(1)} copy-done((f32[2,2,64,128]{3,2,1,0:T(8,128)S(1)}, f32[2,2,64,128]{3,2,1,0:T(8,128)}, u32[]{:S(2)}) %copy-start.32) | copy-done | bytes 131096
  59.7 0.9 %copy-done.34 = f32[2,2,64,128]{3,2,1,0:T(8,128)S(1)} copy-done((f32[2,2,64,128]{3,2,1,0:T(8,128)S(1)}, f32[2,2,64,128]{3,2,1,0:T(8,128)}, u32[]{:S(2)}) %copy-start.34) | copy-done | bytes 131096
  60.6 2.6 %shard_map.55 = (f32[4,64,256]{2,1,0:T(8,128)}, f32[1]{0:T(128)}) custom-call(f32[2,3,2,64,128]{4,3,2,1,0:T(8,128)} %collective-permute-done.4.of_chip, f32[6,2,64,128]{3,2,1,0:T(8,128)S(1)} %get-tuple-element.46.mx.mx_a, f32[6,2,80,128]{3,2,1,0:T(8,128)S(1)} %get-tuple-element.47.my.my_a, f32[6,2,64,128]{3,2,1,0:T(8,128)S(1)} %get-tuple-element.48.mz.mz_a, ...), custom_call_target="tpu_custom_call" | custom-call | flops 5898240 | bytes 8753156 | tf_op jit(solution)/shard_map/pallas_call | solution.py:531
  (42 shorter events, 0.1 us)
Async XLA Ops:
  0.6 9.8 %collective-permute-start.2 = (f32[2,4,64,256]{3,2,1,0:T(8,128)}, f32[2,4,64,256]{3,2,1,0:T(8,128)S(1)}, u32[]{:S(2)}, u32[]{:S(2)}) collective-permute-start(f32[2,4,64,256]{3,2,1,0:T(8,128)} %initial.1), channel_id=1, source_target_pairs={{0,1},{1,0},{2,3},{3,2},{4,5},{5,4},{6,7},{7,6},{8,9},{9,8},{10,11... | collective-permute-start | bytes 1572872 | tf_op jit(solution)/shard_map/ppermute | solution.py:551
  1.1 12.8 %collective-permute-start.1 = (f32[2,4,64,256]{3,2,1,0:T(8,128)}, f32[2,4,64,256]{3,2,1,0:T(8,128)S(1)}, u32[]{:S(2)}, u32[]{:S(2)}) collective-permute-start(f32[2,4,64,256]{3,2,1,0:T(8,128)} %initial.1), channel_id=1, source_target_pairs={{0,15},{1,2},{2,1},{3,4},{4,3},{5,6},{6,5},{7,8},{8,7},{9,10},{10,... | collective-permute-start | bytes 1572872 | tf_op jit(solution)/shard_map/ppermute | solution.py:552
  6.8 1.1 %copy-start.17 = (f32[2,4,64,256]{3,2,1,0:T(8,128)S(1)}, f32[2,4,64,256]{3,2,1,0:T(8,128)}, u32[]{:S(2)}) copy-start(f32[2,4,64,256]{3,2,1,0:T(8,128)} %initial.1) | copy-start | bytes 1572868
  7.9 0.9 %copy-start.22 = (f32[4,64,256]{2,1,0:T(8,128)S(1)}, f32[4,64,256]{2,1,0:T(8,128)}, u32[]{:S(2)}) copy-start(f32[4,64,256]{2,1,0:T(8,128)} %mobility.1) | copy-start | bytes 786436
  8.9 1.5 %collective-permute-start.3 = (f32[3,2,64,128]{3,2,1,0:T(8,128)S(1)}, f32[3,2,64,128]{3,2,1,0:T(8,128)S(1)}, u32[]{:S(2)}, u32[]{:S(2)}) collective-permute-start(f32[3,2,64,128]{3,2,1,0:T(8,128)S(1)} %get-tuple-element.43), channel_id=1, source_target_pairs={{0,1},{1,0},{2,3},{3,2},{4,5},{5,4},{6,7},{7,6},{8,9},{9,8},{10,11... | collective-permute-start | bytes 589832 | tf_op jit(solution)/shard_map/ppermute | solution.py:551
  9.0 8.0 %collective-permute-start = (f32[3,2,64,128]{3,2,1,0:T(8,128)S(1)}, f32[3,2,64,128]{3,2,1,0:T(8,128)S(1)}, u32[]{:S(2)}, u32[]{:S(2)}) collective-permute-start(f32[3,2,64,128]{3,2,1,0:T(8,128)S(1)} %get-tuple-element.40), channel_id=1, source_target_pairs={{0,15},{1,2},{2,1},{3,4},{4,3},{5,6},{6,5},{7,8},{8,7},{9,10},{10,... | collective-permute-start | bytes 589832 | tf_op jit(solution)/shard_map/ppermute | solution.py:552
  10.4 3.6 %copy-start.2 = (f32[2,4,64,256]{3,2,1,0:T(8,128)S(1)}, f32[2,4,64,256]{3,2,1,0:T(8,128)}, u32[]{:S(2)}) copy-start(f32[2,4,64,256]{3,2,1,0:T(8,128)} %observed.3) | copy-start | bytes 1572868
  11.3 16.2 %copy-start = (f32[5,2,64,128]{3,2,1,0:T(8,128)}, f32[5,2,64,128]{3,2,1,0:T(8,128)S(1)}, u32[]{:S(2)}) copy-start(f32[5,2,64,128]{3,2,1,0:T(8,128)S(1)} %get-tuple-element.50.m_all.all_a) | copy-start | bytes 983044
  18.8 10.8 %copy-start.3 = (f32[2,3,2,80,128]{4,3,2,1,0:T(8,128)}, f32[2,3,2,80,128]{4,3,2,1,0:T(8,128)S(1)}, u32[]{:S(2)}) copy-start(f32[2,3,2,80,128]{4,3,2,1,0:T(8,128)S(1)} %get-tuple-element.63.chem1_b) | copy-start | bytes 1474564
  18.8 10.8 %copy-start.5 = (f32[2,3,2,80,128]{4,3,2,1,0:T(8,128)}, f32[2,3,2,80,128]{4,3,2,1,0:T(8,128)S(1)}, u32[]{:S(2)}) copy-start(f32[2,3,2,80,128]{4,3,2,1,0:T(8,128)S(1)} %get-tuple-element.64.adjoint2_b) | copy-start | bytes 1474564
  18.8 10.8 %copy-start.9 = (f32[3,2,64,128]{3,2,1,0:T(8,128)}, f32[3,2,64,128]{3,2,1,0:T(8,128)S(1)}, u32[]{:S(2)}) copy-start(f32[3,2,64,128]{3,2,1,0:T(8,128)S(1)} %get-tuple-element.62.all_b) | copy-start | bytes 589828
  18.9 10.8 %copy-start.11 = (f32[2,2,80,128]{3,2,1,0:T(8,128)}, f32[2,2,80,128]{3,2,1,0:T(8,128)S(1)}, u32[]{:S(2)}) copy-start(f32[2,2,80,128]{3,2,1,0:T(8,128)S(1)} %get-tuple-element.59.my_b) | copy-start | bytes 491524
  18.9 10.8 %copy-start.13 = (f32[2,2,64,128]{3,2,1,0:T(8,128)}, f32[2,2,64,128]{3,2,1,0:T(8,128)S(1)}, u32[]{:S(2)}) copy-start(f32[2,2,64,128]{3,2,1,0:T(8,128)S(1)} %get-tuple-element.60.mz_b) | copy-start | bytes 393220
  18.9 10.8 %copy-start.15 = (f32[2,2,64,128]{3,2,1,0:T(8,128)}, f32[2,2,64,128]{3,2,1,0:T(8,128)S(1)}, u32[]{:S(2)}) copy-start(f32[2,2,64,128]{3,2,1,0:T(8,128)S(1)} %get-tuple-element.61.mz_low_b) | copy-start | bytes 393220
  18.9 8.6 %collective-permute-start.5 = (f32[2,3,2,72,128]{4,3,2,1,0:T(8,128)S(1)}, f32[2,3,2,72,128]{4,3,2,1,0:T(8,128)S(1)}, u32[]{:S(2)}, u32[]{:S(2)}) collective-permute-start(f32[2,3,2,72,128]{4,3,2,1,0:T(8,128)S(1)} %get-tuple-element.65), channel_id=1, source_target_pairs={{0,1},{1,0},{2,3},{3,2},{4,5},{5,4},{6,7},{7,6},{8,9},{9,8},{10,11... | collective-permute-start | bytes 1327112 | tf_op jit(solution)/shard_map/ppermute | solution.py:551
  22.7 16.7 %collective-permute-start.4 = (f32[2,3,2,64,128]{4,3,2,1,0:T(8,128)}, f32[2,3,2,64,128]{4,3,2,1,0:T(8,128)}, u32[]{:S(2)}, u32[]{:S(2)}) collective-permute-start(f32[2,3,2,64,128]{4,3,2,1,0:T(8,128)} %get-tuple-element.57), channel_id=1, source_target_pairs={{0,15},{1,2},{2,1},{3,4},{4,3},{5,6},{6,5},{7,8},{8,7},{9,10},{10,... | collective-permute-start | bytes 1179656 | tf_op jit(solution)/shard_map/ppermute | solution.py:552
  29.6 0.9 %copy-start.7 = (f32[2,5,2,80,128]{4,3,2,1,0:T(8,128)}, f32[2,5,2,80,128]{4,3,2,1,0:T(8,128)S(1)}, u32[]{:S(2)}) copy-start(f32[2,5,2,80,128]{4,3,2,1,0:T(8,128)S(1)} %get-tuple-element.68.flow_a) | copy-start | bytes 2457604
  30.5 0.8 %copy-start.18 = (f32[2,3,2,80,128]{4,3,2,1,0:T(8,128)}, f32[2,3,2,80,128]{4,3,2,1,0:T(8,128)S(1)}, u32[]{:S(2)}) copy-start(f32[2,3,2,80,128]{4,3,2,1,0:T(8,128)S(1)} %get-tuple-element.70.adjoint1_a) | copy-start | bytes 1474564
  31.3 0.7 %copy-start.20 = (f32[2,3,2,64,128]{4,3,2,1,0:T(8,128)}, f32[2,3,2,64,128]{4,3,2,1,0:T(8,128)S(1)}, u32[]{:S(2)}) copy-start(f32[2,3,2,64,128]{4,3,2,1,0:T(8,128)S(1)} %get-tuple-element.71.weight_b) | copy-start | bytes 1179652
  32.1 0.7 %copy-start.23 = (f32[2,2,2,64,128]{4,3,2,1,0:T(8,128)}, f32[2,2,2,64,128]{4,3,2,1,0:T(8,128)S(1)}, u32[]{:S(2)}) copy-start(f32[2,2,2,64,128]{4,3,2,1,0:T(8,128)S(1)} %get-tuple-element.72.step_z_b) | copy-start | bytes 786436
  32.8 0.7 %copy-start.25 = (f32[2,1,2,80,128]{4,3,2,1,0:T(8,128)}, f32[2,1,2,80,128]{4,3,2,1,0:T(8,128)S(1)}, u32[]{:S(2)}) copy-start(f32[2,1,2,80,128]{4,3,2,1,0:T(8,128)S(1)} %get-tuple-element.69.flow_part) | copy-start | bytes 491524
  33.5 0.7 %copy-start.27 = (f32[2,2,64,128]{3,2,1,0:T(8,128)}, f32[2,2,64,128]{3,2,1,0:T(8,128)S(1)}, u32[]{:S(2)}) copy-start(f32[2,2,64,128]{3,2,1,0:T(8,128)S(1)} %get-tuple-element.73.part) | copy-start | bytes 393220
  34.1 0.7 %copy-start.29 = (f32[2,2,64,128]{3,2,1,0:T(8,128)}, f32[2,2,64,128]{3,2,1,0:T(8,128)S(1)}, u32[]{:S(2)}) copy-start(f32[2,2,64,128]{3,2,1,0:T(8,128)S(1)} %get-tuple-element.74.sum_x_b) | copy-start | bytes 393220
  34.8 0.7 %copy-start.31 = (f32[2,2,64,128]{3,2,1,0:T(8,128)}, f32[2,2,64,128]{3,2,1,0:T(8,128)S(1)}, u32[]{:S(2)}) copy-start(f32[2,2,64,128]{3,2,1,0:T(8,128)S(1)} %get-tuple-element.75.sum_y_b) | copy-start | bytes 393220
  35.4 0.7 %copy-start.33 = (f32[2,2,64,128]{3,2,1,0:T(8,128)}, f32[2,2,64,128]{3,2,1,0:T(8,128)S(1)}, u32[]{:S(2)}) copy-start(f32[2,2,64,128]{3,2,1,0:T(8,128)S(1)} %get-tuple-element.76.sum_z_b) | copy-start | bytes 393220
  36.1 9.2 %all-to-all-start = ((f32[8,1,128]{2,1,0:T(1,128)}), f32[8,1,128]{2,1,0:T(1,128)S(1)}, u32[]{:S(2)}, u32[]{:S(2)}) async-start(f32[8,1,128]{2,1,0:T(1,128)} %get-tuple-element.77), calls=%async_computation | async-start | bytes 8192 | tf_op jit(solution)/shard_map/all_to_all | solution.py:614
  45.2 1.0 %copy-start.1 = (f32[5,2,64,128]{3,2,1,0:T(8,128)S(1)}, f32[5,2,64,128]{3,2,1,0:T(8,128)}, u32[]{:S(2)}) copy-start(f32[5,2,64,128]{3,2,1,0:T(8,128)} %copy-done) | copy-start | bytes 983044
  46.2 1.0 %copy-start.4 = (f32[2,3,2,80,128]{4,3,2,1,0:T(8,128)S(1)}, f32[2,3,2,80,128]{4,3,2,1,0:T(8,128)}, u32[]{:S(2)}) copy-start(f32[2,3,2,80,128]{4,3,2,1,0:T(8,128)} %copy-done.3) | copy-start | bytes 1474564
  47.2 1.0 %copy-start.6 = (f32[2,3,2,80,128]{4,3,2,1,0:T(8,128)S(1)}, f32[2,3,2,80,128]{4,3,2,1,0:T(8,128)}, u32[]{:S(2)}) copy-start(f32[2,3,2,80,128]{4,3,2,1,0:T(8,128)} %copy-done.5) | copy-start | bytes 1474564
  48.3 1.1 %copy-start.8 = (f32[2,5,2,80,128]{4,3,2,1,0:T(8,128)S(1)}, f32[2,5,2,80,128]{4,3,2,1,0:T(8,128)}, u32[]{:S(2)}) copy-start(f32[2,5,2,80,128]{4,3,2,1,0:T(8,128)} %copy-done.7) | copy-start | bytes 2457604
  49.4 0.9 %copy-start.10 = (f32[3,2,64,128]{3,2,1,0:T(8,128)S(1)}, f32[3,2,64,128]{3,2,1,0:T(8,128)}, u32[]{:S(2)}) copy-start(f32[3,2,64,128]{3,2,1,0:T(8,128)} %copy-done.9) | copy-start | bytes 589828
  50.3 0.9 %copy-start.12 = (f32[2,2,80,128]{3,2,1,0:T(8,128)S(1)}, f32[2,2,80,128]{3,2,1,0:T(8,128)}, u32[]{:S(2)}) copy-start(f32[2,2,80,128]{3,2,1,0:T(8,128)} %copy-done.11) | copy-start | bytes 491524
  51.3 0.9 %copy-start.14 = (f32[2,2,64,128]{3,2,1,0:T(8,128)S(1)}, f32[2,2,64,128]{3,2,1,0:T(8,128)}, u32[]{:S(2)}) copy-start(f32[2,2,64,128]{3,2,1,0:T(8,128)} %copy-done.13) | copy-start | bytes 393220
  52.2 0.9 %copy-start.16 = (f32[2,2,64,128]{3,2,1,0:T(8,128)S(1)}, f32[2,2,64,128]{3,2,1,0:T(8,128)}, u32[]{:S(2)}) copy-start(f32[2,2,64,128]{3,2,1,0:T(8,128)} %copy-done.15) | copy-start | bytes 393220
  53.1 1.0 %copy-start.19 = (f32[2,3,2,80,128]{4,3,2,1,0:T(8,128)S(1)}, f32[2,3,2,80,128]{4,3,2,1,0:T(8,128)}, u32[]{:S(2)}) copy-start(f32[2,3,2,80,128]{4,3,2,1,0:T(8,128)} %copy-done.18) | copy-start | bytes 1474564
  54.1 1.0 %copy-start.21 = (f32[2,3,2,64,128]{4,3,2,1,0:T(8,128)S(1)}, f32[2,3,2,64,128]{4,3,2,1,0:T(8,128)}, u32[]{:S(2)}) copy-start(f32[2,3,2,64,128]{4,3,2,1,0:T(8,128)} %copy-done.20) | copy-start | bytes 1179652
  55.1 0.9 %copy-start.24 = (f32[2,2,2,64,128]{4,3,2,1,0:T(8,128)S(1)}, f32[2,2,2,64,128]{4,3,2,1,0:T(8,128)}, u32[]{:S(2)}) copy-start(f32[2,2,2,64,128]{4,3,2,1,0:T(8,128)} %copy-done.23) | copy-start | bytes 786436
  56.0 0.9 %copy-start.26 = (f32[2,1,2,80,128]{4,3,2,1,0:T(8,128)S(1)}, f32[2,1,2,80,128]{4,3,2,1,0:T(8,128)}, u32[]{:S(2)}) copy-start(f32[2,1,2,80,128]{4,3,2,1,0:T(8,128)} %copy-done.25) | copy-start | bytes 491524
  57.0 0.9 %copy-start.28 = (f32[2,2,64,128]{3,2,1,0:T(8,128)S(1)}, f32[2,2,64,128]{3,2,1,0:T(8,128)}, u32[]{:S(2)}) copy-start(f32[2,2,64,128]{3,2,1,0:T(8,128)} %copy-done.27) | copy-start | bytes 393220
  57.9 0.9 %copy-start.30 = (f32[2,2,64,128]{3,2,1,0:T(8,128)S(1)}, f32[2,2,64,128]{3,2,1,0:T(8,128)}, u32[]{:S(2)}) copy-start(f32[2,2,64,128]{3,2,1,0:T(8,128)} %copy-done.29) | copy-start | bytes 393220
  58.8 0.9 %copy-start.32 = (f32[2,2,64,128]{3,2,1,0:T(8,128)S(1)}, f32[2,2,64,128]{3,2,1,0:T(8,128)}, u32[]{:S(2)}) copy-start(f32[2,2,64,128]{3,2,1,0:T(8,128)} %copy-done.31) | copy-start | bytes 393220
  59.7 0.9 %copy-start.34 = (f32[2,2,64,128]{3,2,1,0:T(8,128)S(1)}, f32[2,2,64,128]{3,2,1,0:T(8,128)}, u32[]{:S(2)}) copy-start(f32[2,2,64,128]{3,2,1,0:T(8,128)} %copy-done.33) | copy-start | bytes 393220

commit v11 on v9

--- a/solution.py
+++ b/solution.py
@@ -451,9 +451,8 @@
 def late_kernel(
     of_chip, mx_a, my_a, mz_a, mz_low_a, all_a, mx_b, my_b, mz_b, mz_low_b, all_b,
     chem0_a, chem0_b, chem1_b, adjoint2_b, flow_a, flow_part, adjoint1_a, weight_b, step_z_b,
-    part, sum_x_b, sum_y_b, sum_z_b, share, far, result, misfit, rim, flow_b, adjoint1_b, sum_x, sum_y, sum_z,
+    part, sum_x_b, sum_y_b, sum_z_b, result, rim, flow_b, adjoint1_b, sum_x, sum_y, sum_z,
 ):
-    misfit[0] = (share[...] + far[...])[0, 0]
     runs = of_chip.shape[0]
     n, ny, _ = result.shape
     faces = Faces(n, (mx_a, my_a, mz_a, mz_low_a, all_a, mx_b, my_b, mz_b, mz_low_b, all_b))
@@ -524,6 +523,14 @@
             put_plain(result, (place[n - 2 + at],), row, value)
 
 
+def counts(at):
+    return (at ^ (at >> 1)) & 1
+
+
+def misfit_kernel(total, handed, misfit):
+    misfit[0] = jnp.where(counts(lax.axis_index("gx")) == 1, total[0, 0], handed[0, 0])
+
+
 def call(kernel, outs, scratch, args, flops, scalar=None):
     moved = 4 * (sum(a.size for a in args) + sum(math.prod(o) for o in outs))
     return pl.pallas_call(
@@ -600,16 +607,12 @@
     of_chip, of_core = neighbours(to_chip, to_core)
     bits = range(count.bit_length() - 2)
 
-    def target(at, step):
-        apart = (at ^ at >> 1) & 1
-        bit = bits[-1 - step] if apart else bits[step]
-        return at ^ (3 if bit == 0 else 2 << bit)
-
-    def hop(value, step):
-        return lax.ppermute(value, "gx", [(at, target(at, step)) for at in range(count)])
+    def hop(value, bit):
+        apart = 3 if bit == 0 else 2 << bit
+        return lax.ppermute(value, "gx", [(at, at ^ apart) for at in range(count) if counts(at)])
 
     share = share + of_core[0, 0, 0, ny:]
-    far = hop(share, 0)
+    far = hop(share, bits[-1])
     flow_a, flow_part, adjoint1_a, weight_b, step_z_b, part, *sums_b, share = call(
         early_kernel,
         (
@@ -620,23 +623,26 @@
         (of_core, *faces, chem0_a, chem0_b, state1_a, state1_b, chem1_a, chem1_b, adjoint2_a, adjoint2_b, share),
         60 * runs * n * cell,
     )
-    for step in bits[1:]:
+    for bit in bits[-2::-1]:
         share = share + far
-        far = hop(share, step)
-    return call(
+        far = hop(share, bit)
+    share = share + far
+    handed = lax.ppermute(share, "gx", over_cores)
+    (result,) = call(
         late_kernel,
-        ((n, ny, nz), (1,)),
+        ((n, ny, nz),),
         (
             lies_padded(runs, 3), lies_padded(runs, 3), lies_padded(runs, 3),
             lies(3), lies_padded(2), lies(2),
         ),
         (
             of_chip, *faces, chem0_a, chem0_b, chem1_b, adjoint2_b, flow_a, flow_part, adjoint1_a,
-            weight_b, step_z_b, part, *sums_b, share, far,
+            weight_b, step_z_b, part, *sums_b,
         ),
         60 * runs * 3 * cell,
-        scalar=1,
-    )
+    )
+    (misfit,) = call(misfit_kernel, ((1,),), (), (share, handed), 1, scalar=0)
+    return (result, misfit)
 
 
 def solution(mesh):

time: 42.6 us -> 43.6 us (1.023)
  starting transfers between devices: 16.4 us -> 27.6 us
  waiting for transfers between devices: 16.1 us -> 5.16 us
  Pallas kernels: 7.2 us -> 7.74 us
    ppermute x3 -> x4, starting transfers between devices: 0.93 us -> 12.2 us  [the longest x1 10.2 us: on_device(): handed = lax.ppermute(share, 'gx', over_cores)]
    ppermute x3 -> x4, waiting for transfers between devices: 10.9 us -> 0.01 us  [the longest x3 0.01 us: hop(): lax.ppermute(value, 'gx', [(at, at ^ apart) for at in range(count) if cou...]
    pallas_call x6 -> x7, Pallas kernels: 7.2 us -> 7.74 us  [call(): pl.pallas_call(kernel, out_shape=tuple((jax.ShapeDtypeStruct(o, jnp.float...]
  transfers between devices with their start and end apart: 9 -> 10, of which waited for: 6 -> 3; matrix products, arithmetic and copies ran while one was open for 0% -> 0% of each run, Pallas kernels for 10% -> 14%
where the time goes in v11:
time: 43.6 us; the launch traced here: 43.3 us
  starting transfers between devices  27.6 us (63%)
  Pallas kernels  7.74 us (18%)
  waiting for transfers between devices  5.16 us (12%)
  local copies, waits for them, and re-layouts  2.03 us (5%)
  between operations  0.75 us (2%)
    ppermute x3, starting transfers between devices, neighbours(): return (lax.ppermute(to_chip, 'gx', over_chips), of_core)  11.1 us
    ppermute x1, starting transfers between devices, on_device(): handed = lax.ppermute(share, 'gx', over_cores)  10.2 us
    pallas_call x7, Pallas kernels, call(): pl.pallas_call(kernel, out_shape=tuple((jax.ShapeDtypeStruct(o, jnp.float...  7.74 us
    ppermute x3, starting transfers between devices, neighbours(): of_core = lax.ppermute(to_core, 'gx', over_cores)  4.37 us
    ppermute x3, waiting for transfers between devices, neighbours(): return (lax.ppermute(to_chip, 'gx', over_chips), of_core)  4.32 us
    unnamed x6, local copies, waits for them, and re-layouts  2.03 us
    ppermute x3, starting transfers between devices, hop(): lax.ppermute(value, 'gx', [(at, at ^ apart) for at in range(count) if cou...  1.97 us
  transfers between devices with their start and end apart: 10, of which 3 were waited for; matrix products, arithmetic and copies ran while one was open for 0% of the time, Pallas kernels for 14%

profile of v11, /device:TPU:0, one launch (start us, length us, event | category | flops | bytes accessed | tf_op | source)
XLA Modules:
  0.0 43.3 jit_solution(8097061679017370110)
XLA Ops:
  0.6 0.5 %collective-permute-start.2 = (f32[2,4,64,256]{3,2,1,0:T(8,128)}, f32[2,4,64,256]{3,2,1,0:T(8,128)S(1)}, u32[]{:S(2)}, u32[]{:S(2)}) collective-permute-start(f32[2,4,64,256]{3,2,1,0:T(8,128)} %initial.1), channel_id=1, source_target_pairs={{0,1},{1,0},{2,3},{3,2},{4,5},{5,4},{6,7},{7,6},{8,9},{9,8},{10,11... | collective-permute-start | bytes 1572872 | tf_op jit(solution)/shard_map/ppermute | solution.py:556
  1.1 5.7 %collective-permute-start.1 = (f32[2,4,64,256]{3,2,1,0:T(8,128)}, f32[2,4,64,256]{3,2,1,0:T(8,128)S(1)}, u32[]{:S(2)}, u32[]{:S(2)}) collective-permute-start(f32[2,4,64,256]{3,2,1,0:T(8,128)} %initial.1), channel_id=1, source_target_pairs={{0,15},{1,2},{2,1},{3,4},{4,3},{5,6},{6,5},{7,8},{8,7},{9,10},{10,... | collective-permute-start | bytes 1572872 | tf_op jit(solution)/shard_map/ppermute | solution.py:557
  6.8 0.0 copy-start.1
  6.8 1.1 %copy-done.1 = f32[2,4,64,256]{3,2,1,0:T(8,128)S(1)} copy-done((f32[2,4,64,256]{3,2,1,0:T(8,128)S(1)}, f32[2,4,64,256]{3,2,1,0:T(8,128)}, u32[]{:S(2)}) %copy-start.1) | copy-done | bytes 524312
  7.9 0.0 copy-start.2
  7.9 0.9 %copy-done.2 = f32[4,64,256]{2,1,0:T(8,128)S(1)} copy-done((f32[4,64,256]{2,1,0:T(8,128)S(1)}, f32[4,64,256]{2,1,0:T(8,128)}, u32[]{:S(2)}) %copy-start.2) | copy-done | bytes 262168
  8.8 0.1 shard_map.50
  8.9 0.1 collective-permute-start.3
  9.0 0.6 %collective-permute-start = (f32[3,2,64,128]{3,2,1,0:T(8,128)S(1)}, f32[3,2,64,128]{3,2,1,0:T(8,128)S(1)}, u32[]{:S(2)}, u32[]{:S(2)}) collective-permute-start(f32[3,2,64,128]{3,2,1,0:T(8,128)S(1)} %get-tuple-element.40), channel_id=1, source_target_pairs={{0,15},{1,2},{2,1},{3,4},{4,3},{5,6},{6,5},{7,8},{8,7},{9,10},{10,... | collective-permute-start | bytes 589832 | tf_op jit(solution)/shard_map/ppermute | solution.py:557
  9.6 0.8 %collective-permute-done.3.m_core = f32[3,2,64,128]{3,2,1,0:T(8,128)S(1)} collective-permute-done((f32[3,2,64,128]{3,2,1,0:T(8,128)S(1)}, f32[3,2,64,128]{3,2,1,0:T(8,128)S(1)}, u32[]{:S(2)}, u32[]{:S(2)}) %collective-permute-start.3) | collective-permute-done | bytes 196640 | tf_op jit(solution)/shard_map/ppermute | solution.py:556
  10.4 0.0 collective-permute-done.2.of_core
  10.4 0.0 copy-start
  10.5 0.9 %shard_map.51 = (f32[2,4,2,80,128]{4,3,2,1,0:T(8,128)S(1)}, f32[2,6,2,80,128]{4,3,2,1,0:T(8,128)S(1)}, f32[6,2,64,128]{3,2,1,0:T(8,128)S(1)}, f32[6,2,80,128]{3,...) custom-call(f32[2,4,64,256]{3,2,1,0:T(8,128)S(1)} %collective-permut, ...), custom_call_target="tpu_custom_call" | custom-call | flops 3932160 | bytes 5341184 | tf_op jit(solution)/shard_map/pallas_call | solution.py:536
  11.3 2.7 %collective-permute-done.1.of_chip = f32[2,4,64,256]{3,2,1,0:T(8,128)S(1)} collective-permute-done((f32[2,4,64,256]{3,2,1,0:T(8,128)}, f32[2,4,64,256]{3,2,1,0:T(8,128)S(1)}, u32[]{:S(2)}, u32[]{:S(2)}) %collective-permute-start.1) | collective-permute-done | bytes 524320 | tf_op jit(solution)/shard_map/ppermute | solution.py:557
  14.0 0.0 copy-done
  14.0 1.3 %shard_map.52 = (f32[2,4,2,80,128]{4,3,2,1,0:T(8,128)S(1)}, f32[2,4,2,80,128]{4,3,2,1,0:T(8,128)S(1)}, f32[2,5,2,80,128]{4,3,2,1,0:T(8,128)S(1)}, f32[2,3,2,80,1...) custom-call(f32[2,4,64,256]{3,2,1,0:T(8,128)S(1)} %collective-permute-done.1.of_chip, ...), custom_call_target="tpu_custom_call" | custom-call | flops 5898240 | bytes 8134656 | tf_op jit(solution)/shard_map/pallas_call | solution.py:536
  15.3 1.7 %collective-permute-done.m_chip = f32[3,2,64,128]{3,2,1,0:T(8,128)S(1)} collective-permute-done((f32[3,2,64,128]{3,2,1,0:T(8,128)S(1)}, f32[3,2,64,128]{3,2,1,0:T(8,128)S(1)}, u32[]{:S(2)}, u32[]{:S(2)}) %collective-permute-start) | collective-permute-done | bytes 196640 | tf_op jit(solution)/shard_map/ppermute | solution.py:557
  17.0 1.3 %shard_map.53 = (f32[3,2,64,128]{3,2,1,0:T(8,128)S(1)}, f32[2,2,80,128]{3,2,1,0:T(8,128)S(1)}, f32[2,2,64,128]{3,2,1,0:T(8,128)S(1)}, f32[2,2,64,128]{3,2,1,0:T(...) custom-call(f32[3,2,64,128]{3,2,1,0:T(8,128)S(1)} %collective-permut, ...), custom_call_target="tpu_custom_call" | custom-call | flops 5898240 | bytes 10612736 | tf_op jit(solution)/shard_map/pallas_call | solution.py:536
  18.3 3.8 %collective-permute-start.5 = (f32[2,3,2,72,128]{4,3,2,1,0:T(8,128)S(1)}, f32[2,3,2,72,128]{4,3,2,1,0:T(8,128)S(1)}, u32[]{:S(2)}, u32[]{:S(2)}) collective-permute-start(f32[2,3,2,72,128]{4,3,2,1,0:T(8,128)S(1)} %get-tuple-element.65), channel_id=1, source_target_pairs={{0,1},{1,0},{2,3},{3,2},{4,5},{5,4},{6,7},{7,6},{8,9},{9,8},{10,11... | collective-permute-start | bytes 1327112 | tf_op jit(solution)/shard_map/ppermute | solution.py:556
  22.1 4.8 %collective-permute-start.4 = (f32[2,3,2,64,128]{4,3,2,1,0:T(8,128)S(1)}, f32[2,3,2,64,128]{4,3,2,1,0:T(8,128)S(1)}, u32[]{:S(2)}, u32[]{:S(2)}) collective-permute-start(f32[2,3,2,64,128]{4,3,2,1,0:T(8,128)S(1)} %get-tuple-element.57), channel_id=1, source_target_pairs={{0,15},{1,2},{2,1},{3,4},{4,3},{5,6},{6,5},{7,8},{8,7},{9,10},{10,... | collective-permute-start | bytes 1179656 | tf_op jit(solution)/shard_map/ppermute | solution.py:557
  26.8 0.0 collective-permute-done.5.of_core
  26.8 0.7 %collective-permute-start.6 = (f32[8,128]{1,0:T(8,128)S(1)}, f32[8,128]{1,0:T(8,128)S(1)}, u32[]{:S(2)}, u32[]{:S(2)}) collective-permute-start(f32[8,128]{1,0:T(8,128)S(1)} %fusion.share_in), channel_id=1, source_target_pairs={{1,9},{2,10},{5,13},{6,14},{9,1},{10,2},{13,5},{14,6},{17,25},{18,... | collective-permute-start | bytes 12296 | tf_op jit(solution)/shard_map/ppermute | solution.py:612
  27.5 2.0 %shard_map.54 = (f32[2,5,2,80,128]{4,3,2,1,0:T(8,128)S(1)}, f32[2,1,2,80,128]{4,3,2,1,0:T(8,128)S(1)}, f32[2,3,2,80,128]{4,3,2,1,0:T(8,128)S(1)}, f32[2,3,2,64,1...) custom-call(f32[2,3,2,72,128]{4,3,2,1,0:T(8,128)S(1)} %collective-pe, ...), custom_call_target="tpu_custom_call" | custom-call | flops 7864320 | bytes 10510336 | tf_op jit(solution)/shard_map/pallas_call | solution.py:536
  29.5 0.0 collective-permute-done.6
  29.5 0.7 %collective-permute-start.7 = (f32[8,128]{1,0:T(8,128)S(1)}, f32[8,128]{1,0:T(8,128)S(1)}, u32[]{:S(2)}, u32[]{:S(2)}) collective-permute-start(f32[8,128]{1,0:T(8,128)S(1)} %add.13), channel_id=1, source_target_pairs={{1,5},{2,6},{5,1},{6,2},{9,13},{10,14},{13,9},{14,10},{17,21},{18,... | collective-permute-start | bytes 12296 | tf_op jit(solution)/shard_map/ppermute | solution.py:612
  30.2 0.0 collective-permute-done.7
  30.2 0.7 %collective-permute-start.8 = (f32[8,128]{1,0:T(8,128)S(1)}, f32[8,128]{1,0:T(8,128)S(1)}, u32[]{:S(2)}, u32[]{:S(2)}) collective-permute-start(f32[8,128]{1,0:T(8,128)S(1)} %add.14), channel_id=1, source_target_pairs={{1,2},{2,1},{5,6},{6,5},{9,10},{10,9},{13,14},{14,13},{17,18},{18,... | collective-permute-start | bytes 12296 | tf_op jit(solution)/shard_map/ppermute | solution.py:612
  30.9 0.0 collective-permute-done.8
  30.9 10.2 %collective-permute-start.9 = (f32[8,128]{1,0:T(8,128)S(1)}, f32[8,128]{1,0:T(8,128)S(1)}, u32[]{:S(2)}, u32[]{:S(2)}) collective-permute-start(f32[8,128]{1,0:T(8,128)S(1)} %add.15.total), channel_id=1, source_target_pairs={{0,1},{1,0},{2,3},{3,2},{4,5},{5,4},{6,7},{7,6},{8,9},{9,8},{10,11... | collective-permute-start | bytes 12296 | tf_op jit(solution)/shard_map/ppermute | solution.py:630
  41.1 0.0 collective-permute-done.4.of_chip
  41.1 1.7 %shard_map.55 = f32[4,64,256]{2,1,0:T(8,128)} custom-call(f32[2,3,2,64,128]{4,3,2,1,0:T(8,128)S(1)} %collective-permute-done.4.of_chip, f32[6,2,64,128]{3,2,1,0:T(8,128)S(1)} %get-tuple-element.46.mx.mx_a, f32[6,2,80,128]{3,2,1,0:T(8,128)S(1)} %get-tuple-element.47.my.my_a, f32[6,2,64,128]{3,2,1,0:T(8,128)S(1)} %get-tuple-element.48.mz.mz_a, ...), custom_call_target="tpu_custom_call" | custom-call | flops 5898240 | bytes 8749056 | tf_op jit(solution)/shard_map/pallas_call | solution.py:536
  42.8 0.0 collective-permute-done.9.handed
  42.8 0.6 %shard_map.56 = f32[1]{0:T(128)} custom-call(f32[8,128]{1,0:T(8,128)S(1)} %add.15.total, f32[8,128]{1,0:T(8,128)S(1)} %collective-permute-done.9.handed), custom_call_target="tpu_custom_call" | custom-call | flops 1 | bytes 8196 | tf_op jit(solution)/shard_map/pallas_call | solution.py:536
  (4 shorter events, 0.0 us)
Async XLA Ops:
  0.6 9.8 %collective-permute-start.2 = (f32[2,4,64,256]{3,2,1,0:T(8,128)}, f32[2,4,64,256]{3,2,1,0:T(8,128)S(1)}, u32[]{:S(2)}, u32[]{:S(2)}) collective-permute-start(f32[2,4,64,256]{3,2,1,0:T(8,128)} %initial.1), channel_id=1, source_target_pairs={{0,1},{1,0},{2,3},{3,2},{4,5},{5,4},{6,7},{7,6},{8,9},{9,8},{10,11... | collective-permute-start | bytes 1572872 | tf_op jit(solution)/shard_map/ppermute | solution.py:556
  1.1 12.8 %collective-permute-start.1 = (f32[2,4,64,256]{3,2,1,0:T(8,128)}, f32[2,4,64,256]{3,2,1,0:T(8,128)S(1)}, u32[]{:S(2)}, u32[]{:S(2)}) collective-permute-start(f32[2,4,64,256]{3,2,1,0:T(8,128)} %initial.1), channel_id=1, source_target_pairs={{0,15},{1,2},{2,1},{3,4},{4,3},{5,6},{6,5},{7,8},{8,7},{9,10},{10,... | collective-permute-start | bytes 1572872 | tf_op jit(solution)/shard_map/ppermute | solution.py:557
  6.8 1.1 %copy-start.1 = (f32[2,4,64,256]{3,2,1,0:T(8,128)S(1)}, f32[2,4,64,256]{3,2,1,0:T(8,128)}, u32[]{:S(2)}) copy-start(f32[2,4,64,256]{3,2,1,0:T(8,128)} %initial.1) | copy-start | bytes 1572868
  7.9 0.9 %copy-start.2 = (f32[4,64,256]{2,1,0:T(8,128)S(1)}, f32[4,64,256]{2,1,0:T(8,128)}, u32[]{:S(2)}) copy-start(f32[4,64,256]{2,1,0:T(8,128)} %mobility.1) | copy-start | bytes 786436
  8.9 1.5 %collective-permute-start.3 = (f32[3,2,64,128]{3,2,1,0:T(8,128)S(1)}, f32[3,2,64,128]{3,2,1,0:T(8,128)S(1)}, u32[]{:S(2)}, u32[]{:S(2)}) collective-permute-start(f32[3,2,64,128]{3,2,1,0:T(8,128)S(1)} %get-tuple-element.43), channel_id=1, source_target_pairs={{0,1},{1,0},{2,3},{3,2},{4,5},{5,4},{6,7},{7,6},{8,9},{9,8},{10,11... | collective-permute-start | bytes 589832 | tf_op jit(solution)/shard_map/ppermute | solution.py:556
  9.0 8.0 %collective-permute-start = (f32[3,2,64,128]{3,2,1,0:T(8,128)S(1)}, f32[3,2,64,128]{3,2,1,0:T(8,128)S(1)}, u32[]{:S(2)}, u32[]{:S(2)}) collective-permute-start(f32[3,2,64,128]{3,2,1,0:T(8,128)S(1)} %get-tuple-element.40), channel_id=1, source_target_pairs={{0,15},{1,2},{2,1},{3,4},{4,3},{5,6},{6,5},{7,8},{8,7},{9,10},{10,... | collective-permute-start | bytes 589832 | tf_op jit(solution)/shard_map/ppermute | solution.py:557
  10.4 3.6 %copy-start = (f32[2,4,64,256]{3,2,1,0:T(8,128)S(1)}, f32[2,4,64,256]{3,2,1,0:T(8,128)}, u32[]{:S(2)}) copy-start(f32[2,4,64,256]{3,2,1,0:T(8,128)} %observed.3) | copy-start | bytes 1572868
  18.3 8.6 %collective-permute-start.5 = (f32[2,3,2,72,128]{4,3,2,1,0:T(8,128)S(1)}, f32[2,3,2,72,128]{4,3,2,1,0:T(8,128)S(1)}, u32[]{:S(2)}, u32[]{:S(2)}) collective-permute-start(f32[2,3,2,72,128]{4,3,2,1,0:T(8,128)S(1)} %get-tuple-element.65), channel_id=1, source_target_pairs={{0,1},{1,0},{2,3},{3,2},{4,5},{5,4},{6,7},{7,6},{8,9},{9,8},{10,11... | collective-permute-start | bytes 1327112 | tf_op jit(solution)/shard_map/ppermute | solution.py:556
  22.1 19.1 %collective-permute-start.4 = (f32[2,3,2,64,128]{4,3,2,1,0:T(8,128)S(1)}, f32[2,3,2,64,128]{4,3,2,1,0:T(8,128)S(1)}, u32[]{:S(2)}, u32[]{:S(2)}) collective-permute-start(f32[2,3,2,64,128]{4,3,2,1,0:T(8,128)S(1)} %get-tuple-element.57), channel_id=1, source_target_pairs={{0,15},{1,2},{2,1},{3,4},{4,3},{5,6},{6,5},{7,8},{8,7},{9,10},{10,... | collective-permute-start | bytes 1179656 | tf_op jit(solution)/shard_map/ppermute | solution.py:557
  26.8 2.6 %collective-permute-start.6 = (f32[8,128]{1,0:T(8,128)S(1)}, f32[8,128]{1,0:T(8,128)S(1)}, u32[]{:S(2)}, u32[]{:S(2)}) collective-permute-start(f32[8,128]{1,0:T(8,128)S(1)} %fusion.share_in), channel_id=1, source_target_pairs={{1,9},{2,10},{5,13},{6,14},{9,1},{10,2},{13,5},{14,6},{17,25},{18,... | collective-permute-start | bytes 12296 | tf_op jit(solution)/shard_map/ppermute | solution.py:612
  29.5 0.7 %collective-permute-start.7 = (f32[8,128]{1,0:T(8,128)S(1)}, f32[8,128]{1,0:T(8,128)S(1)}, u32[]{:S(2)}, u32[]{:S(2)}) collective-permute-start(f32[8,128]{1,0:T(8,128)S(1)} %add.13), channel_id=1, source_target_pairs={{1,5},{2,6},{5,1},{6,2},{9,13},{10,14},{13,9},{14,10},{17,21},{18,... | collective-permute-start | bytes 12296 | tf_op jit(solution)/shard_map/ppermute | solution.py:612
  30.2 0.7 %collective-permute-start.8 = (f32[8,128]{1,0:T(8,128)S(1)}, f32[8,128]{1,0:T(8,128)S(1)}, u32[]{:S(2)}, u32[]{:S(2)}) collective-permute-start(f32[8,128]{1,0:T(8,128)S(1)} %add.14), channel_id=1, source_target_pairs={{1,2},{2,1},{5,6},{6,5},{9,10},{10,9},{13,14},{14,13},{17,18},{18,... | collective-permute-start | bytes 12296 | tf_op jit(solution)/shard_map/ppermute | solution.py:612
  30.9 11.9 %collective-permute-start.9 = (f32[8,128]{1,0:T(8,128)S(1)}, f32[8,128]{1,0:T(8,128)S(1)}, u32[]{:S(2)}, u32[]{:S(2)}) collective-permute-start(f32[8,128]{1,0:T(8,128)S(1)} %add.15.total), channel_id=1, source_target_pairs={{0,1},{1,0},{2,3},{3,2},{4,5},{5,4},{6,7},{7,6},{8,9},{9,8},{10,11... | collective-permute-start | bytes 12296 | tf_op jit(solution)/shard_map/ppermute | solution.py:630

commit v12 on v8

--- a/solution.py
+++ b/solution.py
@@ -11,6 +11,7 @@
 stiffness = 0.5
 time_step = 0.005
 VMEM = pl.BlockSpec(memory_space=pltpu.VMEM)
+SMEM = pl.BlockSpec(memory_space=pltpu.SMEM)
 LANES = 128
 ROWS = 8
 PAD = ROWS
@@ -110,14 +111,8 @@
 
 
 class Faces:
-    def __init__(self, n, refs):
-        mx_a, my_a, mz_a, mz_low_a, all_a, *late = refs
-        two = lambda ref, first, last, at: ((ref, first, last), *(((late[at], last + 1, n + 1),) if late else ()))
-        self.mx = Line(*two(mx_a, -3, n - 2, 0))
-        self.my = Line(*two(my_a, -2, n - 1, 1))
-        self.mz = Line(*two(mz_a, -2, n - 1, 2))
-        self.mz_low = Line(*two(mz_low_a, -2, n - 1, 3))
-        self.all = Line(*two(all_a, -2, n - 2, 4))
+    def __init__(self, mx, my, mz, mz_low, m_all):
+        self.mx, self.my, self.mz, self.mz_low, self.all = mx, my, mz, mz_low, m_all
 
     def flow(self, row, at, mid, up, down, low=None, high=None):
         total = each(
@@ -147,7 +142,12 @@
     def one_run(run, carry):
         for row in chunks(ny):
             for at in range(n):
-                put_padded(conc, (run, at), row, plain(initial, (run, place[at]), row))
+                value = plain(initial, (run, place[at]), row)
+                put_padded(conc, (run, at), row, value)
+                if at < 2:
+                    put_flat(to_core, (2 * run + at,), row, value)
+                if at >= n - 2:
+                    put_flat(to_chip, (2 * run + n - 1 - at,), row, value)
         return carry
 
     lax.fori_loop(0, runs, one_run, 0)
@@ -155,10 +155,10 @@
         for at in range(n):
             value = plain(mobility, (place[at],), row)
             put_padded(mob, (at,), row, value)
-            if at < 3:
-                put_flat(to_core, (at,), row, value)
-            if at >= n - 3:
-                put_flat(to_chip, (n - 1 - at,), row, value)
+            if at == 0:
+                put_flat(to_core, (2 * runs,), row, value)
+            if at == n - 1:
+                put_flat(to_chip, (2 * runs,), row, value)
 
 
 def mean(a, b):
@@ -210,128 +210,161 @@
     return adjoint, sum(part * part for part in miss)
 
 
-def core_kernel(of_core, m_core, conc_own, mob_own, conc_core, chem0, mx, my, mz, mz_low, m_all, rim):
-    runs, n = conc_own.shape[:2]
-    ny = of_core.shape[2]
-    mob = Line((rim, -3, -1), (mob_own, 0, n - 1))
-    faces = Faces(n, (mx, my, mz, mz_low, m_all))
-    for row in chunks(ny):
-        for at in range(3):
-            put_padded(rim, (2 - at,), row, flat(m_core, (at,), row))
-    for row in chunks(ny):
-        mids = [padded(*mob(at), row) for at in range(-3, n)]
-        for at in range(n + 2):
-            put_flat(mx, (at,), row, each(mean, mids[at], mids[at + 1]))
-        put_faces(row, mob, range(-2, n), faces.my, faces.mz, faces.mz_low)
-    for row in chunks(ny):
-        put_all(row, faces, range(-2, n - 1))
-    place = [either(at, 3 - at) for at in range(4)]
-    conc = Line((conc_core, -4, -1), (conc_own, 0, n - 1))
-
-    def one_run(run, carry):
-        for row in chunks(ny):
-            for at in range(4):
-                put_padded(conc_core, (run, 3 - at), row, plain(of_core, (run, place[at]), row))
-        for row in chunks(ny):
-            put_potential(row, conc, run, range(-3, n - 1), Line((chem0, -3, n - 2)))
-        return carry
-
-    lax.fori_loop(0, runs, one_run, 0)
-
-
-def chip_kernel(
-    of_chip, conc_own, conc_core, chem0_a, observed, mx, my, mz, mz_low, m_all,
-    conc_chip, chem0_b, state1_a, chem1_a, adjoint2_a, squares,
+def core_kernel(
+    of_core, conc_own, mob_own, mob_low, mx, my, mz, mz_low, m_all, chem0, state1, rim,
 ):
     runs, n = conc_own.shape[:2]
-    ny = observed.shape[2]
-    faces = Faces(n, (mx, my, mz, mz_low, m_all))
-    message = [either(3 - at, at) for at in range(4)]
-    place = [either(n - 1 - at, at) for at in range(n)]
-    conc = Line((conc_core, -4, -1), (conc_own, 0, n - 1), (conc_chip, n, n + 3))
-    chem0 = Line((chem0_a, -3, n - 2), (chem0_b, n - 1, n + 2))
-    state1 = Line((state1_a, -2, n - 2))
-    chem1 = Line((chem1_a, -1, n - 3))
-    adjoint2 = Line((adjoint2_a, 0, n - 4))
-    squares[...] = jnp.zeros_like(squares)
+    ny = of_core.shape[-2]
+    mob = Line((mob_low, -1, -1), (mob_own, 0, n - 1))
+    faces = Faces(
+        Line((mx, -1, n - 2)), Line((my, 0, n - 1)), Line((mz, 0, n - 1)), Line((mz_low, 0, n - 1)),
+        Line((m_all, 0, n - 2)),
+    )
+    conc = Line((rim, -2, -1), (conc_own, 0, n - 1))
+    chem = Line((chem0, -1, n - 2))
+    for row in chunks(ny):
+        put_padded(mob_low, (0,), row, flat(of_core, (2 * runs,), row))
+    for row in chunks(ny):
+        mids = [padded(*mob(at), row) for at in range(-1, n)]
+        for at in range(n):
+            put_flat(mx, (at,), row, each(mean, mids[at], mids[at + 1]))
+        put_faces(row, mob, range(n), faces.my, faces.mz, faces.mz_low)
+    for row in chunks(ny):
+        put_all(row, faces, range(n - 1))
 
     def one_run(run, carry):
         for row in chunks(ny):
-            for at in range(4):
-                put_padded(conc_chip, (run, at), row, plain(of_chip, (run, message[at]), row))
-        for row in chunks(ny):
-            put_potential(row, conc, run, range(n - 1, n + 3), chem0)
+            for at in range(2):
+                put_padded(rim, (run, 1 - at), row, flat(of_core, (2 * run + at,), row))
+        for row in chunks(ny):
+            put_potential(row, conc, run, range(-1, n - 1), chem)
         for row in chunks(ny):
             put_step(
-                row, faces, chem0, conc, run, range(-2, n - 1),
-                lambda at, value: put_padded(*state1(at, run), row, value),
+                row, faces, chem, conc, run, range(n - 2),
+                lambda at, value: put_padded(state1, (run, at), row, value),
             )
-        for row in chunks(ny):
-            put_potential(row, state1, run, range(-1, n - 2), chem1)
-        for row in chunks(ny):
-
-            def target(at, value):
-                squares[...] += put_miss(row, runs, observed, place, run, at, value, adjoint2)[1]
-
-            put_step(row, faces, chem1, state1, run, range(0, n - 3), target)
         return carry
 
     lax.fori_loop(0, runs, one_run, 0)
 
 
-def forward_kernel(
-    m_chip, mob_own, conc_own, conc_chip, chem0_a, chem0_b, state1_a, chem1_a, adjoint2_a, squares, observed,
-    mx_a, my_a, mz_a, mz_low_a, all_a,
-    mx_b, my_b, mz_b, mz_low_b, all_b, state1_b, chem1_b, adjoint2_b, to_core, to_chip, share, rim, total,
+def chip_kernel(
+    of_chip, conc_own, mob_own, mx_a, my_a, mz_a, mz_low_a, all_a, chem0_a, state1_a,
+    mob_high, mx_b, all_b, chem0_b, state1_b, to_chip, to_core, rim,
 ):
     runs, n = conc_own.shape[:2]
-    ny = observed.shape[2]
-    faces = Faces(n, (mx_a, my_a, mz_a, mz_low_a, all_a, mx_b, my_b, mz_b, mz_low_b, all_b))
-    mob = Line((mob_own, 0, n - 1), (rim, n, n + 2))
+    ny = of_chip.shape[-2]
+    mob = Line((mob_own, 0, n - 1), (mob_high, n, n))
+    faces = Faces(
+        Line((mx_a, -1, n - 2), (mx_b, n - 1, n - 1)), Line((my_a, 0, n - 1)), Line((mz_a, 0, n - 1)),
+        Line((mz_low_a, 0, n - 1)), Line((all_a, 0, n - 2), (all_b, n - 1, n - 1)),
+    )
+    conc = Line((conc_own, 0, n - 1), (rim, n, n + 1))
+    chem = Line((chem0_a, -1, n - 2), (chem0_b, n - 1, n))
+    state1 = Line((state1_a, 0, n - 3), (state1_b, n - 2, n - 1))
+    for row in chunks(ny):
+        value = flat(of_chip, (2 * runs,), row)
+        put_padded(mob_high, (0,), row, value)
+        put_flat(mx_b, (0,), row, each(mean, padded(*mob(n - 1), row), value))
+        put_all(row, faces, range(n - 1, n))
+
+    def one_run(run, carry):
+        for row in chunks(ny):
+            for at in range(2):
+                put_padded(rim, (run, at), row, flat(of_chip, (2 * run + at,), row))
+        for row in chunks(ny):
+            put_potential(row, conc, run, range(n - 1, n + 1), chem)
+        for row in chunks(ny):
+
+            def target(at, value):
+                put_padded(state1_b, (run, at - (n - 2)), row, value)
+                put_flat(to_chip, (2 * run + n - 1 - at,), row, value)
+
+            put_step(row, faces, chem, conc, run, range(n - 2, n), target)
+            for at in range(2):
+                put_flat(to_core, (2 * run + at,), row, padded(*state1(at, run), row))
+        return carry
+
+    lax.fori_loop(0, runs, one_run, 0)
+
+
+def second_core_kernel(
+    of_core, state1_a, state1_b, observed, mx_a, my_a, mz_a, mz_low_a, all_a,
+    state1_low, chem1, adjoint2, squares,
+):
+    runs, n, ny, _ = observed.shape
+    faces = Faces(
+        Line((mx_a, -1, n - 2)), Line((my_a, 0, n - 1)), Line((mz_a, 0, n - 1)), Line((mz_low_a, 0, n - 1)),
+        Line((all_a, 0, n - 2)),
+    )
     place = [either(n - 1 - at, at) for at in range(n)]
-    conc = Line((conc_own, 0, n - 1), (conc_chip, n, n + 3))
-    chem0 = Line((chem0_a, -3, n - 2), (chem0_b, n - 1, n + 2))
-    state1 = Line((state1_a, -2, n - 2), (state1_b, n - 1, n + 1))
-    chem1 = Line((chem1_a, -1, n - 3), (chem1_b, n - 2, n))
-    adjoint2 = Line((adjoint2_a, 0, n - 4), (adjoint2_b, n - 3, n - 1))
-    for row in chunks(ny):
-        for at in range(3):
-            put_padded(rim, (at,), row, flat(m_chip, (at,), row))
-    for row in chunks(ny):
-        mids = [padded(*mob(at), row) for at in range(n - 1, n + 3)]
-        for at in range(3):
-            put_flat(mx_b, (at,), row, each(mean, mids[at], mids[at + 1]))
-        put_faces(row, mob, range(n, n + 2), faces.my, faces.mz, faces.mz_low)
-    for row in chunks(ny):
-        put_all(row, faces, range(n - 1, n + 2))
+    state1 = Line((state1_low, -2, -1), (state1_a, 0, n - 3), (state1_b, n - 2, n - 1))
+    chem = Line((chem1, -1, n - 2))
+    squares[...] = jnp.zeros_like(squares)
+
+    def one_run(run, carry):
+        for row in chunks(ny):
+            for at in range(2):
+                put_padded(state1_low, (run, 1 - at), row, flat(of_core, (2 * run + at,), row))
+        for row in chunks(ny):
+            put_potential(row, state1, run, range(-1, n - 1), chem)
+        for row in chunks(ny):
+
+            def target(at, value):
+                squares[...] += put_miss(row, runs, observed, place, run, at, value, Line((adjoint2, 0, n - 3)))[1]
+
+            put_step(row, faces, chem, state1, run, range(n - 2), target)
+        return carry
+
+    lax.fori_loop(0, runs, one_run, 0)
+
+
+def second_chip_kernel(
+    of_chip, state1_a, state1_b, chem1_a, adjoint2_a, squares, observed, mob,
+    mx_a, my_a, mz_a, mz_low_a, all_a, mx_b, all_b,
+    state1_high, chem1_b, adjoint2_b, to_core, to_chip, share, total,
+):
+    runs, n, ny, _ = observed.shape
+    faces = Faces(
+        Line((mx_a, -1, n - 2), (mx_b, n - 1, n - 1)), Line((my_a, 0, n - 1)), Line((mz_a, 0, n - 1)),
+        Line((mz_low_a, 0, n - 1)), Line((all_a, 0, n - 2), (all_b, n - 1, n - 1)),
+    )
+    place = [either(n - 1 - at, at) for at in range(n)]
+    state1 = Line((state1_a, 0, n - 3), (state1_b, n - 2, n - 1), (state1_high, n, n + 1))
+    chem = Line((chem1_a, -1, n - 2), (chem1_b, n - 1, n))
+    adjoint2 = Line((adjoint2_a, 0, n - 3), (adjoint2_b, n - 2, n - 1))
     total[...] = squares[...]
 
     def one_run(run, carry):
         for row in chunks(ny):
-            put_step(
-                row, faces, chem0, conc, run, range(n - 1, n + 2),
-                lambda at, value: put_padded(*state1(at, run), row, value),
-            )
-        for row in chunks(ny):
-            put_potential(row, state1, run, range(n - 2, n + 1), chem1)
+            for at in range(2):
+                put_padded(state1_high, (run, at), row, flat(of_chip, (2 * run + at,), row))
+        for row in chunks(ny):
+            put_potential(row, state1, run, range(n - 1, n + 1), chem)
         for row in chunks(ny):
 
             def target(at, value):
                 adjoint, square = put_miss(row, runs, observed, place, run, at, value, adjoint2)
                 total[...] += square
-                put_flat(to_chip, (run, n - 1 - at), row, adjoint)
+                put_flat(to_chip, (3 * run + n - 1 - at,), row, adjoint)
                 if at < 3:
-                    put_flat(to_core, (run, at), row, adjoint)
-
-            put_step(row, faces, chem1, state1, run, range(n - 3, n), target)
-            for at in range(min(3, n - 3)):
-                put_flat(to_core, (run, at), row, padded(*adjoint2(at, run), row))
+                    put_flat(to_core, (3 * run + at,), row, adjoint)
+
+            put_step(row, faces, chem, state1, run, range(n - 2, n), target)
+            put_flat(to_chip, (3 * run + 2,), row, padded(*adjoint2(n - 3, run), row))
+            for at in range(min(3, n - 2)):
+                put_flat(to_core, (3 * run + at,), row, padded(*adjoint2(at, run), row))
         return carry
 
     lax.fori_loop(0, runs, one_run, 0)
+    for row in chunks(ny):
+        for at in range(2):
+            put_flat(to_chip, (3 * runs + at,), row, padded(mob, (n - 2 - at,), row))
+            put_flat(to_core, (3 * runs + at,), row, padded(mob, (1 + at,), row))
     columns = (0.5 / runs) * jnp.sum(total[...], axis=0, keepdims=True)
     mine = jnp.broadcast_to(jnp.sum(columns, axis=1, keepdims=True), share.shape)
     share[...] = mine
+    to_core[0, 0, ny:] = mine
 
 
 def put_adjoint1(row, flow, adjoint2, run, places, weight, target):
@@ -364,29 +397,70 @@
     return sub(after_z(mid), mid)
 
 
-def early_kernel(
-    of_core, mx_a, my_a, mz_a, mz_low_a, all_a, mx_b, my_b, mz_b, mz_low_b, all_b,
-    chem0_a, chem0_b, state1_a, state1_b, chem1_a, chem1_b, adjoint2_a, adjoint2_b,
-    flow_a, flow_part, adjoint1_a, weight_b, step_z_b, part, sum_x_b, sum_y_b, sum_z_b,
-    rim, sum_x, sum_y, sum_z,
-):
-    runs = of_core.shape[0]
+class Backward:
+    names = (
+        "mx_a", "my_a", "mz_a", "mz_low_a", "all_a", "mx_b", "all_b",
+        "chem0_a", "chem0_b", "state1_low", "state1_a", "state1_b", "state1_high", "chem1_a", "chem1_b",
+        "adjoint2_a", "adjoint2_b",
+    )
+
+    def __init__(self, n, refs, low=None, high=None):
+        at = dict(zip(self.names, refs))
+
+        def line(which, shift, *own):
+            outer = ((low[which], shift - 2, shift - 1),) if low else ((high[which], n, n + 1),)
+            return Line(*own, *outer)
+
+        self.faces = Faces(
+            line(0, -1, (at["mx_a"], -1, n - 2), (at["mx_b"], n - 1, n - 1)),
+            *(line(1 + which, 0, (at[name], 0, n - 1)) for which, name in enumerate(("my_a", "mz_a", "mz_low_a"))),
+            line(4, 0, (at["all_a"], 0, n - 2), (at["all_b"], n - 1, n - 1)),
+        )
+        self.chem0 = Line((at["chem0_a"], -1, n - 2), (at["chem0_b"], n - 1, n))
+        self.state1 = Line(
+            (at["state1_low"], -2, -1), (at["state1_a"], 0, n - 3), (at["state1_b"], n - 2, n - 1),
+            (at["state1_high"], n, n + 1),
+        )
+        self.chem1 = Line((at["chem1_a"], -1, n - 2), (at["chem1_b"], n - 1, n))
+        self.adjoint2 = ((at["adjoint2_a"], 0, n - 3), (at["adjoint2_b"], n - 2, n - 1))
+
+
+def put_outer(ny, message, first, mob, to, faces, places):
+    for row in chunks(ny):
+        for at in range(2):
+            put_padded(*mob(to[at]), row, flat(message, (first + at,), row))
+    for row in chunks(ny):
+        mids = {at: padded(*mob(at), row) for at in range(min(places[0], *to), max(places[1], *to) + 1)}
+        for at in sorted(mids)[:-1]:
+            put_flat(*faces.mx(at), row, each(mean, mids[at], mids[at + 1]))
+        put_faces(row, mob, places, faces.my, faces.mz, faces.mz_low)
+    for row in chunks(ny):
+        put_all(row, faces, places)
+
+
+def early_kernel(of_core, mob_low, share_in, *refs):
+    count = len(Backward.names)
+    kept, refs = refs[:count], refs[count:]
+    flow_a, flow_part, adjoint1_a, weight_b, step_z_b, part, sum_x_b, sum_y_b, sum_z_b, share = refs[:10]
+    rim, sum_x, sum_y, sum_z, m_rim, *low = refs[10:]
+    share[...] = share_in[...]
     n = part.shape[0] + 2
+    runs = flow_a.shape[0]
     ny = part.shape[-2]
-    faces = Faces(n, (mx_a, my_a, mz_a, mz_low_a, all_a, mx_b, my_b, mz_b, mz_low_b, all_b))
-    chem0 = Line((chem0_a, -3, n - 2), (chem0_b, n - 1, n + 2))
-    state1 = Line((state1_a, -2, n - 2), (state1_b, n - 1, n + 1))
-    chem1 = Line((chem1_a, -1, n - 3), (chem1_b, n - 2, n))
-    adjoint2 = Line((rim, -3, -1), (adjoint2_a, 0, n - 4), (adjoint2_b, n - 3, n - 1))
+    at_ = Backward(n, kept, low=low)
+    faces, chem0, state1, chem1 = at_.faces, at_.chem0, at_.state1, at_.chem1
+    adjoint2 = Line((rim, -3, -1), *at_.adjoint2)
     flow = Line((flow_a, -2, n - 2), (flow_part, n - 1, n - 1))
     adjoint1 = Line((adjoint1_a, -1, n - 3))
+    mob = Line((m_rim, -3, -2), (mob_low, -1, -1))
+    put_outer(ny, of_core, 3 * runs, mob, (-2, -3), faces, (-2, -1))
     for sums in (sum_x, sum_y, sum_z):
         sums[...] = jnp.zeros_like(sums)
 
     def one_run(run, carry):
         for row in chunks(ny):
             for at in range(3):
-                put_padded(rim, (run, 2 - at), row, flat(of_core, (run, at), row))
+                put_padded(rim, (run, 2 - at), row, flat(of_core, (3 * run + at,), row))
         for row in chunks(ny):
             mids = {at: padded(*adjoint2(at, run), row) for at in range(-3, n)}
             for at in range(-2, n):
@@ -430,10 +504,10 @@
     lax.fori_loop(0, runs, one_run, 0)
     for row in chunks(ny):
         for at in range(n - 2):
-            sides = flat(sum_z, (at,), row)
+            sides_z = flat(sum_z, (at,), row)
             value = each(
                 lambda a, b, c, d, e: -0.5 * ((a + b) + (c + d) + e),
-                padded(sum_y, (at,), row), padded(sum_y, (at,), row, -1), sides, before_z(sides),
+                padded(sum_y, (at,), row), padded(sum_y, (at,), row, -1), sides_z, before_z(sides_z),
                 flat(sum_x, (at,), row),
             )
             if at < n - 3:
@@ -445,18 +519,19 @@
             put_flat(sum_z_b, (at,), row, flat(sum_z, (n - 2 + at,), row))
 
 
-def late_kernel(
-    of_chip, mx_a, my_a, mz_a, mz_low_a, all_a, mx_b, my_b, mz_b, mz_low_b, all_b,
-    chem0_a, chem0_b, chem1_b, adjoint2_b, flow_a, flow_part, adjoint1_a, weight_b, step_z_b,
-    part, sum_x_b, sum_y_b, sum_z_b, result, rim, flow_b, adjoint1_b, sum_x, sum_y, sum_z,
-):
-    runs = of_chip.shape[0]
+def late_kernel(of_chip, mob_high, *refs):
+    count = len(Backward.names)
+    kept, refs = refs[:count], refs[count:]
+    flow_a, flow_part, adjoint1_a, weight_b, step_z_b, part, sum_x_b, sum_y_b, sum_z_b, result = refs[:10]
+    rim, flow_b, adjoint1_b, sum_x, sum_y, sum_z, m_rim, *high = refs[10:]
+    runs = flow_a.shape[0]
     n, ny, _ = result.shape
-    faces = Faces(n, (mx_a, my_a, mz_a, mz_low_a, all_a, mx_b, my_b, mz_b, mz_low_b, all_b))
+    at_ = Backward(n, kept, high=high)
+    faces, chem0, chem1 = at_.faces, at_.chem0, at_.chem1
+    mob = Line((mob_high, n, n), (m_rim, n + 1, n + 2))
+    put_outer(ny, of_chip, 3 * runs, mob, (n + 1, n + 2), faces, (n, n + 1))
     place = [either(n - 1 - at, at) for at in range(n)]
-    chem0 = Line((chem0_a, -3, n - 2), (chem0_b, n - 1, n + 2))
-    chem1 = Line((chem1_b, n - 2, n))
-    adjoint2 = Line((adjoint2_b, n - 3, n - 1), (rim, n, n + 2))
+    adjoint2 = Line(*at_.adjoint2, (rim, n, n + 2))
     flow = Line((flow_a, -2, n - 2), (flow_b, n - 1, n + 1))
     adjoint1 = Line((adjoint1_a, -1, n - 3), (adjoint1_b, n - 2, n))
     for row in chunks(ny):
@@ -469,7 +544,7 @@
     def one_run(run, carry):
         for row in chunks(ny):
             for at in range(3):
-                put_padded(rim, (run, at), row, flat(of_chip, (run, at), row))
+                put_padded(rim, (run, at), row, flat(of_chip, (3 * run + at,), row))
         for row in chunks(ny):
             mids = {at: padded(*adjoint2(at, run), row) for at in range(n - 1, n + 3)}
             value = add_product(padded(flow_part, (run, 0), row), flat(*faces.mx(n - 1), row), mids[n])
@@ -520,17 +595,17 @@
             put_plain(result, (place[n - 2 + at],), row, value)
 
 
-def misfit_kernel(shares, misfit):
-    misfit[...] = jnp.sum(shares[...], axis=0)
-
-
-def call(kernel, outs, scratch, args, flops):
+def misfit_kernel(share, far, misfit):
+    misfit[0] = (share[...] + far[...])[0, 0]
+
+
+def call(kernel, outs, scratch, args, flops, spaces=(VMEM, VMEM)):
     moved = 4 * (sum(a.size for a in args) + sum(math.prod(o) for o in outs))
     return pl.pallas_call(
         kernel,
         out_shape=tuple(jax.ShapeDtypeStruct(o, jnp.float32) for o in outs),
-        in_specs=[VMEM] * len(args),
-        out_specs=tuple([VMEM] * len(outs)),
+        in_specs=[spaces[0]] * len(args),
+        out_specs=tuple([spaces[1]] * len(outs)),
         scratch_shapes=[pltpu.VMEM(s, jnp.float32) for s in scratch],
         compiler_params=pltpu.CompilerParams(vmem_limit_bytes=16 * 1024 * 1024),
         cost_estimate=pl.CostEstimate(flops=flops, bytes_accessed=moved, transcendentals=0),
@@ -555,75 +630,92 @@
     def lies_padded(*lead):
         return (*lead, blocks, ny + 2 * PAD, LANES)
 
-    if n == 4:
-        near = (initial, initial)
-    else:
-        near = [lax.dynamic_slice_in_dim(initial, at, 4, 1) for at in (either(0, n - 4), either(n - 4, 0))]
-    of_chip, of_core = neighbours(*near)
     conc, mob, to_chip, to_core = call(
-        own_kernel, (lies_padded(runs, n), lies_padded(n), lies(3), lies(3)), (), (initial, mobility),
+        own_kernel,
+        (
+            lies_padded(runs, n), lies_padded(n), lies(2 * runs + 1), lies(2 * runs + 1),
+        ),
+        (),
+        (initial, mobility),
         runs * n * cell,
     )
-    m_chip, m_core = neighbours(to_chip, to_core)
-    conc_core, chem0_a, *faces_a = call(
+    of_chip, of_core = neighbours(to_chip, to_core)
+    mob_low, *faces_a, chem0_a, state1_a = call(
         core_kernel,
         (
-            lies_padded(runs, 4), lies_padded(runs, n + 2),
-            lies(n + 2), lies_padded(n + 2), lies(n + 2), lies(n + 2), lies(n + 1),
+            lies_padded(1), lies(n), lies_padded(n), lies(n), lies(n), lies(n - 1),
+            lies_padded(runs, n), lies_padded(runs, n - 2),
         ),
-        (lies_padded(3),),
-        (of_core, m_core, conc, mob),
-        20 * runs * (n + 2) * cell,
-    )
-    conc_chip, chem0_b, state1_a, chem1_a, adjoint2_a, squares = call(
+        (lies_padded(runs, 2),),
+        (of_core, conc, mob),
+        30 * runs * 2 * n * cell,
+    )
+    mob_high, *faces_b, chem0_b, state1_b, to_chip, to_core = call(
         chip_kernel,
         (
-            lies_padded(runs, 4), lies_padded(runs, 4), lies_padded(runs, n + 1),
-            lies_padded(runs, n - 1), lies_padded(runs, n - 3), (CHUNK, LANES),
+            lies_padded(1), lies(1), lies(1), lies_padded(runs, 2), lies_padded(runs, 2),
+            lies(2 * runs), lies(2 * runs),
         ),
+        (lies_padded(runs, 2),),
+        (of_chip, conc, mob, *faces_a, chem0_a, state1_a),
+        30 * runs * 4 * cell,
+    )
+    of_chip, of_core = neighbours(to_chip, to_core)
+    state1_low, chem1_a, adjoint2_a, squares = call(
+        second_core_kernel,
+        (lies_padded(runs, 2), lies_padded(runs, n), lies_padded(runs, n - 2), (CHUNK, LANES)),
         (),
-        (of_chip, conc, conc_core, chem0_a, observed, *faces_a),
-        60 * runs * (n - 1) * cell,
-    )
-    *faces_b, state1_b, chem1_b, adjoint2_b, to_core, to_chip, share = call(
-        forward_kernel,
+        (of_core, state1_a, state1_b, observed, *faces_a),
+        30 * runs * (2 * n - 2) * cell,
+    )
+    state1_high, chem1_b, adjoint2_b, to_core, to_chip, share = call(
+        second_chip_kernel,
         (
-            lies(3), lies_padded(2), lies(2), lies(2), lies(3),
-            lies_padded(runs, 3), lies_padded(runs, 3), lies_padded(runs, 3),
-            lies(runs, 3), lies(runs, 3), (LANES, LANES),
+            lies_padded(runs, 2), lies_padded(runs, 2), lies_padded(runs, 2),
+            (3 * runs + 2, blocks, ny + ROWS, LANES), lies(3 * runs + 2), (ROWS, LANES),
         ),
-        (lies_padded(3), (CHUNK, LANES)),
-        (m_chip, mob, conc, conc_chip, chem0_a, chem0_b, state1_a, chem1_a, adjoint2_a, squares, observed, *faces_a),
-        60 * runs * 3 * cell,
-    )
-    faces = (*faces_a, *faces_b)
+        ((CHUNK, LANES),),
+        (of_chip, state1_a, state1_b, chem1_a, adjoint2_a, squares, observed, mob, *faces_a, *faces_b),
+        30 * runs * 4 * cell,
+    )
+    kept = (
+        *faces_a, *faces_b, chem0_a, chem0_b, state1_low, state1_a, state1_b, state1_high, chem1_a, chem1_b,
+        adjoint2_a, adjoint2_b,
+    )
     of_chip, of_core = neighbours(to_chip, to_core)
-    shares = lax.all_gather(share, "gx")
-    flow_a, flow_part, adjoint1_a, weight_b, step_z_b, part, *sums_b = call(
+    hops = [1 << bit for bit in range(count.bit_length() - 2, 0, -1)]
+
+    def hop_of(value, hop):
+        return lax.ppermute(value, "gx", [(i, i ^ hop) for i in range(count)])
+
+    share = share + of_core[0, 0, ny:]
+    far = hop_of(share, hops[0])
+    outer = (lies_padded(2), lies(2), lies_padded(2), lies(2), lies(2), lies(2))
+    *done, share = call(
         early_kernel,
         (
             lies_padded(runs, n + 1), lies_padded(runs, 1), lies_padded(runs, n - 1), lies(runs, 3), lies(runs, 2),
-            lies(n - 2), lies(2), lies(2), lies(2),
+            lies(n - 2), lies(2), lies(2), lies(2), (ROWS, LANES),
         ),
-        (lies_padded(runs, 3), lies(n), lies_padded(n), lies(n)),
-        (of_core, *faces, chem0_a, chem0_b, state1_a, state1_b, chem1_a, chem1_b, adjoint2_a, adjoint2_b),
+        (lies_padded(runs, 3), lies(n), lies_padded(n), lies(n), *outer),
+        (of_core, mob_low, share, *kept),
         60 * runs * n * cell,
     )
+    for hop in hops[1:]:
+        share = share + far
+        far = hop_of(share, hop)
     (result,) = call(
         late_kernel,
         ((n, ny, nz),),
         (
             lies_padded(runs, 3), lies_padded(runs, 3), lies_padded(runs, 3),
-            lies(3), lies_padded(2), lies(2),
+            lies(3), lies_padded(2), lies(2), *outer,
         ),
-        (
-            of_chip, *faces, chem0_a, chem0_b, chem1_b, adjoint2_b, flow_a, flow_part, adjoint1_a,
-            weight_b, step_z_b, part, *sums_b,
-        ),
+        (of_chip, mob_high, *kept, *done),
         60 * runs * 3 * cell,
     )
-    (misfit,) = call(misfit_kernel, ((1, LANES),), (), (shares[:, :1],), count)
-    return (result, misfit[0, :1])
+    (misfit,) = call(misfit_kernel, ((1,),), (), (share, far), 1, (VMEM, SMEM))
+    return (result, misfit)
 
 
 def solution(mesh):

time: 103 us -> 43.6 us (0.42)
  local copies, waits for them, and re-layouts: 42.6 us -> 1.99 us
  between operations: 14.2 us -> 0.7 us
  waiting for transfers between devices: 21.5 us -> 15.9 us
  starting transfers between devices: 15.5 us -> 17.6 us
    unnamed x106 -> x6, local copies, waits for them, and re-layouts: 41.8 us -> 1.99 us
    all_gather x1 -> x0, waiting for transfers between devices: 16.1 us -> none  [on_device(): shares = lax.all_gather(share, 'gx')]
    ppermute x0 -> x3, waiting for transfers between devices: none -> 8.43 us  [hop_of(): return lax.ppermute(value, 'gx', [(i, i ^ hop) for i in range(count)])]
    ppermute x3, starting transfers between devices: 11.1 us -> 14.9 us  [neighbours(): return (lax.ppermute(to_chip, 'gx', over_chips), of_core)]
    ppermute x3, starting transfers between devices: 4.44 us -> 1.03 us  [neighbours(): of_core = lax.ppermute(to_core, 'gx', over_cores)]
    ppermute x3, waiting for transfers between devices: 4.47 us -> 7.43 us  [neighbours(): return (lax.ppermute(to_chip, 'gx', over_chips), of_core)]
    ppermute x0 -> x3, starting transfers between devices: none -> 1.69 us  [hop_of(): return lax.ppermute(value, 'gx', [(i, i ^ hop) for i in range(count)])]
    pallas_call x7 -> x8, Pallas kernels: 8.13 us -> 7.22 us  [call(): pl.pallas_call(kernel, out_shape=tuple((jax.ShapeDtypeStruct(o, jnp.float...]
  transfers between devices with their start and end apart: 7 -> 9, of which waited for: 4 -> 5; matrix products, arithmetic and copies ran while one was open for 1% -> 0% of each run, Pallas kernels for 4% -> 12%
where the time goes in v12:
time: 43.6 us; the launch traced here: 43.4 us
  starting transfers between devices  17.6 us (40%)
  waiting for transfers between devices  15.9 us (36%)
  Pallas kernels  7.22 us (17%)
  local copies, waits for them, and re-layouts  1.99 us (5%)
  between operations  0.7 us (2%)
    ppermute x3, starting transfers between devices, neighbours(): return (lax.ppermute(to_chip, 'gx', over_chips), of_core)  14.9 us
    ppermute x3, waiting for transfers between devices, hop_of(): return lax.ppermute(value, 'gx', [(i, i ^ hop) for i in range(count)])  8.43 us
    ppermute x3, waiting for transfers between devices, neighbours(): return (lax.ppermute(to_chip, 'gx', over_chips), of_core)  7.43 us
    pallas_call x8, Pallas kernels, call(): pl.pallas_call(kernel, out_shape=tuple((jax.ShapeDtypeStruct(o, jnp.float...  7.22 us
    unnamed x6, local copies, waits for them, and re-layouts  1.99 us
    ppermute x3, starting transfers between devices, hop_of(): return lax.ppermute(value, 'gx', [(i, i ^ hop) for i in range(count)])  1.69 us
    ppermute x3, starting transfers between devices, neighbours(): of_core = lax.ppermute(to_core, 'gx', over_cores)  1.03 us
  transfers between devices with their start and end apart: 9, of which 5 were waited for; matrix products, arithmetic and copies ran while one was open for 0% of the time, Pallas kernels for 12%

profile of v12, /device:TPU:0, one launch (start us, length us, event | category | flops | bytes accessed | tf_op | source)
XLA Modules:
  0.0 43.4 jit_solution(4486726827746048675)
XLA Ops:
  0.6 0.0 copy-start.1
  0.6 1.0 %copy-done.1 = f32[2,4,64,256]{3,2,1,0:T(8,128)S(1)} copy-done((f32[2,4,64,256]{3,2,1,0:T(8,128)S(1)}, f32[2,4,64,256]{3,2,1,0:T(8,128)}, u32[]{:S(2)}) %copy-start.1) | copy-done | bytes 524312
  1.7 0.0 copy-start.2
  1.7 0.9 %copy-done.2 = f32[4,64,256]{2,1,0:T(8,128)S(1)} copy-done((f32[4,64,256]{2,1,0:T(8,128)S(1)}, f32[4,64,256]{2,1,0:T(8,128)}, u32[]{:S(2)}) %copy-start.2) | copy-done | bytes 262168
  2.6 0.1 shard_map.50
  2.7 0.5 %collective-permute-start.1 = (f32[5,2,64,128]{3,2,1,0:T(8,128)S(1)}, f32[5,2,64,128]{3,2,1,0:T(8,128)S(1)}, u32[]{:S(2)}, u32[]{:S(2)}) collective-permute-start(f32[5,2,64,128]{3,2,1,0:T(8,128)S(1)} %get-tuple-element.44), channel_id=1, source_target_pairs={{0,1},{1,0},{2,3},{3,2},{4,5},{5,4},{6,7},{7,6},{8,9},{9,8},{10,11... | collective-permute-start | bytes 983048 | tf_op jit(solution)/shard_map/ppermute | solution.py:624
  3.3 5.7 %collective-permute-start = (f32[5,2,64,128]{3,2,1,0:T(8,128)S(1)}, f32[5,2,64,128]{3,2,1,0:T(8,128)S(1)}, u32[]{:S(2)}, u32[]{:S(2)}) collective-permute-start(f32[5,2,64,128]{3,2,1,0:T(8,128)S(1)} %get-tuple-element.41), channel_id=1, source_target_pairs={{0,15},{1,2},{2,1},{3,4},{4,3},{5,6},{6,5},{7,8},{8,7},{9,10},{10,... | collective-permute-start | bytes 983048 | tf_op jit(solution)/shard_map/ppermute | solution.py:625
  8.9 0.0 collective-permute-done.1.of_core
  8.9 0.8 %shard_map.51 = (f32[1,2,80,128]{3,2,1,0:T(8,128)S(1)}, f32[4,2,64,128]{3,2,1,0:T(8,128)S(1)}, f32[4,2,80,128]{3,2,1,0:T(8,128)S(1)}, f32[4,2,64,128]{3,2,1,0:T(...) custom-call(f32[5,2,64,128]{3,2,1,0:T(8,128)S(1)} %collective-permut, ...), custom_call_target="tpu_custom_call" | custom-call | flops 7864320 | bytes 3686400 | tf_op jit(solution)/shard_map/pallas_call | solution.py:604
  9.7 4.1 %collective-permute-done.of_chip = f32[5,2,64,128]{3,2,1,0:T(8,128)S(1)} collective-permute-done((f32[5,2,64,128]{3,2,1,0:T(8,128)S(1)}, f32[5,2,64,128]{3,2,1,0:T(8,128)S(1)}, u32[]{:S(2)}, u32[]{:S(2)}) %collective-permute-start) | collective-permute-done | bytes 327712 | tf_op jit(solution)/shard_map/ppermute | solution.py:625
  13.8 0.0 copy-start
  13.8 0.5 %shard_map.52 = (f32[1,2,80,128]{3,2,1,0:T(8,128)S(1)}, f32[1,2,64,128]{3,2,1,0:T(8,128)S(1)}, f32[1,2,64,128]{3,2,1,0:T(8,128)S(1)}, f32[2,2,2,80,128]{4,3,2,1,...) custom-call(f32[5,2,64,128]{3,2,1,0:T(8,128)S(1)} %collective-permut, ...), custom_call_target="tpu_custom_call" | custom-call | flops 3932160 | bytes 4997120 | tf_op jit(solution)/shard_map/pallas_call | solution.py:604
  14.3 0.5 %collective-permute-start.3 = (f32[4,2,64,128]{3,2,1,0:T(8,128)S(1)}, f32[4,2,64,128]{3,2,1,0:T(8,128)S(1)}, u32[]{:S(2)}, u32[]{:S(2)}) collective-permute-start(f32[4,2,64,128]{3,2,1,0:T(8,128)S(1)} %get-tuple-element.54), channel_id=1, source_target_pairs={{0,1},{1,0},{2,3},{3,2},{4,5},{5,4},{6,7},{7,6},{8,9},{9,8},{10,11... | collective-permute-start | bytes 786440 | tf_op jit(solution)/shard_map/ppermute | solution.py:624
  14.8 4.8 %collective-permute-start.2 = (f32[4,2,64,128]{3,2,1,0:T(8,128)S(1)}, f32[4,2,64,128]{3,2,1,0:T(8,128)S(1)}, u32[]{:S(2)}, u32[]{:S(2)}) collective-permute-start(f32[4,2,64,128]{3,2,1,0:T(8,128)S(1)} %get-tuple-element.52), channel_id=1, source_target_pairs={{0,15},{1,2},{2,1},{3,4},{4,3},{5,6},{6,5},{7,8},{8,7},{9,10},{10,... | collective-permute-start | bytes 786440 | tf_op jit(solution)/shard_map/ppermute | solution.py:625
  19.6 0.0 collective-permute-done.3.of_core
  19.6 0.0 copy-done
  19.6 0.7 %shard_map.53 = (f32[2,2,2,80,128]{4,3,2,1,0:T(8,128)S(1)}, f32[2,4,2,80,128]{4,3,2,1,0:T(8,128)S(1)}, f32[2,2,2,80,128]{4,3,2,1,0:T(8,128)S(1)}, f32[16,128]{1,0:T(8,128)S(1)}) custom-call(f32[4,2,64,128]{3,2,1,0:T(8,128)S(1)} %collective-permute-done.3.of_core, f32[2,2,2,80,128]{4,3,2,1,0:T(8,128)S(1)} %get-tuple-element.51.state1_a.refs_10_, ...), custom_call_target="tpu_custom_call" | custom-call | flops 5898240 | bytes 4071424 | tf_op jit(solution)/shard_map/pallas_call | solution.py:604
  20.3 3.4 %collective-permute-done.2.of_chip = f32[4,2,64,128]{3,2,1,0:T(8,128)S(1)} collective-permute-done((f32[4,2,64,128]{3,2,1,0:T(8,128)S(1)}, f32[4,2,64,128]{3,2,1,0:T(8,128)S(1)}, u32[]{:S(2)}, u32[]{:S(2)}) %collective-permute-start.2) | collective-permute-done | bytes 262176 | tf_op jit(solution)/shard_map/ppermute | solution.py:625
  23.7 0.6 %shard_map.54 = (f32[2,2,2,80,128]{4,3,2,1,0:T(8,128)S(1)}, f32[2,2,2,80,128]{4,3,2,1,0:T(8,128)S(1)}, f32[2,2,2,80,128]{4,3,2,1,0:T(8,128)S(1)}, f32[8,2,72,128...) custom-call(f32[4,2,64,128]{3,2,1,0:T(8,128)S(1)} %collective-permute-done.2.of_chip, ...), custom_call_target="tpu_custom_call" | custom-call | flops 3932160 | bytes 6303744 | tf_op jit(solution)/shard_map/pallas_call | solution.py:604
  24.3 0.0 collective-permute-start.5
  24.3 4.5 %collective-permute-start.4 = (f32[8,2,64,128]{3,2,1,0:T(8,128)S(1)}, f32[8,2,64,128]{3,2,1,0:T(8,128)S(1)}, u32[]{:S(2)}, u32[]{:S(2)}) collective-permute-start(f32[8,2,64,128]{3,2,1,0:T(8,128)S(1)} %get-tuple-element.60), channel_id=1, source_target_pairs={{0,15},{1,2},{2,1},{3,4},{4,3},{5,6},{6,5},{7,8},{8,7},{9,10},{10,... | collective-permute-start | bytes 1572872 | tf_op jit(solution)/shard_map/ppermute | solution.py:625
  28.8 0.0 collective-permute-done.5.of_core
  28.8 0.1 collective-permute-start.6
  28.9 2.1 %shard_map.55 = (f32[2,5,2,80,128]{4,3,2,1,0:T(8,128)S(1)}, f32[2,1,2,80,128]{4,3,2,1,0:T(8,128)S(1)}, f32[2,3,2,80,128]{4,3,2,1,0:T(8,128)S(1)}, f32[2,3,2,64,1...) custom-call(f32[8,2,72,128]{3,2,1,0:T(8,128)S(1)} %collective-permut, ...), custom_call_target="tpu_custom_call" | custom-call | flops 7864320 | bytes 8708096 | tf_op jit(solution)/shard_map/pallas_call | solution.py:604
  31.0 4.7 %collective-permute-done.6 = f32[8,128]{1,0:T(8,128)S(1)} collective-permute-done((f32[8,128]{1,0:T(8,128)S(1)}, f32[8,128]{1,0:T(8,128)S(1)}, u32[]{:S(2)}, u32[]{:S(2)}) %collective-permute-start.6) | collective-permute-done | bytes 4128 | tf_op jit(solution)/shard_map/ppermute | solution.py:689
  35.6 1.6 %collective-permute-start.7 = (f32[8,128]{1,0:T(8,128)S(1)}, f32[8,128]{1,0:T(8,128)S(1)}, u32[]{:S(2)}, u32[]{:S(2)}) collective-permute-start(f32[8,128]{1,0:T(8,128)S(1)} %add.10), channel_id=1, source_target_pairs={{0,4},{1,5},{2,6},{3,7},{4,0},{5,1},{6,2},{7,3},{8,12},{9,13},{10,... | collective-permute-start | bytes 12296 | tf_op jit(solution)/shard_map/ppermute | solution.py:689
  37.2 2.0 %collective-permute-done.7 = f32[8,128]{1,0:T(8,128)S(1)} collective-permute-done((f32[8,128]{1,0:T(8,128)S(1)}, f32[8,128]{1,0:T(8,128)S(1)}, u32[]{:S(2)}, u32[]{:S(2)}) %collective-permute-start.7) | collective-permute-done | bytes 4128 | tf_op jit(solution)/shard_map/ppermute | solution.py:689
  39.3 0.0 collective-permute-start.8
  39.3 0.0 collective-permute-done.4.of_chip
  39.3 1.8 %shard_map.56 = f32[4,64,256]{2,1,0:T(8,128)} custom-call(f32[8,2,64,128]{3,2,1,0:T(8,128)S(1)} %collective-permute-done.4.of_chip, f32[1,2,80,128]{3,2,1,0:T(8,128)S(1)} %get-tuple-element.61.mob_high, f32[4,2,64,128]{3,2,1,0:T(8,128)S(1)} %get-tuple-element.45.mx_a.refs_0_, f32[4,2,80,128]{3,2,1,0:T(8,128)S(1)} %get-tuple-element.46.my_a.refs_1_, ...), custom_call_target="tpu_custom_call" | custom-call | flops 5898240 | bytes 8896512 | tf_op jit(solution)/shard_map/pallas_call | solution.py:604
  41.1 1.7 %collective-permute-done.8.far = f32[8,128]{1,0:T(8,128)S(1)} collective-permute-done((f32[8,128]{1,0:T(8,128)S(1)}, f32[8,128]{1,0:T(8,128)S(1)}, u32[]{:S(2)}, u32[]{:S(2)}) %collective-permute-start.8) | collective-permute-done | bytes 4128 | tf_op jit(solution)/shard_map/ppermute | solution.py:689
  42.9 0.6 %shard_map.57 = f32[1]{0:T(128)} custom-call(f32[8,128]{1,0:T(8,128)S(1)} %add.11.share, f32[8,128]{1,0:T(8,128)S(1)} %collective-permute-done.8.far), custom_call_target="tpu_custom_call" | custom-call | flops 1 | bytes 8196 | tf_op jit(solution)/shard_map/pallas_call | solution.py:604
  (3 shorter events, 0.0 us)
Async XLA Ops:
  0.6 1.0 %copy-start.1 = (f32[2,4,64,256]{3,2,1,0:T(8,128)S(1)}, f32[2,4,64,256]{3,2,1,0:T(8,128)}, u32[]{:S(2)}) copy-start(f32[2,4,64,256]{3,2,1,0:T(8,128)} %initial.1) | copy-start | bytes 1572868
  1.7 0.9 %copy-start.2 = (f32[4,64,256]{2,1,0:T(8,128)S(1)}, f32[4,64,256]{2,1,0:T(8,128)}, u32[]{:S(2)}) copy-start(f32[4,64,256]{2,1,0:T(8,128)} %mobility.1) | copy-start | bytes 786436
  2.7 6.2 %collective-permute-start.1 = (f32[5,2,64,128]{3,2,1,0:T(8,128)S(1)}, f32[5,2,64,128]{3,2,1,0:T(8,128)S(1)}, u32[]{:S(2)}, u32[]{:S(2)}) collective-permute-start(f32[5,2,64,128]{3,2,1,0:T(8,128)S(1)} %get-tuple-element.44), channel_id=1, source_target_pairs={{0,1},{1,0},{2,3},{3,2},{4,5},{5,4},{6,7},{7,6},{8,9},{9,8},{10,11... | collective-permute-start | bytes 983048 | tf_op jit(solution)/shard_map/ppermute | solution.py:624
  3.3 10.5 %collective-permute-start = (f32[5,2,64,128]{3,2,1,0:T(8,128)S(1)}, f32[5,2,64,128]{3,2,1,0:T(8,128)S(1)}, u32[]{:S(2)}, u32[]{:S(2)}) collective-permute-start(f32[5,2,64,128]{3,2,1,0:T(8,128)S(1)} %get-tuple-element.41), channel_id=1, source_target_pairs={{0,15},{1,2},{2,1},{3,4},{4,3},{5,6},{6,5},{7,8},{8,7},{9,10},{10,... | collective-permute-start | bytes 983048 | tf_op jit(solution)/shard_map/ppermute | solution.py:625
  13.8 5.8 %copy-start = (f32[2,4,64,256]{3,2,1,0:T(8,128)S(1)}, f32[2,4,64,256]{3,2,1,0:T(8,128)}, u32[]{:S(2)}) copy-start(f32[2,4,64,256]{3,2,1,0:T(8,128)} %observed.3) | copy-start | bytes 1572868
  14.3 5.3 %collective-permute-start.3 = (f32[4,2,64,128]{3,2,1,0:T(8,128)S(1)}, f32[4,2,64,128]{3,2,1,0:T(8,128)S(1)}, u32[]{:S(2)}, u32[]{:S(2)}) collective-permute-start(f32[4,2,64,128]{3,2,1,0:T(8,128)S(1)} %get-tuple-element.54), channel_id=1, source_target_pairs={{0,1},{1,0},{2,3},{3,2},{4,5},{5,4},{6,7},{7,6},{8,9},{9,8},{10,11... | collective-permute-start | bytes 786440 | tf_op jit(solution)/shard_map/ppermute | solution.py:624
  14.8 8.9 %collective-permute-start.2 = (f32[4,2,64,128]{3,2,1,0:T(8,128)S(1)}, f32[4,2,64,128]{3,2,1,0:T(8,128)S(1)}, u32[]{:S(2)}, u32[]{:S(2)}) collective-permute-start(f32[4,2,64,128]{3,2,1,0:T(8,128)S(1)} %get-tuple-element.52), channel_id=1, source_target_pairs={{0,15},{1,2},{2,1},{3,4},{4,3},{5,6},{6,5},{7,8},{8,7},{9,10},{10,... | collective-permute-start | bytes 786440 | tf_op jit(solution)/shard_map/ppermute | solution.py:625
  24.3 4.5 %collective-permute-start.5 = (f32[8,2,72,128]{3,2,1,0:T(8,128)S(1)}, f32[8,2,72,128]{3,2,1,0:T(8,128)S(1)}, u32[]{:S(2)}, u32[]{:S(2)}) collective-permute-start(f32[8,2,72,128]{3,2,1,0:T(8,128)S(1)} %get-tuple-element.67), channel_id=1, source_target_pairs={{0,1},{1,0},{2,3},{3,2},{4,5},{5,4},{6,7},{7,6},{8,9},{9,8},{10,11... | collective-permute-start | bytes 1769480 | tf_op jit(solution)/shard_map/ppermute | solution.py:624
  24.3 14.9 %collective-permute-start.4 = (f32[8,2,64,128]{3,2,1,0:T(8,128)S(1)}, f32[8,2,64,128]{3,2,1,0:T(8,128)S(1)}, u32[]{:S(2)}, u32[]{:S(2)}) collective-permute-start(f32[8,2,64,128]{3,2,1,0:T(8,128)S(1)} %get-tuple-element.60), channel_id=1, source_target_pairs={{0,15},{1,2},{2,1},{3,4},{4,3},{5,6},{6,5},{7,8},{8,7},{9,10},{10,... | collective-permute-start | bytes 1572872 | tf_op jit(solution)/shard_map/ppermute | solution.py:625
  28.8 6.8 %collective-permute-start.6 = (f32[8,128]{1,0:T(8,128)S(1)}, f32[8,128]{1,0:T(8,128)S(1)}, u32[]{:S(2)}, u32[]{:S(2)}) collective-permute-start(f32[8,128]{1,0:T(8,128)S(1)} %fusion.share_in), channel_id=1, source_target_pairs={{0,8},{1,9},{2,10},{3,11},{4,12},{5,13},{6,14},{7,15},{8,0},{9,1},... | collective-permute-start | bytes 12296 | tf_op jit(solution)/shard_map/ppermute | solution.py:689
  35.6 3.6 %collective-permute-start.7 = (f32[8,128]{1,0:T(8,128)S(1)}, f32[8,128]{1,0:T(8,128)S(1)}, u32[]{:S(2)}, u32[]{:S(2)}) collective-permute-start(f32[8,128]{1,0:T(8,128)S(1)} %add.10), channel_id=1, source_target_pairs={{0,4},{1,5},{2,6},{3,7},{4,0},{5,1},{6,2},{7,3},{8,12},{9,13},{10,... | collective-permute-start | bytes 12296 | tf_op jit(solution)/shard_map/ppermute | solution.py:689
  39.3 3.6 %collective-permute-start.8 = (f32[8,128]{1,0:T(8,128)S(1)}, f32[8,128]{1,0:T(8,128)S(1)}, u32[]{:S(2)}, u32[]{:S(2)}) collective-permute-start(f32[8,128]{1,0:T(8,128)S(1)} %add.11.share), channel_id=1, source_target_pairs={{0,2},{1,3},{2,0},{3,1},{4,6},{5,7},{6,4},{7,5},{8,10},{9,11},{10,... | collective-permute-start | bytes 12296 | tf_op jit(solution)/shard_map/ppermute | solution.py:689

commit v13 on v10

v13 whole, which is shorter than its diff:
```python
import functools
import math

import jax
import jax.numpy as jnp
from jax import lax
from jax.experimental import pallas as pl
from jax.experimental.pallas import tpu as pltpu
from jax.sharding import PartitionSpec as P

stiffness = 0.5
time_step = 0.005
VMEM = pl.BlockSpec(memory_space=pltpu.VMEM)
SMEM = pl.BlockSpec(memory_space=pltpu.SMEM)
LANES = 128
ROWS = 8
PAD = ROWS
CHUNK = 16


def chunks(ny):
    return range(0, ny, CHUNK)


def plain(ref, lead, row):
    return [
        ref[(*lead, pl.ds(row, CHUNK), pl.ds(at, LANES))] for at in range(0, ref.shape[-1], LANES)
    ]


def put_plain(ref, lead, row, value):
    for block, part in enumerate(value):
        ref[(*lead, pl.ds(row, CHUNK), pl.ds(block * LANES, LANES))] = part


def flat(ref, lead, row):
    return [ref[(*lead, block, pl.ds(row, CHUNK))] for block in range(ref.shape[-3])]


def put_flat(ref, lead, row, value):
    for block, part in enumerate(value):
        ref[(*lead, block, pl.ds(row, CHUNK))] = part


def padded(ref, lead, row, shift=0):
    return [ref[(*lead, block, pl.ds(PAD + row + shift, CHUNK))] for block in range(ref.shape[-3])]


def put_padded(ref, lead, row, value):
    ny = ref.shape[-2] - 2 * PAD
    for block, part in enumerate(value):
        ref[(*lead, block, pl.ds(PAD + row, CHUNK))] = part
        if row == 0:
            ref[(*lead, block, pl.ds(PAD + ny, 1))] = part[:1]
        if row + CHUNK == ny:
            ref[(*lead, block, pl.ds(PAD - 1, 1))] = part[CHUNK - 1 :]


def lane():
    return lax.broadcasted_iota(jnp.int32, (CHUNK, LANES), 1)


def after_z(value):
    turned = [pltpu.roll(part, LANES - 1, 1) for part in value]
    turned.append(turned[0])
    edge = lane() == LANES - 1
    return [jnp.where(edge, turned[at + 1], turned[at]) for at in range(len(value))]


def before_z(value):
    turned = [pltpu.roll(part, 1, 1) for part in value]
    edge = lane() == 0
    return [jnp.where(edge, turned[at - 1], turned[at]) for at in range(len(value))]


def side():
    return lax.rem(lax.axis_index("gx"), 2)


def either(first, second):
    return first + side() * (second - first)


class Line:
    def __init__(self, *parts):
        self.parts = parts

    def __call__(self, at, *lead):
        for ref, first, last in self.parts:
            if first <= at <= last:
                return ref, (*lead, at - first)
        raise IndexError(at)


def each(function, *values):
    return [function(*parts) for parts in zip(*values)]


def beside(low, high, up, down, mid):
    return each(
        lambda a, b, c, d, e, f: (a + b) + (c + d) + (e + f),
        low, high, up, down, after_z(mid), before_z(mid),
    )


def potential(low, mid, high, up, down):
    return each(
        lambda c, total: c * (c * c + (6.0 * stiffness - 1.0)) - stiffness * total,
        mid, beside(low, high, up, down, mid),
    )


class Faces:
    def __init__(self, mx, my, mz, mz_low, m_all):
        self.mx, self.my, self.mz, self.mz_low, self.all = mx, my, mz, mz_low, m_all

    def flow(self, row, at, mid, up, down, low=None, high=None):
        total = each(
            lambda a, b, c, d, e, u, v, w, x, y: (a * u + b * v) + (c * w + d * x) - e * y,
            padded(*self.my(at), row), padded(*self.my(at), row, -1), flat(*self.mz(at), row),
            flat(*self.mz_low(at), row), flat(*self.all(at), row), up, down, after_z(mid), before_z(mid), mid,
        )
        if low is not None:
            total = add_product(total, flat(*self.mx(at - 1), row), low)
        if high is not None:
            total = add_product(total, flat(*self.mx(at), row), high)
        return total


def add_product(total, a, b):
    return each(lambda t, x, y: t + x * y, total, a, b)


def sub(a, b):
    return each(lambda x, y: x - y, a, b)


def own_kernel(initial, mobility, conc, mob, to_chip, to_core):
    runs, n, ny, _ = initial.shape
    place = [either(n - 1 - at, at) for at in range(n)]

    def one_run(run, carry):
        for row in chunks(ny):
            for at in range(n):
                value = plain(initial, (run, place[at]), row)
                put_padded(conc, (run, at), row, value)
                if at < 2:
                    put_flat(to_core, (2 * run + at,), row, value)
                if at >= n - 2:
                    put_flat(to_chip, (2 * run + n - 1 - at,), row, value)
        return carry

    lax.fori_loop(0, runs, one_run, 0)
    for row in chunks(ny):
        for at in range(n):
            value = plain(mobility, (place[at],), row)
            put_padded(mob, (at,), row, value)
            if at == 0:
                put_flat(to_core, (2 * runs,), row, value)
            if at == n - 1:
                put_flat(to_chip, (2 * runs,), row, value)


def mean(a, b):
    return 0.5 * (a + b)


def put_faces(row, mob, places, my, mz, mz_low):
    for at in places:
        mid = padded(*mob(at), row)
        put_padded(*my(at), row, each(mean, mid, padded(*mob(at), row, 1)))
        put_flat(*mz(at), row, each(mean, mid, after_z(mid)))
        put_flat(*mz_low(at), row, each(mean, mid, before_z(mid)))


def put_all(row, faces, places):
    for at in places:
        put_flat(*faces.all(at), row, each(
            lambda a, b, c, d, e, f: (a + b) + (c + d) + (e + f),
            flat(*faces.mx(at - 1), row), flat(*faces.mx(at), row), padded(*faces.my(at), row),
            padded(*faces.my(at), row, -1), flat(*faces.mz(at), row), flat(*faces.mz_low(at), row),
        ))


def put_potential(row, field, run, places, target):
    mids = {at: padded(*field(at, run), row) for at in range(places[0] - 1, places[-1] + 2)}
    for at in places:
        value = potential(
            mids[at - 1], mids[at], mids[at + 1],
            padded(*field(at, run), row, 1), padded(*field(at, run), row, -1),
        )
        put_padded(*target(at, run), row, value)


def put_step(row, faces, chem, state, run, places, target):
    mids = {at: padded(*chem(at, run), row) for at in range(places[0] - 1, places[-1] + 2)}
    for at in places:
        flow = faces.flow(
            row, at, mids[at], padded(*chem(at, run), row, 1), padded(*chem(at, run), row, -1),
            mids[at - 1], mids[at + 1],
        )
        value = each(lambda a, b: a + time_step * b, padded(*state(at, run), row), flow)
        target(at, value)


def put_miss(row, runs, observed, place, run, at, value, adjoint2):
    miss = sub(value, plain(observed, (run, place[at]), row))
    adjoint = each(lambda a: a * (1.0 / runs), miss)
    put_padded(*adjoint2(at, run), row, adjoint)
    return adjoint, sum(part * part for part in miss)


def first_own_kernel(conc_own, mob_own, mx, my, mz, mz_low, m_all, chem0):
    runs, n = conc_own.shape[:2]
    ny = conc_own.shape[-2] - 2 * PAD
    mob = Line((mob_own, 0, n - 1))
    conc = Line((conc_own, 0, n - 1))
    faces = Faces(
        Line((mx, 0, n - 2)), Line((my, 0, n - 1)), Line((mz, 0, n - 1)), Line((mz_low, 0, n - 1)),
        Line((m_all, 1, n - 2)),
    )
    for row in chunks(ny):
        mids = [padded(*mob(at), row) for at in range(n)]
        for at in range(n - 1):
            put_flat(mx, (at,), row, each(mean, mids[at], mids[at + 1]))
        put_faces(row, mob, range(n), faces.my, faces.mz, faces.mz_low)
    for row in chunks(ny):
        put_all(row, faces, range(1, n - 1))

    def one_run(run, carry):
        for row in chunks(ny):
            put_potential(row, conc, run, range(1, n - 1), Line((chem0, 1, n - 2)))
        return carry

    lax.fori_loop(0, runs, one_run, 0)


def all_faces(n, refs):
    mx, my, mz, mz_low, m_all, mx_low, mx_high, all_low, all_high = refs
    return Faces(
        Line((mx_low, -1, -1), (mx, 0, n - 2), (mx_high, n - 1, n - 1)),
        Line((my, 0, n - 1)), Line((mz, 0, n - 1)), Line((mz_low, 0, n - 1)),
        Line((all_low, 0, 0), (m_all, 1, n - 2), (all_high, n - 1, n - 1)),
    )


def ends(n, low, own, high):
    return Line((low, -1, 0), (own, 1, n - 2), (high, n - 1, n))


def first_kernel(
    of_chip, of_core, conc_own, mob_own, chem0_own, mx, my, mz, mz_low, m_all,
    mob_low, mob_high, mx_low, mx_high, all_low, all_high, chem0_low, chem0_high, state1, to_chip, to_core,
    rim_low, rim_high,
):
    runs, n = conc_own.shape[:2]
    ny = of_chip.shape[-2]
    mob = Line((mob_low, -1, -1), (mob_own, 0, n - 1), (mob_high, n, n))
    conc = Line((rim_low, -2, -1), (conc_own, 0, n - 1), (rim_high, n, n + 1))
    faces = all_faces(n, (mx, my, mz, mz_low, m_all, mx_low, mx_high, all_low, all_high))
    chem = ends(n, chem0_low, chem0_own, chem0_high)
    for row in chunks(ny):
        put_padded(mob_low, (0,), row, flat(of_core, (2 * runs,), row))
        put_padded(mob_high, (0,), row, flat(of_chip, (2 * runs,), row))
        for at in (-1, n - 1):
            put_flat(*faces.mx(at), row, each(mean, padded(*mob(at), row), padded(*mob(at + 1), row)))
        put_all(row, faces, (0, n - 1))

    def one_run(run, carry):
        for row in chunks(ny):
            for at in range(2):
                put_padded(rim_low, (run, 1 - at), row, flat(of_core, (2 * run + at,), row))
                put_padded(rim_high, (run, at), row, flat(of_chip, (2 * run + at,), row))
        for row in chunks(ny):
            put_potential(row, conc, run, range(-1, 1), chem)
            put_potential(row, conc, run, range(n - 1, n + 1), chem)
        for row in chunks(ny):

            def target(at, value):
                put_padded(state1, (run, at), row, value)
                if at < 2:
                    put_flat(to_core, (2 * run + at,), row, value)
                if at >= n - 2:
                    put_flat(to_chip, (2 * run + n - 1 - at,), row, value)

            put_step(row, faces, chem, conc, run, range(n), target)
        return carry

    lax.fori_loop(0, runs, one_run, 0)


def second_own_kernel(state1, chem1):
    runs, n = state1.shape[:2]

    def one_run(run, carry):
        for row in chunks(state1.shape[-2] - 2 * PAD):
            put_potential(row, Line((state1, 0, n - 1)), run, range(1, n - 1), Line((chem1, 1, n - 2)))
        return carry

    lax.fori_loop(0, runs, one_run, 0)


def second_kernel(
    of_chip, of_core, state1_own, chem1_own, observed, mob, *refs,
):
    faces, refs = refs[:9], refs[9:]
    state1_low, state1_high, chem1_low, chem1_high, adjoint2, to_chip, to_core, share, total = refs
    runs, n, ny, _ = observed.shape
    faces = all_faces(n, faces)
    place = [either(n - 1 - at, at) for at in range(n)]
    state1 = Line((state1_low, -2, -1), (state1_own, 0, n - 1), (state1_high, n, n + 1))
    chem = ends(n, chem1_low, chem1_own, chem1_high)
    total[...] = jnp.zeros_like(total)

    def one_run(run, carry):
        for row in chunks(ny):
            for at in range(2):
                put_padded(state1_low, (run, 1 - at), row, flat(of_core, (2 * run + at,), row))
                put_padded(state1_high, (run, at), row, flat(of_chip, (2 * run + at,), row))
        for row in chunks(ny):
            put_potential(row, state1, run, range(-1, 1), chem)
            put_potential(row, state1, run, range(n - 1, n + 1), chem)
        for row in chunks(ny):
            squares = []

            def target(at, value):
                adjoint, square = put_miss(row, runs, observed, place, run, at, value, Line((adjoint2, 0, n - 1)))
                squares.append(square)
                if at < 3:
                    put_flat(to_core, (3 * run + at,), row, adjoint)
                if at >= n - 3:
                    put_flat(to_chip, (3 * run + n - 1 - at,), row, adjoint)

            put_step(row, faces, chem, state1, run, range(n), target)
            total[...] += sum(squares)
        return carry

    lax.fori_loop(0, runs, one_run, 0)
    for row in chunks(ny):
        for at in range(2):
            put_flat(to_chip, (3 * runs + at,), row, padded(mob, (n - 2 - at,), row))
            put_flat(to_core, (3 * runs + at,), row, padded(mob, (1 + at,), row))
    columns = (0.5 / runs) * jnp.sum(total[...], axis=0, keepdims=True)
    share[...] = jnp.broadcast_to(jnp.sum(columns, axis=1, keepdims=True), share.shape)


def put_adjoint1(row, flow, adjoint2, run, places, weight, target):
    mids = {at: padded(*flow(at, run), row) for at in range(places[0] - 1, places[-1] + 2)}
    for at in places:
        total = beside(
            mids[at - 1], mids[at + 1], padded(*flow(at, run), row, 1), padded(*flow(at, run), row, -1), mids[at]
        )
        value = each(
            lambda a, w, f, t: a + w * f - (time_step * stiffness) * t,
            padded(*adjoint2(at, run), row), weight(at), mids[at], total,
        )
        put_padded(*target(at, run), row, value)


def slope(state):
    return each(lambda c: time_step * (3.0 * c * c + (6.0 * stiffness - 1.0)), state)


def step_x(field, run, at, row):
    return sub(padded(*field(at + 1, run), row), padded(*field(at, run), row))


def step_y(field, run, at, row):
    return sub(padded(*field(at, run), row, 1), padded(*field(at, run), row))


def step_z(field, run, at, row):
    mid = padded(*field(at, run), row)
    return sub(after_z(mid), mid)


def third_own_kernel(
    adjoint2_own, state1_low, state1_own, state1_high, chem0_low, chem0_own, chem0_high,
    chem1_low, chem1_own, chem1_high, share, *refs,
):
    faces, refs = refs[:9], refs[9:]
    flow_own, weight, step_z0, sum_x, sum_y, sum_z, shares = refs
    runs, n = adjoint2_own.shape[:2]
    ny = weight.shape[-2]
    faces = all_faces(n, faces)
    state1 = Line((state1_low, -2, -1), (state1_own, 0, n - 1), (state1_high, n, n + 1))
    chem0 = ends(n, chem0_low, chem0_own, chem0_high)
    chem1 = ends(n, chem1_low, chem1_own, chem1_high)
    adjoint2 = Line((adjoint2_own, 0, n - 1))
    shares[...] = jnp.broadcast_to(share[:1][None], shares.shape)
    for sums in (sum_x, sum_y, sum_z):
        sums[...] = jnp.zeros_like(sums)

    def one_run(run, carry):
        for row in chunks(ny):
            mids = {at: padded(*adjoint2(at, run), row) for at in range(n)}
            for at in range(n):
                value = faces.flow(
                    row, at, mids[at], padded(*adjoint2(at, run), row, 1), padded(*adjoint2(at, run), row, -1),
                    mids.get(at - 1), mids.get(at + 1),
                )
                put_padded(flow_own, (run, at), row, value)
                put_flat(sum_y, (at,), row, add_product(
                    flat(sum_y, (at,), row), step_y(adjoint2, run, at, row), step_y(chem1, run, at, row)
                ))
                put_flat(sum_z, (at,), row, add_product(
                    flat(sum_z, (at,), row), step_z(adjoint2, run, at, row), step_z(chem1, run, at, row)
                ))
                put_flat(step_z0, (run, at), row, step_z(chem0, run, at, row))
            for at in range(n - 1):
                put_flat(sum_x, (at + 1,), row, add_product(
                    flat(sum_x, (at + 1,), row), sub(mids[at + 1], mids[at]), step_x(chem1, run, at, row)
                ))
            for at in range(-1, n + 1):
                put_flat(weight, (run, at + 1), row, slope(padded(*state1(at, run), row)))
        return carry

    lax.fori_loop(0, runs, one_run, 0)


def third_kernel(
    of_chip, of_core, shares, mob_low, mob_high, adjoint2_own, chem0_low, chem0_own, chem0_high,
    chem1_low, chem1_own, chem1_high, flow_own, weight, step_z0, sum_x_in, sum_y_in, sum_z_in, *refs,
):
    faces, refs = refs[:9], refs[9:]
    result, misfit, rim_low, rim_high, flow_low, flow_high, adjoint1, sum_x, sum_y, sum_z, m_low, m_high, *outer = refs
    runs = flow_own.shape[0]
    n, ny, _ = result.shape
    faces = all_faces(n, faces)
    for line, low, high, shift in zip(
        (faces.mx, faces.my, faces.mz, faces.mz_low, faces.all), outer[:5], outer[5:], (1, 0, 0, 0, 0)
    ):
        line.parts += ((low, -2 - shift, -1 - shift), (high, n, n + 1))
    place = [either(n - 1 - at, at) for at in range(n)]
    mob = Line((m_low, -3, -2), (mob_low, -1, -1), (mob_high, n, n), (m_high, n + 1, n + 2))
    chem0 = ends(n, chem0_low, chem0_own, chem0_high)
    chem1 = ends(n, chem1_low, chem1_own, chem1_high)
    adjoint2 = Line((rim_low, -3, -1), (adjoint2_own, 0, n - 1), (rim_high, n, n + 2))
    flow = Line((flow_low, -2, 0), (flow_high, n - 1, n + 1), (flow_own, 0, n - 1))
    misfit[0] = jnp.sum(shares[...], axis=0)[0, 0]
    for row in chunks(ny):
        for at in range(2):
            put_padded(m_low, (1 - at,), row, flat(of_core, (3 * runs + at,), row))
            put_padded(m_high, (at,), row, flat(of_chip, (3 * runs + at,), row))
    for row in chunks(ny):
        for first in (-3, n):
            mids = [padded(*mob(first + at), row) for at in range(3)]
            for at in range(2):
                put_flat(*faces.mx(first + at), row, each(mean, mids[at], mids[at + 1]))
        for first in (-2, n):
            put_faces(row, mob, range(first, first + 2), faces.my, faces.mz, faces.mz_low)
    for row in chunks(ny):
        put_all(row, faces, (-2, -1, n, n + 1))
    sum_x[...] = sum_x_in[...]
    sum_z[...] = sum_z_in[...]
    for row in chunks(ny):
        for at in range(n):
            put_padded(sum_y, (at,), row, flat(sum_y_in, (at,), row))

    def one_run(run, carry):
        for row in chunks(ny):
            for at in range(3):
                put_padded(rim_low, (run, 2 - at), row, flat(of_core, (3 * run + at,), row))
                put_padded(rim_high, (run, at), row, flat(of_chip, (3 * run + at,), row))
        for row in chunks(ny):
            mids = {at: padded(*adjoint2(at, run), row) for at in (-3, -2, -1, 0, n - 1, n, n + 1, n + 2)}
            for at in (-2, -1, n, n + 1):
                value = faces.flow(
                    row, at, mids[at], padded(*adjoint2(at, run), row, 1), padded(*adjoint2(at, run), row, -1),
                    mids[at - 1], mids[at + 1],
                )
                put_padded(*flow(at, run), row, value)
            for at, face, beyond in ((0, -1, -1), (n - 1, n - 1, n)):
                value = add_product(padded(flow_own, (run, at), row), flat(*faces.mx(face), row), mids[beyond])
                put_padded(*flow(at, run), row, value)
        for row in chunks(ny):
            put_adjoint1(
                row, flow, adjoint2, run, range(-1, n + 1),
                lambda at: flat(weight, (run, at + 1), row), Line((adjoint1, -1, n)),
            )
        adj1 = Line((adjoint1, -1, n))
        for row in chunks(ny):
            for at in range(-1, n):
                total = add_product(
                    flat(sum_x, (at + 1,), row), step_x(adj1, run, at, row), step_x(chem0, run, at, row)
                )
                if at in (-1, n - 1):
                    total = add_product(total, step_x(adjoint2, run, at, row), step_x(chem1, run, at, row))
                put_flat(sum_x, (at + 1,), row, total)
            for at in range(n):
                put_padded(sum_y, (at,), row, add_product(
                    padded(sum_y, (at,), row), step_y(adj1, run, at, row), step_y(chem0, run, at, row)
                ))
                put_flat(sum_z, (at,), row, add_product(
                    flat(sum_z, (at,), row), step_z(adj1, run, at, row), flat(step_z0, (run, at), row)
                ))
        return carry

    lax.fori_loop(0, runs, one_run, 0)
    for row in chunks(ny):
        for at in range(n):
            sides = flat(sum_z, (at,), row)
            value = each(
                lambda a, b, c, d, e, f: -0.5 * ((a + b) + (c + d) + (e + f)),
                flat(sum_x, (at,), row), flat(sum_x, (at + 1,), row),
                padded(sum_y, (at,), row), padded(sum_y, (at,), row, -1), sides, before_z(sides),
            )
            put_plain(result, (place[at],), row, value)


def call(kernel, outs, scratch, args, flops, scalar=None):
    moved = 4 * (sum(a.size for a in args) + sum(math.prod(o) for o in outs))
    return pl.pallas_call(
        kernel,
        out_shape=tuple(jax.ShapeDtypeStruct(o, jnp.float32) for o in outs),
        in_specs=[VMEM] * len(args),
        out_specs=tuple(SMEM if at == scalar else VMEM for at in range(len(outs))),
        scratch_shapes=[pltpu.VMEM(s, jnp.float32) for s in scratch],
        compiler_params=pltpu.CompilerParams(vmem_limit_bytes=16 * 1024 * 1024),
        cost_estimate=pl.CostEstimate(flops=flops, bytes_accessed=moved, transcendentals=0),
    )(*args)


def on_device(initial, observed, mobility):
    runs, n, ny, nz = initial.shape
    blocks = nz // LANES
    count = lax.axis_size("gx")
    over_chips = [(i, (i - 1 + 2 * (i % 2)) % count) for i in range(count)]
    over_cores = [(i, i ^ 1) for i in range(count)]
    cell = ny * nz

    def neighbours(to_chip, to_core):
        return lax.ppermute(to_chip, "gx", over_chips), lax.ppermute(to_core, "gx", over_cores)

    def lies(*lead):
        return (*lead, blocks, ny, LANES)

    def lies_padded(*lead):
        return (*lead, blocks, ny + 2 * PAD, LANES)

    conc, mob, to_chip, to_core = call(
        own_kernel,
        (
            lies_padded(runs, n), lies_padded(n), lies(2 * runs + 1), lies(2 * runs + 1),
        ),
        (),
        (initial, mobility),
        runs * n * cell,
    )
    of_chip, of_core = neighbours(to_chip, to_core)
    *faces, chem0_own = call(
        first_own_kernel,
        (lies(n - 1), lies_padded(n), lies(n), lies(n), lies(n - 2), lies_padded(runs, n - 2)),
        (),
        (conc, mob),
        15 * runs * n * cell,
    )
    mob_low, mob_high, *more_faces, chem0_low, chem0_high, state1, to_chip, to_core = call(
        first_kernel,
        (
            lies_padded(1), lies_padded(1), lies(1), lies(1), lies(1), lies(1),
            lies_padded(runs, 2), lies_padded(runs, 2), lies_padded(runs, n), lies(2 * runs), lies(2 * runs),
        ),
        (lies_padded(runs, 2), lies_padded(runs, 2)),
        (of_chip, of_core, conc, mob, chem0_own, *faces),
        30 * runs * (n + 4) * cell,
    )
    faces = (*faces, *more_faces)
    of_chip, of_core = neighbours(to_chip, to_core)
    (chem1_own,) = call(
        second_own_kernel, (lies_padded(runs, n - 2),), (), (state1,), 20 * runs * (n - 2) * cell
    )
    state1_low, state1_high, chem1_low, chem1_high, adjoint2, to_chip, to_core, share = call(
        second_kernel,
        (
            lies_padded(runs, 2), lies_padded(runs, 2), lies_padded(runs, 2), lies_padded(runs, 2),
            lies_padded(runs, n), lies(3 * runs + 2), lies(3 * runs + 2), (ROWS, LANES),
        ),
        ((CHUNK, LANES),),
        (of_chip, of_core, state1, chem1_own, observed, mob, *faces),
        30 * runs * (n + 4) * cell,
    )
    of_chip, of_core = neighbours(to_chip, to_core)
    potentials = (chem0_low, chem0_own, chem0_high, chem1_low, chem1_own, chem1_high)
    *done, shares = call(
        third_own_kernel,
        (
            lies_padded(runs, n), lies(runs, n + 2), lies(runs, n), lies(n + 1), lies(n), lies(n),
            (count, 1, LANES),
        ),
        (),
        (adjoint2, state1_low, state1, state1_high, *potentials, share, *faces),
        40 * runs * n * cell,
    )
    shares = lax.all_to_all(shares, "gx", 0, 0)
    outer = (lies(2), lies_padded(2), lies(2), lies(2), lies(2))
    return call(
        third_kernel,
        ((n, ny, nz), (1,)),
        (
            lies_padded(runs, 3), lies_padded(runs, 3), lies_padded(runs, 3), lies_padded(runs, 3),
            lies_padded(runs, n + 2), lies(n + 1), lies_padded(n), lies(n), lies_padded(2), lies_padded(2),
            *outer, *outer,
        ),
        (of_chip, of_core, shares, mob_low, mob_high, adjoint2, *potentials, *done, *faces),
        40 * runs * (n + 2) * cell,
        scalar=1,
    )


def solution(mesh):
    placed = (
        P("group", "gx", None, None),
        P("group", "gx", None, None),
        P(("group", "gx"), None, None),
    )
    return jax.shard_map(
        on_device,
        mesh=mesh,
        in_specs=placed,
        out_specs=(P(("group", "gx"), None, None), P("group")),
        check_vma=False,
    )
```

time: 63.9 us -> 42.1 us (0.66)
  local copies, waits for them, and re-layouts: 23.8 us -> 1.99 us
  blocking collectives: 0 us -> 9.9 us
  starting transfers between devices: 18.8 us -> 14.5 us
  waiting for transfers between devices: 11.1 us -> 8.25 us
  Pallas kernels: 8.66 us -> 6.6 us
    unnamed x70 -> x6, local copies, waits for them, and re-layouts: 23.8 us -> 1.99 us
    all_to_all x0 -> x1, blocking collectives: none -> 9.9 us  [on_device(): shares = lax.all_to_all(shares, 'gx', 0, 0)]
    all_to_all x1 -> x0, waiting for transfers between devices: 5.82 us -> none  [on_device(): shares = lax.all_to_all(shares, 'gx', 0, 0, axis_index_groups=sets)]
    all_to_all x1 -> x0, starting transfers between devices: 3.33 us -> none  [on_device(): shares = lax.all_to_all(shares, 'gx', 0, 0, axis_index_groups=sets)]
    ppermute x6, waiting for transfers between devices: 5.33 us -> 8.25 us  [the longest x3 8.25 us: neighbours(): lax.ppermute(to_chip, 'gx', over_chips)]
    pallas_call x6 -> x7, Pallas kernels: 8.66 us -> 6.6 us  [call(): pl.pallas_call(kernel, out_shape=tuple((jax.ShapeDtypeStruct(o, jnp.float...]
    ppermute x6, starting transfers between devices: 15.5 us -> 14.5 us  [the longest x3 14.5 us: neighbours(): lax.ppermute(to_chip, 'gx', over_chips)]
  transfers between devices with their start and end apart: 7 -> 6, of which waited for: 4 -> 2; matrix products, arithmetic and copies ran while one was open for 0% -> 0% of each run, Pallas kernels for 7% -> 5%
where the time goes in v13:
time: 42.1 us; the launch traced here: 41.9 us
  starting transfers between devices  14.5 us (34%)
  blocking collectives  9.9 us (24%)
  waiting for transfers between devices  8.25 us (20%)
  Pallas kernels  6.6 us (16%)
  local copies, waits for them, and re-layouts  1.99 us (5%)
  between operations  0.69 us (2%)
    ppermute x3, starting transfers between devices, neighbours(): lax.ppermute(to_chip, 'gx', over_chips)  14.5 us
    all_to_all x1, blocking collectives, on_device(): shares = lax.all_to_all(shares, 'gx', 0, 0)  9.9 us
    ppermute x3, waiting for transfers between devices, neighbours(): lax.ppermute(to_chip, 'gx', over_chips)  8.25 us
    pallas_call x7, Pallas kernels, call(): pl.pallas_call(kernel, out_shape=tuple((jax.ShapeDtypeStruct(o, jnp.float...  6.6 us
    unnamed x6, local copies, waits for them, and re-layouts  1.99 us
  transfers between devices with their start and end apart: 6, of which 2 were waited for; matrix products, arithmetic and copies ran while one was open for 0% of the time, Pallas kernels for 5%

profile of v13, /device:TPU:0, one launch (start us, length us, event | category | flops | bytes accessed | tf_op | source)
XLA Modules:
  0.0 41.9 jit_solution(6544078420063035815)
XLA Ops:
  0.6 0.0 copy-start
  0.6 1.0 %copy-done = f32[2,4,64,256]{3,2,1,0:T(8,128)S(1)} copy-done((f32[2,4,64,256]{3,2,1,0:T(8,128)S(1)}, f32[2,4,64,256]{3,2,1,0:T(8,128)}, u32[]{:S(2)}) %copy-start) | copy-done | bytes 524312
  1.7 0.0 copy-start.2
  1.7 0.9 %copy-done.2 = f32[4,64,256]{2,1,0:T(8,128)S(1)} copy-done((f32[4,64,256]{2,1,0:T(8,128)S(1)}, f32[4,64,256]{2,1,0:T(8,128)}, u32[]{:S(2)}) %copy-start.2) | copy-done | bytes 262168
  2.6 0.1 shard_map.50
  2.7 5.5 %collective-permute-start = (f32[5,2,64,128]{3,2,1,0:T(8,128)S(1)}, f32[5,2,64,128]{3,2,1,0:T(8,128)S(1)}, u32[]{:S(2)}, u32[]{:S(2)}) collective-permute-start(f32[5,2,64,128]{3,2,1,0:T(8,128)S(1)} %get-tuple-element.38), channel_id=1, source_target_pairs={{0,15},{1,2},{2,1},{3,4},{4,3},{5,6},{6,5},{7,8},{8,7},{9,10},{10,... | collective-permute-start | bytes 983048 | tf_op jit(solution)/shard_map/ppermute | solution.py:533
  8.2 0.0 collective-permute-start.1
  8.2 0.5 %shard_map.51 = (f32[3,2,64,128]{3,2,1,0:T(8,128)S(1)}, f32[4,2,80,128]{3,2,1,0:T(8,128)S(1)}, f32[4,2,64,128]{3,2,1,0:T(8,128)S(1)}, f32[4,2,64,128]{3,2,1,0:T(...) custom-call(f32[2,4,2,80,128]{4,3,2,1,0:T(8,128)S(1)} %get-tuple-element.40.conc_own, ...), custom_call_target="tpu_custom_call" | custom-call | flops 1966080 | bytes 2490368 | tf_op jit(solution)/shard_map/pallas_call | solution.py:513
  8.7 4.4 %collective-permute-done.of_chip = f32[5,2,64,128]{3,2,1,0:T(8,128)S(1)} collective-permute-done((f32[5,2,64,128]{3,2,1,0:T(8,128)S(1)}, f32[5,2,64,128]{3,2,1,0:T(8,128)S(1)}, u32[]{:S(2)}, u32[]{:S(2)}) %collective-permute-start) | collective-permute-done | bytes 327712 | tf_op jit(solution)/shard_map/ppermute | solution.py:533
  13.1 0.0 collective-permute-done.1.of_core
  13.1 0.9 %shard_map.52 = (f32[1,2,80,128]{3,2,1,0:T(8,128)S(1)}, f32[1,2,80,128]{3,2,1,0:T(8,128)S(1)}, f32[1,2,64,128]{3,2,1,0:T(8,128)S(1)}, f32[1,2,64,128]{3,2,1,0:T(...) custom-call(f32[5,2,64,128]{3,2,1,0:T(8,128)S(1)} %collective-permut, ...), custom_call_target="tpu_custom_call" | custom-call | flops 7864320 | bytes 5406720 | tf_op jit(solution)/shard_map/pallas_call | solution.py:513
  14.0 0.0 copy-start.1
  14.0 4.5 %collective-permute-start.2 = (f32[4,2,64,128]{3,2,1,0:T(8,128)S(1)}, f32[4,2,64,128]{3,2,1,0:T(8,128)S(1)}, u32[]{:S(2)}, u32[]{:S(2)}) collective-permute-start(f32[4,2,64,128]{3,2,1,0:T(8,128)S(1)} %get-tuple-element.48), channel_id=1, source_target_pairs={{0,15},{1,2},{2,1},{3,4},{4,3},{5,6},{6,5},{7,8},{8,7},{9,10},{10,... | collective-permute-start | bytes 786440 | tf_op jit(solution)/shard_map/ppermute | solution.py:533
  18.5 0.0 collective-permute-start.3
  18.5 0.3 shard_map.53.chem1_own
  18.8 3.9 %collective-permute-done.2.of_chip = f32[4,2,64,128]{3,2,1,0:T(8,128)S(1)} collective-permute-done((f32[4,2,64,128]{3,2,1,0:T(8,128)S(1)}, f32[4,2,64,128]{3,2,1,0:T(8,128)S(1)}, u32[]{:S(2)}, u32[]{:S(2)}) %collective-permute-start.2) | collective-permute-done | bytes 262176 | tf_op jit(solution)/shard_map/ppermute | solution.py:533
  22.7 0.0 collective-permute-done.3.of_core
  22.7 0.0 copy-done.1
  22.7 1.1 %shard_map.54 = (f32[2,2,2,80,128]{4,3,2,1,0:T(8,128)S(1)}, f32[2,2,2,80,128]{4,3,2,1,0:T(8,128)S(1)}, f32[2,2,2,80,128]{4,3,2,1,0:T(8,128)S(1)}, f32[2,2,2,80,1...) custom-call(f32[4,2,64,128]{3,2,1,0:T(8,128)S(1)} %collective-permut, ...), custom_call_target="tpu_custom_call" | custom-call | flops 7864320 | bytes 6819840 | tf_op jit(solution)/shard_map/pallas_call | solution.py:513
  23.8 4.4 %collective-permute-start.4 = (f32[8,2,64,128]{3,2,1,0:T(8,128)S(1)}, f32[8,2,64,128]{3,2,1,0:T(8,128)S(1)}, u32[]{:S(2)}, u32[]{:S(2)}) collective-permute-start(f32[8,2,64,128]{3,2,1,0:T(8,128)S(1)} %get-tuple-element.55), channel_id=1, source_target_pairs={{0,15},{1,2},{2,1},{3,4},{4,3},{5,6},{6,5},{7,8},{8,7},{9,10},{10,... | collective-permute-start | bytes 1572872 | tf_op jit(solution)/shard_map/ppermute | solution.py:533
  28.3 0.0 collective-permute-start.5
  28.3 1.2 %shard_map.55 = (f32[2,4,2,80,128]{4,3,2,1,0:T(8,128)S(1)}, f32[2,6,2,64,128]{4,3,2,1,0:T(8,128)S(1)}, f32[2,4,2,64,128]{4,3,2,1,0:T(8,128)S(1)}, f32[5,2,64,128...) custom-call(f32[2,4,2,80,128]{4,3,2,1,0:T(8,128)S(1)} %get-tuple-ele, ...), custom_call_target="tpu_custom_call" | custom-call | flops 5242880 | bytes 8204288 | tf_op jit(solution)/shard_map/pallas_call | solution.py:513
  29.4 9.9 %all_to_all.5.shares = f32[16,1,128]{2,1,0:T(1,128)S(1)} all-to-all(f32[16,1,128]{2,1,0:T(1,128)S(1)} %get-tuple-element.65), channel_id=1, replica_groups=mesh['group'=2,'gx'=16] {'gx'}, dimensions={0} | all-to-all | bytes 16384 | tf_op jit(solution)/shard_map/all_to_all | solution.py:595
  39.3 0.0 collective-permute-done.4.of_chip
  39.3 0.0 collective-permute-done.5.of_core
  39.3 2.6 %shard_map.56 = (f32[4,64,256]{2,1,0:T(8,128)}, f32[1]{0:T(128)}) custom-call(f32[8,2,64,128]{3,2,1,0:T(8,128)S(1)} %collective-permute-done.4.of_chip, f32[8,2,64,128]{3,2,1,0:T(8,128)S(1)} %collective-permute-done.5.of_core, f32[16,1,128]{2,1,0:T(1,128)S(1)} %all_to_all.5.shares, f32[1,2,80,128]{3,2,1,0:T(8,128)S(1)} %get-tuple-element.66.mob_low, ...), custom_call_target="tpu_custom_call" | custom-call | flops 7864320 | bytes 8364036 | tf_op jit(solution)/shard_map/pallas_call | solution.py:513
Async XLA Ops:
  0.6 1.0 %copy-start = (f32[2,4,64,256]{3,2,1,0:T(8,128)S(1)}, f32[2,4,64,256]{3,2,1,0:T(8,128)}, u32[]{:S(2)}) copy-start(f32[2,4,64,256]{3,2,1,0:T(8,128)} %initial.1) | copy-start | bytes 1572868
  1.7 0.9 %copy-start.2 = (f32[4,64,256]{2,1,0:T(8,128)S(1)}, f32[4,64,256]{2,1,0:T(8,128)}, u32[]{:S(2)}) copy-start(f32[4,64,256]{2,1,0:T(8,128)} %mobility.1) | copy-start | bytes 786436
  2.7 10.4 %collective-permute-start = (f32[5,2,64,128]{3,2,1,0:T(8,128)S(1)}, f32[5,2,64,128]{3,2,1,0:T(8,128)S(1)}, u32[]{:S(2)}, u32[]{:S(2)}) collective-permute-start(f32[5,2,64,128]{3,2,1,0:T(8,128)S(1)} %get-tuple-element.38), channel_id=1, source_target_pairs={{0,15},{1,2},{2,1},{3,4},{4,3},{5,6},{6,5},{7,8},{8,7},{9,10},{10,... | collective-permute-start | bytes 983048 | tf_op jit(solution)/shard_map/ppermute | solution.py:533
  8.2 4.9 %collective-permute-start.1 = (f32[5,2,64,128]{3,2,1,0:T(8,128)S(1)}, f32[5,2,64,128]{3,2,1,0:T(8,128)S(1)}, u32[]{:S(2)}, u32[]{:S(2)}) collective-permute-start(f32[5,2,64,128]{3,2,1,0:T(8,128)S(1)} %get-tuple-element.39), channel_id=1, source_target_pairs={{0,1},{1,0},{2,3},{3,2},{4,5},{5,4},{6,7},{7,6},{8,9},{9,8},{10,11... | collective-permute-start | bytes 983048 | tf_op jit(solution)/shard_map/ppermute | solution.py:533
  14.0 8.7 %copy-start.1 = (f32[2,4,64,256]{3,2,1,0:T(8,128)S(1)}, f32[2,4,64,256]{3,2,1,0:T(8,128)}, u32[]{:S(2)}) copy-start(f32[2,4,64,256]{3,2,1,0:T(8,128)} %observed.1) | copy-start | bytes 1572868
  14.0 8.7 %collective-permute-start.2 = (f32[4,2,64,128]{3,2,1,0:T(8,128)S(1)}, f32[4,2,64,128]{3,2,1,0:T(8,128)S(1)}, u32[]{:S(2)}, u32[]{:S(2)}) collective-permute-start(f32[4,2,64,128]{3,2,1,0:T(8,128)S(1)} %get-tuple-element.48), channel_id=1, source_target_pairs={{0,15},{1,2},{2,1},{3,4},{4,3},{5,6},{6,5},{7,8},{8,7},{9,10},{10,... | collective-permute-start | bytes 786440 | tf_op jit(solution)/shard_map/ppermute | solution.py:533
  18.5 4.2 %collective-permute-start.3 = (f32[4,2,64,128]{3,2,1,0:T(8,128)S(1)}, f32[4,2,64,128]{3,2,1,0:T(8,128)S(1)}, u32[]{:S(2)}, u32[]{:S(2)}) collective-permute-start(f32[4,2,64,128]{3,2,1,0:T(8,128)S(1)} %get-tuple-element.49), channel_id=1, source_target_pairs={{0,1},{1,0},{2,3},{3,2},{4,5},{5,4},{6,7},{7,6},{8,9},{9,8},{10,11... | collective-permute-start | bytes 786440 | tf_op jit(solution)/shard_map/ppermute | solution.py:533
  23.8 15.5 %collective-permute-start.4 = (f32[8,2,64,128]{3,2,1,0:T(8,128)S(1)}, f32[8,2,64,128]{3,2,1,0:T(8,128)S(1)}, u32[]{:S(2)}, u32[]{:S(2)}) collective-permute-start(f32[8,2,64,128]{3,2,1,0:T(8,128)S(1)} %get-tuple-element.55), channel_id=1, source_target_pairs={{0,15},{1,2},{2,1},{3,4},{4,3},{5,6},{6,5},{7,8},{8,7},{9,10},{10,... | collective-permute-start | bytes 1572872 | tf_op jit(solution)/shard_map/ppermute | solution.py:533
  28.3 11.1 %collective-permute-start.5 = (f32[8,2,64,128]{3,2,1,0:T(8,128)S(1)}, f32[8,2,64,128]{3,2,1,0:T(8,128)S(1)}, u32[]{:S(2)}, u32[]{:S(2)}) collective-permute-start(f32[8,2,64,128]{3,2,1,0:T(8,128)S(1)} %get-tuple-element.56), channel_id=1, source_target_pairs={{0,1},{1,0},{2,3},{3,2},{4,5},{5,4},{6,7},{7,6},{8,9},{9,8},{10,11... | collective-permute-start | bytes 1572872 | tf_op jit(solution)/shard_map/ppermute | solution.py:533

commit v14 on v11

--- a/solution.py
+++ b/solution.py
@@ -609,7 +609,7 @@
 
     def hop(value, bit):
         apart = 3 if bit == 0 else 2 << bit
-        return lax.ppermute(value, "gx", [(at, at ^ apart) for at in range(count) if counts(at)])
+        return lax.ppermute(value, "gx", [(at, at ^ apart * counts(at)) for at in range(count)])
 
     share = share + of_core[0, 0, 0, ny:]
     far = hop(share, bits[-1])

time: 43.6 us -> 43.6 us (level)
  no operation moved by 1% of the time
where the time goes in v14:
time: 43.6 us; the launch traced here: 43.3 us
  starting transfers between devices  27.6 us (63%)
  Pallas kernels  7.74 us (18%)
  waiting for transfers between devices  5.16 us (12%)
  local copies, waits for them, and re-layouts  2.03 us (5%)
  between operations  0.75 us (2%)
    ppermute x3, starting transfers between devices, neighbours(): return (lax.ppermute(to_chip, 'gx', over_chips), of_core)  11.1 us
    ppermute x1, starting transfers between devices, on_device(): handed = lax.ppermute(share, 'gx', over_cores)  10.2 us
    pallas_call x7, Pallas kernels, call(): pl.pallas_call(kernel, out_shape=tuple((jax.ShapeDtypeStruct(o, jnp.float...  7.74 us
    ppermute x3, starting transfers between devices, neighbours(): of_core = lax.ppermute(to_core, 'gx', over_cores)  4.37 us
    ppermute x3, waiting for transfers between devices, neighbours(): return (lax.ppermute(to_chip, 'gx', over_chips), of_core)  4.32 us
    unnamed x6, local copies, waits for them, and re-layouts  2.03 us
    ppermute x3, starting transfers between devices, hop(): lax.ppermute(value, 'gx', [(at, at ^ apart * counts(at)) for at in range(...  1.97 us
  transfers between devices with their start and end apart: 10, of which 3 were waited for; matrix products, arithmetic and copies ran while one was open for 0% of the time, Pallas kernels for 14%

profile of v14, /device:TPU:0, one launch (start us, length us, event | category | flops | bytes accessed | tf_op | source)
XLA Modules:
  0.0 43.3 jit_solution(8447185185875236468)
XLA Ops:
  0.6 0.5 %collective-permute-start.2 = (f32[2,4,64,256]{3,2,1,0:T(8,128)}, f32[2,4,64,256]{3,2,1,0:T(8,128)S(1)}, u32[]{:S(2)}, u32[]{:S(2)}) collective-permute-start(f32[2,4,64,256]{3,2,1,0:T(8,128)} %initial.1), channel_id=1, source_target_pairs={{0,1},{1,0},{2,3},{3,2},{4,5},{5,4},{6,7},{7,6},{8,9},{9,8},{10,11... | collective-permute-start | bytes 1572872 | tf_op jit(solution)/shard_map/ppermute | solution.py:556
  1.1 5.7 %collective-permute-start.1 = (f32[2,4,64,256]{3,2,1,0:T(8,128)}, f32[2,4,64,256]{3,2,1,0:T(8,128)S(1)}, u32[]{:S(2)}, u32[]{:S(2)}) collective-permute-start(f32[2,4,64,256]{3,2,1,0:T(8,128)} %initial.1), channel_id=1, source_target_pairs={{0,15},{1,2},{2,1},{3,4},{4,3},{5,6},{6,5},{7,8},{8,7},{9,10},{10,... | collective-permute-start | bytes 1572872 | tf_op jit(solution)/shard_map/ppermute | solution.py:557
  6.8 0.0 copy-start.1
  6.8 1.1 %copy-done.1 = f32[2,4,64,256]{3,2,1,0:T(8,128)S(1)} copy-done((f32[2,4,64,256]{3,2,1,0:T(8,128)S(1)}, f32[2,4,64,256]{3,2,1,0:T(8,128)}, u32[]{:S(2)}) %copy-start.1) | copy-done | bytes 524312
  7.9 0.0 copy-start.2
  7.9 0.9 %copy-done.2 = f32[4,64,256]{2,1,0:T(8,128)S(1)} copy-done((f32[4,64,256]{2,1,0:T(8,128)S(1)}, f32[4,64,256]{2,1,0:T(8,128)}, u32[]{:S(2)}) %copy-start.2) | copy-done | bytes 262168
  8.8 0.1 shard_map.50
  8.9 0.1 collective-permute-start.3
  9.0 0.6 %collective-permute-start = (f32[3,2,64,128]{3,2,1,0:T(8,128)S(1)}, f32[3,2,64,128]{3,2,1,0:T(8,128)S(1)}, u32[]{:S(2)}, u32[]{:S(2)}) collective-permute-start(f32[3,2,64,128]{3,2,1,0:T(8,128)S(1)} %get-tuple-element.40), channel_id=1, source_target_pairs={{0,15},{1,2},{2,1},{3,4},{4,3},{5,6},{6,5},{7,8},{8,7},{9,10},{10,... | collective-permute-start | bytes 589832 | tf_op jit(solution)/shard_map/ppermute | solution.py:557
  9.6 0.8 %collective-permute-done.3.m_core = f32[3,2,64,128]{3,2,1,0:T(8,128)S(1)} collective-permute-done((f32[3,2,64,128]{3,2,1,0:T(8,128)S(1)}, f32[3,2,64,128]{3,2,1,0:T(8,128)S(1)}, u32[]{:S(2)}, u32[]{:S(2)}) %collective-permute-start.3) | collective-permute-done | bytes 196640 | tf_op jit(solution)/shard_map/ppermute | solution.py:556
  10.4 0.0 collective-permute-done.2.of_core
  10.4 0.0 copy-start
  10.5 0.9 %shard_map.51 = (f32[2,4,2,80,128]{4,3,2,1,0:T(8,128)S(1)}, f32[2,6,2,80,128]{4,3,2,1,0:T(8,128)S(1)}, f32[6,2,64,128]{3,2,1,0:T(8,128)S(1)}, f32[6,2,80,128]{3,...) custom-call(f32[2,4,64,256]{3,2,1,0:T(8,128)S(1)} %collective-permut, ...), custom_call_target="tpu_custom_call" | custom-call | flops 3932160 | bytes 5341184 | tf_op jit(solution)/shard_map/pallas_call | solution.py:536
  11.3 2.7 %collective-permute-done.1.of_chip = f32[2,4,64,256]{3,2,1,0:T(8,128)S(1)} collective-permute-done((f32[2,4,64,256]{3,2,1,0:T(8,128)}, f32[2,4,64,256]{3,2,1,0:T(8,128)S(1)}, u32[]{:S(2)}, u32[]{:S(2)}) %collective-permute-start.1) | collective-permute-done | bytes 524320 | tf_op jit(solution)/shard_map/ppermute | solution.py:557
  14.0 0.0 copy-done
  14.0 1.3 %shard_map.52 = (f32[2,4,2,80,128]{4,3,2,1,0:T(8,128)S(1)}, f32[2,4,2,80,128]{4,3,2,1,0:T(8,128)S(1)}, f32[2,5,2,80,128]{4,3,2,1,0:T(8,128)S(1)}, f32[2,3,2,80,1...) custom-call(f32[2,4,64,256]{3,2,1,0:T(8,128)S(1)} %collective-permute-done.1.of_chip, ...), custom_call_target="tpu_custom_call" | custom-call | flops 5898240 | bytes 8134656 | tf_op jit(solution)/shard_map/pallas_call | solution.py:536
  15.3 1.7 %collective-permute-done.m_chip = f32[3,2,64,128]{3,2,1,0:T(8,128)S(1)} collective-permute-done((f32[3,2,64,128]{3,2,1,0:T(8,128)S(1)}, f32[3,2,64,128]{3,2,1,0:T(8,128)S(1)}, u32[]{:S(2)}, u32[]{:S(2)}) %collective-permute-start) | collective-permute-done | bytes 196640 | tf_op jit(solution)/shard_map/ppermute | solution.py:557
  17.0 1.3 %shard_map.53 = (f32[3,2,64,128]{3,2,1,0:T(8,128)S(1)}, f32[2,2,80,128]{3,2,1,0:T(8,128)S(1)}, f32[2,2,64,128]{3,2,1,0:T(8,128)S(1)}, f32[2,2,64,128]{3,2,1,0:T(...) custom-call(f32[3,2,64,128]{3,2,1,0:T(8,128)S(1)} %collective-permut, ...), custom_call_target="tpu_custom_call" | custom-call | flops 5898240 | bytes 10612736 | tf_op jit(solution)/shard_map/pallas_call | solution.py:536
  18.3 3.8 %collective-permute-start.5 = (f32[2,3,2,72,128]{4,3,2,1,0:T(8,128)S(1)}, f32[2,3,2,72,128]{4,3,2,1,0:T(8,128)S(1)}, u32[]{:S(2)}, u32[]{:S(2)}) collective-permute-start(f32[2,3,2,72,128]{4,3,2,1,0:T(8,128)S(1)} %get-tuple-element.65), channel_id=1, source_target_pairs={{0,1},{1,0},{2,3},{3,2},{4,5},{5,4},{6,7},{7,6},{8,9},{9,8},{10,11... | collective-permute-start | bytes 1327112 | tf_op jit(solution)/shard_map/ppermute | solution.py:556
  22.1 4.8 %collective-permute-start.4 = (f32[2,3,2,64,128]{4,3,2,1,0:T(8,128)S(1)}, f32[2,3,2,64,128]{4,3,2,1,0:T(8,128)S(1)}, u32[]{:S(2)}, u32[]{:S(2)}) collective-permute-start(f32[2,3,2,64,128]{4,3,2,1,0:T(8,128)S(1)} %get-tuple-element.57), channel_id=1, source_target_pairs={{0,15},{1,2},{2,1},{3,4},{4,3},{5,6},{6,5},{7,8},{8,7},{9,10},{10,... | collective-permute-start | bytes 1179656 | tf_op jit(solution)/shard_map/ppermute | solution.py:557
  26.8 0.0 collective-permute-done.5.of_core
  26.8 0.7 %collective-permute-start.6 = (f32[8,128]{1,0:T(8,128)S(1)}, f32[8,128]{1,0:T(8,128)S(1)}, u32[]{:S(2)}, u32[]{:S(2)}) collective-permute-start(f32[8,128]{1,0:T(8,128)S(1)} %fusion.share_in), channel_id=1, source_target_pairs={{0,0},{1,9},{2,10},{3,3},{4,4},{5,13},{6,14},{7,7},{8,8},{9,1},{10... | collective-permute-start | bytes 12296 | tf_op jit(solution)/shard_map/ppermute | solution.py:612
  27.5 2.0 %shard_map.54 = (f32[2,5,2,80,128]{4,3,2,1,0:T(8,128)S(1)}, f32[2,1,2,80,128]{4,3,2,1,0:T(8,128)S(1)}, f32[2,3,2,80,128]{4,3,2,1,0:T(8,128)S(1)}, f32[2,3,2,64,1...) custom-call(f32[2,3,2,72,128]{4,3,2,1,0:T(8,128)S(1)} %collective-pe, ...), custom_call_target="tpu_custom_call" | custom-call | flops 7864320 | bytes 10510336 | tf_op jit(solution)/shard_map/pallas_call | solution.py:536
  29.5 0.0 collective-permute-done.6
  29.5 0.7 %collective-permute-start.7 = (f32[8,128]{1,0:T(8,128)S(1)}, f32[8,128]{1,0:T(8,128)S(1)}, u32[]{:S(2)}, u32[]{:S(2)}) collective-permute-start(f32[8,128]{1,0:T(8,128)S(1)} %add.13), channel_id=1, source_target_pairs={{0,0},{1,5},{2,6},{3,3},{4,4},{5,1},{6,2},{7,7},{8,8},{9,13},{10,1... | collective-permute-start | bytes 12296 | tf_op jit(solution)/shard_map/ppermute | solution.py:612
  30.2 0.0 collective-permute-done.7
  30.2 0.7 %collective-permute-start.8 = (f32[8,128]{1,0:T(8,128)S(1)}, f32[8,128]{1,0:T(8,128)S(1)}, u32[]{:S(2)}, u32[]{:S(2)}) collective-permute-start(f32[8,128]{1,0:T(8,128)S(1)} %add.14), channel_id=1, source_target_pairs={{0,0},{1,2},{2,1},{3,3},{4,4},{5,6},{6,5},{7,7},{8,8},{9,10},{10,9... | collective-permute-start | bytes 12296 | tf_op jit(solution)/shard_map/ppermute | solution.py:612
  30.9 0.0 collective-permute-done.8
  30.9 10.2 %collective-permute-start.9 = (f32[8,128]{1,0:T(8,128)S(1)}, f32[8,128]{1,0:T(8,128)S(1)}, u32[]{:S(2)}, u32[]{:S(2)}) collective-permute-start(f32[8,128]{1,0:T(8,128)S(1)} %add.15.total), channel_id=1, source_target_pairs={{0,1},{1,0},{2,3},{3,2},{4,5},{5,4},{6,7},{7,6},{8,9},{9,8},{10,11... | collective-permute-start | bytes 12296 | tf_op jit(solution)/shard_map/ppermute | solution.py:630
  41.1 0.0 collective-permute-done.4.of_chip
  41.1 1.7 %shard_map.55 = f32[4,64,256]{2,1,0:T(8,128)} custom-call(f32[2,3,2,64,128]{4,3,2,1,0:T(8,128)S(1)} %collective-permute-done.4.of_chip, f32[6,2,64,128]{3,2,1,0:T(8,128)S(1)} %get-tuple-element.46.mx.mx_a, f32[6,2,80,128]{3,2,1,0:T(8,128)S(1)} %get-tuple-element.47.my.my_a, f32[6,2,64,128]{3,2,1,0:T(8,128)S(1)} %get-tuple-element.48.mz.mz_a, ...), custom_call_target="tpu_custom_call" | custom-call | flops 5898240 | bytes 8749056 | tf_op jit(solution)/shard_map/pallas_call | solution.py:536
  42.8 0.0 collective-permute-done.9.handed
  42.8 0.6 %shard_map.56 = f32[1]{0:T(128)} custom-call(f32[8,128]{1,0:T(8,128)S(1)} %add.15.total, f32[8,128]{1,0:T(8,128)S(1)} %collective-permute-done.9.handed), custom_call_target="tpu_custom_call" | custom-call | flops 1 | bytes 8196 | tf_op jit(solution)/shard_map/pallas_call | solution.py:536
  (4 shorter events, 0.0 us)
Async XLA Ops:
  0.6 9.8 %collective-permute-start.2 = (f32[2,4,64,256]{3,2,1,0:T(8,128)}, f32[2,4,64,256]{3,2,1,0:T(8,128)S(1)}, u32[]{:S(2)}, u32[]{:S(2)}) collective-permute-start(f32[2,4,64,256]{3,2,1,0:T(8,128)} %initial.1), channel_id=1, source_target_pairs={{0,1},{1,0},{2,3},{3,2},{4,5},{5,4},{6,7},{7,6},{8,9},{9,8},{10,11... | collective-permute-start | bytes 1572872 | tf_op jit(solution)/shard_map/ppermute | solution.py:556
  1.1 12.8 %collective-permute-start.1 = (f32[2,4,64,256]{3,2,1,0:T(8,128)}, f32[2,4,64,256]{3,2,1,0:T(8,128)S(1)}, u32[]{:S(2)}, u32[]{:S(2)}) collective-permute-start(f32[2,4,64,256]{3,2,1,0:T(8,128)} %initial.1), channel_id=1, source_target_pairs={{0,15},{1,2},{2,1},{3,4},{4,3},{5,6},{6,5},{7,8},{8,7},{9,10},{10,... | collective-permute-start | bytes 1572872 | tf_op jit(solution)/shard_map/ppermute | solution.py:557
  6.8 1.1 %copy-start.1 = (f32[2,4,64,256]{3,2,1,0:T(8,128)S(1)}, f32[2,4,64,256]{3,2,1,0:T(8,128)}, u32[]{:S(2)}) copy-start(f32[2,4,64,256]{3,2,1,0:T(8,128)} %initial.1) | copy-start | bytes 1572868
  7.9 0.9 %copy-start.2 = (f32[4,64,256]{2,1,0:T(8,128)S(1)}, f32[4,64,256]{2,1,0:T(8,128)}, u32[]{:S(2)}) copy-start(f32[4,64,256]{2,1,0:T(8,128)} %mobility.1) | copy-start | bytes 786436
  8.9 1.5 %collective-permute-start.3 = (f32[3,2,64,128]{3,2,1,0:T(8,128)S(1)}, f32[3,2,64,128]{3,2,1,0:T(8,128)S(1)}, u32[]{:S(2)}, u32[]{:S(2)}) collective-permute-start(f32[3,2,64,128]{3,2,1,0:T(8,128)S(1)} %get-tuple-element.43), channel_id=1, source_target_pairs={{0,1},{1,0},{2,3},{3,2},{4,5},{5,4},{6,7},{7,6},{8,9},{9,8},{10,11... | collective-permute-start | bytes 589832 | tf_op jit(solution)/shard_map/ppermute | solution.py:556
  9.0 8.0 %collective-permute-start = (f32[3,2,64,128]{3,2,1,0:T(8,128)S(1)}, f32[3,2,64,128]{3,2,1,0:T(8,128)S(1)}, u32[]{:S(2)}, u32[]{:S(2)}) collective-permute-start(f32[3,2,64,128]{3,2,1,0:T(8,128)S(1)} %get-tuple-element.40), channel_id=1, source_target_pairs={{0,15},{1,2},{2,1},{3,4},{4,3},{5,6},{6,5},{7,8},{8,7},{9,10},{10,... | collective-permute-start | bytes 589832 | tf_op jit(solution)/shard_map/ppermute | solution.py:557
  10.4 3.6 %copy-start = (f32[2,4,64,256]{3,2,1,0:T(8,128)S(1)}, f32[2,4,64,256]{3,2,1,0:T(8,128)}, u32[]{:S(2)}) copy-start(f32[2,4,64,256]{3,2,1,0:T(8,128)} %observed.3) | copy-start | bytes 1572868
  18.3 8.6 %collective-permute-start.5 = (f32[2,3,2,72,128]{4,3,2,1,0:T(8,128)S(1)}, f32[2,3,2,72,128]{4,3,2,1,0:T(8,128)S(1)}, u32[]{:S(2)}, u32[]{:S(2)}) collective-permute-start(f32[2,3,2,72,128]{4,3,2,1,0:T(8,128)S(1)} %get-tuple-element.65), channel_id=1, source_target_pairs={{0,1},{1,0},{2,3},{3,2},{4,5},{5,4},{6,7},{7,6},{8,9},{9,8},{10,11... | collective-permute-start | bytes 1327112 | tf_op jit(solution)/shard_map/ppermute | solution.py:556
  22.1 19.1 %collective-permute-start.4 = (f32[2,3,2,64,128]{4,3,2,1,0:T(8,128)S(1)}, f32[2,3,2,64,128]{4,3,2,1,0:T(8,128)S(1)}, u32[]{:S(2)}, u32[]{:S(2)}) collective-permute-start(f32[2,3,2,64,128]{4,3,2,1,0:T(8,128)S(1)} %get-tuple-element.57), channel_id=1, source_target_pairs={{0,15},{1,2},{2,1},{3,4},{4,3},{5,6},{6,5},{7,8},{8,7},{9,10},{10,... | collective-permute-start | bytes 1179656 | tf_op jit(solution)/shard_map/ppermute | solution.py:557
  26.8 2.6 %collective-permute-start.6 = (f32[8,128]{1,0:T(8,128)S(1)}, f32[8,128]{1,0:T(8,128)S(1)}, u32[]{:S(2)}, u32[]{:S(2)}) collective-permute-start(f32[8,128]{1,0:T(8,128)S(1)} %fusion.share_in), channel_id=1, source_target_pairs={{0,0},{1,9},{2,10},{3,3},{4,4},{5,13},{6,14},{7,7},{8,8},{9,1},{10... | collective-permute-start | bytes 12296 | tf_op jit(solution)/shard_map/ppermute | solution.py:612
  29.5 0.7 %collective-permute-start.7 = (f32[8,128]{1,0:T(8,128)S(1)}, f32[8,128]{1,0:T(8,128)S(1)}, u32[]{:S(2)}, u32[]{:S(2)}) collective-permute-start(f32[8,128]{1,0:T(8,128)S(1)} %add.13), channel_id=1, source_target_pairs={{0,0},{1,5},{2,6},{3,3},{4,4},{5,1},{6,2},{7,7},{8,8},{9,13},{10,1... | collective-permute-start | bytes 12296 | tf_op jit(solution)/shard_map/ppermute | solution.py:612
  30.2 0.7 %collective-permute-start.8 = (f32[8,128]{1,0:T(8,128)S(1)}, f32[8,128]{1,0:T(8,128)S(1)}, u32[]{:S(2)}, u32[]{:S(2)}) collective-permute-start(f32[8,128]{1,0:T(8,128)S(1)} %add.14), channel_id=1, source_target_pairs={{0,0},{1,2},{2,1},{3,3},{4,4},{5,6},{6,5},{7,7},{8,8},{9,10},{10,9... | collective-permute-start | bytes 12296 | tf_op jit(solution)/shard_map/ppermute | solution.py:612
  30.9 11.9 %collective-permute-start.9 = (f32[8,128]{1,0:T(8,128)S(1)}, f32[8,128]{1,0:T(8,128)S(1)}, u32[]{:S(2)}, u32[]{:S(2)}) collective-permute-start(f32[8,128]{1,0:T(8,128)S(1)} %add.15.total), channel_id=1, source_target_pairs={{0,1},{1,0},{2,3},{3,2},{4,5},{5,4},{6,7},{7,6},{8,9},{9,8},{10,11... | collective-permute-start | bytes 12296 | tf_op jit(solution)/shard_map/ppermute | solution.py:630

commit v15 on v14

--- a/solution.py
+++ b/solution.py
@@ -607,9 +607,19 @@
     of_chip, of_core = neighbours(to_chip, to_core)
     bits = range(count.bit_length() - 2)
 
+    groups = lax.axis_size("group")
+
+    def target(group, at, apart):
+        if counts(at):
+            return group * count + (at ^ apart)
+        return min(group ^ 1, groups - 1) * count + at
+
     def hop(value, bit):
         apart = 3 if bit == 0 else 2 << bit
-        return lax.ppermute(value, "gx", [(at, at ^ apart * counts(at)) for at in range(count)])
+        pairs = [
+            (group * count + at, target(group, at, apart)) for group in range(groups) for at in range(count)
+        ]
+        return lax.ppermute(value, ("group", "gx"), pairs)
 
     share = share + of_core[0, 0, 0, ny:]
     far = hop(share, bits[-1])

time: 43.6 us -> 40.2 us (0.922)
  starting transfers between devices: 27.6 us -> 19.9 us
  waiting for transfers between devices: 5.16 us -> 9.55 us
    ppermute x1, starting transfers between devices: 10.2 us -> 0.01 us  [on_device(): handed = lax.ppermute(share, 'gx', over_cores)]
    ppermute x3, waiting for transfers between devices: 0.01 us -> 4.4 us  [hop(): return lax.ppermute(value, ('group', 'gx'), pairs)]
    ppermute x3, starting transfers between devices: 1.97 us -> 4.47 us  [hop(): return lax.ppermute(value, ('group', 'gx'), pairs)]
  transfers between devices with their start and end apart: 10 -> 10, of which waited for: 3 -> 6; matrix products, arithmetic and copies ran while one was open for 0% -> 0% of each run, Pallas kernels for 14% -> 15%
where the time goes in v15:
time: 40.2 us; the launch traced here: 39.9 us
  starting transfers between devices  19.9 us (50%)
  waiting for transfers between devices  9.55 us (24%)
  Pallas kernels  7.74 us (19%)
  local copies, waits for them, and re-layouts  2.03 us (5%)
  between operations  0.69 us (2%)
    ppermute x3, starting transfers between devices, neighbours(): return (lax.ppermute(to_chip, 'gx', over_chips), of_core)  11.1 us
    pallas_call x7, Pallas kernels, call(): pl.pallas_call(kernel, out_shape=tuple((jax.ShapeDtypeStruct(o, jnp.float...  7.74 us
    ppermute x3, starting transfers between devices, hop(): return lax.ppermute(value, ('group', 'gx'), pairs)  4.47 us
    ppermute x3, waiting for transfers between devices, hop(): return lax.ppermute(value, ('group', 'gx'), pairs)  4.4 us
    ppermute x3, starting transfers between devices, neighbours(): of_core = lax.ppermute(to_core, 'gx', over_cores)  4.37 us
    ppermute x3, waiting for transfers between devices, neighbours(): return (lax.ppermute(to_chip, 'gx', over_chips), of_core)  4.32 us
    unnamed x6, local copies, waits for them, and re-layouts  2.03 us
    ppermute x3, waiting for transfers between devices, neighbours(): of_core = lax.ppermute(to_core, 'gx', over_cores)  0.83 us
  transfers between devices with their start and end apart: 10, of which 6 were waited for; matrix products, arithmetic and copies ran while one was open for 0% of the time, Pallas kernels for 15%

profile of v15, /device:TPU:0, one launch (start us, length us, event | category | flops | bytes accessed | tf_op | source)
XLA Modules:
  0.0 39.9 jit_solution(1291871660620858)
XLA Ops:
  0.6 0.5 %collective-permute-start.2 = (f32[2,4,64,256]{3,2,1,0:T(8,128)}, f32[2,4,64,256]{3,2,1,0:T(8,128)S(1)}, u32[]{:S(2)}, u32[]{:S(2)}) collective-permute-start(f32[2,4,64,256]{3,2,1,0:T(8,128)} %initial.1), channel_id=1, source_target_pairs={{0,1},{1,0},{2,3},{3,2},{4,5},{5,4},{6,7},{7,6},{8,9},{9,8},{10,11... | collective-permute-start | bytes 1572872 | tf_op jit(solution)/shard_map/ppermute | solution.py:556
  1.1 5.7 %collective-permute-start.1 = (f32[2,4,64,256]{3,2,1,0:T(8,128)}, f32[2,4,64,256]{3,2,1,0:T(8,128)S(1)}, u32[]{:S(2)}, u32[]{:S(2)}) collective-permute-start(f32[2,4,64,256]{3,2,1,0:T(8,128)} %initial.1), channel_id=1, source_target_pairs={{0,15},{1,2},{2,1},{3,4},{4,3},{5,6},{6,5},{7,8},{8,7},{9,10},{10,... | collective-permute-start | bytes 1572872 | tf_op jit(solution)/shard_map/ppermute | solution.py:557
  6.8 0.0 copy-start.1
  6.8 1.1 %copy-done.1 = f32[2,4,64,256]{3,2,1,0:T(8,128)S(1)} copy-done((f32[2,4,64,256]{3,2,1,0:T(8,128)S(1)}, f32[2,4,64,256]{3,2,1,0:T(8,128)}, u32[]{:S(2)}) %copy-start.1) | copy-done | bytes 524312
  7.9 0.0 copy-start.2
  7.9 0.9 %copy-done.2 = f32[4,64,256]{2,1,0:T(8,128)S(1)} copy-done((f32[4,64,256]{2,1,0:T(8,128)S(1)}, f32[4,64,256]{2,1,0:T(8,128)}, u32[]{:S(2)}) %copy-start.2) | copy-done | bytes 262168
  8.8 0.1 shard_map.50
  8.9 0.1 collective-permute-start.3
  9.0 0.6 %collective-permute-start = (f32[3,2,64,128]{3,2,1,0:T(8,128)S(1)}, f32[3,2,64,128]{3,2,1,0:T(8,128)S(1)}, u32[]{:S(2)}, u32[]{:S(2)}) collective-permute-start(f32[3,2,64,128]{3,2,1,0:T(8,128)S(1)} %get-tuple-element.40), channel_id=1, source_target_pairs={{0,15},{1,2},{2,1},{3,4},{4,3},{5,6},{6,5},{7,8},{8,7},{9,10},{10,... | collective-permute-start | bytes 589832 | tf_op jit(solution)/shard_map/ppermute | solution.py:557
  9.6 0.8 %collective-permute-done.3.m_core = f32[3,2,64,128]{3,2,1,0:T(8,128)S(1)} collective-permute-done((f32[3,2,64,128]{3,2,1,0:T(8,128)S(1)}, f32[3,2,64,128]{3,2,1,0:T(8,128)S(1)}, u32[]{:S(2)}, u32[]{:S(2)}) %collective-permute-start.3) | collective-permute-done | bytes 196640 | tf_op jit(solution)/shard_map/ppermute | solution.py:556
  10.4 0.0 collective-permute-done.2.of_core
  10.4 0.0 copy-start
  10.5 0.9 %shard_map.51 = (f32[2,4,2,80,128]{4,3,2,1,0:T(8,128)S(1)}, f32[2,6,2,80,128]{4,3,2,1,0:T(8,128)S(1)}, f32[6,2,64,128]{3,2,1,0:T(8,128)S(1)}, f32[6,2,80,128]{3,...) custom-call(f32[2,4,64,256]{3,2,1,0:T(8,128)S(1)} %collective-permut, ...), custom_call_target="tpu_custom_call" | custom-call | flops 3932160 | bytes 5341184 | tf_op jit(solution)/shard_map/pallas_call | solution.py:536
  11.3 2.7 %collective-permute-done.1.of_chip = f32[2,4,64,256]{3,2,1,0:T(8,128)S(1)} collective-permute-done((f32[2,4,64,256]{3,2,1,0:T(8,128)}, f32[2,4,64,256]{3,2,1,0:T(8,128)S(1)}, u32[]{:S(2)}, u32[]{:S(2)}) %collective-permute-start.1) | collective-permute-done | bytes 524320 | tf_op jit(solution)/shard_map/ppermute | solution.py:557
  14.0 0.0 copy-done
  14.0 1.3 %shard_map.52 = (f32[2,4,2,80,128]{4,3,2,1,0:T(8,128)S(1)}, f32[2,4,2,80,128]{4,3,2,1,0:T(8,128)S(1)}, f32[2,5,2,80,128]{4,3,2,1,0:T(8,128)S(1)}, f32[2,3,2,80,1...) custom-call(f32[2,4,64,256]{3,2,1,0:T(8,128)S(1)} %collective-permute-done.1.of_chip, ...), custom_call_target="tpu_custom_call" | custom-call | flops 5898240 | bytes 8134656 | tf_op jit(solution)/shard_map/pallas_call | solution.py:536
  15.3 1.7 %collective-permute-done.m_chip = f32[3,2,64,128]{3,2,1,0:T(8,128)S(1)} collective-permute-done((f32[3,2,64,128]{3,2,1,0:T(8,128)S(1)}, f32[3,2,64,128]{3,2,1,0:T(8,128)S(1)}, u32[]{:S(2)}, u32[]{:S(2)}) %collective-permute-start) | collective-permute-done | bytes 196640 | tf_op jit(solution)/shard_map/ppermute | solution.py:557
  17.0 1.3 %shard_map.53 = (f32[3,2,64,128]{3,2,1,0:T(8,128)S(1)}, f32[2,2,80,128]{3,2,1,0:T(8,128)S(1)}, f32[2,2,64,128]{3,2,1,0:T(8,128)S(1)}, f32[2,2,64,128]{3,2,1,0:T(...) custom-call(f32[3,2,64,128]{3,2,1,0:T(8,128)S(1)} %collective-permut, ...), custom_call_target="tpu_custom_call" | custom-call | flops 5898240 | bytes 10612736 | tf_op jit(solution)/shard_map/pallas_call | solution.py:536
  18.3 3.8 %collective-permute-start.5 = (f32[2,3,2,72,128]{4,3,2,1,0:T(8,128)S(1)}, f32[2,3,2,72,128]{4,3,2,1,0:T(8,128)S(1)}, u32[]{:S(2)}, u32[]{:S(2)}) collective-permute-start(f32[2,3,2,72,128]{4,3,2,1,0:T(8,128)S(1)} %get-tuple-element.65), channel_id=1, source_target_pairs={{0,1},{1,0},{2,3},{3,2},{4,5},{5,4},{6,7},{7,6},{8,9},{9,8},{10,11... | collective-permute-start | bytes 1327112 | tf_op jit(solution)/shard_map/ppermute | solution.py:556
  22.1 4.8 %collective-permute-start.4 = (f32[2,3,2,64,128]{4,3,2,1,0:T(8,128)S(1)}, f32[2,3,2,64,128]{4,3,2,1,0:T(8,128)S(1)}, u32[]{:S(2)}, u32[]{:S(2)}) collective-permute-start(f32[2,3,2,64,128]{4,3,2,1,0:T(8,128)S(1)} %get-tuple-element.57), channel_id=1, source_target_pairs={{0,15},{1,2},{2,1},{3,4},{4,3},{5,6},{6,5},{7,8},{8,7},{9,10},{10,... | collective-permute-start | bytes 1179656 | tf_op jit(solution)/shard_map/ppermute | solution.py:557
  26.8 0.0 collective-permute-done.5.of_core
  26.8 1.5 %collective-permute-start.6 = (f32[8,128]{1,0:T(8,128)S(1)}, f32[8,128]{1,0:T(8,128)S(1)}, u32[]{:S(2)}, u32[]{:S(2)}) collective-permute-start(f32[8,128]{1,0:T(8,128)S(1)} %fusion.share_in), channel_id=1, source_target_pairs={{0,16},{1,9},{2,10},{3,19},{4,20},{5,13},{6,14},{7,23},{8,24},{9,1... | collective-permute-start | bytes 12296 | tf_op jit(solution)/shard_map/ppermute | solution.py:622
  28.3 1.9 %shard_map.54 = (f32[2,5,2,80,128]{4,3,2,1,0:T(8,128)S(1)}, f32[2,1,2,80,128]{4,3,2,1,0:T(8,128)S(1)}, f32[2,3,2,80,128]{4,3,2,1,0:T(8,128)S(1)}, f32[2,3,2,64,1...) custom-call(f32[2,3,2,72,128]{4,3,2,1,0:T(8,128)S(1)} %collective-pe, ...), custom_call_target="tpu_custom_call" | custom-call | flops 7864320 | bytes 10510336 | tf_op jit(solution)/shard_map/pallas_call | solution.py:536
  30.3 0.2 collective-permute-done.6
  30.5 1.5 %collective-permute-start.7 = (f32[8,128]{1,0:T(8,128)S(1)}, f32[8,128]{1,0:T(8,128)S(1)}, u32[]{:S(2)}, u32[]{:S(2)}) collective-permute-start(f32[8,128]{1,0:T(8,128)S(1)} %add.13), channel_id=1, source_target_pairs={{0,16},{1,5},{2,6},{3,19},{4,20},{5,1},{6,2},{7,23},{8,24},{9,13},... | collective-permute-start | bytes 12296 | tf_op jit(solution)/shard_map/ppermute | solution.py:622
  31.9 2.1 %collective-permute-done.7 = f32[8,128]{1,0:T(8,128)S(1)} collective-permute-done((f32[8,128]{1,0:T(8,128)S(1)}, f32[8,128]{1,0:T(8,128)S(1)}, u32[]{:S(2)}, u32[]{:S(2)}) %collective-permute-start.7) | collective-permute-done | bytes 4128 | tf_op jit(solution)/shard_map/ppermute | solution.py:622
  34.1 1.5 %collective-permute-start.8 = (f32[8,128]{1,0:T(8,128)S(1)}, f32[8,128]{1,0:T(8,128)S(1)}, u32[]{:S(2)}, u32[]{:S(2)}) collective-permute-start(f32[8,128]{1,0:T(8,128)S(1)} %add.14), channel_id=1, source_target_pairs={{0,16},{1,2},{2,1},{3,19},{4,20},{5,6},{6,5},{7,23},{8,24},{9,10},... | collective-permute-start | bytes 12296 | tf_op jit(solution)/shard_map/ppermute | solution.py:622
  35.6 2.1 %collective-permute-done.8 = f32[8,128]{1,0:T(8,128)S(1)} collective-permute-done((f32[8,128]{1,0:T(8,128)S(1)}, f32[8,128]{1,0:T(8,128)S(1)}, u32[]{:S(2)}, u32[]{:S(2)}) %collective-permute-start.8) | collective-permute-done | bytes 4128 | tf_op jit(solution)/shard_map/ppermute | solution.py:622
  37.7 0.0 collective-permute-start.9
  37.7 0.0 collective-permute-done.4.of_chip
  37.7 1.7 %shard_map.55 = f32[4,64,256]{2,1,0:T(8,128)} custom-call(f32[2,3,2,64,128]{4,3,2,1,0:T(8,128)S(1)} %collective-permute-done.4.of_chip, f32[6,2,64,128]{3,2,1,0:T(8,128)S(1)} %get-tuple-element.46.mx.mx_a, f32[6,2,80,128]{3,2,1,0:T(8,128)S(1)} %get-tuple-element.47.my.my_a, f32[6,2,64,128]{3,2,1,0:T(8,128)S(1)} %get-tuple-element.48.mz.mz_a, ...), custom_call_target="tpu_custom_call" | custom-call | flops 5898240 | bytes 8749056 | tf_op jit(solution)/shard_map/pallas_call | solution.py:536
  39.4 0.0 collective-permute-done.9.handed
  39.4 0.6 %shard_map.56 = f32[1]{0:T(128)} custom-call(f32[8,128]{1,0:T(8,128)S(1)} %add.15.total, f32[8,128]{1,0:T(8,128)S(1)} %collective-permute-done.9.handed), custom_call_target="tpu_custom_call" | custom-call | flops 1 | bytes 8196 | tf_op jit(solution)/shard_map/pallas_call | solution.py:536
  (4 shorter events, 0.0 us)
Async XLA Ops:
  0.6 9.8 %collective-permute-start.2 = (f32[2,4,64,256]{3,2,1,0:T(8,128)}, f32[2,4,64,256]{3,2,1,0:T(8,128)S(1)}, u32[]{:S(2)}, u32[]{:S(2)}) collective-permute-start(f32[2,4,64,256]{3,2,1,0:T(8,128)} %initial.1), channel_id=1, source_target_pairs={{0,1},{1,0},{2,3},{3,2},{4,5},{5,4},{6,7},{7,6},{8,9},{9,8},{10,11... | collective-permute-start | bytes 1572872 | tf_op jit(solution)/shard_map/ppermute | solution.py:556
  1.1 12.8 %collective-permute-start.1 = (f32[2,4,64,256]{3,2,1,0:T(8,128)}, f32[2,4,64,256]{3,2,1,0:T(8,128)S(1)}, u32[]{:S(2)}, u32[]{:S(2)}) collective-permute-start(f32[2,4,64,256]{3,2,1,0:T(8,128)} %initial.1), channel_id=1, source_target_pairs={{0,15},{1,2},{2,1},{3,4},{4,3},{5,6},{6,5},{7,8},{8,7},{9,10},{10,... | collective-permute-start | bytes 1572872 | tf_op jit(solution)/shard_map/ppermute | solution.py:557
  6.8 1.1 %copy-start.1 = (f32[2,4,64,256]{3,2,1,0:T(8,128)S(1)}, f32[2,4,64,256]{3,2,1,0:T(8,128)}, u32[]{:S(2)}) copy-start(f32[2,4,64,256]{3,2,1,0:T(8,128)} %initial.1) | copy-start | bytes 1572868
  7.9 0.9 %copy-start.2 = (f32[4,64,256]{2,1,0:T(8,128)S(1)}, f32[4,64,256]{2,1,0:T(8,128)}, u32[]{:S(2)}) copy-start(f32[4,64,256]{2,1,0:T(8,128)} %mobility.1) | copy-start | bytes 786436
  8.9 1.5 %collective-permute-start.3 = (f32[3,2,64,128]{3,2,1,0:T(8,128)S(1)}, f32[3,2,64,128]{3,2,1,0:T(8,128)S(1)}, u32[]{:S(2)}, u32[]{:S(2)}) collective-permute-start(f32[3,2,64,128]{3,2,1,0:T(8,128)S(1)} %get-tuple-element.43), channel_id=1, source_target_pairs={{0,1},{1,0},{2,3},{3,2},{4,5},{5,4},{6,7},{7,6},{8,9},{9,8},{10,11... | collective-permute-start | bytes 589832 | tf_op jit(solution)/shard_map/ppermute | solution.py:556
  9.0 8.0 %collective-permute-start = (f32[3,2,64,128]{3,2,1,0:T(8,128)S(1)}, f32[3,2,64,128]{3,2,1,0:T(8,128)S(1)}, u32[]{:S(2)}, u32[]{:S(2)}) collective-permute-start(f32[3,2,64,128]{3,2,1,0:T(8,128)S(1)} %get-tuple-element.40), channel_id=1, source_target_pairs={{0,15},{1,2},{2,1},{3,4},{4,3},{5,6},{6,5},{7,8},{8,7},{9,10},{10,... | collective-permute-start | bytes 589832 | tf_op jit(solution)/shard_map/ppermute | solution.py:557
  10.4 3.6 %copy-start = (f32[2,4,64,256]{3,2,1,0:T(8,128)S(1)}, f32[2,4,64,256]{3,2,1,0:T(8,128)}, u32[]{:S(2)}) copy-start(f32[2,4,64,256]{3,2,1,0:T(8,128)} %observed.3) | copy-start | bytes 1572868
  18.3 8.6 %collective-permute-start.5 = (f32[2,3,2,72,128]{4,3,2,1,0:T(8,128)S(1)}, f32[2,3,2,72,128]{4,3,2,1,0:T(8,128)S(1)}, u32[]{:S(2)}, u32[]{:S(2)}) collective-permute-start(f32[2,3,2,72,128]{4,3,2,1,0:T(8,128)S(1)} %get-tuple-element.65), channel_id=1, source_target_pairs={{0,1},{1,0},{2,3},{3,2},{4,5},{5,4},{6,7},{7,6},{8,9},{9,8},{10,11... | collective-permute-start | bytes 1327112 | tf_op jit(solution)/shard_map/ppermute | solution.py:556
  22.1 15.6 %collective-permute-start.4 = (f32[2,3,2,64,128]{4,3,2,1,0:T(8,128)S(1)}, f32[2,3,2,64,128]{4,3,2,1,0:T(8,128)S(1)}, u32[]{:S(2)}, u32[]{:S(2)}) collective-permute-start(f32[2,3,2,64,128]{4,3,2,1,0:T(8,128)S(1)} %get-tuple-element.57), channel_id=1, source_target_pairs={{0,15},{1,2},{2,1},{3,4},{4,3},{5,6},{6,5},{7,8},{8,7},{9,10},{10,... | collective-permute-start | bytes 1179656 | tf_op jit(solution)/shard_map/ppermute | solution.py:557
  26.8 3.6 %collective-permute-start.6 = (f32[8,128]{1,0:T(8,128)S(1)}, f32[8,128]{1,0:T(8,128)S(1)}, u32[]{:S(2)}, u32[]{:S(2)}) collective-permute-start(f32[8,128]{1,0:T(8,128)S(1)} %fusion.share_in), channel_id=1, source_target_pairs={{0,16},{1,9},{2,10},{3,19},{4,20},{5,13},{6,14},{7,23},{8,24},{9,1... | collective-permute-start | bytes 12296 | tf_op jit(solution)/shard_map/ppermute | solution.py:622
  30.5 3.6 %collective-permute-start.7 = (f32[8,128]{1,0:T(8,128)S(1)}, f32[8,128]{1,0:T(8,128)S(1)}, u32[]{:S(2)}, u32[]{:S(2)}) collective-permute-start(f32[8,128]{1,0:T(8,128)S(1)} %add.13), channel_id=1, source_target_pairs={{0,16},{1,5},{2,6},{3,19},{4,20},{5,1},{6,2},{7,23},{8,24},{9,13},... | collective-permute-start | bytes 12296 | tf_op jit(solution)/shard_map/ppermute | solution.py:622
  34.1 3.6 %collective-permute-start.8 = (f32[8,128]{1,0:T(8,128)S(1)}, f32[8,128]{1,0:T(8,128)S(1)}, u32[]{:S(2)}, u32[]{:S(2)}) collective-permute-start(f32[8,128]{1,0:T(8,128)S(1)} %add.14), channel_id=1, source_target_pairs={{0,16},{1,2},{2,1},{3,19},{4,20},{5,6},{6,5},{7,23},{8,24},{9,10},... | collective-permute-start | bytes 12296 | tf_op jit(solution)/shard_map/ppermute | solution.py:622
  37.7 1.7 %collective-permute-start.9 = (f32[8,128]{1,0:T(8,128)S(1)}, f32[8,128]{1,0:T(8,128)S(1)}, u32[]{:S(2)}, u32[]{:S(2)}) collective-permute-start(f32[8,128]{1,0:T(8,128)S(1)} %add.15.total), channel_id=1, source_target_pairs={{0,1},{1,0},{2,3},{3,2},{4,5},{5,4},{6,7},{7,6},{8,9},{9,8},{10,11... | collective-permute-start | bytes 12296 | tf_op jit(solution)/shard_map/ppermute | solution.py:640

commit v16 on v15

--- a/solution.py
+++ b/solution.py
@@ -15,7 +15,7 @@
 LANES = 128
 ROWS = 8
 PAD = ROWS
-CHUNK = 16
+CHUNK = 8
 
 
 def chunks(ny):
@@ -451,8 +451,9 @@
 def late_kernel(
     of_chip, mx_a, my_a, mz_a, mz_low_a, all_a, mx_b, my_b, mz_b, mz_low_b, all_b,
     chem0_a, chem0_b, chem1_b, adjoint2_b, flow_a, flow_part, adjoint1_a, weight_b, step_z_b,
-    part, sum_x_b, sum_y_b, sum_z_b, result, rim, flow_b, adjoint1_b, sum_x, sum_y, sum_z,
+    part, sum_x_b, sum_y_b, sum_z_b, share_in, result, share, rim, flow_b, adjoint1_b, sum_x, sum_y, sum_z,
 ):
+    share[...] = share_in[...]
     runs = of_chip.shape[0]
     n, ny, _ = result.shape
     faces = Faces(n, (mx_a, my_a, mz_a, mz_low_a, all_a, mx_b, my_b, mz_b, mz_low_b, all_b))
@@ -636,21 +637,21 @@
     for bit in bits[-2::-1]:
         share = share + far
         far = hop(share, bit)
-    share = share + far
-    handed = lax.ppermute(share, "gx", over_cores)
-    (result,) = call(
+    result, share = call(
         late_kernel,
-        ((n, ny, nz),),
+        ((n, ny, nz), (ROWS, LANES)),
         (
             lies_padded(runs, 3), lies_padded(runs, 3), lies_padded(runs, 3),
             lies(3), lies_padded(2), lies(2),
         ),
         (
             of_chip, *faces, chem0_a, chem0_b, chem1_b, adjoint2_b, flow_a, flow_part, adjoint1_a,
-            weight_b, step_z_b, part, *sums_b,
+            weight_b, step_z_b, part, *sums_b, share,
         ),
         60 * runs * 3 * cell,
     )
+    share = share + far
+    handed = lax.ppermute(share, "gx", over_cores)
     (misfit,) = call(misfit_kernel, ((1,),), (), (share, handed), 1, scalar=0)
     return (result, misfit)
 

time: 40.2 us -> 39.6 us (0.985)
  waiting for transfers between devices: 9.55 us -> 8.94 us
    ppermute x3, waiting for transfers between devices: 4.4 us -> 2.66 us  [hop(): return lax.ppermute(value, ('group', 'gx'), pairs)]
    ppermute x1, waiting for transfers between devices: 0.01 us -> 1.16 us  [on_device(): handed = lax.ppermute(share, 'gx', over_cores)]
  transfers between devices with their start and end apart: 10 -> 10, of which waited for: 6 -> 7; matrix products, arithmetic and copies ran while one was open for 0% -> 0% of each run, Pallas kernels for 15% -> 15%
where the time goes in v16:
time: 39.6 us; the launch traced here: 39.4 us
  starting transfers between devices  19.9 us (50%)
  waiting for transfers between devices  8.94 us (23%)
  Pallas kernels  7.87 us (20%)
  local copies, waits for them, and re-layouts  2.03 us (5%)
  between operations  0.68 us (2%)
    ppermute x3, starting transfers between devices, neighbours(): return (lax.ppermute(to_chip, 'gx', over_chips), of_core)  11.1 us
    pallas_call x7, Pallas kernels, call(): pl.pallas_call(kernel, out_shape=tuple((jax.ShapeDtypeStruct(o, jnp.float...  7.87 us
    ppermute x3, starting transfers between devices, hop(): return lax.ppermute(value, ('group', 'gx'), pairs)  4.47 us
    ppermute x3, starting transfers between devices, neighbours(): of_core = lax.ppermute(to_core, 'gx', over_cores)  4.37 us
    ppermute x3, waiting for transfers between devices, neighbours(): return (lax.ppermute(to_chip, 'gx', over_chips), of_core)  4.3 us
    ppermute x3, waiting for transfers between devices, hop(): return lax.ppermute(value, ('group', 'gx'), pairs)  2.66 us
    unnamed x6, local copies, waits for them, and re-layouts  2.03 us
    ppermute x1, waiting for transfers between devices, on_device(): handed = lax.ppermute(share, 'gx', over_cores)  1.16 us
  transfers between devices with their start and end apart: 10, of which 7 were waited for; matrix products, arithmetic and copies ran while one was open for 0% of the time, Pallas kernels for 15%

profile of v16, /device:TPU:0, one launch (start us, length us, event | category | flops | bytes accessed | tf_op | source)
XLA Modules:
  0.0 39.4 jit_solution(17226115382521376582)
XLA Ops:
  0.6 0.5 %collective-permute-start.2 = (f32[2,4,64,256]{3,2,1,0:T(8,128)}, f32[2,4,64,256]{3,2,1,0:T(8,128)S(1)}, u32[]{:S(2)}, u32[]{:S(2)}) collective-permute-start(f32[2,4,64,256]{3,2,1,0:T(8,128)} %initial.1), channel_id=1, source_target_pairs={{0,1},{1,0},{2,3},{3,2},{4,5},{5,4},{6,7},{7,6},{8,9},{9,8},{10,11... | collective-permute-start | bytes 1572872 | tf_op jit(solution)/shard_map/ppermute | solution.py:557
  1.1 5.7 %collective-permute-start.1 = (f32[2,4,64,256]{3,2,1,0:T(8,128)}, f32[2,4,64,256]{3,2,1,0:T(8,128)S(1)}, u32[]{:S(2)}, u32[]{:S(2)}) collective-permute-start(f32[2,4,64,256]{3,2,1,0:T(8,128)} %initial.1), channel_id=1, source_target_pairs={{0,15},{1,2},{2,1},{3,4},{4,3},{5,6},{6,5},{7,8},{8,7},{9,10},{10,... | collective-permute-start | bytes 1572872 | tf_op jit(solution)/shard_map/ppermute | solution.py:558
  6.8 0.0 copy-start.1
  6.8 1.1 %copy-done.1 = f32[2,4,64,256]{3,2,1,0:T(8,128)S(1)} copy-done((f32[2,4,64,256]{3,2,1,0:T(8,128)S(1)}, f32[2,4,64,256]{3,2,1,0:T(8,128)}, u32[]{:S(2)}) %copy-start.1) | copy-done | bytes 524312
  7.9 0.0 copy-start.2
  7.9 0.9 %copy-done.2 = f32[4,64,256]{2,1,0:T(8,128)S(1)} copy-done((f32[4,64,256]{2,1,0:T(8,128)S(1)}, f32[4,64,256]{2,1,0:T(8,128)}, u32[]{:S(2)}) %copy-start.2) | copy-done | bytes 262168
  8.8 0.1 shard_map.50
  8.9 0.1 collective-permute-start.3
  9.0 0.6 %collective-permute-start = (f32[3,2,64,128]{3,2,1,0:T(8,128)S(1)}, f32[3,2,64,128]{3,2,1,0:T(8,128)S(1)}, u32[]{:S(2)}, u32[]{:S(2)}) collective-permute-start(f32[3,2,64,128]{3,2,1,0:T(8,128)S(1)} %get-tuple-element.42), channel_id=1, source_target_pairs={{0,15},{1,2},{2,1},{3,4},{4,3},{5,6},{6,5},{7,8},{8,7},{9,10},{10,... | collective-permute-start | bytes 589832 | tf_op jit(solution)/shard_map/ppermute | solution.py:558
  9.6 0.8 %collective-permute-done.3.m_core = f32[3,2,64,128]{3,2,1,0:T(8,128)S(1)} collective-permute-done((f32[3,2,64,128]{3,2,1,0:T(8,128)S(1)}, f32[3,2,64,128]{3,2,1,0:T(8,128)S(1)}, u32[]{:S(2)}, u32[]{:S(2)}) %collective-permute-start.3) | collective-permute-done | bytes 196640 | tf_op jit(solution)/shard_map/ppermute | solution.py:557
  10.4 0.0 collective-permute-done.2.of_core
  10.5 0.0 copy-start
  10.5 0.9 %shard_map.51 = (f32[2,4,2,80,128]{4,3,2,1,0:T(8,128)S(1)}, f32[2,6,2,80,128]{4,3,2,1,0:T(8,128)S(1)}, f32[6,2,64,128]{3,2,1,0:T(8,128)S(1)}, f32[6,2,80,128]{3,...) custom-call(f32[2,4,64,256]{3,2,1,0:T(8,128)S(1)} %collective-permut, ...), custom_call_target="tpu_custom_call" | custom-call | flops 3932160 | bytes 5341184 | tf_op jit(solution)/shard_map/pallas_call | solution.py:537
  11.3 2.7 %collective-permute-done.1.of_chip = f32[2,4,64,256]{3,2,1,0:T(8,128)S(1)} collective-permute-done((f32[2,4,64,256]{3,2,1,0:T(8,128)}, f32[2,4,64,256]{3,2,1,0:T(8,128)S(1)}, u32[]{:S(2)}, u32[]{:S(2)}) %collective-permute-start.1) | collective-permute-done | bytes 524320 | tf_op jit(solution)/shard_map/ppermute | solution.py:558
  14.0 0.0 copy-done
  14.0 1.3 %shard_map.52 = (f32[2,4,2,80,128]{4,3,2,1,0:T(8,128)S(1)}, f32[2,4,2,80,128]{4,3,2,1,0:T(8,128)S(1)}, f32[2,5,2,80,128]{4,3,2,1,0:T(8,128)S(1)}, f32[2,3,2,80,1...) custom-call(f32[2,4,64,256]{3,2,1,0:T(8,128)S(1)} %collective-permute-done.1.of_chip, ...), custom_call_target="tpu_custom_call" | custom-call | flops 5898240 | bytes 8130560 | tf_op jit(solution)/shard_map/pallas_call | solution.py:537
  15.3 1.6 %collective-permute-done.m_chip = f32[3,2,64,128]{3,2,1,0:T(8,128)S(1)} collective-permute-done((f32[3,2,64,128]{3,2,1,0:T(8,128)S(1)}, f32[3,2,64,128]{3,2,1,0:T(8,128)S(1)}, u32[]{:S(2)}, u32[]{:S(2)}) %collective-permute-start) | collective-permute-done | bytes 196640 | tf_op jit(solution)/shard_map/ppermute | solution.py:558
  17.0 1.3 %shard_map.53 = (f32[3,2,64,128]{3,2,1,0:T(8,128)S(1)}, f32[2,2,80,128]{3,2,1,0:T(8,128)S(1)}, f32[2,2,64,128]{3,2,1,0:T(8,128)S(1)}, f32[2,2,64,128]{3,2,1,0:T(...) custom-call(f32[3,2,64,128]{3,2,1,0:T(8,128)S(1)} %collective-permut, ...), custom_call_target="tpu_custom_call" | custom-call | flops 5898240 | bytes 10608640 | tf_op jit(solution)/shard_map/pallas_call | solution.py:537
  18.3 3.8 %collective-permute-start.5 = (f32[2,3,2,72,128]{4,3,2,1,0:T(8,128)S(1)}, f32[2,3,2,72,128]{4,3,2,1,0:T(8,128)S(1)}, u32[]{:S(2)}, u32[]{:S(2)}) collective-permute-start(f32[2,3,2,72,128]{4,3,2,1,0:T(8,128)S(1)} %get-tuple-element.67), channel_id=1, source_target_pairs={{0,1},{1,0},{2,3},{3,2},{4,5},{5,4},{6,7},{7,6},{8,9},{9,8},{10,11... | collective-permute-start | bytes 1327112 | tf_op jit(solution)/shard_map/ppermute | solution.py:557
  22.1 4.8 %collective-permute-start.4 = (f32[2,3,2,64,128]{4,3,2,1,0:T(8,128)S(1)}, f32[2,3,2,64,128]{4,3,2,1,0:T(8,128)S(1)}, u32[]{:S(2)}, u32[]{:S(2)}) collective-permute-start(f32[2,3,2,64,128]{4,3,2,1,0:T(8,128)S(1)} %get-tuple-element.59), channel_id=1, source_target_pairs={{0,15},{1,2},{2,1},{3,4},{4,3},{5,6},{6,5},{7,8},{8,7},{9,10},{10,... | collective-permute-start | bytes 1179656 | tf_op jit(solution)/shard_map/ppermute | solution.py:558
  26.9 0.0 collective-permute-done.5.of_core
  26.9 1.5 %collective-permute-start.6 = (f32[8,128]{1,0:T(8,128)S(1)}, f32[8,128]{1,0:T(8,128)S(1)}, u32[]{:S(2)}, u32[]{:S(2)}) collective-permute-start(f32[8,128]{1,0:T(8,128)S(1)} %fusion.share_in), channel_id=1, source_target_pairs={{0,16},{1,9},{2,10},{3,19},{4,20},{5,13},{6,14},{7,23},{8,24},{9,1... | collective-permute-start | bytes 12296 | tf_op jit(solution)/shard_map/ppermute | solution.py:623
  28.4 2.0 %shard_map.54 = (f32[2,5,2,80,128]{4,3,2,1,0:T(8,128)S(1)}, f32[2,1,2,80,128]{4,3,2,1,0:T(8,128)S(1)}, f32[2,3,2,80,128]{4,3,2,1,0:T(8,128)S(1)}, f32[2,3,2,64,1...) custom-call(f32[2,3,2,72,128]{4,3,2,1,0:T(8,128)S(1)} %collective-pe, ...), custom_call_target="tpu_custom_call" | custom-call | flops 7864320 | bytes 10510336 | tf_op jit(solution)/shard_map/pallas_call | solution.py:537
  30.4 0.1 collective-permute-done.6
  30.5 1.5 %collective-permute-start.7 = (f32[8,128]{1,0:T(8,128)S(1)}, f32[8,128]{1,0:T(8,128)S(1)}, u32[]{:S(2)}, u32[]{:S(2)}) collective-permute-start(f32[8,128]{1,0:T(8,128)S(1)} %add.13), channel_id=1, source_target_pairs={{0,16},{1,5},{2,6},{3,19},{4,20},{5,1},{6,2},{7,23},{8,24},{9,13},... | collective-permute-start | bytes 12296 | tf_op jit(solution)/shard_map/ppermute | solution.py:623
  32.0 2.1 %collective-permute-done.7 = f32[8,128]{1,0:T(8,128)S(1)} collective-permute-done((f32[8,128]{1,0:T(8,128)S(1)}, f32[8,128]{1,0:T(8,128)S(1)}, u32[]{:S(2)}, u32[]{:S(2)}) %collective-permute-start.7) | collective-permute-done | bytes 4128 | tf_op jit(solution)/shard_map/ppermute | solution.py:623
  34.1 1.5 %collective-permute-start.8 = (f32[8,128]{1,0:T(8,128)S(1)}, f32[8,128]{1,0:T(8,128)S(1)}, u32[]{:S(2)}, u32[]{:S(2)}) collective-permute-start(f32[8,128]{1,0:T(8,128)S(1)} %add.14.share_in), channel_id=1, source_target_pairs={{0,16},{1,2},{2,1},{3,19},{4,20},{5,6},{6,5},{7,23},{8,24},{9,10},... | collective-permute-start | bytes 12296 | tf_op jit(solution)/shard_map/ppermute | solution.py:623
  35.6 0.0 collective-permute-done.4.of_chip
  35.6 1.7 %shard_map.55 = (f32[4,64,256]{2,1,0:T(8,128)}, f32[8,128]{1,0:T(8,128)S(1)}) custom-call(f32[2,3,2,64,128]{4,3,2,1,0:T(8,128)S(1)} %collective-permute-done.4.of_chip, f32[6,2,64,128]{3,2,1,0:T(8,128)S(1)} %get-tuple-element.48.mx.mx_a, f32[6,2,80,128]{3,2,1,0:T(8,128)S(1)} %get-tuple-element.49.my.my_a, f32[6,2,64,128]{3,2,1,0:T(8,128)S(1)} %get-tuple-element.50.mz.mz_a, ...), custom_call_target="tpu_custom_call" | custom-call | flops 5898240 | bytes 8757248 | tf_op jit(solution)/shard_map/pallas_call | solution.py:537
  37.3 0.4 %collective-permute-done.8 = f32[8,128]{1,0:T(8,128)S(1)} collective-permute-done((f32[8,128]{1,0:T(8,128)S(1)}, f32[8,128]{1,0:T(8,128)S(1)}, u32[]{:S(2)}, u32[]{:S(2)}) %collective-permute-start.8) | collective-permute-done | bytes 4128 | tf_op jit(solution)/shard_map/ppermute | solution.py:623
  37.7 0.0 collective-permute-start.9
  37.7 1.2 %collective-permute-done.9.handed = f32[8,128]{1,0:T(8,128)S(1)} collective-permute-done((f32[8,128]{1,0:T(8,128)S(1)}, f32[8,128]{1,0:T(8,128)S(1)}, u32[]{:S(2)}, u32[]{:S(2)}) %collective-permute-start.9) | collective-permute-done | bytes 4128 | tf_op jit(solution)/shard_map/ppermute | solution.py:654
  38.9 0.6 %shard_map.56 = f32[1]{0:T(128)} custom-call(f32[8,128]{1,0:T(8,128)S(1)} %add.15.total, f32[8,128]{1,0:T(8,128)S(1)} %collective-permute-done.9.handed), custom_call_target="tpu_custom_call" | custom-call | flops 1 | bytes 8196 | tf_op jit(solution)/shard_map/pallas_call | solution.py:537
  (4 shorter events, 0.0 us)
Async XLA Ops:
  0.6 9.8 %collective-permute-start.2 = (f32[2,4,64,256]{3,2,1,0:T(8,128)}, f32[2,4,64,256]{3,2,1,0:T(8,128)S(1)}, u32[]{:S(2)}, u32[]{:S(2)}) collective-permute-start(f32[2,4,64,256]{3,2,1,0:T(8,128)} %initial.1), channel_id=1, source_target_pairs={{0,1},{1,0},{2,3},{3,2},{4,5},{5,4},{6,7},{7,6},{8,9},{9,8},{10,11... | collective-permute-start | bytes 1572872 | tf_op jit(solution)/shard_map/ppermute | solution.py:557
  1.1 12.8 %collective-permute-start.1 = (f32[2,4,64,256]{3,2,1,0:T(8,128)}, f32[2,4,64,256]{3,2,1,0:T(8,128)S(1)}, u32[]{:S(2)}, u32[]{:S(2)}) collective-permute-start(f32[2,4,64,256]{3,2,1,0:T(8,128)} %initial.1), channel_id=1, source_target_pairs={{0,15},{1,2},{2,1},{3,4},{4,3},{5,6},{6,5},{7,8},{8,7},{9,10},{10,... | collective-permute-start | bytes 1572872 | tf_op jit(solution)/shard_map/ppermute | solution.py:558
  6.8 1.1 %copy-start.1 = (f32[2,4,64,256]{3,2,1,0:T(8,128)S(1)}, f32[2,4,64,256]{3,2,1,0:T(8,128)}, u32[]{:S(2)}) copy-start(f32[2,4,64,256]{3,2,1,0:T(8,128)} %initial.1) | copy-start | bytes 1572868
  7.9 0.9 %copy-start.2 = (f32[4,64,256]{2,1,0:T(8,128)S(1)}, f32[4,64,256]{2,1,0:T(8,128)}, u32[]{:S(2)}) copy-start(f32[4,64,256]{2,1,0:T(8,128)} %mobility.1) | copy-start | bytes 786436
  8.9 1.5 %collective-permute-start.3 = (f32[3,2,64,128]{3,2,1,0:T(8,128)S(1)}, f32[3,2,64,128]{3,2,1,0:T(8,128)S(1)}, u32[]{:S(2)}, u32[]{:S(2)}) collective-permute-start(f32[3,2,64,128]{3,2,1,0:T(8,128)S(1)} %get-tuple-element.45), channel_id=1, source_target_pairs={{0,1},{1,0},{2,3},{3,2},{4,5},{5,4},{6,7},{7,6},{8,9},{9,8},{10,11... | collective-permute-start | bytes 589832 | tf_op jit(solution)/shard_map/ppermute | solution.py:557
  9.0 8.0 %collective-permute-start = (f32[3,2,64,128]{3,2,1,0:T(8,128)S(1)}, f32[3,2,64,128]{3,2,1,0:T(8,128)S(1)}, u32[]{:S(2)}, u32[]{:S(2)}) collective-permute-start(f32[3,2,64,128]{3,2,1,0:T(8,128)S(1)} %get-tuple-element.42), channel_id=1, source_target_pairs={{0,15},{1,2},{2,1},{3,4},{4,3},{5,6},{6,5},{7,8},{8,7},{9,10},{10,... | collective-permute-start | bytes 589832 | tf_op jit(solution)/shard_map/ppermute | solution.py:558
  10.5 3.5 %copy-start = (f32[2,4,64,256]{3,2,1,0:T(8,128)S(1)}, f32[2,4,64,256]{3,2,1,0:T(8,128)}, u32[]{:S(2)}) copy-start(f32[2,4,64,256]{3,2,1,0:T(8,128)} %observed.3) | copy-start | bytes 1572868
  18.3 8.6 %collective-permute-start.5 = (f32[2,3,2,72,128]{4,3,2,1,0:T(8,128)S(1)}, f32[2,3,2,72,128]{4,3,2,1,0:T(8,128)S(1)}, u32[]{:S(2)}, u32[]{:S(2)}) collective-permute-start(f32[2,3,2,72,128]{4,3,2,1,0:T(8,128)S(1)} %get-tuple-element.67), channel_id=1, source_target_pairs={{0,1},{1,0},{2,3},{3,2},{4,5},{5,4},{6,7},{7,6},{8,9},{9,8},{10,11... | collective-permute-start | bytes 1327112 | tf_op jit(solution)/shard_map/ppermute | solution.py:557
  22.1 13.5 %collective-permute-start.4 = (f32[2,3,2,64,128]{4,3,2,1,0:T(8,128)S(1)}, f32[2,3,2,64,128]{4,3,2,1,0:T(8,128)S(1)}, u32[]{:S(2)}, u32[]{:S(2)}) collective-permute-start(f32[2,3,2,64,128]{4,3,2,1,0:T(8,128)S(1)} %get-tuple-element.59), channel_id=1, source_target_pairs={{0,15},{1,2},{2,1},{3,4},{4,3},{5,6},{6,5},{7,8},{8,7},{9,10},{10,... | collective-permute-start | bytes 1179656 | tf_op jit(solution)/shard_map/ppermute | solution.py:558
  26.9 3.6 %collective-permute-start.6 = (f32[8,128]{1,0:T(8,128)S(1)}, f32[8,128]{1,0:T(8,128)S(1)}, u32[]{:S(2)}, u32[]{:S(2)}) collective-permute-start(f32[8,128]{1,0:T(8,128)S(1)} %fusion.share_in), channel_id=1, source_target_pairs={{0,16},{1,9},{2,10},{3,19},{4,20},{5,13},{6,14},{7,23},{8,24},{9,1... | collective-permute-start | bytes 12296 | tf_op jit(solution)/shard_map/ppermute | solution.py:623
  30.5 3.6 %collective-permute-start.7 = (f32[8,128]{1,0:T(8,128)S(1)}, f32[8,128]{1,0:T(8,128)S(1)}, u32[]{:S(2)}, u32[]{:S(2)}) collective-permute-start(f32[8,128]{1,0:T(8,128)S(1)} %add.13), channel_id=1, source_target_pairs={{0,16},{1,5},{2,6},{3,19},{4,20},{5,1},{6,2},{7,23},{8,24},{9,13},... | collective-permute-start | bytes 12296 | tf_op jit(solution)/shard_map/ppermute | solution.py:623
  34.1 3.6 %collective-permute-start.8 = (f32[8,128]{1,0:T(8,128)S(1)}, f32[8,128]{1,0:T(8,128)S(1)}, u32[]{:S(2)}, u32[]{:S(2)}) collective-permute-start(f32[8,128]{1,0:T(8,128)S(1)} %add.14.share_in), channel_id=1, source_target_pairs={{0,16},{1,2},{2,1},{3,19},{4,20},{5,6},{6,5},{7,23},{8,24},{9,10},... | collective-permute-start | bytes 12296 | tf_op jit(solution)/shard_map/ppermute | solution.py:623
  37.7 1.2 %collective-permute-start.9 = (f32[8,128]{1,0:T(8,128)S(1)}, f32[8,128]{1,0:T(8,128)S(1)}, u32[]{:S(2)}, u32[]{:S(2)}) collective-permute-start(f32[8,128]{1,0:T(8,128)S(1)} %add.15.total), channel_id=1, source_target_pairs={{0,1},{1,0},{2,3},{3,2},{4,5},{5,4},{6,7},{7,6},{8,9},{9,8},{10,11... | collective-permute-start | bytes 12296 | tf_op jit(solution)/shard_map/ppermute | solution.py:654

commit v17 on v16

--- a/solution.py
+++ b/solution.py
@@ -112,18 +112,19 @@
 
 class Faces:
     def __init__(self, n, refs):
-        mx_a, my_a, mz_a, mz_low_a, all_a, *late = refs
+        mx_a, my_a, my_low_a, mz_a, mz_low_a, all_a, *late = refs
         two = lambda ref, first, last, at: ((ref, first, last), *(((late[at], last + 1, n + 1),) if late else ()))
         self.mx = Line(*two(mx_a, -3, n - 2, 0))
         self.my = Line(*two(my_a, -2, n - 1, 1))
-        self.mz = Line(*two(mz_a, -2, n - 1, 2))
-        self.mz_low = Line(*two(mz_low_a, -2, n - 1, 3))
-        self.all = Line(*two(all_a, -2, n - 2, 4))
+        self.my_low = Line(*two(my_low_a, -2, n - 1, 2))
+        self.mz = Line(*two(mz_a, -2, n - 1, 3))
+        self.mz_low = Line(*two(mz_low_a, -2, n - 1, 4))
+        self.all = Line(*two(all_a, -2, n - 2, 5))
 
     def flow(self, row, at, mid, up, down, low=None, high=None):
         total = each(
             lambda a, b, c, d, e, u, v, w, x, y: (a * u + b * v) + (c * w + d * x) - e * y,
-            padded(*self.my(at), row), padded(*self.my(at), row, -1), flat(*self.mz(at), row),
+            flat(*self.my(at), row), flat(*self.my_low(at), row), flat(*self.mz(at), row),
             flat(*self.mz_low(at), row), flat(*self.all(at), row), up, down, after_z(mid), before_z(mid), mid,
         )
         if low is not None:
@@ -166,20 +167,21 @@
     return 0.5 * (a + b)
 
 
-def put_faces(row, mob, places, my, mz, mz_low):
+def put_faces(row, mob, places, faces):
     for at in places:
         mid = padded(*mob(at), row)
-        put_padded(*my(at), row, each(mean, mid, padded(*mob(at), row, 1)))
-        put_flat(*mz(at), row, each(mean, mid, after_z(mid)))
-        put_flat(*mz_low(at), row, each(mean, mid, before_z(mid)))
+        put_flat(*faces.my(at), row, each(mean, mid, padded(*mob(at), row, 1)))
+        put_flat(*faces.my_low(at), row, each(mean, mid, padded(*mob(at), row, -1)))
+        put_flat(*faces.mz(at), row, each(mean, mid, after_z(mid)))
+        put_flat(*faces.mz_low(at), row, each(mean, mid, before_z(mid)))
 
 
 def put_all(row, faces, places):
     for at in places:
         put_flat(*faces.all(at), row, each(
             lambda a, b, c, d, e, f: (a + b) + (c + d) + (e + f),
-            flat(*faces.mx(at - 1), row), flat(*faces.mx(at), row), padded(*faces.my(at), row),
-            padded(*faces.my(at), row, -1), flat(*faces.mz(at), row), flat(*faces.mz_low(at), row),
+            flat(*faces.mx(at - 1), row), flat(*faces.mx(at), row), flat(*faces.my(at), row),
+            flat(*faces.my_low(at), row), flat(*faces.mz(at), row), flat(*faces.mz_low(at), row),
         ))
 
 
@@ -211,11 +213,11 @@
     return adjoint, sum(part * part for part in miss)
 
 
-def core_kernel(of_core, m_core, conc_own, mob_own, conc_core, chem0, mx, my, mz, mz_low, m_all, rim):
+def core_kernel(of_core, m_core, conc_own, mob_own, conc_core, chem0, mx, my, my_low, mz, mz_low, m_all, rim):
     runs, n = conc_own.shape[:2]
     ny = of_core.shape[2]
     mob = Line((rim, -3, -1), (mob_own, 0, n - 1))
-    faces = Faces(n, (mx, my, mz, mz_low, m_all))
+    faces = Faces(n, (mx, my, my_low, mz, mz_low, m_all))
     for row in chunks(ny):
         for at in range(3):
             put_padded(rim, (2 - at,), row, flat(m_core, (at,), row))
@@ -223,7 +225,7 @@
         mids = [padded(*mob(at), row) for at in range(-3, n)]
         for at in range(n + 2):
             put_flat(mx, (at,), row, each(mean, mids[at], mids[at + 1]))
-        put_faces(row, mob, range(-2, n), faces.my, faces.mz, faces.mz_low)
+        put_faces(row, mob, range(-2, n), faces)
     for row in chunks(ny):
         put_all(row, faces, range(-2, n - 1))
     place = [either(at, 3 - at) for at in range(4)]
@@ -241,12 +243,12 @@
 
 
 def chip_kernel(
-    of_chip, conc_own, conc_core, chem0_a, observed, mx, my, mz, mz_low, m_all,
+    of_chip, conc_own, conc_core, chem0_a, observed, mx, my, my_low, mz, mz_low, m_all,
     conc_chip, chem0_b, state1_a, chem1_a, adjoint2_a, squares,
 ):
     runs, n = conc_own.shape[:2]
     ny = observed.shape[2]
-    faces = Faces(n, (mx, my, mz, mz_low, m_all))
+    faces = Faces(n, (mx, my, my_low, mz, mz_low, m_all))
     message = [either(3 - at, at) for at in range(4)]
     place = [either(n - 1 - at, at) for at in range(n)]
     conc = Line((conc_core, -4, -1), (conc_own, 0, n - 1), (conc_chip, n, n + 3))
@@ -282,12 +284,12 @@
 
 def forward_kernel(
     m_chip, mob_own, conc_own, conc_chip, chem0_a, chem0_b, state1_a, chem1_a, adjoint2_a, squares, observed,
-    mx_a, my_a, mz_a, mz_low_a, all_a,
-    mx_b, my_b, mz_b, mz_low_b, all_b, state1_b, chem1_b, adjoint2_b, to_core, to_chip, share, rim, total,
+    mx_a, my_a, my_low_a, mz_a, mz_low_a, all_a,
+    mx_b, my_b, my_low_b, mz_b, mz_low_b, all_b, state1_b, chem1_b, adjoint2_b, to_core, to_chip, share, rim, total,
 ):
     runs, n = conc_own.shape[:2]
     ny = observed.shape[2]
-    faces = Faces(n, (mx_a, my_a, mz_a, mz_low_a, all_a, mx_b, my_b, mz_b, mz_low_b, all_b))
+    faces = Faces(n, (mx_a, my_a, my_low_a, mz_a, mz_low_a, all_a, mx_b, my_b, my_low_b, mz_b, mz_low_b, all_b))
     mob = Line((mob_own, 0, n - 1), (rim, n, n + 2))
     place = [either(n - 1 - at, at) for at in range(n)]
     conc = Line((conc_own, 0, n - 1), (conc_chip, n, n + 3))
@@ -302,7 +304,7 @@
         mids = [padded(*mob(at), row) for at in range(n - 1, n + 3)]
         for at in range(3):
             put_flat(mx_b, (at,), row, each(mean, mids[at], mids[at + 1]))
-        put_faces(row, mob, range(n, n + 2), faces.my, faces.mz, faces.mz_low)
+        put_faces(row, mob, range(n, n + 2), faces)
     for row in chunks(ny):
         put_all(row, faces, range(n - 1, n + 2))
     total[...] = squares[...]
@@ -367,7 +369,7 @@
 
 
 def early_kernel(
-    of_core, mx_a, my_a, mz_a, mz_low_a, all_a, mx_b, my_b, mz_b, mz_low_b, all_b,
+    of_core, mx_a, my_a, my_low_a, mz_a, mz_low_a, all_a, mx_b, my_b, my_low_b, mz_b, mz_low_b, all_b,
     chem0_a, chem0_b, state1_a, state1_b, chem1_a, chem1_b, adjoint2_a, adjoint2_b,
     share_in, flow_a, flow_part, adjoint1_a, weight_b, step_z_b, part, sum_x_b, sum_y_b, sum_z_b, share,
     rim, sum_x, sum_y, sum_z,
@@ -376,7 +378,7 @@
     runs = of_core.shape[0]
     n = part.shape[0] + 2
     ny = part.shape[-2]
-    faces = Faces(n, (mx_a, my_a, mz_a, mz_low_a, all_a, mx_b, my_b, mz_b, mz_low_b, all_b))
+    faces = Faces(n, (mx_a, my_a, my_low_a, mz_a, mz_low_a, all_a, mx_b, my_b, my_low_b, mz_b, mz_low_b, all_b))
     chem0 = Line((chem0_a, -3, n - 2), (chem0_b, n - 1, n + 2))
     state1 = Line((state1_a, -2, n - 2), (state1_b, n - 1, n + 1))
     chem1 = Line((chem1_a, -1, n - 3), (chem1_b, n - 2, n))
@@ -449,14 +451,14 @@
 
 
 def late_kernel(
-    of_chip, mx_a, my_a, mz_a, mz_low_a, all_a, mx_b, my_b, mz_b, mz_low_b, all_b,
+    of_chip, mx_a, my_a, my_low_a, mz_a, mz_low_a, all_a, mx_b, my_b, my_low_b, mz_b, mz_low_b, all_b,
     chem0_a, chem0_b, chem1_b, adjoint2_b, flow_a, flow_part, adjoint1_a, weight_b, step_z_b,
     part, sum_x_b, sum_y_b, sum_z_b, share_in, result, share, rim, flow_b, adjoint1_b, sum_x, sum_y, sum_z,
 ):
     share[...] = share_in[...]
     runs = of_chip.shape[0]
     n, ny, _ = result.shape
-    faces = Faces(n, (mx_a, my_a, mz_a, mz_low_a, all_a, mx_b, my_b, mz_b, mz_low_b, all_b))
+    faces = Faces(n, (mx_a, my_a, my_low_a, mz_a, mz_low_a, all_a, mx_b, my_b, my_low_b, mz_b, mz_low_b, all_b))
     place = [either(n - 1 - at, at) for at in range(n)]
     chem0 = Line((chem0_a, -3, n - 2), (chem0_b, n - 1, n + 2))
     chem1 = Line((chem1_b, n - 2, n))
@@ -577,7 +579,7 @@
         core_kernel,
         (
             lies_padded(runs, 4), lies_padded(runs, n + 2),
-            lies(n + 2), lies_padded(n + 2), lies(n + 2), lies(n + 2), lies(n + 1),
+            lies(n + 2), lies(n + 2), lies(n + 2), lies(n + 2), lies(n + 2), lies(n + 1),
         ),
         (lies_padded(3),),
         (of_core, m_core, conc, mob),
@@ -596,7 +598,7 @@
     *faces_b, state1_b, chem1_b, adjoint2_b, to_core, to_chip, share = call(
         forward_kernel,
         (
-            lies(3), lies_padded(2), lies(2), lies(2), lies(3),
+            lies(3), lies(2), lies(2), lies(2), lies(2), lies(3),
             lies_padded(runs, 3), lies_padded(runs, 3), lies_padded(runs, 3),
             (runs, 3, blocks, ny + ROWS, LANES), lies(runs, 3), (ROWS, LANES),
         ),
@@ -606,8 +608,6 @@
     )
     faces = (*faces_a, *faces_b)
     of_chip, of_core = neighbours(to_chip, to_core)
-    bits = range(count.bit_length() - 2)
-
     groups = lax.axis_size("group")
 
     def target(group, at, apart):
@@ -615,15 +615,20 @@
             return group * count + (at ^ apart)
         return min(group ^ 1, groups - 1) * count + at
 
-    def hop(value, bit):
-        apart = 3 if bit == 0 else 2 << bit
+    def hop(value, apart):
         pairs = [
             (group * count + at, target(group, at, apart)) for group in range(groups) for at in range(count)
         ]
         return lax.ppermute(value, ("group", "gx"), pairs)
 
+    def hops(value, bits):
+        aparts = [sum(2 << bit for at, bit in enumerate(bits) if which >> at & 1) for which in range(1, 1 << len(bits))]
+        return [hop(value, apart) for apart in aparts]
+
     share = share + of_core[0, 0, 0, ny:]
-    far = hop(share, bits[-1])
+    upper = range(count.bit_length() - 3, 0, -1)
+    steps = [upper[at : at + 2] for at in range(0, len(upper), 2)]
+    fars = hops(share, steps[0])
     flow_a, flow_part, adjoint1_a, weight_b, step_z_b, part, *sums_b, share = call(
         early_kernel,
         (
@@ -634,9 +639,11 @@
         (of_core, *faces, chem0_a, chem0_b, state1_a, state1_b, chem1_a, chem1_b, adjoint2_a, adjoint2_b, share),
         60 * runs * n * cell,
     )
-    for bit in bits[-2::-1]:
-        share = share + far
-        far = hop(share, bit)
+    for bits in steps[1:]:
+        share = share + sum(fars)
+        fars = hops(share, bits)
+    share = share + sum(fars)
+    far = hop(share, 3)
     result, share = call(
         late_kernel,
         ((n, ny, nz), (ROWS, LANES)),

time: 39.6 us -> 38.1 us (0.962)
  waiting for transfers between devices: 8.94 us -> 6.83 us
  starting transfers between devices: 19.9 us -> 20.4 us
    ppermute x3 -> x4, waiting for transfers between devices: 2.66 us -> 0.58 us  [hop(): return lax.ppermute(value, ('group', 'gx'), pairs)]
    ppermute x3 -> x4, starting transfers between devices: 4.47 us -> 5.01 us  [hop(): return lax.ppermute(value, ('group', 'gx'), pairs)]
  transfers between devices with their start and end apart: 10 -> 11, of which waited for: 7 -> 6; matrix products, arithmetic and copies ran while one was open for 0% -> 0% of each run, Pallas kernels for 15% -> 16%
where the time goes in v17:
time: 38.1 us; the launch traced here: 37.9 us
  starting transfers between devices  20.4 us (54%)
  Pallas kernels  7.86 us (21%)
  waiting for transfers between devices  6.83 us (18%)
  local copies, waits for them, and re-layouts  2.03 us (5%)
  between operations  0.7 us (2%)
    ppermute x3, starting transfers between devices, neighbours(): return (lax.ppermute(to_chip, 'gx', over_chips), of_core)  11.1 us
    pallas_call x7, Pallas kernels, call(): pl.pallas_call(kernel, out_shape=tuple((jax.ShapeDtypeStruct(o, jnp.float...  7.86 us
    ppermute x4, starting transfers between devices, hop(): return lax.ppermute(value, ('group', 'gx'), pairs)  5.01 us
    ppermute x3, starting transfers between devices, neighbours(): of_core = lax.ppermute(to_core, 'gx', over_cores)  4.37 us
    ppermute x3, waiting for transfers between devices, neighbours(): return (lax.ppermute(to_chip, 'gx', over_chips), of_core)  4.26 us
    unnamed x6, local copies, waits for them, and re-layouts  2.03 us
    ppermute x1, waiting for transfers between devices, on_device(): handed = lax.ppermute(share, 'gx', over_cores)  1.16 us
    ppermute x3, waiting for transfers between devices, neighbours(): of_core = lax.ppermute(to_core, 'gx', over_cores)  0.83 us
  transfers between devices with their start and end apart: 11, of which 6 were waited for; matrix products, arithmetic and copies ran while one was open for 0% of the time, Pallas kernels for 16%

profile of v17, /device:TPU:0, one launch (start us, length us, event | category | flops | bytes accessed | tf_op | source)
XLA Modules:
  0.0 37.9 jit_solution(9686862986289281549)
XLA Ops:
  0.6 0.5 %collective-permute-start.2 = (f32[2,4,64,256]{3,2,1,0:T(8,128)}, f32[2,4,64,256]{3,2,1,0:T(8,128)S(1)}, u32[]{:S(2)}, u32[]{:S(2)}) collective-permute-start(f32[2,4,64,256]{3,2,1,0:T(8,128)} %initial.1), channel_id=1, source_target_pairs={{0,1},{1,0},{2,3},{3,2},{4,5},{5,4},{6,7},{7,6},{8,9},{9,8},{10,11... | collective-permute-start | bytes 1572872 | tf_op jit(solution)/shard_map/ppermute | solution.py:559
  1.1 5.7 %collective-permute-start.1 = (f32[2,4,64,256]{3,2,1,0:T(8,128)}, f32[2,4,64,256]{3,2,1,0:T(8,128)S(1)}, u32[]{:S(2)}, u32[]{:S(2)}) collective-permute-start(f32[2,4,64,256]{3,2,1,0:T(8,128)} %initial.1), channel_id=1, source_target_pairs={{0,15},{1,2},{2,1},{3,4},{4,3},{5,6},{6,5},{7,8},{8,7},{9,10},{10,... | collective-permute-start | bytes 1572872 | tf_op jit(solution)/shard_map/ppermute | solution.py:560
  6.8 0.0 copy-start.1
  6.8 1.1 %copy-done.1 = f32[2,4,64,256]{3,2,1,0:T(8,128)S(1)} copy-done((f32[2,4,64,256]{3,2,1,0:T(8,128)S(1)}, f32[2,4,64,256]{3,2,1,0:T(8,128)}, u32[]{:S(2)}) %copy-start.1) | copy-done | bytes 524312
  7.9 0.0 copy-start.2
  7.9 0.9 %copy-done.2 = f32[4,64,256]{2,1,0:T(8,128)S(1)} copy-done((f32[4,64,256]{2,1,0:T(8,128)S(1)}, f32[4,64,256]{2,1,0:T(8,128)}, u32[]{:S(2)}) %copy-start.2) | copy-done | bytes 262168
  8.8 0.1 shard_map.50
  8.9 0.1 collective-permute-start.3
  9.0 0.6 %collective-permute-start = (f32[3,2,64,128]{3,2,1,0:T(8,128)S(1)}, f32[3,2,64,128]{3,2,1,0:T(8,128)S(1)}, u32[]{:S(2)}, u32[]{:S(2)}) collective-permute-start(f32[3,2,64,128]{3,2,1,0:T(8,128)S(1)} %get-tuple-element.44), channel_id=1, source_target_pairs={{0,15},{1,2},{2,1},{3,4},{4,3},{5,6},{6,5},{7,8},{8,7},{9,10},{10,... | collective-permute-start | bytes 589832 | tf_op jit(solution)/shard_map/ppermute | solution.py:560
  9.6 0.8 %collective-permute-done.3.m_core = f32[3,2,64,128]{3,2,1,0:T(8,128)S(1)} collective-permute-done((f32[3,2,64,128]{3,2,1,0:T(8,128)S(1)}, f32[3,2,64,128]{3,2,1,0:T(8,128)S(1)}, u32[]{:S(2)}, u32[]{:S(2)}) %collective-permute-start.3) | collective-permute-done | bytes 196640 | tf_op jit(solution)/shard_map/ppermute | solution.py:559
  10.4 0.0 collective-permute-done.2.of_core
  10.5 0.0 copy-start
  10.5 0.9 %shard_map.51 = (f32[2,4,2,80,128]{4,3,2,1,0:T(8,128)S(1)}, f32[2,6,2,80,128]{4,3,2,1,0:T(8,128)S(1)}, f32[6,2,64,128]{3,2,1,0:T(8,128)S(1)}, f32[6,2,64,128]{3,...) custom-call(f32[2,4,64,256]{3,2,1,0:T(8,128)S(1)} %collective-permut, ...), custom_call_target="tpu_custom_call" | custom-call | flops 3932160 | bytes 5636096 | tf_op jit(solution)/shard_map/pallas_call | solution.py:539
  11.3 2.7 %collective-permute-done.1.of_chip = f32[2,4,64,256]{3,2,1,0:T(8,128)S(1)} collective-permute-done((f32[2,4,64,256]{3,2,1,0:T(8,128)}, f32[2,4,64,256]{3,2,1,0:T(8,128)S(1)}, u32[]{:S(2)}, u32[]{:S(2)}) %collective-permute-start.1) | collective-permute-done | bytes 524320 | tf_op jit(solution)/shard_map/ppermute | solution.py:560
  14.0 0.0 copy-done
  14.0 1.4 %shard_map.52 = (f32[2,4,2,80,128]{4,3,2,1,0:T(8,128)S(1)}, f32[2,4,2,80,128]{4,3,2,1,0:T(8,128)S(1)}, f32[2,5,2,80,128]{4,3,2,1,0:T(8,128)S(1)}, f32[2,3,2,80,1...) custom-call(f32[2,4,64,256]{3,2,1,0:T(8,128)S(1)} %collective-permute-done.1.of_chip, ...), custom_call_target="tpu_custom_call" | custom-call | flops 5898240 | bytes 8425472 | tf_op jit(solution)/shard_map/pallas_call | solution.py:539
  15.4 1.6 %collective-permute-done.m_chip = f32[3,2,64,128]{3,2,1,0:T(8,128)S(1)} collective-permute-done((f32[3,2,64,128]{3,2,1,0:T(8,128)S(1)}, f32[3,2,64,128]{3,2,1,0:T(8,128)S(1)}, u32[]{:S(2)}, u32[]{:S(2)}) %collective-permute-start) | collective-permute-done | bytes 196640 | tf_op jit(solution)/shard_map/ppermute | solution.py:560
  17.0 1.3 %shard_map.53 = (f32[3,2,64,128]{3,2,1,0:T(8,128)S(1)}, f32[2,2,64,128]{3,2,1,0:T(8,128)S(1)}, f32[2,2,64,128]{3,2,1,0:T(8,128)S(1)}, f32[2,2,64,128]{3,2,1,0:T(...) custom-call(f32[3,2,64,128]{3,2,1,0:T(8,128)S(1)} %collective-permut, ...), custom_call_target="tpu_custom_call" | custom-call | flops 5898240 | bytes 11001856 | tf_op jit(solution)/shard_map/pallas_call | solution.py:539
  18.3 3.8 %collective-permute-start.5 = (f32[2,3,2,72,128]{4,3,2,1,0:T(8,128)S(1)}, f32[2,3,2,72,128]{4,3,2,1,0:T(8,128)S(1)}, u32[]{:S(2)}, u32[]{:S(2)}) collective-permute-start(f32[2,3,2,72,128]{4,3,2,1,0:T(8,128)S(1)} %get-tuple-element.71), channel_id=1, source_target_pairs={{0,1},{1,0},{2,3},{3,2},{4,5},{5,4},{6,7},{7,6},{8,9},{9,8},{10,11... | collective-permute-start | bytes 1327112 | tf_op jit(solution)/shard_map/ppermute | solution.py:559
  22.1 4.8 %collective-permute-start.4 = (f32[2,3,2,64,128]{4,3,2,1,0:T(8,128)S(1)}, f32[2,3,2,64,128]{4,3,2,1,0:T(8,128)S(1)}, u32[]{:S(2)}, u32[]{:S(2)}) collective-permute-start(f32[2,3,2,64,128]{4,3,2,1,0:T(8,128)S(1)} %get-tuple-element.62), channel_id=1, source_target_pairs={{0,15},{1,2},{2,1},{3,4},{4,3},{5,6},{6,5},{7,8},{8,7},{9,10},{10,... | collective-permute-start | bytes 1179656 | tf_op jit(solution)/shard_map/ppermute | solution.py:560
  26.9 0.0 collective-permute-done.5.of_core
  26.9 1.5 %collective-permute-start.8 = (f32[8,128]{1,0:T(8,128)S(1)}, f32[8,128]{1,0:T(8,128)S(1)}, u32[]{:S(2)}, u32[]{:S(2)}) collective-permute-start(f32[8,128]{1,0:T(8,128)S(1)} %fusion.share_in), channel_id=1, source_target_pairs={{0,16},{1,13},{2,14},{3,19},{4,20},{5,9},{6,10},{7,23},{8,24},{9,5... | collective-permute-start | bytes 12296 | tf_op jit(solution)/shard_map/ppermute | solution.py:622
  28.4 0.5 %collective-permute-start.6 = (f32[8,128]{1,0:T(8,128)S(1)}, f32[8,128]{1,0:T(8,128)S(1)}, u32[]{:S(2)}, u32[]{:S(2)}) collective-permute-start(f32[8,128]{1,0:T(8,128)S(1)} %fusion.share_in), channel_id=1, source_target_pairs={{0,16},{1,9},{2,10},{3,19},{4,20},{5,13},{6,14},{7,23},{8,24},{9,1... | collective-permute-start | bytes 12296 | tf_op jit(solution)/shard_map/ppermute | solution.py:622
  28.9 1.5 %collective-permute-start.7 = (f32[8,128]{1,0:T(8,128)S(1)}, f32[8,128]{1,0:T(8,128)S(1)}, u32[]{:S(2)}, u32[]{:S(2)}) collective-permute-start(f32[8,128]{1,0:T(8,128)S(1)} %fusion.share_in), channel_id=1, source_target_pairs={{0,16},{1,5},{2,6},{3,19},{4,20},{5,1},{6,2},{7,23},{8,24},{9,13},... | collective-permute-start | bytes 12296 | tf_op jit(solution)/shard_map/ppermute | solution.py:622
  30.4 2.0 %shard_map.54 = (f32[2,5,2,80,128]{4,3,2,1,0:T(8,128)S(1)}, f32[2,1,2,80,128]{4,3,2,1,0:T(8,128)S(1)}, f32[2,3,2,80,128]{4,3,2,1,0:T(8,128)S(1)}, f32[2,3,2,64,1...) custom-call(f32[2,3,2,72,128]{4,3,2,1,0:T(8,128)S(1)} %collective-pe, ...), custom_call_target="tpu_custom_call" | custom-call | flops 7864320 | bytes 10903552 | tf_op jit(solution)/shard_map/pallas_call | solution.py:539
  32.4 0.0 collective-permute-done.8
  32.4 0.0 collective-permute-done.6
  32.4 0.1 collective-permute-done.7
  32.5 1.5 %collective-permute-start.9 = (f32[8,128]{1,0:T(8,128)S(1)}, f32[8,128]{1,0:T(8,128)S(1)}, u32[]{:S(2)}, u32[]{:S(2)}) collective-permute-start(f32[8,128]{1,0:T(8,128)S(1)} %add_add_fusion.share_in), channel_id=1, source_target_pairs={{0,16},{1,2},{2,1},{3,19},{4,20},{5,6},{6,5},{7,23},{8,24},{9,10},... | collective-permute-start | bytes 12296 | tf_op jit(solution)/shard_map/ppermute | solution.py:622
  34.0 0.0 collective-permute-done.4.of_chip
  34.0 1.7 %shard_map.55 = (f32[4,64,256]{2,1,0:T(8,128)}, f32[8,128]{1,0:T(8,128)S(1)}) custom-call(f32[2,3,2,64,128]{4,3,2,1,0:T(8,128)S(1)} %collective-permute-done.4.of_chip, f32[6,2,64,128]{3,2,1,0:T(8,128)S(1)} %get-tuple-element.50.mx.mx_a, f32[6,2,64,128]{3,2,1,0:T(8,128)S(1)} %get-tuple-element.51.my.my_a, ...), custom_call_target="tpu_custom_call" | custom-call | flops 5898240 | bytes 9150464 | tf_op jit(solution)/shard_map/pallas_call | solution.py:539
  35.7 0.5 %collective-permute-done.9 = f32[8,128]{1,0:T(8,128)S(1)} collective-permute-done((f32[8,128]{1,0:T(8,128)S(1)}, f32[8,128]{1,0:T(8,128)S(1)}, u32[]{:S(2)}, u32[]{:S(2)}) %collective-permute-start.9) | collective-permute-done | bytes 4128 | tf_op jit(solution)/shard_map/ppermute | solution.py:622
  36.1 0.0 collective-permute-start.10
  36.1 1.2 %collective-permute-done.10.handed = f32[8,128]{1,0:T(8,128)S(1)} collective-permute-done((f32[8,128]{1,0:T(8,128)S(1)}, f32[8,128]{1,0:T(8,128)S(1)}, u32[]{:S(2)}, u32[]{:S(2)}) %collective-permute-start.10) | collective-permute-done | bytes 4128 | tf_op jit(solution)/shard_map/ppermute | solution.py:661
  37.3 0.6 %shard_map.56 = f32[1]{0:T(128)} custom-call(f32[8,128]{1,0:T(8,128)S(1)} %add.19.total, f32[8,128]{1,0:T(8,128)S(1)} %collective-permute-done.10.handed), custom_call_target="tpu_custom_call" | custom-call | flops 1 | bytes 8196 | tf_op jit(solution)/shard_map/pallas_call | solution.py:539
  (3 shorter events, 0.0 us)
Async XLA Ops:
  0.6 9.8 %collective-permute-start.2 = (f32[2,4,64,256]{3,2,1,0:T(8,128)}, f32[2,4,64,256]{3,2,1,0:T(8,128)S(1)}, u32[]{:S(2)}, u32[]{:S(2)}) collective-permute-start(f32[2,4,64,256]{3,2,1,0:T(8,128)} %initial.1), channel_id=1, source_target_pairs={{0,1},{1,0},{2,3},{3,2},{4,5},{5,4},{6,7},{7,6},{8,9},{9,8},{10,11... | collective-permute-start | bytes 1572872 | tf_op jit(solution)/shard_map/ppermute | solution.py:559
  1.1 12.8 %collective-permute-start.1 = (f32[2,4,64,256]{3,2,1,0:T(8,128)}, f32[2,4,64,256]{3,2,1,0:T(8,128)S(1)}, u32[]{:S(2)}, u32[]{:S(2)}) collective-permute-start(f32[2,4,64,256]{3,2,1,0:T(8,128)} %initial.1), channel_id=1, source_target_pairs={{0,15},{1,2},{2,1},{3,4},{4,3},{5,6},{6,5},{7,8},{8,7},{9,10},{10,... | collective-permute-start | bytes 1572872 | tf_op jit(solution)/shard_map/ppermute | solution.py:560
  6.8 1.1 %copy-start.1 = (f32[2,4,64,256]{3,2,1,0:T(8,128)S(1)}, f32[2,4,64,256]{3,2,1,0:T(8,128)}, u32[]{:S(2)}) copy-start(f32[2,4,64,256]{3,2,1,0:T(8,128)} %initial.1) | copy-start | bytes 1572868
  7.9 0.9 %copy-start.2 = (f32[4,64,256]{2,1,0:T(8,128)S(1)}, f32[4,64,256]{2,1,0:T(8,128)}, u32[]{:S(2)}) copy-start(f32[4,64,256]{2,1,0:T(8,128)} %mobility.1) | copy-start | bytes 786436
  8.9 1.5 %collective-permute-start.3 = (f32[3,2,64,128]{3,2,1,0:T(8,128)S(1)}, f32[3,2,64,128]{3,2,1,0:T(8,128)S(1)}, u32[]{:S(2)}, u32[]{:S(2)}) collective-permute-start(f32[3,2,64,128]{3,2,1,0:T(8,128)S(1)} %get-tuple-element.47), channel_id=1, source_target_pairs={{0,1},{1,0},{2,3},{3,2},{4,5},{5,4},{6,7},{7,6},{8,9},{9,8},{10,11... | collective-permute-start | bytes 589832 | tf_op jit(solution)/shard_map/ppermute | solution.py:559
  9.0 8.0 %collective-permute-start = (f32[3,2,64,128]{3,2,1,0:T(8,128)S(1)}, f32[3,2,64,128]{3,2,1,0:T(8,128)S(1)}, u32[]{:S(2)}, u32[]{:S(2)}) collective-permute-start(f32[3,2,64,128]{3,2,1,0:T(8,128)S(1)} %get-tuple-element.44), channel_id=1, source_target_pairs={{0,15},{1,2},{2,1},{3,4},{4,3},{5,6},{6,5},{7,8},{8,7},{9,10},{10,... | collective-permute-start | bytes 589832 | tf_op jit(solution)/shard_map/ppermute | solution.py:560
  10.5 3.5 %copy-start = (f32[2,4,64,256]{3,2,1,0:T(8,128)S(1)}, f32[2,4,64,256]{3,2,1,0:T(8,128)}, u32[]{:S(2)}) copy-start(f32[2,4,64,256]{3,2,1,0:T(8,128)} %observed.3) | copy-start | bytes 1572868
  18.3 8.6 %collective-permute-start.5 = (f32[2,3,2,72,128]{4,3,2,1,0:T(8,128)S(1)}, f32[2,3,2,72,128]{4,3,2,1,0:T(8,128)S(1)}, u32[]{:S(2)}, u32[]{:S(2)}) collective-permute-start(f32[2,3,2,72,128]{4,3,2,1,0:T(8,128)S(1)} %get-tuple-element.71), channel_id=1, source_target_pairs={{0,1},{1,0},{2,3},{3,2},{4,5},{5,4},{6,7},{7,6},{8,9},{9,8},{10,11... | collective-permute-start | bytes 1327112 | tf_op jit(solution)/shard_map/ppermute | solution.py:559
  22.1 11.9 %collective-permute-start.4 = (f32[2,3,2,64,128]{4,3,2,1,0:T(8,128)S(1)}, f32[2,3,2,64,128]{4,3,2,1,0:T(8,128)S(1)}, u32[]{:S(2)}, u32[]{:S(2)}) collective-permute-start(f32[2,3,2,64,128]{4,3,2,1,0:T(8,128)S(1)} %get-tuple-element.62), channel_id=1, source_target_pairs={{0,15},{1,2},{2,1},{3,4},{4,3},{5,6},{6,5},{7,8},{8,7},{9,10},{10,... | collective-permute-start | bytes 1179656 | tf_op jit(solution)/shard_map/ppermute | solution.py:560
  26.9 5.5 %collective-permute-start.8 = (f32[8,128]{1,0:T(8,128)S(1)}, f32[8,128]{1,0:T(8,128)S(1)}, u32[]{:S(2)}, u32[]{:S(2)}) collective-permute-start(f32[8,128]{1,0:T(8,128)S(1)} %fusion.share_in), channel_id=1, source_target_pairs={{0,16},{1,13},{2,14},{3,19},{4,20},{5,9},{6,10},{7,23},{8,24},{9,5... | collective-permute-start | bytes 12296 | tf_op jit(solution)/shard_map/ppermute | solution.py:622
  28.4 4.0 %collective-permute-start.6 = (f32[8,128]{1,0:T(8,128)S(1)}, f32[8,128]{1,0:T(8,128)S(1)}, u32[]{:S(2)}, u32[]{:S(2)}) collective-permute-start(f32[8,128]{1,0:T(8,128)S(1)} %fusion.share_in), channel_id=1, source_target_pairs={{0,16},{1,9},{2,10},{3,19},{4,20},{5,13},{6,14},{7,23},{8,24},{9,1... | collective-permute-start | bytes 12296 | tf_op jit(solution)/shard_map/ppermute | solution.py:622
  28.9 3.6 %collective-permute-start.7 = (f32[8,128]{1,0:T(8,128)S(1)}, f32[8,128]{1,0:T(8,128)S(1)}, u32[]{:S(2)}, u32[]{:S(2)}) collective-permute-start(f32[8,128]{1,0:T(8,128)S(1)} %fusion.share_in), channel_id=1, source_target_pairs={{0,16},{1,5},{2,6},{3,19},{4,20},{5,1},{6,2},{7,23},{8,24},{9,13},... | collective-permute-start | bytes 12296 | tf_op jit(solution)/shard_map/ppermute | solution.py:622
  32.5 3.6 %collective-permute-start.9 = (f32[8,128]{1,0:T(8,128)S(1)}, f32[8,128]{1,0:T(8,128)S(1)}, u32[]{:S(2)}, u32[]{:S(2)}) collective-permute-start(f32[8,128]{1,0:T(8,128)S(1)} %add_add_fusion.share_in), channel_id=1, source_target_pairs={{0,16},{1,2},{2,1},{3,19},{4,20},{5,6},{6,5},{7,23},{8,24},{9,10},... | collective-permute-start | bytes 12296 | tf_op jit(solution)/shard_map/ppermute | solution.py:622
  36.1 1.2 %collective-permute-start.10 = (f32[8,128]{1,0:T(8,128)S(1)}, f32[8,128]{1,0:T(8,128)S(1)}, u32[]{:S(2)}, u32[]{:S(2)}) collective-permute-start(f32[8,128]{1,0:T(8,128)S(1)} %add.19.total), channel_id=1, source_target_pairs={{0,1},{1,0},{2,3},{3,2},{4,5},{5,4},{6,7},{7,6},{8,9},{9,8},{10,11... | collective-permute-start | bytes 12296 | tf_op jit(solution)/shard_map/ppermute | solution.py:661

commit v18 on v17

--- a/solution.py
+++ b/solution.py
@@ -152,7 +152,8 @@
                 put_padded(conc, (run, at), row, plain(initial, (run, place[at]), row))
         return carry
 
-    lax.fori_loop(0, runs, one_run, 0)
+    for run in range(runs):
+        one_run(run, 0)
     for row in chunks(ny):
         for at in range(n):
             value = plain(mobility, (place[at],), row)
@@ -239,7 +240,8 @@
             put_potential(row, conc, run, range(-3, n - 1), Line((chem0, -3, n - 2)))
         return carry
 
-    lax.fori_loop(0, runs, one_run, 0)
+    for run in range(runs):
+        one_run(run, 0)
 
 
 def chip_kernel(
@@ -279,7 +281,8 @@
             put_step(row, faces, chem1, state1, run, range(0, n - 3), target)
         return carry
 
-    lax.fori_loop(0, runs, one_run, 0)
+    for run in range(runs):
+        one_run(run, 0)
 
 
 def forward_kernel(
@@ -331,7 +334,8 @@
                 put_flat(to_core, (run, at), row, padded(*adjoint2(at, run), row))
         return carry
 
-    lax.fori_loop(0, runs, one_run, 0)
+    for run in range(runs):
+        one_run(run, 0)
     columns = (0.5 / runs) * jnp.sum(total[...], axis=0, keepdims=True)
     mine = jnp.broadcast_to(jnp.sum(columns, axis=1, keepdims=True), share.shape)
     share[...] = mine
@@ -432,7 +436,8 @@
                 put_flat(sum_z, (at,), row, total_z)
         return carry
 
-    lax.fori_loop(0, runs, one_run, 0)
+    for run in range(runs):
+        one_run(run, 0)
     for row in chunks(ny):
         for at in range(n - 2):
             sides = flat(sum_z, (at,), row)
@@ -509,7 +514,8 @@
                 ))
         return carry
 
-    lax.fori_loop(0, runs, one_run, 0)
+    for run in range(runs):
+        one_run(run, 0)
     for row in chunks(ny):
         for at in range(n - 2):
             value = flat(part, (at,), row)

time: 38.1 us -> 37.9 us (level)
  transfers between devices with their start and end apart: 11 -> 11, of which waited for: 6 -> 6; matrix products, arithmetic and copies ran while one was open for 0% -> 0% of each run, Pallas kernels for 16% -> 15%
where the time goes in v18:
time: 37.9 us; the launch traced here: 37.8 us
  starting transfers between devices  20.4 us (54%)
  Pallas kernels  7.52 us (20%)
  waiting for transfers between devices  7.06 us (19%)
  local copies, waits for them, and re-layouts  2.03 us (5%)
  between operations  0.7 us (2%)
    ppermute x3, starting transfers between devices, neighbours(): return (lax.ppermute(to_chip, 'gx', over_chips), of_core)  11.1 us
    pallas_call x7, Pallas kernels, call(): pl.pallas_call(kernel, out_shape=tuple((jax.ShapeDtypeStruct(o, jnp.float...  7.52 us
    ppermute x4, starting transfers between devices, hop(): return lax.ppermute(value, ('group', 'gx'), pairs)  5.01 us
    ppermute x3, waiting for transfers between devices, neighbours(): return (lax.ppermute(to_chip, 'gx', over_chips), of_core)  4.44 us
    ppermute x3, starting transfers between devices, neighbours(): of_core = lax.ppermute(to_core, 'gx', over_cores)  4.37 us
    unnamed x6, local copies, waits for them, and re-layouts  2.03 us
    ppermute x1, waiting for transfers between devices, on_device(): handed = lax.ppermute(share, 'gx', over_cores)  1.16 us
    ppermute x3, waiting for transfers between devices, neighbours(): of_core = lax.ppermute(to_core, 'gx', over_cores)  0.83 us
  transfers between devices with their start and end apart: 11, of which 6 were waited for; matrix products, arithmetic and copies ran while one was open for 0% of the time, Pallas kernels for 15%

profile of v18, /device:TPU:0, one launch (start us, length us, event | category | flops | bytes accessed | tf_op | source)
XLA Modules:
  0.0 37.8 jit_solution(6605948908276261467)
XLA Ops:
  0.6 0.5 %collective-permute-start.2 = (f32[2,4,64,256]{3,2,1,0:T(8,128)}, f32[2,4,64,256]{3,2,1,0:T(8,128)S(1)}, u32[]{:S(2)}, u32[]{:S(2)}) collective-permute-start(f32[2,4,64,256]{3,2,1,0:T(8,128)} %initial.1), channel_id=1, source_target_pairs={{0,1},{1,0},{2,3},{3,2},{4,5},{5,4},{6,7},{7,6},{8,9},{9,8},{10,11... | collective-permute-start | bytes 1572872 | tf_op jit(solution)/shard_map/ppermute | solution.py:565
  1.1 5.7 %collective-permute-start.1 = (f32[2,4,64,256]{3,2,1,0:T(8,128)}, f32[2,4,64,256]{3,2,1,0:T(8,128)S(1)}, u32[]{:S(2)}, u32[]{:S(2)}) collective-permute-start(f32[2,4,64,256]{3,2,1,0:T(8,128)} %initial.1), channel_id=1, source_target_pairs={{0,15},{1,2},{2,1},{3,4},{4,3},{5,6},{6,5},{7,8},{8,7},{9,10},{10,... | collective-permute-start | bytes 1572872 | tf_op jit(solution)/shard_map/ppermute | solution.py:566
  6.8 0.0 copy-start.1
  6.8 1.1 %copy-done.1 = f32[2,4,64,256]{3,2,1,0:T(8,128)S(1)} copy-done((f32[2,4,64,256]{3,2,1,0:T(8,128)S(1)}, f32[2,4,64,256]{3,2,1,0:T(8,128)}, u32[]{:S(2)}) %copy-start.1) | copy-done | bytes 524312
  7.9 0.0 copy-start.2
  7.9 0.9 %copy-done.2 = f32[4,64,256]{2,1,0:T(8,128)S(1)} copy-done((f32[4,64,256]{2,1,0:T(8,128)S(1)}, f32[4,64,256]{2,1,0:T(8,128)}, u32[]{:S(2)}) %copy-start.2) | copy-done | bytes 262168
  8.8 0.1 shard_map.50
  8.9 0.1 collective-permute-start.3
  9.0 0.6 %collective-permute-start = (f32[3,2,64,128]{3,2,1,0:T(8,128)S(1)}, f32[3,2,64,128]{3,2,1,0:T(8,128)S(1)}, u32[]{:S(2)}, u32[]{:S(2)}) collective-permute-start(f32[3,2,64,128]{3,2,1,0:T(8,128)S(1)} %get-tuple-element.44), channel_id=1, source_target_pairs={{0,15},{1,2},{2,1},{3,4},{4,3},{5,6},{6,5},{7,8},{8,7},{9,10},{10,... | collective-permute-start | bytes 589832 | tf_op jit(solution)/shard_map/ppermute | solution.py:566
  9.6 0.8 %collective-permute-done.3.m_core = f32[3,2,64,128]{3,2,1,0:T(8,128)S(1)} collective-permute-done((f32[3,2,64,128]{3,2,1,0:T(8,128)S(1)}, f32[3,2,64,128]{3,2,1,0:T(8,128)S(1)}, u32[]{:S(2)}, u32[]{:S(2)}) %collective-permute-start.3) | collective-permute-done | bytes 196640 | tf_op jit(solution)/shard_map/ppermute | solution.py:565
  10.5 0.0 collective-permute-done.2.of_core
  10.5 0.0 copy-start
  10.5 0.7 %shard_map.51 = (f32[2,4,2,80,128]{4,3,2,1,0:T(8,128)S(1)}, f32[2,6,2,80,128]{4,3,2,1,0:T(8,128)S(1)}, f32[6,2,64,128]{3,2,1,0:T(8,128)S(1)}, f32[6,2,64,128]{3,...) custom-call(f32[2,4,64,256]{3,2,1,0:T(8,128)S(1)} %collective-permut, ...), custom_call_target="tpu_custom_call" | custom-call | flops 3932160 | bytes 5636096 | tf_op jit(solution)/shard_map/pallas_call | solution.py:545
  11.2 2.8 %collective-permute-done.1.of_chip = f32[2,4,64,256]{3,2,1,0:T(8,128)S(1)} collective-permute-done((f32[2,4,64,256]{3,2,1,0:T(8,128)}, f32[2,4,64,256]{3,2,1,0:T(8,128)S(1)}, u32[]{:S(2)}, u32[]{:S(2)}) %collective-permute-start.1) | collective-permute-done | bytes 524320 | tf_op jit(solution)/shard_map/ppermute | solution.py:566
  14.0 0.0 copy-done
  14.0 1.3 %shard_map.52 = (f32[2,4,2,80,128]{4,3,2,1,0:T(8,128)S(1)}, f32[2,4,2,80,128]{4,3,2,1,0:T(8,128)S(1)}, f32[2,5,2,80,128]{4,3,2,1,0:T(8,128)S(1)}, f32[2,3,2,80,1...) custom-call(f32[2,4,64,256]{3,2,1,0:T(8,128)S(1)} %collective-permute-done.1.of_chip, ...), custom_call_target="tpu_custom_call" | custom-call | flops 5898240 | bytes 8425472 | tf_op jit(solution)/shard_map/pallas_call | solution.py:545
  15.4 1.6 %collective-permute-done.m_chip = f32[3,2,64,128]{3,2,1,0:T(8,128)S(1)} collective-permute-done((f32[3,2,64,128]{3,2,1,0:T(8,128)S(1)}, f32[3,2,64,128]{3,2,1,0:T(8,128)S(1)}, u32[]{:S(2)}, u32[]{:S(2)}) %collective-permute-start) | collective-permute-done | bytes 196640 | tf_op jit(solution)/shard_map/ppermute | solution.py:566
  17.0 1.2 %shard_map.53 = (f32[3,2,64,128]{3,2,1,0:T(8,128)S(1)}, f32[2,2,64,128]{3,2,1,0:T(8,128)S(1)}, f32[2,2,64,128]{3,2,1,0:T(8,128)S(1)}, f32[2,2,64,128]{3,2,1,0:T(...) custom-call(f32[3,2,64,128]{3,2,1,0:T(8,128)S(1)} %collective-permut, ...), custom_call_target="tpu_custom_call" | custom-call | flops 5898240 | bytes 11001856 | tf_op jit(solution)/shard_map/pallas_call | solution.py:545
  18.2 3.8 %collective-permute-start.5 = (f32[2,3,2,72,128]{4,3,2,1,0:T(8,128)S(1)}, f32[2,3,2,72,128]{4,3,2,1,0:T(8,128)S(1)}, u32[]{:S(2)}, u32[]{:S(2)}) collective-permute-start(f32[2,3,2,72,128]{4,3,2,1,0:T(8,128)S(1)} %get-tuple-element.71), channel_id=1, source_target_pairs={{0,1},{1,0},{2,3},{3,2},{4,5},{5,4},{6,7},{7,6},{8,9},{9,8},{10,11... | collective-permute-start | bytes 1327112 | tf_op jit(solution)/shard_map/ppermute | solution.py:565
  22.0 4.8 %collective-permute-start.4 = (f32[2,3,2,64,128]{4,3,2,1,0:T(8,128)S(1)}, f32[2,3,2,64,128]{4,3,2,1,0:T(8,128)S(1)}, u32[]{:S(2)}, u32[]{:S(2)}) collective-permute-start(f32[2,3,2,64,128]{4,3,2,1,0:T(8,128)S(1)} %get-tuple-element.62), channel_id=1, source_target_pairs={{0,15},{1,2},{2,1},{3,4},{4,3},{5,6},{6,5},{7,8},{8,7},{9,10},{10,... | collective-permute-start | bytes 1179656 | tf_op jit(solution)/shard_map/ppermute | solution.py:566
  26.8 0.0 collective-permute-done.5.of_core
  26.8 1.5 %collective-permute-start.8 = (f32[8,128]{1,0:T(8,128)S(1)}, f32[8,128]{1,0:T(8,128)S(1)}, u32[]{:S(2)}, u32[]{:S(2)}) collective-permute-start(f32[8,128]{1,0:T(8,128)S(1)} %fusion.share_in), channel_id=1, source_target_pairs={{0,16},{1,13},{2,14},{3,19},{4,20},{5,9},{6,10},{7,23},{8,24},{9,5... | collective-permute-start | bytes 12296 | tf_op jit(solution)/shard_map/ppermute | solution.py:628
  28.3 0.5 %collective-permute-start.6 = (f32[8,128]{1,0:T(8,128)S(1)}, f32[8,128]{1,0:T(8,128)S(1)}, u32[]{:S(2)}, u32[]{:S(2)}) collective-permute-start(f32[8,128]{1,0:T(8,128)S(1)} %fusion.share_in), channel_id=1, source_target_pairs={{0,16},{1,9},{2,10},{3,19},{4,20},{5,13},{6,14},{7,23},{8,24},{9,1... | collective-permute-start | bytes 12296 | tf_op jit(solution)/shard_map/ppermute | solution.py:628
  28.8 1.5 %collective-permute-start.7 = (f32[8,128]{1,0:T(8,128)S(1)}, f32[8,128]{1,0:T(8,128)S(1)}, u32[]{:S(2)}, u32[]{:S(2)}) collective-permute-start(f32[8,128]{1,0:T(8,128)S(1)} %fusion.share_in), channel_id=1, source_target_pairs={{0,16},{1,5},{2,6},{3,19},{4,20},{5,1},{6,2},{7,23},{8,24},{9,13},... | collective-permute-start | bytes 12296 | tf_op jit(solution)/shard_map/ppermute | solution.py:628
  30.3 2.0 %shard_map.54 = (f32[2,5,2,80,128]{4,3,2,1,0:T(8,128)S(1)}, f32[2,1,2,80,128]{4,3,2,1,0:T(8,128)S(1)}, f32[2,3,2,80,128]{4,3,2,1,0:T(8,128)S(1)}, f32[2,3,2,64,1...) custom-call(f32[2,3,2,72,128]{4,3,2,1,0:T(8,128)S(1)} %collective-pe, ...), custom_call_target="tpu_custom_call" | custom-call | flops 7864320 | bytes 10903552 | tf_op jit(solution)/shard_map/pallas_call | solution.py:545
  32.3 0.0 collective-permute-done.8
  32.3 0.0 collective-permute-done.6
  32.3 0.1 collective-permute-done.7
  32.4 1.5 %collective-permute-start.9 = (f32[8,128]{1,0:T(8,128)S(1)}, f32[8,128]{1,0:T(8,128)S(1)}, u32[]{:S(2)}, u32[]{:S(2)}) collective-permute-start(f32[8,128]{1,0:T(8,128)S(1)} %add_add_fusion.share_in), channel_id=1, source_target_pairs={{0,16},{1,2},{2,1},{3,19},{4,20},{5,6},{6,5},{7,23},{8,24},{9,10},... | collective-permute-start | bytes 12296 | tf_op jit(solution)/shard_map/ppermute | solution.py:628
  33.9 0.0 collective-permute-done.4.of_chip
  33.9 1.6 %shard_map.55 = (f32[4,64,256]{2,1,0:T(8,128)}, f32[8,128]{1,0:T(8,128)S(1)}) custom-call(f32[2,3,2,64,128]{4,3,2,1,0:T(8,128)S(1)} %collective-permute-done.4.of_chip, f32[6,2,64,128]{3,2,1,0:T(8,128)S(1)} %get-tuple-element.50.mx.mx_a, f32[6,2,64,128]{3,2,1,0:T(8,128)S(1)} %get-tuple-element.51.my.my_a, ...), custom_call_target="tpu_custom_call" | custom-call | flops 5898240 | bytes 9150464 | tf_op jit(solution)/shard_map/pallas_call | solution.py:545
  35.5 0.5 %collective-permute-done.9 = f32[8,128]{1,0:T(8,128)S(1)} collective-permute-done((f32[8,128]{1,0:T(8,128)S(1)}, f32[8,128]{1,0:T(8,128)S(1)}, u32[]{:S(2)}, u32[]{:S(2)}) %collective-permute-start.9) | collective-permute-done | bytes 4128 | tf_op jit(solution)/shard_map/ppermute | solution.py:628
  36.0 0.0 collective-permute-start.10
  36.0 1.2 %collective-permute-done.10.handed = f32[8,128]{1,0:T(8,128)S(1)} collective-permute-done((f32[8,128]{1,0:T(8,128)S(1)}, f32[8,128]{1,0:T(8,128)S(1)}, u32[]{:S(2)}, u32[]{:S(2)}) %collective-permute-start.10) | collective-permute-done | bytes 4128 | tf_op jit(solution)/shard_map/ppermute | solution.py:667
  37.2 0.6 %shard_map.56 = f32[1]{0:T(128)} custom-call(f32[8,128]{1,0:T(8,128)S(1)} %add.19.total, f32[8,128]{1,0:T(8,128)S(1)} %collective-permute-done.10.handed), custom_call_target="tpu_custom_call" | custom-call | flops 1 | bytes 8196 | tf_op jit(solution)/shard_map/pallas_call | solution.py:545
  (3 shorter events, 0.0 us)
Async XLA Ops:
  0.6 9.8 %collective-permute-start.2 = (f32[2,4,64,256]{3,2,1,0:T(8,128)}, f32[2,4,64,256]{3,2,1,0:T(8,128)S(1)}, u32[]{:S(2)}, u32[]{:S(2)}) collective-permute-start(f32[2,4,64,256]{3,2,1,0:T(8,128)} %initial.1), channel_id=1, source_target_pairs={{0,1},{1,0},{2,3},{3,2},{4,5},{5,4},{6,7},{7,6},{8,9},{9,8},{10,11... | collective-permute-start | bytes 1572872 | tf_op jit(solution)/shard_map/ppermute | solution.py:565
  1.1 12.8 %collective-permute-start.1 = (f32[2,4,64,256]{3,2,1,0:T(8,128)}, f32[2,4,64,256]{3,2,1,0:T(8,128)S(1)}, u32[]{:S(2)}, u32[]{:S(2)}) collective-permute-start(f32[2,4,64,256]{3,2,1,0:T(8,128)} %initial.1), channel_id=1, source_target_pairs={{0,15},{1,2},{2,1},{3,4},{4,3},{5,6},{6,5},{7,8},{8,7},{9,10},{10,... | collective-permute-start | bytes 1572872 | tf_op jit(solution)/shard_map/ppermute | solution.py:566
  6.8 1.1 %copy-start.1 = (f32[2,4,64,256]{3,2,1,0:T(8,128)S(1)}, f32[2,4,64,256]{3,2,1,0:T(8,128)}, u32[]{:S(2)}) copy-start(f32[2,4,64,256]{3,2,1,0:T(8,128)} %initial.1) | copy-start | bytes 1572868
  7.9 0.9 %copy-start.2 = (f32[4,64,256]{2,1,0:T(8,128)S(1)}, f32[4,64,256]{2,1,0:T(8,128)}, u32[]{:S(2)}) copy-start(f32[4,64,256]{2,1,0:T(8,128)} %mobility.1) | copy-start | bytes 786436
  8.9 1.5 %collective-permute-start.3 = (f32[3,2,64,128]{3,2,1,0:T(8,128)S(1)}, f32[3,2,64,128]{3,2,1,0:T(8,128)S(1)}, u32[]{:S(2)}, u32[]{:S(2)}) collective-permute-start(f32[3,2,64,128]{3,2,1,0:T(8,128)S(1)} %get-tuple-element.47), channel_id=1, source_target_pairs={{0,1},{1,0},{2,3},{3,2},{4,5},{5,4},{6,7},{7,6},{8,9},{9,8},{10,11... | collective-permute-start | bytes 589832 | tf_op jit(solution)/shard_map/ppermute | solution.py:565
  9.0 8.0 %collective-permute-start = (f32[3,2,64,128]{3,2,1,0:T(8,128)S(1)}, f32[3,2,64,128]{3,2,1,0:T(8,128)S(1)}, u32[]{:S(2)}, u32[]{:S(2)}) collective-permute-start(f32[3,2,64,128]{3,2,1,0:T(8,128)S(1)} %get-tuple-element.44), channel_id=1, source_target_pairs={{0,15},{1,2},{2,1},{3,4},{4,3},{5,6},{6,5},{7,8},{8,7},{9,10},{10,... | collective-permute-start | bytes 589832 | tf_op jit(solution)/shard_map/ppermute | solution.py:566
  10.5 3.5 %copy-start = (f32[2,4,64,256]{3,2,1,0:T(8,128)S(1)}, f32[2,4,64,256]{3,2,1,0:T(8,128)}, u32[]{:S(2)}) copy-start(f32[2,4,64,256]{3,2,1,0:T(8,128)} %observed.3) | copy-start | bytes 1572868
  18.2 8.6 %collective-permute-start.5 = (f32[2,3,2,72,128]{4,3,2,1,0:T(8,128)S(1)}, f32[2,3,2,72,128]{4,3,2,1,0:T(8,128)S(1)}, u32[]{:S(2)}, u32[]{:S(2)}) collective-permute-start(f32[2,3,2,72,128]{4,3,2,1,0:T(8,128)S(1)} %get-tuple-element.71), channel_id=1, source_target_pairs={{0,1},{1,0},{2,3},{3,2},{4,5},{5,4},{6,7},{7,6},{8,9},{9,8},{10,11... | collective-permute-start | bytes 1327112 | tf_op jit(solution)/shard_map/ppermute | solution.py:565
  22.0 11.9 %collective-permute-start.4 = (f32[2,3,2,64,128]{4,3,2,1,0:T(8,128)S(1)}, f32[2,3,2,64,128]{4,3,2,1,0:T(8,128)S(1)}, u32[]{:S(2)}, u32[]{:S(2)}) collective-permute-start(f32[2,3,2,64,128]{4,3,2,1,0:T(8,128)S(1)} %get-tuple-element.62), channel_id=1, source_target_pairs={{0,15},{1,2},{2,1},{3,4},{4,3},{5,6},{6,5},{7,8},{8,7},{9,10},{10,... | collective-permute-start | bytes 1179656 | tf_op jit(solution)/shard_map/ppermute | solution.py:566
  26.8 5.5 %collective-permute-start.8 = (f32[8,128]{1,0:T(8,128)S(1)}, f32[8,128]{1,0:T(8,128)S(1)}, u32[]{:S(2)}, u32[]{:S(2)}) collective-permute-start(f32[8,128]{1,0:T(8,128)S(1)} %fusion.share_in), channel_id=1, source_target_pairs={{0,16},{1,13},{2,14},{3,19},{4,20},{5,9},{6,10},{7,23},{8,24},{9,5... | collective-permute-start | bytes 12296 | tf_op jit(solution)/shard_map/ppermute | solution.py:628
  28.3 4.0 %collective-permute-start.6 = (f32[8,128]{1,0:T(8,128)S(1)}, f32[8,128]{1,0:T(8,128)S(1)}, u32[]{:S(2)}, u32[]{:S(2)}) collective-permute-start(f32[8,128]{1,0:T(8,128)S(1)} %fusion.share_in), channel_id=1, source_target_pairs={{0,16},{1,9},{2,10},{3,19},{4,20},{5,13},{6,14},{7,23},{8,24},{9,1... | collective-permute-start | bytes 12296 | tf_op jit(solution)/shard_map/ppermute | solution.py:628
  28.8 3.6 %collective-permute-start.7 = (f32[8,128]{1,0:T(8,128)S(1)}, f32[8,128]{1,0:T(8,128)S(1)}, u32[]{:S(2)}, u32[]{:S(2)}) collective-permute-start(f32[8,128]{1,0:T(8,128)S(1)} %fusion.share_in), channel_id=1, source_target_pairs={{0,16},{1,5},{2,6},{3,19},{4,20},{5,1},{6,2},{7,23},{8,24},{9,13},... | collective-permute-start | bytes 12296 | tf_op jit(solution)/shard_map/ppermute | solution.py:628
  32.4 3.6 %collective-permute-start.9 = (f32[8,128]{1,0:T(8,128)S(1)}, f32[8,128]{1,0:T(8,128)S(1)}, u32[]{:S(2)}, u32[]{:S(2)}) collective-permute-start(f32[8,128]{1,0:T(8,128)S(1)} %add_add_fusion.share_in), channel_id=1, source_target_pairs={{0,16},{1,2},{2,1},{3,19},{4,20},{5,6},{6,5},{7,23},{8,24},{9,10},... | collective-permute-start | bytes 12296 | tf_op jit(solution)/shard_map/ppermute | solution.py:628
  36.0 1.2 %collective-permute-start.10 = (f32[8,128]{1,0:T(8,128)S(1)}, f32[8,128]{1,0:T(8,128)S(1)}, u32[]{:S(2)}, u32[]{:S(2)}) collective-permute-start(f32[8,128]{1,0:T(8,128)S(1)} %add.19.total), channel_id=1, source_target_pairs={{0,1},{1,0},{2,3},{3,2},{4,5},{5,4},{6,7},{7,6},{8,9},{9,8},{10,11... | collective-permute-start | bytes 12296 | tf_op jit(solution)/shard_map/ppermute | solution.py:667

commit v19 on v18

--- a/solution.py
+++ b/solution.py
@@ -338,8 +338,9 @@
         one_run(run, 0)
     columns = (0.5 / runs) * jnp.sum(total[...], axis=0, keepdims=True)
     mine = jnp.broadcast_to(jnp.sum(columns, axis=1, keepdims=True), share.shape)
-    share[...] = mine
-    to_core[0, 0, 0, ny:] = mine
+    sums = counts(lax.axis_index("gx")) == 1
+    share[...] = jnp.where(sums, mine, 0.0)
+    to_core[0, 0, 0, ny:] = jnp.where(sums, 0.0, mine)
 
 
 def put_adjoint1(row, flow, adjoint2, run, places, weight, target):
@@ -536,8 +537,8 @@
     return (at ^ (at >> 1)) & 1
 
 
-def misfit_kernel(total, handed, misfit):
-    misfit[0] = jnp.where(counts(lax.axis_index("gx")) == 1, total[0, 0], handed[0, 0])
+def misfit_kernel(share, far, misfit):
+    misfit[0] = (share[...] + far[...])[0, 0]
 
 
 def call(kernel, outs, scratch, args, flops, scalar=None):
@@ -649,7 +650,8 @@
         share = share + sum(fars)
         fars = hops(share, bits)
     share = share + sum(fars)
-    far = hop(share, 3)
+    share = share + lax.ppermute(share, "gx", over_cores)
+    far = lax.ppermute(share, "gx", [(at, at ^ 3) for at in range(count)])
     result, share = call(
         late_kernel,
         ((n, ny, nz), (ROWS, LANES)),
@@ -663,9 +665,7 @@
         ),
         60 * runs * 3 * cell,
     )
-    share = share + far
-    handed = lax.ppermute(share, "gx", over_cores)
-    (misfit,) = call(misfit_kernel, ((1,),), (), (share, handed), 1, scalar=0)
+    (misfit,) = call(misfit_kernel, ((1,),), (), (share, far), 1, scalar=0)
     return (result, misfit)
 
 

time: 37.9 us -> 37.4 us (0.987)
  starting transfers between devices: 20.4 us -> 19.9 us
    ppermute x4 -> x3, starting transfers between devices: 5.01 us -> 3.52 us  [hop(): return lax.ppermute(value, ('group', 'gx'), pairs)]
    ppermute x1 -> x2, starting transfers between devices: 0.01 us -> 0.96 us  [the longest x1 0.95 us: on_device(): far = lax.ppermute(share, 'gx', [(at, at ^ 3) for at in range(count)])]
    ppermute x4 -> x3, waiting for transfers between devices: 0.63 us -> 0.12 us  [hop(): return lax.ppermute(value, ('group', 'gx'), pairs)]
    ppermute x1 -> x2, waiting for transfers between devices: 1.16 us -> 1.64 us  [the longest x1 1.16 us: on_device(): share = share + lax.ppermute(share, 'gx', over_cores)]
where the time goes in v19:
time: 37.4 us; the launch traced here: 37.2 us
  starting transfers between devices  19.9 us (53%)
  Pallas kernels  7.52 us (20%)
  waiting for transfers between devices  7.02 us (19%)
  local copies, waits for them, and re-layouts  2.03 us (5%)
  between operations  0.7 us (2%)
    ppermute x3, starting transfers between devices, neighbours(): return (lax.ppermute(to_chip, 'gx', over_chips), of_core)  11.1 us
    pallas_call x7, Pallas kernels, call(): pl.pallas_call(kernel, out_shape=tuple((jax.ShapeDtypeStruct(o, jnp.float...  7.52 us
    ppermute x3, waiting for transfers between devices, neighbours(): return (lax.ppermute(to_chip, 'gx', over_chips), of_core)  4.44 us
    ppermute x3, starting transfers between devices, neighbours(): of_core = lax.ppermute(to_core, 'gx', over_cores)  4.37 us
    ppermute x3, starting transfers between devices, hop(): return lax.ppermute(value, ('group', 'gx'), pairs)  3.52 us
    unnamed x6, local copies, waits for them, and re-layouts  2.03 us
    ppermute x1, waiting for transfers between devices, on_device(): share = share + lax.ppermute(share, 'gx', over_cores)  1.16 us
    ppermute x1, starting transfers between devices, on_device(): far = lax.ppermute(share, 'gx', [(at, at ^ 3) for at in range(count)])  0.95 us
  transfers between devices with their start and end apart: 11, of which 6 were waited for; matrix products, arithmetic and copies ran while one was open for 0% of the time, Pallas kernels for 15%

profile of v19, /device:TPU:0, one launch (start us, length us, event | category | flops | bytes accessed | tf_op | source)
XLA Modules:
  0.0 37.2 jit_solution(10628841123520103352)
XLA Ops:
  0.6 0.5 %collective-permute-start.2 = (f32[2,4,64,256]{3,2,1,0:T(8,128)}, f32[2,4,64,256]{3,2,1,0:T(8,128)S(1)}, u32[]{:S(2)}, u32[]{:S(2)}) collective-permute-start(f32[2,4,64,256]{3,2,1,0:T(8,128)} %initial.1), channel_id=1, source_target_pairs={{0,1},{1,0},{2,3},{3,2},{4,5},{5,4},{6,7},{7,6},{8,9},{9,8},{10,11... | collective-permute-start | bytes 1572872 | tf_op jit(solution)/shard_map/ppermute | solution.py:566
  1.1 5.7 %collective-permute-start.1 = (f32[2,4,64,256]{3,2,1,0:T(8,128)}, f32[2,4,64,256]{3,2,1,0:T(8,128)S(1)}, u32[]{:S(2)}, u32[]{:S(2)}) collective-permute-start(f32[2,4,64,256]{3,2,1,0:T(8,128)} %initial.1), channel_id=1, source_target_pairs={{0,15},{1,2},{2,1},{3,4},{4,3},{5,6},{6,5},{7,8},{8,7},{9,10},{10,... | collective-permute-start | bytes 1572872 | tf_op jit(solution)/shard_map/ppermute | solution.py:567
  6.8 0.0 copy-start.1
  6.8 1.1 %copy-done.1 = f32[2,4,64,256]{3,2,1,0:T(8,128)S(1)} copy-done((f32[2,4,64,256]{3,2,1,0:T(8,128)S(1)}, f32[2,4,64,256]{3,2,1,0:T(8,128)}, u32[]{:S(2)}) %copy-start.1) | copy-done | bytes 524312
  7.9 0.0 copy-start.2
  7.9 0.9 %copy-done.2 = f32[4,64,256]{2,1,0:T(8,128)S(1)} copy-done((f32[4,64,256]{2,1,0:T(8,128)S(1)}, f32[4,64,256]{2,1,0:T(8,128)}, u32[]{:S(2)}) %copy-start.2) | copy-done | bytes 262168
  8.8 0.1 shard_map.50
  8.9 0.1 collective-permute-start.3
  9.0 0.6 %collective-permute-start = (f32[3,2,64,128]{3,2,1,0:T(8,128)S(1)}, f32[3,2,64,128]{3,2,1,0:T(8,128)S(1)}, u32[]{:S(2)}, u32[]{:S(2)}) collective-permute-start(f32[3,2,64,128]{3,2,1,0:T(8,128)S(1)} %get-tuple-element.44), channel_id=1, source_target_pairs={{0,15},{1,2},{2,1},{3,4},{4,3},{5,6},{6,5},{7,8},{8,7},{9,10},{10,... | collective-permute-start | bytes 589832 | tf_op jit(solution)/shard_map/ppermute | solution.py:567
  9.6 0.8 %collective-permute-done.3.m_core = f32[3,2,64,128]{3,2,1,0:T(8,128)S(1)} collective-permute-done((f32[3,2,64,128]{3,2,1,0:T(8,128)S(1)}, f32[3,2,64,128]{3,2,1,0:T(8,128)S(1)}, u32[]{:S(2)}, u32[]{:S(2)}) %collective-permute-start.3) | collective-permute-done | bytes 196640 | tf_op jit(solution)/shard_map/ppermute | solution.py:566
  10.5 0.0 collective-permute-done.2.of_core
  10.5 0.0 copy-start
  10.5 0.7 %shard_map.51 = (f32[2,4,2,80,128]{4,3,2,1,0:T(8,128)S(1)}, f32[2,6,2,80,128]{4,3,2,1,0:T(8,128)S(1)}, f32[6,2,64,128]{3,2,1,0:T(8,128)S(1)}, f32[6,2,64,128]{3,...) custom-call(f32[2,4,64,256]{3,2,1,0:T(8,128)S(1)} %collective-permut, ...), custom_call_target="tpu_custom_call" | custom-call | flops 3932160 | bytes 5636096 | tf_op jit(solution)/shard_map/pallas_call | solution.py:546
  11.2 2.8 %collective-permute-done.1.of_chip = f32[2,4,64,256]{3,2,1,0:T(8,128)S(1)} collective-permute-done((f32[2,4,64,256]{3,2,1,0:T(8,128)}, f32[2,4,64,256]{3,2,1,0:T(8,128)S(1)}, u32[]{:S(2)}, u32[]{:S(2)}) %collective-permute-start.1) | collective-permute-done | bytes 524320 | tf_op jit(solution)/shard_map/ppermute | solution.py:567
  14.0 0.0 copy-done
  14.0 1.3 %shard_map.52 = (f32[2,4,2,80,128]{4,3,2,1,0:T(8,128)S(1)}, f32[2,4,2,80,128]{4,3,2,1,0:T(8,128)S(1)}, f32[2,5,2,80,128]{4,3,2,1,0:T(8,128)S(1)}, f32[2,3,2,80,1...) custom-call(f32[2,4,64,256]{3,2,1,0:T(8,128)S(1)} %collective-permute-done.1.of_chip, ...), custom_call_target="tpu_custom_call" | custom-call | flops 5898240 | bytes 8425472 | tf_op jit(solution)/shard_map/pallas_call | solution.py:546
  15.4 1.6 %collective-permute-done.m_chip = f32[3,2,64,128]{3,2,1,0:T(8,128)S(1)} collective-permute-done((f32[3,2,64,128]{3,2,1,0:T(8,128)S(1)}, f32[3,2,64,128]{3,2,1,0:T(8,128)S(1)}, u32[]{:S(2)}, u32[]{:S(2)}) %collective-permute-start) | collective-permute-done | bytes 196640 | tf_op jit(solution)/shard_map/ppermute | solution.py:567
  17.0 1.2 %shard_map.53 = (f32[3,2,64,128]{3,2,1,0:T(8,128)S(1)}, f32[2,2,64,128]{3,2,1,0:T(8,128)S(1)}, f32[2,2,64,128]{3,2,1,0:T(8,128)S(1)}, f32[2,2,64,128]{3,2,1,0:T(...) custom-call(f32[3,2,64,128]{3,2,1,0:T(8,128)S(1)} %collective-permut, ...), custom_call_target="tpu_custom_call" | custom-call | flops 5898240 | bytes 11001856 | tf_op jit(solution)/shard_map/pallas_call | solution.py:546
  18.2 3.8 %collective-permute-start.5 = (f32[2,3,2,72,128]{4,3,2,1,0:T(8,128)S(1)}, f32[2,3,2,72,128]{4,3,2,1,0:T(8,128)S(1)}, u32[]{:S(2)}, u32[]{:S(2)}) collective-permute-start(f32[2,3,2,72,128]{4,3,2,1,0:T(8,128)S(1)} %get-tuple-element.71), channel_id=1, source_target_pairs={{0,1},{1,0},{2,3},{3,2},{4,5},{5,4},{6,7},{7,6},{8,9},{9,8},{10,11... | collective-permute-start | bytes 1327112 | tf_op jit(solution)/shard_map/ppermute | solution.py:566
  22.0 4.8 %collective-permute-start.4 = (f32[2,3,2,64,128]{4,3,2,1,0:T(8,128)S(1)}, f32[2,3,2,64,128]{4,3,2,1,0:T(8,128)S(1)}, u32[]{:S(2)}, u32[]{:S(2)}) collective-permute-start(f32[2,3,2,64,128]{4,3,2,1,0:T(8,128)S(1)} %get-tuple-element.62), channel_id=1, source_target_pairs={{0,15},{1,2},{2,1},{3,4},{4,3},{5,6},{6,5},{7,8},{8,7},{9,10},{10,... | collective-permute-start | bytes 1179656 | tf_op jit(solution)/shard_map/ppermute | solution.py:567
  26.8 0.0 collective-permute-done.5.of_core
  26.8 1.5 %collective-permute-start.8 = (f32[8,128]{1,0:T(8,128)S(1)}, f32[8,128]{1,0:T(8,128)S(1)}, u32[]{:S(2)}, u32[]{:S(2)}) collective-permute-start(f32[8,128]{1,0:T(8,128)S(1)} %fusion.share_in), channel_id=1, source_target_pairs={{0,16},{1,13},{2,14},{3,19},{4,20},{5,9},{6,10},{7,23},{8,24},{9,5... | collective-permute-start | bytes 12296 | tf_op jit(solution)/shard_map/ppermute | solution.py:629
  28.3 0.5 %collective-permute-start.6 = (f32[8,128]{1,0:T(8,128)S(1)}, f32[8,128]{1,0:T(8,128)S(1)}, u32[]{:S(2)}, u32[]{:S(2)}) collective-permute-start(f32[8,128]{1,0:T(8,128)S(1)} %fusion.share_in), channel_id=1, source_target_pairs={{0,16},{1,9},{2,10},{3,19},{4,20},{5,13},{6,14},{7,23},{8,24},{9,1... | collective-permute-start | bytes 12296 | tf_op jit(solution)/shard_map/ppermute | solution.py:629
  28.8 1.5 %collective-permute-start.7 = (f32[8,128]{1,0:T(8,128)S(1)}, f32[8,128]{1,0:T(8,128)S(1)}, u32[]{:S(2)}, u32[]{:S(2)}) collective-permute-start(f32[8,128]{1,0:T(8,128)S(1)} %fusion.share_in), channel_id=1, source_target_pairs={{0,16},{1,5},{2,6},{3,19},{4,20},{5,1},{6,2},{7,23},{8,24},{9,13},... | collective-permute-start | bytes 12296 | tf_op jit(solution)/shard_map/ppermute | solution.py:629
  30.3 2.0 %shard_map.54 = (f32[2,5,2,80,128]{4,3,2,1,0:T(8,128)S(1)}, f32[2,1,2,80,128]{4,3,2,1,0:T(8,128)S(1)}, f32[2,3,2,80,128]{4,3,2,1,0:T(8,128)S(1)}, f32[2,3,2,64,1...) custom-call(f32[2,3,2,72,128]{4,3,2,1,0:T(8,128)S(1)} %collective-pe, ...), custom_call_target="tpu_custom_call" | custom-call | flops 7864320 | bytes 10903552 | tf_op jit(solution)/shard_map/pallas_call | solution.py:546
  32.3 0.0 collective-permute-done.8
  32.3 0.0 collective-permute-done.6
  32.3 0.1 collective-permute-done.7
  32.4 0.0 collective-permute-start.9
  32.4 1.2 %collective-permute-done.9 = f32[8,128]{1,0:T(8,128)S(1)} collective-permute-done((f32[8,128]{1,0:T(8,128)S(1)}, f32[8,128]{1,0:T(8,128)S(1)}, u32[]{:S(2)}, u32[]{:S(2)}) %collective-permute-start.9) | collective-permute-done | bytes 4128 | tf_op jit(solution)/shard_map/ppermute | solution.py:653
  33.6 1.0 %collective-permute-start.10 = (f32[8,128]{1,0:T(8,128)S(1)}, f32[8,128]{1,0:T(8,128)S(1)}, u32[]{:S(2)}, u32[]{:S(2)}) collective-permute-start(f32[8,128]{1,0:T(8,128)S(1)} %add.19.share_in), channel_id=1, source_target_pairs={{0,3},{1,2},{2,1},{3,0},{4,7},{5,6},{6,5},{7,4},{8,11},{9,10},{10,... | collective-permute-start | bytes 12296 | tf_op jit(solution)/shard_map/ppermute | solution.py:654
  34.5 0.0 collective-permute-done.4.of_chip
  34.5 1.6 %shard_map.55 = (f32[4,64,256]{2,1,0:T(8,128)}, f32[8,128]{1,0:T(8,128)S(1)}) custom-call(f32[2,3,2,64,128]{4,3,2,1,0:T(8,128)S(1)} %collective-permute-done.4.of_chip, f32[6,2,64,128]{3,2,1,0:T(8,128)S(1)} %get-tuple-element.50.mx.mx_a, f32[6,2,64,128]{3,2,1,0:T(8,128)S(1)} %get-tuple-element.51.my.my_a, ...), custom_call_target="tpu_custom_call" | custom-call | flops 5898240 | bytes 9150464 | tf_op jit(solution)/shard_map/pallas_call | solution.py:546
  36.1 0.5 %collective-permute-done.10.far = f32[8,128]{1,0:T(8,128)S(1)} collective-permute-done((f32[8,128]{1,0:T(8,128)S(1)}, f32[8,128]{1,0:T(8,128)S(1)}, u32[]{:S(2)}, u32[]{:S(2)}) %collective-permute-start.10) | collective-permute-done | bytes 4128 | tf_op jit(solution)/shard_map/ppermute | solution.py:654
  36.6 0.6 %shard_map.56 = f32[1]{0:T(128)} custom-call(f32[8,128]{1,0:T(8,128)S(1)} %get-tuple-element.85.share, f32[8,128]{1,0:T(8,128)S(1)} %collective-permute-done.10.far), custom_call_target="tpu_custom_call" | custom-call | flops 1 | bytes 8196 | tf_op jit(solution)/shard_map/pallas_call | solution.py:546
  (3 shorter events, 0.0 us)
Async XLA Ops:
  0.6 9.8 %collective-permute-start.2 = (f32[2,4,64,256]{3,2,1,0:T(8,128)}, f32[2,4,64,256]{3,2,1,0:T(8,128)S(1)}, u32[]{:S(2)}, u32[]{:S(2)}) collective-permute-start(f32[2,4,64,256]{3,2,1,0:T(8,128)} %initial.1), channel_id=1, source_target_pairs={{0,1},{1,0},{2,3},{3,2},{4,5},{5,4},{6,7},{7,6},{8,9},{9,8},{10,11... | collective-permute-start | bytes 1572872 | tf_op jit(solution)/shard_map/ppermute | solution.py:566
  1.1 12.8 %collective-permute-start.1 = (f32[2,4,64,256]{3,2,1,0:T(8,128)}, f32[2,4,64,256]{3,2,1,0:T(8,128)S(1)}, u32[]{:S(2)}, u32[]{:S(2)}) collective-permute-start(f32[2,4,64,256]{3,2,1,0:T(8,128)} %initial.1), channel_id=1, source_target_pairs={{0,15},{1,2},{2,1},{3,4},{4,3},{5,6},{6,5},{7,8},{8,7},{9,10},{10,... | collective-permute-start | bytes 1572872 | tf_op jit(solution)/shard_map/ppermute | solution.py:567
  6.8 1.1 %copy-start.1 = (f32[2,4,64,256]{3,2,1,0:T(8,128)S(1)}, f32[2,4,64,256]{3,2,1,0:T(8,128)}, u32[]{:S(2)}) copy-start(f32[2,4,64,256]{3,2,1,0:T(8,128)} %initial.1) | copy-start | bytes 1572868
  7.9 0.9 %copy-start.2 = (f32[4,64,256]{2,1,0:T(8,128)S(1)}, f32[4,64,256]{2,1,0:T(8,128)}, u32[]{:S(2)}) copy-start(f32[4,64,256]{2,1,0:T(8,128)} %mobility.1) | copy-start | bytes 786436
  8.9 1.5 %collective-permute-start.3 = (f32[3,2,64,128]{3,2,1,0:T(8,128)S(1)}, f32[3,2,64,128]{3,2,1,0:T(8,128)S(1)}, u32[]{:S(2)}, u32[]{:S(2)}) collective-permute-start(f32[3,2,64,128]{3,2,1,0:T(8,128)S(1)} %get-tuple-element.47), channel_id=1, source_target_pairs={{0,1},{1,0},{2,3},{3,2},{4,5},{5,4},{6,7},{7,6},{8,9},{9,8},{10,11... | collective-permute-start | bytes 589832 | tf_op jit(solution)/shard_map/ppermute | solution.py:566
  9.0 8.0 %collective-permute-start = (f32[3,2,64,128]{3,2,1,0:T(8,128)S(1)}, f32[3,2,64,128]{3,2,1,0:T(8,128)S(1)}, u32[]{:S(2)}, u32[]{:S(2)}) collective-permute-start(f32[3,2,64,128]{3,2,1,0:T(8,128)S(1)} %get-tuple-element.44), channel_id=1, source_target_pairs={{0,15},{1,2},{2,1},{3,4},{4,3},{5,6},{6,5},{7,8},{8,7},{9,10},{10,... | collective-permute-start | bytes 589832 | tf_op jit(solution)/shard_map/ppermute | solution.py:567
  10.5 3.5 %copy-start = (f32[2,4,64,256]{3,2,1,0:T(8,128)S(1)}, f32[2,4,64,256]{3,2,1,0:T(8,128)}, u32[]{:S(2)}) copy-start(f32[2,4,64,256]{3,2,1,0:T(8,128)} %observed.3) | copy-start | bytes 1572868
  18.2 8.6 %collective-permute-start.5 = (f32[2,3,2,72,128]{4,3,2,1,0:T(8,128)S(1)}, f32[2,3,2,72,128]{4,3,2,1,0:T(8,128)S(1)}, u32[]{:S(2)}, u32[]{:S(2)}) collective-permute-start(f32[2,3,2,72,128]{4,3,2,1,0:T(8,128)S(1)} %get-tuple-element.71), channel_id=1, source_target_pairs={{0,1},{1,0},{2,3},{3,2},{4,5},{5,4},{6,7},{7,6},{8,9},{9,8},{10,11... | collective-permute-start | bytes 1327112 | tf_op jit(solution)/shard_map/ppermute | solution.py:566
  22.0 12.6 %collective-permute-start.4 = (f32[2,3,2,64,128]{4,3,2,1,0:T(8,128)S(1)}, f32[2,3,2,64,128]{4,3,2,1,0:T(8,128)S(1)}, u32[]{:S(2)}, u32[]{:S(2)}) collective-permute-start(f32[2,3,2,64,128]{4,3,2,1,0:T(8,128)S(1)} %get-tuple-element.62), channel_id=1, source_target_pairs={{0,15},{1,2},{2,1},{3,4},{4,3},{5,6},{6,5},{7,8},{8,7},{9,10},{10,... | collective-permute-start | bytes 1179656 | tf_op jit(solution)/shard_map/ppermute | solution.py:567
  26.8 5.5 %collective-permute-start.8 = (f32[8,128]{1,0:T(8,128)S(1)}, f32[8,128]{1,0:T(8,128)S(1)}, u32[]{:S(2)}, u32[]{:S(2)}) collective-permute-start(f32[8,128]{1,0:T(8,128)S(1)} %fusion.share_in), channel_id=1, source_target_pairs={{0,16},{1,13},{2,14},{3,19},{4,20},{5,9},{6,10},{7,23},{8,24},{9,5... | collective-permute-start | bytes 12296 | tf_op jit(solution)/shard_map/ppermute | solution.py:629
  28.3 4.0 %collective-permute-start.6 = (f32[8,128]{1,0:T(8,128)S(1)}, f32[8,128]{1,0:T(8,128)S(1)}, u32[]{:S(2)}, u32[]{:S(2)}) collective-permute-start(f32[8,128]{1,0:T(8,128)S(1)} %fusion.share_in), channel_id=1, source_target_pairs={{0,16},{1,9},{2,10},{3,19},{4,20},{5,13},{6,14},{7,23},{8,24},{9,1... | collective-permute-start | bytes 12296 | tf_op jit(solution)/shard_map/ppermute | solution.py:629
  28.8 3.6 %collective-permute-start.7 = (f32[8,128]{1,0:T(8,128)S(1)}, f32[8,128]{1,0:T(8,128)S(1)}, u32[]{:S(2)}, u32[]{:S(2)}) collective-permute-start(f32[8,128]{1,0:T(8,128)S(1)} %fusion.share_in), channel_id=1, source_target_pairs={{0,16},{1,5},{2,6},{3,19},{4,20},{5,1},{6,2},{7,23},{8,24},{9,13},... | collective-permute-start | bytes 12296 | tf_op jit(solution)/shard_map/ppermute | solution.py:629
  32.4 1.2 %collective-permute-start.9 = (f32[8,128]{1,0:T(8,128)S(1)}, f32[8,128]{1,0:T(8,128)S(1)}, u32[]{:S(2)}, u32[]{:S(2)}) collective-permute-start(f32[8,128]{1,0:T(8,128)S(1)} %add_add_fusion), channel_id=1, source_target_pairs={{0,1},{1,0},{2,3},{3,2},{4,5},{5,4},{6,7},{7,6},{8,9},{9,8},{10,11... | collective-permute-start | bytes 12296 | tf_op jit(solution)/shard_map/ppermute | solution.py:653
  33.6 3.0 %collective-permute-start.10 = (f32[8,128]{1,0:T(8,128)S(1)}, f32[8,128]{1,0:T(8,128)S(1)}, u32[]{:S(2)}, u32[]{:S(2)}) collective-permute-start(f32[8,128]{1,0:T(8,128)S(1)} %add.19.share_in), channel_id=1, source_target_pairs={{0,3},{1,2},{2,1},{3,0},{4,7},{5,6},{6,5},{7,4},{8,11},{9,10},{10,... | collective-permute-start | bytes 12296 | tf_op jit(solution)/shard_map/ppermute | solution.py:654

commit v20 on v19

--- a/solution.py
+++ b/solution.py
@@ -288,7 +288,7 @@
 def forward_kernel(
     m_chip, mob_own, conc_own, conc_chip, chem0_a, chem0_b, state1_a, chem1_a, adjoint2_a, squares, observed,
     mx_a, my_a, my_low_a, mz_a, mz_low_a, all_a,
-    mx_b, my_b, my_low_b, mz_b, mz_low_b, all_b, state1_b, chem1_b, adjoint2_b, to_core, to_chip, share, rim, total,
+    mx_b, my_b, my_low_b, mz_b, mz_low_b, all_b, state1_b, chem1_b, adjoint2_b, first, to_core, to_chip, share, gift, rim, total,
 ):
     runs, n = conc_own.shape[:2]
     ny = observed.shape[2]
@@ -332,6 +332,10 @@
             put_step(row, faces, chem1, state1, run, range(n - 3, n), target)
             for at in range(min(3, n - 3)):
                 put_flat(to_core, (run, at), row, padded(*adjoint2(at, run), row))
+            for at in range(3):
+                put_flat(first, (run, at), row, choose(
+                    at_wrap(1), flat(to_chip, (run, at), row), flat(to_core, (run, at), row)
+                ))
         return carry
 
     for run in range(runs):
@@ -340,7 +344,7 @@
     mine = jnp.broadcast_to(jnp.sum(columns, axis=1, keepdims=True), share.shape)
     sums = counts(lax.axis_index("gx")) == 1
     share[...] = jnp.where(sums, mine, 0.0)
-    to_core[0, 0, 0, ny:] = jnp.where(sums, 0.0, mine)
+    gift[...] = jnp.where(sums, 0.0, mine)
 
 
 def put_adjoint1(row, flow, adjoint2, run, places, weight, target):
@@ -374,7 +378,7 @@
 
 
 def early_kernel(
-    of_core, mx_a, my_a, my_low_a, mz_a, mz_low_a, all_a, mx_b, my_b, my_low_b, mz_b, mz_low_b, all_b,
+    of_first, of_core, mx_a, my_a, my_low_a, mz_a, mz_low_a, all_a, mx_b, my_b, my_low_b, mz_b, mz_low_b, all_b,
     chem0_a, chem0_b, state1_a, state1_b, chem1_a, chem1_b, adjoint2_a, adjoint2_b,
     share_in, flow_a, flow_part, adjoint1_a, weight_b, step_z_b, part, sum_x_b, sum_y_b, sum_z_b, share,
     rim, sum_x, sum_y, sum_z,
@@ -396,7 +400,9 @@
     def one_run(run, carry):
         for row in chunks(ny):
             for at in range(3):
-                put_padded(rim, (run, 2 - at), row, flat(of_core, (run, at), row))
+                put_padded(rim, (run, 2 - at), row, choose(
+                    at_wrap(2), flat(of_core, (run, at), row), flat(of_first, (run, at), row)
+                ))
         for row in chunks(ny):
             mids = {at: padded(*adjoint2(at, run), row) for at in range(-3, n)}
             for at in range(-2, n):
@@ -457,7 +463,7 @@
 
 
 def late_kernel(
-    of_chip, mx_a, my_a, my_low_a, mz_a, mz_low_a, all_a, mx_b, my_b, my_low_b, mz_b, mz_low_b, all_b,
+    of_first, of_chip, mx_a, my_a, my_low_a, mz_a, mz_low_a, all_a, mx_b, my_b, my_low_b, mz_b, mz_low_b, all_b,
     chem0_a, chem0_b, chem1_b, adjoint2_b, flow_a, flow_part, adjoint1_a, weight_b, step_z_b,
     part, sum_x_b, sum_y_b, sum_z_b, share_in, result, share, rim, flow_b, adjoint1_b, sum_x, sum_y, sum_z,
 ):
@@ -481,7 +487,9 @@
     def one_run(run, carry):
         for row in chunks(ny):
             for at in range(3):
-                put_padded(rim, (run, at), row, flat(of_chip, (run, at), row))
+                put_padded(rim, (run, at), row, choose(
+                    at_wrap(1), flat(of_first, (run, at), row), flat(of_chip, (run, at), row)
+                ))
         for row in chunks(ny):
             mids = {at: padded(*adjoint2(at, run), row) for at in range(n - 1, n + 3)}
             value = add_product(padded(flow_part, (run, 0), row), flat(*faces.mx(n - 1), row), mids[n])
@@ -537,6 +545,15 @@
     return (at ^ (at >> 1)) & 1
 
 
+def at_wrap(cores):
+    at = lax.axis_index("gx")
+    return jnp.logical_or(at < cores, at >= lax.axis_size("gx") - cores)
+
+
+def choose(which, first, second):
+    return each(lambda a, b: jnp.where(which, a, b), first, second)
+
+
 def misfit_kernel(share, far, misfit):
     misfit[0] = (share[...] + far[...])[0, 0]
 
@@ -602,37 +619,42 @@
         (of_chip, conc, conc_core, chem0_a, observed, *faces_a),
         60 * runs * (n - 1) * cell,
     )
-    *faces_b, state1_b, chem1_b, adjoint2_b, to_core, to_chip, share = call(
+    *faces_b, state1_b, chem1_b, adjoint2_b, first, to_core, to_chip, share, gift = call(
         forward_kernel,
         (
             lies(3), lies(2), lies(2), lies(2), lies(2), lies(3),
             lies_padded(runs, 3), lies_padded(runs, 3), lies_padded(runs, 3),
-            (runs, 3, blocks, ny + ROWS, LANES), lies(runs, 3), (ROWS, LANES),
+            lies(runs, 3), lies(runs, 3), lies(runs, 3), (ROWS, LANES), (ROWS, LANES),
         ),
         (lies_padded(3), (CHUNK, LANES)),
         (m_chip, mob, conc, conc_chip, chem0_a, chem0_b, state1_a, chem1_a, adjoint2_a, squares, observed, *faces_a),
         60 * runs * 3 * cell,
     )
     faces = (*faces_a, *faces_b)
-    of_chip, of_core = neighbours(to_chip, to_core)
     groups = lax.axis_size("group")
 
-    def target(group, at, apart):
-        if counts(at):
-            return group * count + (at ^ apart)
-        return min(group ^ 1, groups - 1) * count + at
+    def swap(value, partner):
+        pairs = []
+        for group in range(groups):
+            for at in range(count):
+                to = partner(at)
+                aim = min(group ^ 1, groups - 1) * count + at if to is None else group * count + to
+                pairs.append((group * count + at, aim))
+        return lax.ppermute(value, ("group", "gx"), pairs)
+
+    ends = {0: count - 1, count - 1: 0}
+    of_first = swap(first, lambda at: ends.get(at, None if at in (1, count - 2) else at ^ 1))
+    of_chip = swap(to_chip, lambda at: None if at in ends else dict(over_chips)[at])
+    of_core = lax.ppermute(to_core, "gx", over_cores)
 
     def hop(value, apart):
-        pairs = [
-            (group * count + at, target(group, at, apart)) for group in range(groups) for at in range(count)
-        ]
-        return lax.ppermute(value, ("group", "gx"), pairs)
+        return swap(value, lambda at: at ^ apart if counts(at) else None)
 
     def hops(value, bits):
         aparts = [sum(2 << bit for at, bit in enumerate(bits) if which >> at & 1) for which in range(1, 1 << len(bits))]
         return [hop(value, apart) for apart in aparts]
 
-    share = share + of_core[0, 0, 0, ny:]
+    share = share + lax.ppermute(gift, "gx", over_cores)
     upper = range(count.bit_length() - 3, 0, -1)
     steps = [upper[at : at + 2] for at in range(0, len(upper), 2)]
     fars = hops(share, steps[0])
@@ -643,7 +665,7 @@
             lies(n - 2), lies(2), lies(2), lies(2), (ROWS, LANES),
         ),
         (lies_padded(runs, 3), lies(n), lies_padded(n), lies(n)),
-        (of_core, *faces, chem0_a, chem0_b, state1_a, state1_b, chem1_a, chem1_b, adjoint2_a, adjoint2_b, share),
+        (of_first, of_core, *faces, chem0_a, chem0_b, state1_a, state1_b, chem1_a, chem1_b, adjoint2_a, adjoint2_b, share),
         60 * runs * n * cell,
     )
     for bits in steps[1:]:
@@ -660,7 +682,7 @@
             lies(3), lies_padded(2), lies(2),
         ),
         (
-            of_chip, *faces, chem0_a, chem0_b, chem1_b, adjoint2_b, flow_a, flow_part, adjoint1_a,
+            of_first, of_chip, *faces, chem0_a, chem0_b, chem1_b, adjoint2_b, flow_a, flow_part, adjoint1_a,
             weight_b, step_z_b, part, *sums_b, share,
         ),
         60 * runs * 3 * cell,

time: 37.4 us -> 41.5 us (1.11)
  the two profiles are of different devices: /device:TPU:0 before, /device:TPU:19 now
where the time goes in v20:
time: 41.5 us; the launch traced here: 41.3 us
  starting transfers between devices  16.8 us (40%)
  waiting for transfers between devices  14.3 us (34%)
  Pallas kernels  7.54 us (18%)
  local copies, waits for them, and re-layouts  2.03 us (5%)
  between operations  0.7 us (2%)
    ppermute x2, waiting for transfers between devices, neighbours(): return (lax.ppermute(to_chip, 'gx', over_chips), of_core)  11.5 us
    ppermute x1, starting transfers between devices, on_device(): far = lax.ppermute(share, 'gx', [(at, at ^ 3) for at in range(count)])  8.01 us
    pallas_call x7, Pallas kernels, call(): pl.pallas_call(kernel, out_shape=tuple((jax.ShapeDtypeStruct(o, jnp.float...  7.54 us
    ppermute x5, starting transfers between devices, swap(): return lax.ppermute(value, ('group', 'gx'), pairs)  4.61 us
    ppermute x2, starting transfers between devices, neighbours(): return (lax.ppermute(to_chip, 'gx', over_chips), of_core)  2.52 us
    unnamed x6, local copies, waits for them, and re-layouts  2.03 us
    ppermute x1, waiting for transfers between devices, on_device(): share = share + lax.ppermute(gift, 'gx', over_cores)  1.16 us
    ppermute x1, waiting for transfers between devices, on_device(): share = share + lax.ppermute(share, 'gx', over_cores)  1.16 us
  transfers between devices with their start and end apart: 13, of which 5 were waited for; matrix products, arithmetic and copies ran while one was open for 0% of the time, Pallas kernels for 14%

profile of v20, /device:TPU:19, one launch (start us, length us, event | category | flops | bytes accessed | tf_op | source)
XLA Modules:
  0.0 41.3 jit_solution(17435984434115897259)
XLA Ops:
  0.6 0.7 %collective-permute-start.2 = (f32[2,4,64,256]{3,2,1,0:T(8,128)}, f32[2,4,64,256]{3,2,1,0:T(8,128)S(1)}, u32[]{:S(2)}, u32[]{:S(2)}) collective-permute-start(f32[2,4,64,256]{3,2,1,0:T(8,128)} %initial.1), channel_id=1, source_target_pairs={{0,1},{1,0},{2,3},{3,2},{4,5},{5,4},{6,7},{7,6},{8,9},{9,8},{10,11... | collective-permute-start | bytes 1572872 | tf_op jit(solution)/shard_map/ppermute | solution.py:583
  1.4 1.2 %collective-permute-start.1 = (f32[2,4,64,256]{3,2,1,0:T(8,128)}, f32[2,4,64,256]{3,2,1,0:T(8,128)S(1)}, u32[]{:S(2)}, u32[]{:S(2)}) collective-permute-start(f32[2,4,64,256]{3,2,1,0:T(8,128)} %initial.1), channel_id=1, source_target_pairs={{0,15},{1,2},{2,1},{3,4},{4,3},{5,6},{6,5},{7,8},{8,7},{9,10},{10,... | collective-permute-start | bytes 1572872 | tf_op jit(solution)/shard_map/ppermute | solution.py:584
  2.6 0.0 copy-start.1
  2.6 1.1 %copy-done.1 = f32[2,4,64,256]{3,2,1,0:T(8,128)S(1)} copy-done((f32[2,4,64,256]{3,2,1,0:T(8,128)S(1)}, f32[2,4,64,256]{3,2,1,0:T(8,128)}, u32[]{:S(2)}) %copy-start.1) | copy-done | bytes 524312
  3.6 0.0 copy-start.2
  3.7 0.9 %copy-done.2 = f32[4,64,256]{2,1,0:T(8,128)S(1)} copy-done((f32[4,64,256]{2,1,0:T(8,128)S(1)}, f32[4,64,256]{2,1,0:T(8,128)}, u32[]{:S(2)}) %copy-start.2) | copy-done | bytes 262168
  4.6 0.1 shard_map.50
  4.7 0.4 collective-permute-start.3
  5.1 1.3 %collective-permute-start = (f32[3,2,64,128]{3,2,1,0:T(8,128)S(1)}, f32[3,2,64,128]{3,2,1,0:T(8,128)S(1)}, u32[]{:S(2)}, u32[]{:S(2)}) collective-permute-start(f32[3,2,64,128]{3,2,1,0:T(8,128)S(1)} %get-tuple-element.46), channel_id=1, source_target_pairs={{0,15},{1,2},{2,1},{3,4},{4,3},{5,6},{6,5},{7,8},{8,7},{9,10},{10,... | collective-permute-start | bytes 589832 | tf_op jit(solution)/shard_map/ppermute | solution.py:584
  6.4 0.0 collective-permute-done.3.m_core
  6.4 0.0 collective-permute-done.2.of_core
  6.4 0.0 copy-start
  6.4 0.7 %shard_map.51 = (f32[2,4,2,80,128]{4,3,2,1,0:T(8,128)S(1)}, f32[2,6,2,80,128]{4,3,2,1,0:T(8,128)S(1)}, f32[6,2,64,128]{3,2,1,0:T(8,128)S(1)}, f32[6,2,64,128]{3,...) custom-call(f32[2,4,64,256]{3,2,1,0:T(8,128)S(1)} %collective-permut, ...), custom_call_target="tpu_custom_call" | custom-call | flops 3932160 | bytes 5636096 | tf_op jit(solution)/shard_map/pallas_call | solution.py:563
  7.2 10.7 %collective-permute-done.1.of_chip = f32[2,4,64,256]{3,2,1,0:T(8,128)S(1)} collective-permute-done((f32[2,4,64,256]{3,2,1,0:T(8,128)}, f32[2,4,64,256]{3,2,1,0:T(8,128)S(1)}, u32[]{:S(2)}, u32[]{:S(2)}) %collective-permute-start.1) | collective-permute-done | bytes 524320 | tf_op jit(solution)/shard_map/ppermute | solution.py:584
  17.9 0.0 copy-done
  17.9 1.4 %shard_map.52 = (f32[2,4,2,80,128]{4,3,2,1,0:T(8,128)S(1)}, f32[2,4,2,80,128]{4,3,2,1,0:T(8,128)S(1)}, f32[2,5,2,80,128]{4,3,2,1,0:T(8,128)S(1)}, f32[2,3,2,80,1...) custom-call(f32[2,4,64,256]{3,2,1,0:T(8,128)S(1)} %collective-permute-done.1.of_chip, ...), custom_call_target="tpu_custom_call" | custom-call | flops 5898240 | bytes 8425472 | tf_op jit(solution)/shard_map/pallas_call | solution.py:563
  19.3 0.7 %collective-permute-done.m_chip = f32[3,2,64,128]{3,2,1,0:T(8,128)S(1)} collective-permute-done((f32[3,2,64,128]{3,2,1,0:T(8,128)S(1)}, f32[3,2,64,128]{3,2,1,0:T(8,128)S(1)}, u32[]{:S(2)}, u32[]{:S(2)}) %collective-permute-start) | collective-permute-done | bytes 196640 | tf_op jit(solution)/shard_map/ppermute | solution.py:584
  20.0 1.3 %shard_map.53 = (f32[3,2,64,128]{3,2,1,0:T(8,128)S(1)}, f32[2,2,64,128]{3,2,1,0:T(8,128)S(1)}, f32[2,2,64,128]{3,2,1,0:T(8,128)S(1)}, f32[2,2,64,128]{3,2,1,0:T(...) custom-call(f32[3,2,64,128]{3,2,1,0:T(8,128)S(1)} %collective-permut, ...), custom_call_target="tpu_custom_call" | custom-call | flops 5898240 | bytes 11350016 | tf_op jit(solution)/shard_map/pallas_call | solution.py:563
  21.3 0.0 collective-permute-start.4
  21.3 0.5 %collective-permute-start.6 = (f32[2,3,2,64,128]{4,3,2,1,0:T(8,128)S(1)}, f32[2,3,2,64,128]{4,3,2,1,0:T(8,128)S(1)}, u32[]{:S(2)}, u32[]{:S(2)}) collective-permute-start(f32[2,3,2,64,128]{4,3,2,1,0:T(8,128)S(1)} %get-tuple-element.74), channel_id=1, source_target_pairs={{0,1},{1,0},{2,3},{3,2},{4,5},{5,4},{6,7},{7,6},{8,9},{9,8},{10,11... | collective-permute-start | bytes 1179656 | tf_op jit(solution)/shard_map/ppermute | solution.py:648
  21.8 1.2 %collective-permute-start.5 = (f32[2,3,2,64,128]{4,3,2,1,0:T(8,128)S(1)}, f32[2,3,2,64,128]{4,3,2,1,0:T(8,128)S(1)}, u32[]{:S(2)}, u32[]{:S(2)}) collective-permute-start(f32[2,3,2,64,128]{4,3,2,1,0:T(8,128)S(1)} %get-tuple-element.65), channel_id=1, source_target_pairs={{0,16},{1,2},{2,1},{3,4},{4,3},{5,6},{6,5},{7,8},{8,7},{9,10},{10,... | collective-permute-start | bytes 1179656 | tf_op jit(solution)/shard_map/ppermute | solution.py:643
  23.0 0.0 collective-permute-start.7
  23.0 1.2 %collective-permute-done.7 = f32[8,128]{1,0:T(8,128)S(1)} collective-permute-done((f32[8,128]{1,0:T(8,128)S(1)}, f32[8,128]{1,0:T(8,128)S(1)}, u32[]{:S(2)}, u32[]{:S(2)}) %collective-permute-start.7) | collective-permute-done | bytes 4128 | tf_op jit(solution)/shard_map/ppermute | solution.py:657
  24.2 0.2 collective-permute-start.10
  24.3 3.2 %collective-permute-start.8 = (f32[8,128]{1,0:T(8,128)S(1)}, f32[8,128]{1,0:T(8,128)S(1)}, u32[]{:S(2)}, u32[]{:S(2)}) collective-permute-start(f32[8,128]{1,0:T(8,128)S(1)} %add.15.share_in), channel_id=1, source_target_pairs={{0,16},{1,9},{2,10},{3,19},{4,20},{5,13},{6,14},{7,23},{8,24},{9,1... | collective-permute-start | bytes 12296 | tf_op jit(solution)/shard_map/ppermute | solution.py:643
  27.6 0.0 collective-permute-done.4.of_first
  27.6 0.0 collective-permute-start.9
  27.6 0.0 collective-permute-done.6.of_core
  27.6 2.0 %shard_map.54 = (f32[2,5,2,80,128]{4,3,2,1,0:T(8,128)S(1)}, f32[2,1,2,80,128]{4,3,2,1,0:T(8,128)S(1)}, f32[2,3,2,80,128]{4,3,2,1,0:T(8,128)S(1)}, f32[2,3,2,64,1...) custom-call(f32[2,3,2,64,128]{4,3,2,1,0:T(8,128)S(1)} %collective-pe, ...), custom_call_target="tpu_custom_call" | custom-call | flops 7864320 | bytes 11247616 | tf_op jit(solution)/shard_map/pallas_call | solution.py:563
  29.6 0.0 collective-permute-done.10
  29.6 0.0 collective-permute-done.8
  29.6 0.4 %collective-permute-done.9 = f32[8,128]{1,0:T(8,128)S(1)} collective-permute-done((f32[8,128]{1,0:T(8,128)S(1)}, f32[8,128]{1,0:T(8,128)S(1)}, u32[]{:S(2)}, u32[]{:S(2)}) %collective-permute-start.9) | collective-permute-done | bytes 4128 | tf_op jit(solution)/shard_map/ppermute | solution.py:643
  30.0 0.0 collective-permute-start.11
  30.1 1.2 %collective-permute-done.11 = f32[8,128]{1,0:T(8,128)S(1)} collective-permute-done((f32[8,128]{1,0:T(8,128)S(1)}, f32[8,128]{1,0:T(8,128)S(1)}, u32[]{:S(2)}, u32[]{:S(2)}) %collective-permute-start.11) | collective-permute-done | bytes 4128 | tf_op jit(solution)/shard_map/ppermute | solution.py:675
  31.2 8.0 %collective-permute-start.12 = (f32[8,128]{1,0:T(8,128)S(1)}, f32[8,128]{1,0:T(8,128)S(1)}, u32[]{:S(2)}, u32[]{:S(2)}) collective-permute-start(f32[8,128]{1,0:T(8,128)S(1)} %add.19.share_in), channel_id=1, source_target_pairs={{0,3},{1,2},{2,1},{3,0},{4,7},{5,6},{6,5},{7,4},{8,11},{9,10},{10,... | collective-permute-start | bytes 12296 | tf_op jit(solution)/shard_map/ppermute | solution.py:676
  39.2 0.0 collective-permute-done.5.of_chip
  39.2 1.6 %shard_map.55 = (f32[4,64,256]{2,1,0:T(8,128)}, f32[8,128]{1,0:T(8,128)S(1)}) custom-call(f32[2,3,2,64,128]{4,3,2,1,0:T(8,128)S(1)} %collective-permute-done.4.of_first, f32[2,3,2,64,128]{4,3,2,1,0:T(8,128)S(1)} %collective-permute-done.5.of_chip, f32[6,2,64,128]{3,2,1,0:T(8,128)S(1)} %get-tuple-element.52.mx.mx_a, ...), custom_call_target="tpu_custom_call" | custom-call | flops 5898240 | bytes 9543680 | tf_op jit(solution)/shard_map/pallas_call | solution.py:563
  40.8 0.0 collective-permute-done.12.far
  40.8 0.6 %shard_map.56 = f32[1]{0:T(128)} custom-call(f32[8,128]{1,0:T(8,128)S(1)} %get-tuple-element.89.share, f32[8,128]{1,0:T(8,128)S(1)} %collective-permute-done.12.far), custom_call_target="tpu_custom_call" | custom-call | flops 1 | bytes 8196 | tf_op jit(solution)/shard_map/pallas_call | solution.py:563
  (3 shorter events, 0.0 us)
Async XLA Ops:
  0.6 5.8 %collective-permute-start.2 = (f32[2,4,64,256]{3,2,1,0:T(8,128)}, f32[2,4,64,256]{3,2,1,0:T(8,128)S(1)}, u32[]{:S(2)}, u32[]{:S(2)}) collective-permute-start(f32[2,4,64,256]{3,2,1,0:T(8,128)} %initial.1), channel_id=1, source_target_pairs={{0,1},{1,0},{2,3},{3,2},{4,5},{5,4},{6,7},{7,6},{8,9},{9,8},{10,11... | collective-permute-start | bytes 1572872 | tf_op jit(solution)/shard_map/ppermute | solution.py:583
  1.4 16.5 %collective-permute-start.1 = (f32[2,4,64,256]{3,2,1,0:T(8,128)}, f32[2,4,64,256]{3,2,1,0:T(8,128)S(1)}, u32[]{:S(2)}, u32[]{:S(2)}) collective-permute-start(f32[2,4,64,256]{3,2,1,0:T(8,128)} %initial.1), channel_id=1, source_target_pairs={{0,15},{1,2},{2,1},{3,4},{4,3},{5,6},{6,5},{7,8},{8,7},{9,10},{10,... | collective-permute-start | bytes 1572872 | tf_op jit(solution)/shard_map/ppermute | solution.py:584
  2.6 1.1 %copy-start.1 = (f32[2,4,64,256]{3,2,1,0:T(8,128)S(1)}, f32[2,4,64,256]{3,2,1,0:T(8,128)}, u32[]{:S(2)}) copy-start(f32[2,4,64,256]{3,2,1,0:T(8,128)} %initial.1) | copy-start | bytes 1572868
  3.6 0.9 %copy-start.2 = (f32[4,64,256]{2,1,0:T(8,128)S(1)}, f32[4,64,256]{2,1,0:T(8,128)}, u32[]{:S(2)}) copy-start(f32[4,64,256]{2,1,0:T(8,128)} %mobility.1) | copy-start | bytes 786436
  4.7 1.7 %collective-permute-start.3 = (f32[3,2,64,128]{3,2,1,0:T(8,128)S(1)}, f32[3,2,64,128]{3,2,1,0:T(8,128)S(1)}, u32[]{:S(2)}, u32[]{:S(2)}) collective-permute-start(f32[3,2,64,128]{3,2,1,0:T(8,128)S(1)} %get-tuple-element.49), channel_id=1, source_target_pairs={{0,1},{1,0},{2,3},{3,2},{4,5},{5,4},{6,7},{7,6},{8,9},{9,8},{10,11... | collective-permute-start | bytes 589832 | tf_op jit(solution)/shard_map/ppermute | solution.py:583
  5.1 14.9 %collective-permute-start = (f32[3,2,64,128]{3,2,1,0:T(8,128)S(1)}, f32[3,2,64,128]{3,2,1,0:T(8,128)S(1)}, u32[]{:S(2)}, u32[]{:S(2)}) collective-permute-start(f32[3,2,64,128]{3,2,1,0:T(8,128)S(1)} %get-tuple-element.46), channel_id=1, source_target_pairs={{0,15},{1,2},{2,1},{3,4},{4,3},{5,6},{6,5},{7,8},{8,7},{9,10},{10,... | collective-permute-start | bytes 589832 | tf_op jit(solution)/shard_map/ppermute | solution.py:584
  6.4 11.5 %copy-start = (f32[2,4,64,256]{3,2,1,0:T(8,128)S(1)}, f32[2,4,64,256]{3,2,1,0:T(8,128)}, u32[]{:S(2)}) copy-start(f32[2,4,64,256]{3,2,1,0:T(8,128)} %observed.3) | copy-start | bytes 1572868
  21.3 6.3 %collective-permute-start.4 = (f32[2,3,2,64,128]{4,3,2,1,0:T(8,128)S(1)}, f32[2,3,2,64,128]{4,3,2,1,0:T(8,128)S(1)}, u32[]{:S(2)}, u32[]{:S(2)}) collective-permute-start(f32[2,3,2,64,128]{4,3,2,1,0:T(8,128)S(1)} %get-tuple-element.64), channel_id=1, source_target_pairs={{0,15},{1,17},{2,3},{3,2},{4,5},{5,4},{6,7},{7,6},{8,9},{9,8},{10,... | collective-permute-start | bytes 1179656 | tf_op jit(solution)/shard_map/ppermute | solution.py:643
  21.3 6.3 %collective-permute-start.6 = (f32[2,3,2,64,128]{4,3,2,1,0:T(8,128)S(1)}, f32[2,3,2,64,128]{4,3,2,1,0:T(8,128)S(1)}, u32[]{:S(2)}, u32[]{:S(2)}) collective-permute-start(f32[2,3,2,64,128]{4,3,2,1,0:T(8,128)S(1)} %get-tuple-element.74), channel_id=1, source_target_pairs={{0,1},{1,0},{2,3},{3,2},{4,5},{5,4},{6,7},{7,6},{8,9},{9,8},{10,11... | collective-permute-start | bytes 1179656 | tf_op jit(solution)/shard_map/ppermute | solution.py:648
  21.8 17.4 %collective-permute-start.5 = (f32[2,3,2,64,128]{4,3,2,1,0:T(8,128)S(1)}, f32[2,3,2,64,128]{4,3,2,1,0:T(8,128)S(1)}, u32[]{:S(2)}, u32[]{:S(2)}) collective-permute-start(f32[2,3,2,64,128]{4,3,2,1,0:T(8,128)S(1)} %get-tuple-element.65), channel_id=1, source_target_pairs={{0,16},{1,2},{2,1},{3,4},{4,3},{5,6},{6,5},{7,8},{8,7},{9,10},{10,... | collective-permute-start | bytes 1179656 | tf_op jit(solution)/shard_map/ppermute | solution.py:643
  23.0 1.2 %collective-permute-start.7 = (f32[8,128]{1,0:T(8,128)S(1)}, f32[8,128]{1,0:T(8,128)S(1)}, u32[]{:S(2)}, u32[]{:S(2)}) collective-permute-start(f32[8,128]{1,0:T(8,128)S(1)} %get-tuple-element.77), channel_id=1, source_target_pairs={{0,1},{1,0},{2,3},{3,2},{4,5},{5,4},{6,7},{7,6},{8,9},{9,8},{10,11... | collective-permute-start | bytes 12296 | tf_op jit(solution)/shard_map/ppermute | solution.py:657
  24.2 5.4 %collective-permute-start.10 = (f32[8,128]{1,0:T(8,128)S(1)}, f32[8,128]{1,0:T(8,128)S(1)}, u32[]{:S(2)}, u32[]{:S(2)}) collective-permute-start(f32[8,128]{1,0:T(8,128)S(1)} %add.15.share_in), channel_id=1, source_target_pairs={{0,16},{1,13},{2,14},{3,19},{4,20},{5,9},{6,10},{7,23},{8,24},{9,5... | collective-permute-start | bytes 12296 | tf_op jit(solution)/shard_map/ppermute | solution.py:643
  24.3 5.2 %collective-permute-start.8 = (f32[8,128]{1,0:T(8,128)S(1)}, f32[8,128]{1,0:T(8,128)S(1)}, u32[]{:S(2)}, u32[]{:S(2)}) collective-permute-start(f32[8,128]{1,0:T(8,128)S(1)} %add.15.share_in), channel_id=1, source_target_pairs={{0,16},{1,9},{2,10},{3,19},{4,20},{5,13},{6,14},{7,23},{8,24},{9,1... | collective-permute-start | bytes 12296 | tf_op jit(solution)/shard_map/ppermute | solution.py:643
  27.6 2.5 %collective-permute-start.9 = (f32[8,128]{1,0:T(8,128)S(1)}, f32[8,128]{1,0:T(8,128)S(1)}, u32[]{:S(2)}, u32[]{:S(2)}) collective-permute-start(f32[8,128]{1,0:T(8,128)S(1)} %add.15.share_in), channel_id=1, source_target_pairs={{0,16},{1,5},{2,6},{3,19},{4,20},{5,1},{6,2},{7,23},{8,24},{9,13},... | collective-permute-start | bytes 12296 | tf_op jit(solution)/shard_map/ppermute | solution.py:643
  30.0 1.2 %collective-permute-start.11 = (f32[8,128]{1,0:T(8,128)S(1)}, f32[8,128]{1,0:T(8,128)S(1)}, u32[]{:S(2)}, u32[]{:S(2)}) collective-permute-start(f32[8,128]{1,0:T(8,128)S(1)} %add_add_fusion), channel_id=1, source_target_pairs={{0,1},{1,0},{2,3},{3,2},{4,5},{5,4},{6,7},{7,6},{8,9},{9,8},{10,11... | collective-permute-start | bytes 12296 | tf_op jit(solution)/shard_map/ppermute | solution.py:675
  31.2 9.6 %collective-permute-start.12 = (f32[8,128]{1,0:T(8,128)S(1)}, f32[8,128]{1,0:T(8,128)S(1)}, u32[]{:S(2)}, u32[]{:S(2)}) collective-permute-start(f32[8,128]{1,0:T(8,128)S(1)} %add.19.share_in), channel_id=1, source_target_pairs={{0,3},{1,2},{2,1},{3,0},{4,7},{5,6},{6,5},{7,4},{8,11},{9,10},{10,... | collective-permute-start | bytes 12296 | tf_op jit(solution)/shard_map/ppermute | solution.py:676

commit v21 on v19

--- a/solution.py
+++ b/solution.py
@@ -537,8 +537,8 @@
     return (at ^ (at >> 1)) & 1
 
 
-def misfit_kernel(share, far, misfit):
-    misfit[0] = (share[...] + far[...])[0, 0]
+def misfit_kernel(core, other_core, across, other_across, misfit):
+    misfit[0] = ((core[...] + other_core[...]) + (across[...] + other_across[...]))[0, 0]
 
 
 def call(kernel, outs, scratch, args, flops, scalar=None):
@@ -650,8 +650,7 @@
         share = share + sum(fars)
         fars = hops(share, bits)
     share = share + sum(fars)
-    share = share + lax.ppermute(share, "gx", over_cores)
-    far = lax.ppermute(share, "gx", [(at, at ^ 3) for at in range(count)])
+    fars = [lax.ppermute(share, "gx", [(at, at ^ apart) for at in range(count)]) for apart in (1, 2, 3)]
     result, share = call(
         late_kernel,
         ((n, ny, nz), (ROWS, LANES)),
@@ -665,7 +664,7 @@
         ),
         60 * runs * 3 * cell,
     )
-    (misfit,) = call(misfit_kernel, ((1,),), (), (share, far), 1, scalar=0)
+    (misfit,) = call(misfit_kernel, ((1,),), (), (share, *fars), 1, scalar=0)
     return (result, misfit)
 
 

time: 37.4 us -> 37.5 us (level)
  starting transfers between devices: 19.9 us -> 20.8 us
  waiting for transfers between devices: 7.02 us -> 6.21 us
    ppermute x2 -> x3, starting transfers between devices: 0.96 us -> 1.86 us  [on_device(): lax.ppermute(share, 'gx', [(at, at ^ apart) for at in range(count)])]
    ppermute x2 -> x3, waiting for transfers between devices: 1.64 us -> 0.83 us  [on_device(): lax.ppermute(share, 'gx', [(at, at ^ apart) for at in range(count)])]
  transfers between devices with their start and end apart: 11 -> 12, of which waited for: 6 -> 6; matrix products, arithmetic and copies ran while one was open for 0% -> 0% of each run, Pallas kernels for 15% -> 15%
where the time goes in v21:
time: 37.5 us; the launch traced here: 37.3 us
  starting transfers between devices  20.8 us (55%)
  Pallas kernels  7.53 us (20%)
  waiting for transfers between devices  6.21 us (17%)
  local copies, waits for them, and re-layouts  2.03 us (5%)
  between operations  0.7 us (2%)
    ppermute x3, starting transfers between devices, neighbours(): return (lax.ppermute(to_chip, 'gx', over_chips), of_core)  11.1 us
    pallas_call x7, Pallas kernels, call(): pl.pallas_call(kernel, out_shape=tuple((jax.ShapeDtypeStruct(o, jnp.float...  7.53 us
    ppermute x3, waiting for transfers between devices, neighbours(): return (lax.ppermute(to_chip, 'gx', over_chips), of_core)  4.44 us
    ppermute x3, starting transfers between devices, neighbours(): of_core = lax.ppermute(to_core, 'gx', over_cores)  4.37 us
    ppermute x3, starting transfers between devices, hop(): return lax.ppermute(value, ('group', 'gx'), pairs)  3.52 us
    unnamed x6, local copies, waits for them, and re-layouts  2.03 us
    ppermute x3, starting transfers between devices, on_device(): lax.ppermute(share, 'gx', [(at, at ^ apart) for at in range(count)])  1.86 us
    ppermute x3, waiting for transfers between devices, on_device(): lax.ppermute(share, 'gx', [(at, at ^ apart) for at in range(count)])  0.83 us
  transfers between devices with their start and end apart: 12, of which 6 were waited for; matrix products, arithmetic and copies ran while one was open for 0% of the time, Pallas kernels for 15%

profile of v21, /device:TPU:0, one launch (start us, length us, event | category | flops | bytes accessed | tf_op | source)
XLA Modules:
  0.0 37.3 jit_solution(6762475010034190651)
XLA Ops:
  0.6 0.5 %collective-permute-start.2 = (f32[2,4,64,256]{3,2,1,0:T(8,128)}, f32[2,4,64,256]{3,2,1,0:T(8,128)S(1)}, u32[]{:S(2)}, u32[]{:S(2)}) collective-permute-start(f32[2,4,64,256]{3,2,1,0:T(8,128)} %initial.1), channel_id=1, source_target_pairs={{0,1},{1,0},{2,3},{3,2},{4,5},{5,4},{6,7},{7,6},{8,9},{9,8},{10,11... | collective-permute-start | bytes 1572872 | tf_op jit(solution)/shard_map/ppermute | solution.py:566
  1.1 5.7 %collective-permute-start.1 = (f32[2,4,64,256]{3,2,1,0:T(8,128)}, f32[2,4,64,256]{3,2,1,0:T(8,128)S(1)}, u32[]{:S(2)}, u32[]{:S(2)}) collective-permute-start(f32[2,4,64,256]{3,2,1,0:T(8,128)} %initial.1), channel_id=1, source_target_pairs={{0,15},{1,2},{2,1},{3,4},{4,3},{5,6},{6,5},{7,8},{8,7},{9,10},{10,... | collective-permute-start | bytes 1572872 | tf_op jit(solution)/shard_map/ppermute | solution.py:567
  6.8 0.0 copy-start.1
  6.8 1.1 %copy-done.1 = f32[2,4,64,256]{3,2,1,0:T(8,128)S(1)} copy-done((f32[2,4,64,256]{3,2,1,0:T(8,128)S(1)}, f32[2,4,64,256]{3,2,1,0:T(8,128)}, u32[]{:S(2)}) %copy-start.1) | copy-done | bytes 524312
  7.9 0.0 copy-start.2
  7.9 0.9 %copy-done.2 = f32[4,64,256]{2,1,0:T(8,128)S(1)} copy-done((f32[4,64,256]{2,1,0:T(8,128)S(1)}, f32[4,64,256]{2,1,0:T(8,128)}, u32[]{:S(2)}) %copy-start.2) | copy-done | bytes 262168
  8.8 0.1 shard_map.50
  8.9 0.1 collective-permute-start.3
  9.0 0.6 %collective-permute-start = (f32[3,2,64,128]{3,2,1,0:T(8,128)S(1)}, f32[3,2,64,128]{3,2,1,0:T(8,128)S(1)}, u32[]{:S(2)}, u32[]{:S(2)}) collective-permute-start(f32[3,2,64,128]{3,2,1,0:T(8,128)S(1)} %get-tuple-element.44), channel_id=1, source_target_pairs={{0,15},{1,2},{2,1},{3,4},{4,3},{5,6},{6,5},{7,8},{8,7},{9,10},{10,... | collective-permute-start | bytes 589832 | tf_op jit(solution)/shard_map/ppermute | solution.py:567
  9.6 0.8 %collective-permute-done.3.m_core = f32[3,2,64,128]{3,2,1,0:T(8,128)S(1)} collective-permute-done((f32[3,2,64,128]{3,2,1,0:T(8,128)S(1)}, f32[3,2,64,128]{3,2,1,0:T(8,128)S(1)}, u32[]{:S(2)}, u32[]{:S(2)}) %collective-permute-start.3) | collective-permute-done | bytes 196640 | tf_op jit(solution)/shard_map/ppermute | solution.py:566
  10.5 0.0 collective-permute-done.2.of_core
  10.5 0.0 copy-start
  10.5 0.7 %shard_map.51 = (f32[2,4,2,80,128]{4,3,2,1,0:T(8,128)S(1)}, f32[2,6,2,80,128]{4,3,2,1,0:T(8,128)S(1)}, f32[6,2,64,128]{3,2,1,0:T(8,128)S(1)}, f32[6,2,64,128]{3,...) custom-call(f32[2,4,64,256]{3,2,1,0:T(8,128)S(1)} %collective-permut, ...), custom_call_target="tpu_custom_call" | custom-call | flops 3932160 | bytes 5636096 | tf_op jit(solution)/shard_map/pallas_call | solution.py:546
  11.2 2.8 %collective-permute-done.1.of_chip = f32[2,4,64,256]{3,2,1,0:T(8,128)S(1)} collective-permute-done((f32[2,4,64,256]{3,2,1,0:T(8,128)}, f32[2,4,64,256]{3,2,1,0:T(8,128)S(1)}, u32[]{:S(2)}, u32[]{:S(2)}) %collective-permute-start.1) | collective-permute-done | bytes 524320 | tf_op jit(solution)/shard_map/ppermute | solution.py:567
  14.0 0.0 copy-done
  14.0 1.3 %shard_map.52 = (f32[2,4,2,80,128]{4,3,2,1,0:T(8,128)S(1)}, f32[2,4,2,80,128]{4,3,2,1,0:T(8,128)S(1)}, f32[2,5,2,80,128]{4,3,2,1,0:T(8,128)S(1)}, f32[2,3,2,80,1...) custom-call(f32[2,4,64,256]{3,2,1,0:T(8,128)S(1)} %collective-permute-done.1.of_chip, ...), custom_call_target="tpu_custom_call" | custom-call | flops 5898240 | bytes 8425472 | tf_op jit(solution)/shard_map/pallas_call | solution.py:546
  15.4 1.6 %collective-permute-done.m_chip = f32[3,2,64,128]{3,2,1,0:T(8,128)S(1)} collective-permute-done((f32[3,2,64,128]{3,2,1,0:T(8,128)S(1)}, f32[3,2,64,128]{3,2,1,0:T(8,128)S(1)}, u32[]{:S(2)}, u32[]{:S(2)}) %collective-permute-start) | collective-permute-done | bytes 196640 | tf_op jit(solution)/shard_map/ppermute | solution.py:567
  17.0 1.2 %shard_map.53 = (f32[3,2,64,128]{3,2,1,0:T(8,128)S(1)}, f32[2,2,64,128]{3,2,1,0:T(8,128)S(1)}, f32[2,2,64,128]{3,2,1,0:T(8,128)S(1)}, f32[2,2,64,128]{3,2,1,0:T(...) custom-call(f32[3,2,64,128]{3,2,1,0:T(8,128)S(1)} %collective-permut, ...), custom_call_target="tpu_custom_call" | custom-call | flops 5898240 | bytes 11001856 | tf_op jit(solution)/shard_map/pallas_call | solution.py:546
  18.2 3.8 %collective-permute-start.5 = (f32[2,3,2,72,128]{4,3,2,1,0:T(8,128)S(1)}, f32[2,3,2,72,128]{4,3,2,1,0:T(8,128)S(1)}, u32[]{:S(2)}, u32[]{:S(2)}) collective-permute-start(f32[2,3,2,72,128]{4,3,2,1,0:T(8,128)S(1)} %get-tuple-element.71), channel_id=1, source_target_pairs={{0,1},{1,0},{2,3},{3,2},{4,5},{5,4},{6,7},{7,6},{8,9},{9,8},{10,11... | collective-permute-start | bytes 1327112 | tf_op jit(solution)/shard_map/ppermute | solution.py:566
  22.0 4.8 %collective-permute-start.4 = (f32[2,3,2,64,128]{4,3,2,1,0:T(8,128)S(1)}, f32[2,3,2,64,128]{4,3,2,1,0:T(8,128)S(1)}, u32[]{:S(2)}, u32[]{:S(2)}) collective-permute-start(f32[2,3,2,64,128]{4,3,2,1,0:T(8,128)S(1)} %get-tuple-element.62), channel_id=1, source_target_pairs={{0,15},{1,2},{2,1},{3,4},{4,3},{5,6},{6,5},{7,8},{8,7},{9,10},{10,... | collective-permute-start | bytes 1179656 | tf_op jit(solution)/shard_map/ppermute | solution.py:567
  26.8 0.0 collective-permute-done.5.of_core
  26.8 1.5 %collective-permute-start.8 = (f32[8,128]{1,0:T(8,128)S(1)}, f32[8,128]{1,0:T(8,128)S(1)}, u32[]{:S(2)}, u32[]{:S(2)}) collective-permute-start(f32[8,128]{1,0:T(8,128)S(1)} %fusion.share_in), channel_id=1, source_target_pairs={{0,16},{1,13},{2,14},{3,19},{4,20},{5,9},{6,10},{7,23},{8,24},{9,5... | collective-permute-start | bytes 12296 | tf_op jit(solution)/shard_map/ppermute | solution.py:629
  28.3 0.5 %collective-permute-start.6 = (f32[8,128]{1,0:T(8,128)S(1)}, f32[8,128]{1,0:T(8,128)S(1)}, u32[]{:S(2)}, u32[]{:S(2)}) collective-permute-start(f32[8,128]{1,0:T(8,128)S(1)} %fusion.share_in), channel_id=1, source_target_pairs={{0,16},{1,9},{2,10},{3,19},{4,20},{5,13},{6,14},{7,23},{8,24},{9,1... | collective-permute-start | bytes 12296 | tf_op jit(solution)/shard_map/ppermute | solution.py:629
  28.8 1.5 %collective-permute-start.7 = (f32[8,128]{1,0:T(8,128)S(1)}, f32[8,128]{1,0:T(8,128)S(1)}, u32[]{:S(2)}, u32[]{:S(2)}) collective-permute-start(f32[8,128]{1,0:T(8,128)S(1)} %fusion.share_in), channel_id=1, source_target_pairs={{0,16},{1,5},{2,6},{3,19},{4,20},{5,1},{6,2},{7,23},{8,24},{9,13},... | collective-permute-start | bytes 12296 | tf_op jit(solution)/shard_map/ppermute | solution.py:629
  30.3 2.0 %shard_map.54 = (f32[2,5,2,80,128]{4,3,2,1,0:T(8,128)S(1)}, f32[2,1,2,80,128]{4,3,2,1,0:T(8,128)S(1)}, f32[2,3,2,80,128]{4,3,2,1,0:T(8,128)S(1)}, f32[2,3,2,64,1...) custom-call(f32[2,3,2,72,128]{4,3,2,1,0:T(8,128)S(1)} %collective-pe, ...), custom_call_target="tpu_custom_call" | custom-call | flops 7864320 | bytes 10903552 | tf_op jit(solution)/shard_map/pallas_call | solution.py:546
  32.3 0.0 collective-permute-done.8
  32.3 0.0 collective-permute-done.6
  32.3 0.1 collective-permute-done.7
  32.4 0.0 collective-permute-start.9
  32.4 1.3 %collective-permute-start.10 = (f32[8,128]{1,0:T(8,128)S(1)}, f32[8,128]{1,0:T(8,128)S(1)}, u32[]{:S(2)}, u32[]{:S(2)}) collective-permute-start(f32[8,128]{1,0:T(8,128)S(1)} %add_add_fusion.share_in), channel_id=1, source_target_pairs={{0,2},{1,3},{2,0},{3,1},{4,6},{5,7},{6,4},{7,5},{8,10},{9,11},{10,... | collective-permute-start | bytes 12296 | tf_op jit(solution)/shard_map/ppermute | solution.py:653
  33.7 0.6 %collective-permute-start.11 = (f32[8,128]{1,0:T(8,128)S(1)}, f32[8,128]{1,0:T(8,128)S(1)}, u32[]{:S(2)}, u32[]{:S(2)}) collective-permute-start(f32[8,128]{1,0:T(8,128)S(1)} %add_add_fusion.share_in), channel_id=1, source_target_pairs={{0,3},{1,2},{2,1},{3,0},{4,7},{5,6},{6,5},{7,4},{8,11},{9,10},{10,... | collective-permute-start | bytes 12296 | tf_op jit(solution)/shard_map/ppermute | solution.py:653
  34.3 0.0 collective-permute-done.4.of_chip
  34.3 1.6 %shard_map.55 = (f32[4,64,256]{2,1,0:T(8,128)}, f32[8,128]{1,0:T(8,128)S(1)}) custom-call(f32[2,3,2,64,128]{4,3,2,1,0:T(8,128)S(1)} %collective-permute-done.4.of_chip, f32[6,2,64,128]{3,2,1,0:T(8,128)S(1)} %get-tuple-element.50.mx.mx_a, f32[6,2,64,128]{3,2,1,0:T(8,128)S(1)} %get-tuple-element.51.my.my_a, ...), custom_call_target="tpu_custom_call" | custom-call | flops 5898240 | bytes 9150464 | tf_op jit(solution)/shard_map/pallas_call | solution.py:546
  35.9 0.0 collective-permute-done.9.other_core
  35.9 0.2 collective-permute-done.10.across
  36.1 0.6 %collective-permute-done.11.other_across = f32[8,128]{1,0:T(8,128)S(1)} collective-permute-done((f32[8,128]{1,0:T(8,128)S(1)}, f32[8,128]{1,0:T(8,128)S(1)}, u32[]{:S(2)}, u32[]{:S(2)}) %collective-permute-start.11) | collective-permute-done | bytes 4128 | tf_op jit(solution)/shard_map/ppermute | solution.py:653
  36.7 0.6 %shard_map.56 = f32[1]{0:T(128)} custom-call(f32[8,128]{1,0:T(8,128)S(1)} %get-tuple-element.85.core, f32[8,128]{1,0:T(8,128)S(1)} %collective-permute-done.9.other_core, f32[8,128]{1,0:T(8,128)S(1)} %collective-permute-done.10.across, f32[8,128]{1,0:T(8,128)S(1)} %collective-permute-done.11.other_across), custom_call_target="tpu_custom_call" | custom-call | flops 1 | bytes 16388 | tf_op jit(solution)/shard_map/pallas_call | solution.py:546
  (2 shorter events, 0.0 us)
Async XLA Ops:
  0.6 9.8 %collective-permute-start.2 = (f32[2,4,64,256]{3,2,1,0:T(8,128)}, f32[2,4,64,256]{3,2,1,0:T(8,128)S(1)}, u32[]{:S(2)}, u32[]{:S(2)}) collective-permute-start(f32[2,4,64,256]{3,2,1,0:T(8,128)} %initial.1), channel_id=1, source_target_pairs={{0,1},{1,0},{2,3},{3,2},{4,5},{5,4},{6,7},{7,6},{8,9},{9,8},{10,11... | collective-permute-start | bytes 1572872 | tf_op jit(solution)/shard_map/ppermute | solution.py:566
  1.1 12.8 %collective-permute-start.1 = (f32[2,4,64,256]{3,2,1,0:T(8,128)}, f32[2,4,64,256]{3,2,1,0:T(8,128)S(1)}, u32[]{:S(2)}, u32[]{:S(2)}) collective-permute-start(f32[2,4,64,256]{3,2,1,0:T(8,128)} %initial.1), channel_id=1, source_target_pairs={{0,15},{1,2},{2,1},{3,4},{4,3},{5,6},{6,5},{7,8},{8,7},{9,10},{10,... | collective-permute-start | bytes 1572872 | tf_op jit(solution)/shard_map/ppermute | solution.py:567
  6.8 1.1 %copy-start.1 = (f32[2,4,64,256]{3,2,1,0:T(8,128)S(1)}, f32[2,4,64,256]{3,2,1,0:T(8,128)}, u32[]{:S(2)}) copy-start(f32[2,4,64,256]{3,2,1,0:T(8,128)} %initial.1) | copy-start | bytes 1572868
  7.9 0.9 %copy-start.2 = (f32[4,64,256]{2,1,0:T(8,128)S(1)}, f32[4,64,256]{2,1,0:T(8,128)}, u32[]{:S(2)}) copy-start(f32[4,64,256]{2,1,0:T(8,128)} %mobility.1) | copy-start | bytes 786436
  8.9 1.5 %collective-permute-start.3 = (f32[3,2,64,128]{3,2,1,0:T(8,128)S(1)}, f32[3,2,64,128]{3,2,1,0:T(8,128)S(1)}, u32[]{:S(2)}, u32[]{:S(2)}) collective-permute-start(f32[3,2,64,128]{3,2,1,0:T(8,128)S(1)} %get-tuple-element.47), channel_id=1, source_target_pairs={{0,1},{1,0},{2,3},{3,2},{4,5},{5,4},{6,7},{7,6},{8,9},{9,8},{10,11... | collective-permute-start | bytes 589832 | tf_op jit(solution)/shard_map/ppermute | solution.py:566
  9.0 8.0 %collective-permute-start = (f32[3,2,64,128]{3,2,1,0:T(8,128)S(1)}, f32[3,2,64,128]{3,2,1,0:T(8,128)S(1)}, u32[]{:S(2)}, u32[]{:S(2)}) collective-permute-start(f32[3,2,64,128]{3,2,1,0:T(8,128)S(1)} %get-tuple-element.44), channel_id=1, source_target_pairs={{0,15},{1,2},{2,1},{3,4},{4,3},{5,6},{6,5},{7,8},{8,7},{9,10},{10,... | collective-permute-start | bytes 589832 | tf_op jit(solution)/shard_map/ppermute | solution.py:567
  10.5 3.5 %copy-start = (f32[2,4,64,256]{3,2,1,0:T(8,128)S(1)}, f32[2,4,64,256]{3,2,1,0:T(8,128)}, u32[]{:S(2)}) copy-start(f32[2,4,64,256]{3,2,1,0:T(8,128)} %observed.3) | copy-start | bytes 1572868
  18.2 8.6 %collective-permute-start.5 = (f32[2,3,2,72,128]{4,3,2,1,0:T(8,128)S(1)}, f32[2,3,2,72,128]{4,3,2,1,0:T(8,128)S(1)}, u32[]{:S(2)}, u32[]{:S(2)}) collective-permute-start(f32[2,3,2,72,128]{4,3,2,1,0:T(8,128)S(1)} %get-tuple-element.71), channel_id=1, source_target_pairs={{0,1},{1,0},{2,3},{3,2},{4,5},{5,4},{6,7},{7,6},{8,9},{9,8},{10,11... | collective-permute-start | bytes 1327112 | tf_op jit(solution)/shard_map/ppermute | solution.py:566
  22.0 12.3 %collective-permute-start.4 = (f32[2,3,2,64,128]{4,3,2,1,0:T(8,128)S(1)}, f32[2,3,2,64,128]{4,3,2,1,0:T(8,128)S(1)}, u32[]{:S(2)}, u32[]{:S(2)}) collective-permute-start(f32[2,3,2,64,128]{4,3,2,1,0:T(8,128)S(1)} %get-tuple-element.62), channel_id=1, source_target_pairs={{0,15},{1,2},{2,1},{3,4},{4,3},{5,6},{6,5},{7,8},{8,7},{9,10},{10,... | collective-permute-start | bytes 1179656 | tf_op jit(solution)/shard_map/ppermute | solution.py:567
  26.8 5.5 %collective-permute-start.8 = (f32[8,128]{1,0:T(8,128)S(1)}, f32[8,128]{1,0:T(8,128)S(1)}, u32[]{:S(2)}, u32[]{:S(2)}) collective-permute-start(f32[8,128]{1,0:T(8,128)S(1)} %fusion.share_in), channel_id=1, source_target_pairs={{0,16},{1,13},{2,14},{3,19},{4,20},{5,9},{6,10},{7,23},{8,24},{9,5... | collective-permute-start | bytes 12296 | tf_op jit(solution)/shard_map/ppermute | solution.py:629
  28.3 4.0 %collective-permute-start.6 = (f32[8,128]{1,0:T(8,128)S(1)}, f32[8,128]{1,0:T(8,128)S(1)}, u32[]{:S(2)}, u32[]{:S(2)}) collective-permute-start(f32[8,128]{1,0:T(8,128)S(1)} %fusion.share_in), channel_id=1, source_target_pairs={{0,16},{1,9},{2,10},{3,19},{4,20},{5,13},{6,14},{7,23},{8,24},{9,1... | collective-permute-start | bytes 12296 | tf_op jit(solution)/shard_map/ppermute | solution.py:629
  28.8 3.6 %collective-permute-start.7 = (f32[8,128]{1,0:T(8,128)S(1)}, f32[8,128]{1,0:T(8,128)S(1)}, u32[]{:S(2)}, u32[]{:S(2)}) collective-permute-start(f32[8,128]{1,0:T(8,128)S(1)} %fusion.share_in), channel_id=1, source_target_pairs={{0,16},{1,5},{2,6},{3,19},{4,20},{5,1},{6,2},{7,23},{8,24},{9,13},... | collective-permute-start | bytes 12296 | tf_op jit(solution)/shard_map/ppermute | solution.py:629
  32.4 3.5 %collective-permute-start.9 = (f32[8,128]{1,0:T(8,128)S(1)}, f32[8,128]{1,0:T(8,128)S(1)}, u32[]{:S(2)}, u32[]{:S(2)}) collective-permute-start(f32[8,128]{1,0:T(8,128)S(1)} %add_add_fusion.share_in), channel_id=1, source_target_pairs={{0,1},{1,0},{2,3},{3,2},{4,5},{5,4},{6,7},{7,6},{8,9},{9,8},{10,11... | collective-permute-start | bytes 12296 | tf_op jit(solution)/shard_map/ppermute | solution.py:653
  32.4 3.7 %collective-permute-start.10 = (f32[8,128]{1,0:T(8,128)S(1)}, f32[8,128]{1,0:T(8,128)S(1)}, u32[]{:S(2)}, u32[]{:S(2)}) collective-permute-start(f32[8,128]{1,0:T(8,128)S(1)} %add_add_fusion.share_in), channel_id=1, source_target_pairs={{0,2},{1,3},{2,0},{3,1},{4,6},{5,7},{6,4},{7,5},{8,10},{9,11},{10,... | collective-permute-start | bytes 12296 | tf_op jit(solution)/shard_map/ppermute | solution.py:653
  33.7 3.0 %collective-permute-start.11 = (f32[8,128]{1,0:T(8,128)S(1)}, f32[8,128]{1,0:T(8,128)S(1)}, u32[]{:S(2)}, u32[]{:S(2)}) collective-permute-start(f32[8,128]{1,0:T(8,128)S(1)} %add_add_fusion.share_in), channel_id=1, source_target_pairs={{0,3},{1,2},{2,1},{3,0},{4,7},{5,6},{6,5},{7,4},{8,11},{9,10},{10,... | collective-permute-start | bytes 12296 | tf_op jit(solution)/shard_map/ppermute | solution.py:653

commit v22 on v21

--- a/solution.py
+++ b/solution.py
@@ -142,8 +142,9 @@
     return each(lambda x, y: x - y, a, b)
 
 
-def own_kernel(initial, mobility, conc, mob, to_chip, to_core):
+def own_kernel(initial, mobility, conc, mob, to_chip, to_core, same):
     runs, n, ny, _ = initial.shape
+    same[...] = initial[...]
     place = [either(n - 1 - at, at) for at in range(n)]
 
     def one_run(run, carry):
@@ -572,15 +573,15 @@
     def lies_padded(*lead):
         return (*lead, blocks, ny + 2 * PAD, LANES)
 
-    if n == 4:
-        near = (initial, initial)
-    else:
-        near = [lax.dynamic_slice_in_dim(initial, at, 4, 1) for at in (either(0, n - 4), either(n - 4, 0))]
-    of_chip, of_core = neighbours(*near)
-    conc, mob, to_chip, to_core = call(
-        own_kernel, (lies_padded(runs, n), lies_padded(n), lies(3), lies(3)), (), (initial, mobility),
+    def nearest(field, first, second):
+        return field if n == 4 else lax.dynamic_slice_in_dim(field, either(first, second), 4, 1)
+
+    of_chip = lax.ppermute(nearest(initial, 0, n - 4), "gx", over_chips)
+    conc, mob, to_chip, to_core, same = call(
+        own_kernel, (lies_padded(runs, n), lies_padded(n), lies(3), lies(3), initial.shape), (), (initial, mobility),
         runs * n * cell,
     )
+    of_core = lax.ppermute(nearest(same, n - 4, 0), "gx", over_cores)
     m_chip, m_core = neighbours(to_chip, to_core)
     conc_core, chem0_a, *faces_a = call(
         core_kernel,

time: 37.5 us -> 39.4 us (1.051)
  waiting for transfers between devices: 6.21 us -> 7.43 us
  starting transfers between devices: 20.8 us -> 21.6 us
    ppermute x0 -> x2, starting transfers between devices: none -> 6.18 us  [the longest x1 5.67 us: on_device(): of_chip = lax.ppermute(nearest(initial, 0, n - 4), 'gx', over_chips)]
    ppermute x3 -> x2, starting transfers between devices: 11.1 us -> 5.4 us  [neighbours(): return (lax.ppermute(to_chip, 'gx', over_chips), of_core)]
    ppermute x0 -> x2, waiting for transfers between devices: none -> 4.76 us  [the longest x1 4.75 us: on_device(): of_chip = lax.ppermute(nearest(initial, 0, n - 4), 'gx', over_chips)]
    ppermute x3 -> x2, waiting for transfers between devices: 4.44 us -> 0.76 us  [neighbours(): return (lax.ppermute(to_chip, 'gx', over_chips), of_core)]
    ppermute x3 -> x2, starting transfers between devices: 4.37 us -> 4.67 us  [neighbours(): of_core = lax.ppermute(to_core, 'gx', over_cores)]
    ppermute x3 -> x2, waiting for transfers between devices: 0.83 us -> 0.82 us  [neighbours(): of_core = lax.ppermute(to_core, 'gx', over_cores)]
  transfers between devices with their start and end apart: 12 -> 12, of which waited for: 6 -> 6; matrix products, arithmetic and copies ran while one was open for 0% -> 0% of each run, Pallas kernels for 15% -> 14%
where the time goes in v22:
time: 39.4 us; the launch traced here: 39.2 us
  starting transfers between devices  21.6 us (55%)
  Pallas kernels  7.46 us (19%)
  waiting for transfers between devices  7.43 us (19%)
  local copies, waits for them, and re-layouts  1.99 us (5%)
  between operations  0.7 us (2%)
    pallas_call x7, Pallas kernels, call(): pl.pallas_call(kernel, out_shape=tuple((jax.ShapeDtypeStruct(o, jnp.float...  7.46 us
    ppermute x1, starting transfers between devices, on_device(): of_chip = lax.ppermute(nearest(initial, 0, n - 4), 'gx', over_chips)  5.67 us
    ppermute x2, starting transfers between devices, neighbours(): return (lax.ppermute(to_chip, 'gx', over_chips), of_core)  5.4 us
    ppermute x1, waiting for transfers between devices, on_device(): of_chip = lax.ppermute(nearest(initial, 0, n - 4), 'gx', over_chips)  4.75 us
    ppermute x2, starting transfers between devices, neighbours(): of_core = lax.ppermute(to_core, 'gx', over_cores)  4.67 us
    ppermute x3, starting transfers between devices, hop(): return lax.ppermute(value, ('group', 'gx'), pairs)  3.52 us
    unnamed x6, local copies, waits for them, and re-layouts  1.99 us
    ppermute x3, starting transfers between devices, on_device(): lax.ppermute(share, 'gx', [(at, at ^ apart) for at in range(count)])  1.86 us
  transfers between devices with their start and end apart: 12, of which 6 were waited for; matrix products, arithmetic and copies ran while one was open for 0% of the time, Pallas kernels for 14%

profile of v22, /device:TPU:0, one launch (start us, length us, event | category | flops | bytes accessed | tf_op | source)
XLA Modules:
  0.0 39.2 jit_solution(9638984148308196643)
XLA Ops:
  0.6 0.0 copy-start.1
  0.6 1.0 %copy-done.1 = f32[2,4,64,256]{3,2,1,0:T(8,128)S(1)} copy-done((f32[2,4,64,256]{3,2,1,0:T(8,128)S(1)}, f32[2,4,64,256]{3,2,1,0:T(8,128)}, u32[]{:S(2)}) %copy-start.1) | copy-done | bytes 524312
  1.7 0.0 copy-start.2
  1.7 0.9 %copy-done.2 = f32[4,64,256]{2,1,0:T(8,128)S(1)} copy-done((f32[4,64,256]{2,1,0:T(8,128)S(1)}, f32[4,64,256]{2,1,0:T(8,128)}, u32[]{:S(2)}) %copy-start.2) | copy-done | bytes 262168
  2.6 0.1 shard_map.50
  2.8 0.5 %collective-permute-start.2 = (f32[2,4,64,256]{3,2,1,0:T(8,128)S(1)}, f32[2,4,64,256]{3,2,1,0:T(8,128)S(1)}, u32[]{:S(2)}, u32[]{:S(2)}) collective-permute-start(f32[2,4,64,256]{3,2,1,0:T(8,128)S(1)} %get-tuple-element.48), channel_id=1, source_target_pairs={{0,1},{1,0},{2,3},{3,2},{4,5},{5,4},{6,7},{7,6},{8,9},{9,8},{10,11... | collective-permute-start | bytes 1572872 | tf_op jit(solution)/shard_map/ppermute | solution.py:584
  3.3 5.7 %collective-permute-start.1 = (f32[2,4,64,256]{3,2,1,0:T(8,128)S(1)}, f32[2,4,64,256]{3,2,1,0:T(8,128)S(1)}, u32[]{:S(2)}, u32[]{:S(2)}) collective-permute-start(f32[2,4,64,256]{3,2,1,0:T(8,128)S(1)} %copy-done.1), channel_id=1, source_target_pairs={{0,15},{1,2},{2,1},{3,4},{4,3},{5,6},{6,5},{7,8},{8,7},{9,10},{10,... | collective-permute-start | bytes 1572872 | tf_op jit(solution)/shard_map/ppermute | solution.py:579
  8.9 0.0 collective-permute-start.3
  8.9 0.6 %collective-permute-start = (f32[3,2,64,128]{3,2,1,0:T(8,128)S(1)}, f32[3,2,64,128]{3,2,1,0:T(8,128)S(1)}, u32[]{:S(2)}, u32[]{:S(2)}) collective-permute-start(f32[3,2,64,128]{3,2,1,0:T(8,128)S(1)} %get-tuple-element.45), channel_id=1, source_target_pairs={{0,15},{1,2},{2,1},{3,4},{4,3},{5,6},{6,5},{7,8},{8,7},{9,10},{10,... | collective-permute-start | bytes 589832 | tf_op jit(solution)/shard_map/ppermute | solution.py:568
  9.6 0.8 %collective-permute-done.3.m_core = f32[3,2,64,128]{3,2,1,0:T(8,128)S(1)} collective-permute-done((f32[3,2,64,128]{3,2,1,0:T(8,128)S(1)}, f32[3,2,64,128]{3,2,1,0:T(8,128)S(1)}, u32[]{:S(2)}, u32[]{:S(2)}) %collective-permute-start.3) | collective-permute-done | bytes 196640 | tf_op jit(solution)/shard_map/ppermute | solution.py:567
  10.4 0.0 collective-permute-done.2.of_core
  10.4 0.0 copy-start
  10.4 0.8 %shard_map.51 = (f32[2,4,2,80,128]{4,3,2,1,0:T(8,128)S(1)}, f32[2,6,2,80,128]{4,3,2,1,0:T(8,128)S(1)}, f32[6,2,64,128]{3,2,1,0:T(8,128)S(1)}, f32[6,2,64,128]{3,...) custom-call(f32[2,4,64,256]{3,2,1,0:T(8,128)S(1)} %collective-permut, ...), custom_call_target="tpu_custom_call" | custom-call | flops 3932160 | bytes 5636096 | tf_op jit(solution)/shard_map/pallas_call | solution.py:547
  11.2 4.8 %collective-permute-done.1.of_chip = f32[2,4,64,256]{3,2,1,0:T(8,128)S(1)} collective-permute-done((f32[2,4,64,256]{3,2,1,0:T(8,128)S(1)}, f32[2,4,64,256]{3,2,1,0:T(8,128)S(1)}, u32[]{:S(2)}, u32[]{:S(2)}) %collective-permute-start.1) | collective-permute-done | bytes 524320 | tf_op jit(solution)/shard_map/ppermute | solution.py:579
  15.9 0.0 copy-done
  15.9 1.3 %shard_map.52 = (f32[2,4,2,80,128]{4,3,2,1,0:T(8,128)S(1)}, f32[2,4,2,80,128]{4,3,2,1,0:T(8,128)S(1)}, f32[2,5,2,80,128]{4,3,2,1,0:T(8,128)S(1)}, f32[2,3,2,80,1...) custom-call(f32[2,4,64,256]{3,2,1,0:T(8,128)S(1)} %collective-permute-done.1.of_chip, ...), custom_call_target="tpu_custom_call" | custom-call | flops 5898240 | bytes 8425472 | tf_op jit(solution)/shard_map/pallas_call | solution.py:547
  17.3 0.8 %collective-permute-done.m_chip = f32[3,2,64,128]{3,2,1,0:T(8,128)S(1)} collective-permute-done((f32[3,2,64,128]{3,2,1,0:T(8,128)S(1)}, f32[3,2,64,128]{3,2,1,0:T(8,128)S(1)}, u32[]{:S(2)}, u32[]{:S(2)}) %collective-permute-start) | collective-permute-done | bytes 196640 | tf_op jit(solution)/shard_map/ppermute | solution.py:568
  18.0 1.2 %shard_map.53 = (f32[3,2,64,128]{3,2,1,0:T(8,128)S(1)}, f32[2,2,64,128]{3,2,1,0:T(8,128)S(1)}, f32[2,2,64,128]{3,2,1,0:T(8,128)S(1)}, f32[2,2,64,128]{3,2,1,0:T(...) custom-call(f32[3,2,64,128]{3,2,1,0:T(8,128)S(1)} %collective-permut, ...), custom_call_target="tpu_custom_call" | custom-call | flops 5898240 | bytes 11001856 | tf_op jit(solution)/shard_map/pallas_call | solution.py:547
  19.3 4.7 %collective-permute-start.5 = (f32[2,3,2,72,128]{4,3,2,1,0:T(8,128)S(1)}, f32[2,3,2,72,128]{4,3,2,1,0:T(8,128)S(1)}, u32[]{:S(2)}, u32[]{:S(2)}) collective-permute-start(f32[2,3,2,72,128]{4,3,2,1,0:T(8,128)S(1)} %get-tuple-element.73), channel_id=1, source_target_pairs={{0,1},{1,0},{2,3},{3,2},{4,5},{5,4},{6,7},{7,6},{8,9},{9,8},{10,11... | collective-permute-start | bytes 1327112 | tf_op jit(solution)/shard_map/ppermute | solution.py:567
  23.9 4.8 %collective-permute-start.4 = (f32[2,3,2,64,128]{4,3,2,1,0:T(8,128)S(1)}, f32[2,3,2,64,128]{4,3,2,1,0:T(8,128)S(1)}, u32[]{:S(2)}, u32[]{:S(2)}) collective-permute-start(f32[2,3,2,64,128]{4,3,2,1,0:T(8,128)S(1)} %get-tuple-element.64), channel_id=1, source_target_pairs={{0,15},{1,2},{2,1},{3,4},{4,3},{5,6},{6,5},{7,8},{8,7},{9,10},{10,... | collective-permute-start | bytes 1179656 | tf_op jit(solution)/shard_map/ppermute | solution.py:568
  28.7 0.0 collective-permute-done.5.of_core
  28.7 1.5 %collective-permute-start.8 = (f32[8,128]{1,0:T(8,128)S(1)}, f32[8,128]{1,0:T(8,128)S(1)}, u32[]{:S(2)}, u32[]{:S(2)}) collective-permute-start(f32[8,128]{1,0:T(8,128)S(1)} %fusion.share_in), channel_id=1, source_target_pairs={{0,16},{1,13},{2,14},{3,19},{4,20},{5,9},{6,10},{7,23},{8,24},{9,5... | collective-permute-start | bytes 12296 | tf_op jit(solution)/shard_map/ppermute | solution.py:630
  30.2 0.5 %collective-permute-start.6 = (f32[8,128]{1,0:T(8,128)S(1)}, f32[8,128]{1,0:T(8,128)S(1)}, u32[]{:S(2)}, u32[]{:S(2)}) collective-permute-start(f32[8,128]{1,0:T(8,128)S(1)} %fusion.share_in), channel_id=1, source_target_pairs={{0,16},{1,9},{2,10},{3,19},{4,20},{5,13},{6,14},{7,23},{8,24},{9,1... | collective-permute-start | bytes 12296 | tf_op jit(solution)/shard_map/ppermute | solution.py:630
  30.7 1.5 %collective-permute-start.7 = (f32[8,128]{1,0:T(8,128)S(1)}, f32[8,128]{1,0:T(8,128)S(1)}, u32[]{:S(2)}, u32[]{:S(2)}) collective-permute-start(f32[8,128]{1,0:T(8,128)S(1)} %fusion.share_in), channel_id=1, source_target_pairs={{0,16},{1,5},{2,6},{3,19},{4,20},{5,1},{6,2},{7,23},{8,24},{9,13},... | collective-permute-start | bytes 12296 | tf_op jit(solution)/shard_map/ppermute | solution.py:630
  32.2 1.9 %shard_map.54 = (f32[2,5,2,80,128]{4,3,2,1,0:T(8,128)S(1)}, f32[2,1,2,80,128]{4,3,2,1,0:T(8,128)S(1)}, f32[2,3,2,80,128]{4,3,2,1,0:T(8,128)S(1)}, f32[2,3,2,64,1...) custom-call(f32[2,3,2,72,128]{4,3,2,1,0:T(8,128)S(1)} %collective-pe, ...), custom_call_target="tpu_custom_call" | custom-call | flops 7864320 | bytes 10903552 | tf_op jit(solution)/shard_map/pallas_call | solution.py:547
  34.1 0.0 collective-permute-done.8
  34.2 0.0 collective-permute-done.6
  34.2 0.2 collective-permute-done.7
  34.4 0.0 collective-permute-start.9
  34.4 1.3 %collective-permute-start.10 = (f32[8,128]{1,0:T(8,128)S(1)}, f32[8,128]{1,0:T(8,128)S(1)}, u32[]{:S(2)}, u32[]{:S(2)}) collective-permute-start(f32[8,128]{1,0:T(8,128)S(1)} %add_add_fusion.share_in), channel_id=1, source_target_pairs={{0,2},{1,3},{2,0},{3,1},{4,6},{5,7},{6,4},{7,5},{8,10},{9,11},{10,... | collective-permute-start | bytes 12296 | tf_op jit(solution)/shard_map/ppermute | solution.py:654
  35.6 0.6 %collective-permute-start.11 = (f32[8,128]{1,0:T(8,128)S(1)}, f32[8,128]{1,0:T(8,128)S(1)}, u32[]{:S(2)}, u32[]{:S(2)}) collective-permute-start(f32[8,128]{1,0:T(8,128)S(1)} %add_add_fusion.share_in), channel_id=1, source_target_pairs={{0,3},{1,2},{2,1},{3,0},{4,7},{5,6},{6,5},{7,4},{8,11},{9,10},{10,... | collective-permute-start | bytes 12296 | tf_op jit(solution)/shard_map/ppermute | solution.py:654
  36.2 0.0 collective-permute-done.4.of_chip
  36.2 1.5 %shard_map.55 = (f32[4,64,256]{2,1,0:T(8,128)}, f32[8,128]{1,0:T(8,128)S(1)}) custom-call(f32[2,3,2,64,128]{4,3,2,1,0:T(8,128)S(1)} %collective-permute-done.4.of_chip, f32[6,2,64,128]{3,2,1,0:T(8,128)S(1)} %get-tuple-element.52.mx.mx_a, f32[6,2,64,128]{3,2,1,0:T(8,128)S(1)} %get-tuple-element.53.my.my_a, ...), custom_call_target="tpu_custom_call" | custom-call | flops 5898240 | bytes 9150464 | tf_op jit(solution)/shard_map/pallas_call | solution.py:547
  37.8 0.0 collective-permute-done.9.other_core
  37.8 0.3 collective-permute-done.10.across
  38.0 0.6 %collective-permute-done.11.other_across = f32[8,128]{1,0:T(8,128)S(1)} collective-permute-done((f32[8,128]{1,0:T(8,128)S(1)}, f32[8,128]{1,0:T(8,128)S(1)}, u32[]{:S(2)}, u32[]{:S(2)}) %collective-permute-start.11) | collective-permute-done | bytes 4128 | tf_op jit(solution)/shard_map/ppermute | solution.py:654
  38.7 0.6 %shard_map.56 = f32[1]{0:T(128)} custom-call(f32[8,128]{1,0:T(8,128)S(1)} %get-tuple-element.87.core, f32[8,128]{1,0:T(8,128)S(1)} %collective-permute-done.9.other_core, f32[8,128]{1,0:T(8,128)S(1)} %collective-permute-done.10.across, f32[8,128]{1,0:T(8,128)S(1)} %collective-permute-done.11.other_across), custom_call_target="tpu_custom_call" | custom-call | flops 1 | bytes 16388 | tf_op jit(solution)/shard_map/pallas_call | solution.py:547
  (2 shorter events, 0.0 us)
Async XLA Ops:
  0.6 1.0 %copy-start.1 = (f32[2,4,64,256]{3,2,1,0:T(8,128)S(1)}, f32[2,4,64,256]{3,2,1,0:T(8,128)}, u32[]{:S(2)}) copy-start(f32[2,4,64,256]{3,2,1,0:T(8,128)} %initial.1) | copy-start | bytes 1572868
  1.7 0.9 %copy-start.2 = (f32[4,64,256]{2,1,0:T(8,128)S(1)}, f32[4,64,256]{2,1,0:T(8,128)}, u32[]{:S(2)}) copy-start(f32[4,64,256]{2,1,0:T(8,128)} %mobility.1) | copy-start | bytes 786436
  2.8 7.6 %collective-permute-start.2 = (f32[2,4,64,256]{3,2,1,0:T(8,128)S(1)}, f32[2,4,64,256]{3,2,1,0:T(8,128)S(1)}, u32[]{:S(2)}, u32[]{:S(2)}) collective-permute-start(f32[2,4,64,256]{3,2,1,0:T(8,128)S(1)} %get-tuple-element.48), channel_id=1, source_target_pairs={{0,1},{1,0},{2,3},{3,2},{4,5},{5,4},{6,7},{7,6},{8,9},{9,8},{10,11... | collective-permute-start | bytes 1572872 | tf_op jit(solution)/shard_map/ppermute | solution.py:584
  3.3 12.6 %collective-permute-start.1 = (f32[2,4,64,256]{3,2,1,0:T(8,128)S(1)}, f32[2,4,64,256]{3,2,1,0:T(8,128)S(1)}, u32[]{:S(2)}, u32[]{:S(2)}) collective-permute-start(f32[2,4,64,256]{3,2,1,0:T(8,128)S(1)} %copy-done.1), channel_id=1, source_target_pairs={{0,15},{1,2},{2,1},{3,4},{4,3},{5,6},{6,5},{7,8},{8,7},{9,10},{10,... | collective-permute-start | bytes 1572872 | tf_op jit(solution)/shard_map/ppermute | solution.py:579
  8.9 1.4 %collective-permute-start.3 = (f32[3,2,64,128]{3,2,1,0:T(8,128)S(1)}, f32[3,2,64,128]{3,2,1,0:T(8,128)S(1)}, u32[]{:S(2)}, u32[]{:S(2)}) collective-permute-start(f32[3,2,64,128]{3,2,1,0:T(8,128)S(1)} %get-tuple-element.49), channel_id=1, source_target_pairs={{0,1},{1,0},{2,3},{3,2},{4,5},{5,4},{6,7},{7,6},{8,9},{9,8},{10,11... | collective-permute-start | bytes 589832 | tf_op jit(solution)/shard_map/ppermute | solution.py:567
  8.9 9.1 %collective-permute-start = (f32[3,2,64,128]{3,2,1,0:T(8,128)S(1)}, f32[3,2,64,128]{3,2,1,0:T(8,128)S(1)}, u32[]{:S(2)}, u32[]{:S(2)}) collective-permute-start(f32[3,2,64,128]{3,2,1,0:T(8,128)S(1)} %get-tuple-element.45), channel_id=1, source_target_pairs={{0,15},{1,2},{2,1},{3,4},{4,3},{5,6},{6,5},{7,8},{8,7},{9,10},{10,... | collective-permute-start | bytes 589832 | tf_op jit(solution)/shard_map/ppermute | solution.py:568
  10.4 5.5 %copy-start = (f32[2,4,64,256]{3,2,1,0:T(8,128)S(1)}, f32[2,4,64,256]{3,2,1,0:T(8,128)}, u32[]{:S(2)}) copy-start(f32[2,4,64,256]{3,2,1,0:T(8,128)} %observed.3) | copy-start | bytes 1572868
  19.3 9.4 %collective-permute-start.5 = (f32[2,3,2,72,128]{4,3,2,1,0:T(8,128)S(1)}, f32[2,3,2,72,128]{4,3,2,1,0:T(8,128)S(1)}, u32[]{:S(2)}, u32[]{:S(2)}) collective-permute-start(f32[2,3,2,72,128]{4,3,2,1,0:T(8,128)S(1)} %get-tuple-element.73), channel_id=1, source_target_pairs={{0,1},{1,0},{2,3},{3,2},{4,5},{5,4},{6,7},{7,6},{8,9},{9,8},{10,11... | collective-permute-start | bytes 1327112 | tf_op jit(solution)/shard_map/ppermute | solution.py:567
  23.9 12.3 %collective-permute-start.4 = (f32[2,3,2,64,128]{4,3,2,1,0:T(8,128)S(1)}, f32[2,3,2,64,128]{4,3,2,1,0:T(8,128)S(1)}, u32[]{:S(2)}, u32[]{:S(2)}) collective-permute-start(f32[2,3,2,64,128]{4,3,2,1,0:T(8,128)S(1)} %get-tuple-element.64), channel_id=1, source_target_pairs={{0,15},{1,2},{2,1},{3,4},{4,3},{5,6},{6,5},{7,8},{8,7},{9,10},{10,... | collective-permute-start | bytes 1179656 | tf_op jit(solution)/shard_map/ppermute | solution.py:568
  28.7 5.4 %collective-permute-start.8 = (f32[8,128]{1,0:T(8,128)S(1)}, f32[8,128]{1,0:T(8,128)S(1)}, u32[]{:S(2)}, u32[]{:S(2)}) collective-permute-start(f32[8,128]{1,0:T(8,128)S(1)} %fusion.share_in), channel_id=1, source_target_pairs={{0,16},{1,13},{2,14},{3,19},{4,20},{5,9},{6,10},{7,23},{8,24},{9,5... | collective-permute-start | bytes 12296 | tf_op jit(solution)/shard_map/ppermute | solution.py:630
  30.2 3.9 %collective-permute-start.6 = (f32[8,128]{1,0:T(8,128)S(1)}, f32[8,128]{1,0:T(8,128)S(1)}, u32[]{:S(2)}, u32[]{:S(2)}) collective-permute-start(f32[8,128]{1,0:T(8,128)S(1)} %fusion.share_in), channel_id=1, source_target_pairs={{0,16},{1,9},{2,10},{3,19},{4,20},{5,13},{6,14},{7,23},{8,24},{9,1... | collective-permute-start | bytes 12296 | tf_op jit(solution)/shard_map/ppermute | solution.py:630
  30.7 3.6 %collective-permute-start.7 = (f32[8,128]{1,0:T(8,128)S(1)}, f32[8,128]{1,0:T(8,128)S(1)}, u32[]{:S(2)}, u32[]{:S(2)}) collective-permute-start(f32[8,128]{1,0:T(8,128)S(1)} %fusion.share_in), channel_id=1, source_target_pairs={{0,16},{1,5},{2,6},{3,19},{4,20},{5,1},{6,2},{7,23},{8,24},{9,13},... | collective-permute-start | bytes 12296 | tf_op jit(solution)/shard_map/ppermute | solution.py:630
  34.4 3.4 %collective-permute-start.9 = (f32[8,128]{1,0:T(8,128)S(1)}, f32[8,128]{1,0:T(8,128)S(1)}, u32[]{:S(2)}, u32[]{:S(2)}) collective-permute-start(f32[8,128]{1,0:T(8,128)S(1)} %add_add_fusion.share_in), channel_id=1, source_target_pairs={{0,1},{1,0},{2,3},{3,2},{4,5},{5,4},{6,7},{7,6},{8,9},{9,8},{10,11... | collective-permute-start | bytes 12296 | tf_op jit(solution)/shard_map/ppermute | solution.py:654
  34.4 3.7 %collective-permute-start.10 = (f32[8,128]{1,0:T(8,128)S(1)}, f32[8,128]{1,0:T(8,128)S(1)}, u32[]{:S(2)}, u32[]{:S(2)}) collective-permute-start(f32[8,128]{1,0:T(8,128)S(1)} %add_add_fusion.share_in), channel_id=1, source_target_pairs={{0,2},{1,3},{2,0},{3,1},{4,6},{5,7},{6,4},{7,5},{8,10},{9,11},{10,... | collective-permute-start | bytes 12296 | tf_op jit(solution)/shard_map/ppermute | solution.py:654
  35.6 3.0 %collective-permute-start.11 = (f32[8,128]{1,0:T(8,128)S(1)}, f32[8,128]{1,0:T(8,128)S(1)}, u32[]{:S(2)}, u32[]{:S(2)}) collective-permute-start(f32[8,128]{1,0:T(8,128)S(1)} %add_add_fusion.share_in), channel_id=1, source_target_pairs={{0,3},{1,2},{2,1},{3,0},{4,7},{5,6},{6,5},{7,4},{8,11},{9,10},{10,... | collective-permute-start | bytes 12296 | tf_op jit(solution)/shard_map/ppermute | solution.py:654

commit v23 on v21

--- a/solution.py
+++ b/solution.py
@@ -15,7 +15,7 @@
 LANES = 128
 ROWS = 8
 PAD = ROWS
-CHUNK = 8
+CHUNK = 32
 
 
 def chunks(ny):

time: 37.5 us -> 37.4 us (level)
  no operation moved by 1% of the time
where the time goes in v23:
time: 37.4 us; the launch traced here: 37.2 us
  starting transfers between devices  20.8 us (56%)
  Pallas kernels  7.36 us (20%)
  waiting for transfers between devices  6.35 us (17%)
  local copies, waits for them, and re-layouts  2.03 us (5%)
  between operations  0.69 us (2%)
    ppermute x3, starting transfers between devices, neighbours(): return (lax.ppermute(to_chip, 'gx', over_chips), of_core)  11.1 us
    pallas_call x7, Pallas kernels, call(): pl.pallas_call(kernel, out_shape=tuple((jax.ShapeDtypeStruct(o, jnp.float...  7.36 us
    ppermute x3, waiting for transfers between devices, neighbours(): return (lax.ppermute(to_chip, 'gx', over_chips), of_core)  4.5 us
    ppermute x3, starting transfers between devices, neighbours(): of_core = lax.ppermute(to_core, 'gx', over_cores)  4.38 us
    ppermute x3, starting transfers between devices, hop(): return lax.ppermute(value, ('group', 'gx'), pairs)  3.52 us
    unnamed x6, local copies, waits for them, and re-layouts  2.03 us
    ppermute x3, starting transfers between devices, on_device(): lax.ppermute(share, 'gx', [(at, at ^ apart) for at in range(count)])  1.86 us
    ppermute x3, waiting for transfers between devices, on_device(): lax.ppermute(share, 'gx', [(at, at ^ apart) for at in range(count)])  0.85 us
  transfers between devices with their start and end apart: 12, of which 6 were waited for; matrix products, arithmetic and copies ran while one was open for 0% of the time, Pallas kernels for 15%

profile of v23, /device:TPU:0, one launch (start us, length us, event | category | flops | bytes accessed | tf_op | source)
XLA Modules:
  0.0 37.2 jit_solution(253068979864884246)
XLA Ops:
  0.6 0.5 %collective-permute-start.2 = (f32[2,4,64,256]{3,2,1,0:T(8,128)}, f32[2,4,64,256]{3,2,1,0:T(8,128)S(1)}, u32[]{:S(2)}, u32[]{:S(2)}) collective-permute-start(f32[2,4,64,256]{3,2,1,0:T(8,128)} %initial.1), channel_id=1, source_target_pairs={{0,1},{1,0},{2,3},{3,2},{4,5},{5,4},{6,7},{7,6},{8,9},{9,8},{10,11... | collective-permute-start | bytes 1572872 | tf_op jit(solution)/shard_map/ppermute | solution.py:566
  1.1 5.7 %collective-permute-start.1 = (f32[2,4,64,256]{3,2,1,0:T(8,128)}, f32[2,4,64,256]{3,2,1,0:T(8,128)S(1)}, u32[]{:S(2)}, u32[]{:S(2)}) collective-permute-start(f32[2,4,64,256]{3,2,1,0:T(8,128)} %initial.1), channel_id=1, source_target_pairs={{0,15},{1,2},{2,1},{3,4},{4,3},{5,6},{6,5},{7,8},{8,7},{9,10},{10,... | collective-permute-start | bytes 1572872 | tf_op jit(solution)/shard_map/ppermute | solution.py:567
  6.8 0.0 copy-start.1
  6.8 1.1 %copy-done.1 = f32[2,4,64,256]{3,2,1,0:T(8,128)S(1)} copy-done((f32[2,4,64,256]{3,2,1,0:T(8,128)S(1)}, f32[2,4,64,256]{3,2,1,0:T(8,128)}, u32[]{:S(2)}) %copy-start.1) | copy-done | bytes 524312
  7.9 0.0 copy-start.2
  7.9 0.9 %copy-done.2 = f32[4,64,256]{2,1,0:T(8,128)S(1)} copy-done((f32[4,64,256]{2,1,0:T(8,128)S(1)}, f32[4,64,256]{2,1,0:T(8,128)}, u32[]{:S(2)}) %copy-start.2) | copy-done | bytes 262168
  8.8 0.1 shard_map.50
  8.9 0.1 collective-permute-start.3
  9.0 0.6 %collective-permute-start = (f32[3,2,64,128]{3,2,1,0:T(8,128)S(1)}, f32[3,2,64,128]{3,2,1,0:T(8,128)S(1)}, u32[]{:S(2)}, u32[]{:S(2)}) collective-permute-start(f32[3,2,64,128]{3,2,1,0:T(8,128)S(1)} %get-tuple-element.44), channel_id=1, source_target_pairs={{0,15},{1,2},{2,1},{3,4},{4,3},{5,6},{6,5},{7,8},{8,7},{9,10},{10,... | collective-permute-start | bytes 589832 | tf_op jit(solution)/shard_map/ppermute | solution.py:567
  9.6 0.8 %collective-permute-done.3.m_core = f32[3,2,64,128]{3,2,1,0:T(8,128)S(1)} collective-permute-done((f32[3,2,64,128]{3,2,1,0:T(8,128)S(1)}, f32[3,2,64,128]{3,2,1,0:T(8,128)S(1)}, u32[]{:S(2)}, u32[]{:S(2)}) %collective-permute-start.3) | collective-permute-done | bytes 196640 | tf_op jit(solution)/shard_map/ppermute | solution.py:566
  10.4 0.0 collective-permute-done.2.of_core
  10.4 0.0 copy-start
  10.4 0.7 %shard_map.51 = (f32[2,4,2,80,128]{4,3,2,1,0:T(8,128)S(1)}, f32[2,6,2,80,128]{4,3,2,1,0:T(8,128)S(1)}, f32[6,2,64,128]{3,2,1,0:T(8,128)S(1)}, f32[6,2,64,128]{3,...) custom-call(f32[2,4,64,256]{3,2,1,0:T(8,128)S(1)} %collective-permut, ...), custom_call_target="tpu_custom_call" | custom-call | flops 3932160 | bytes 5636096 | tf_op jit(solution)/shard_map/pallas_call | solution.py:546
  11.2 2.8 %collective-permute-done.1.of_chip = f32[2,4,64,256]{3,2,1,0:T(8,128)S(1)} collective-permute-done((f32[2,4,64,256]{3,2,1,0:T(8,128)}, f32[2,4,64,256]{3,2,1,0:T(8,128)S(1)}, u32[]{:S(2)}, u32[]{:S(2)}) %collective-permute-start.1) | collective-permute-done | bytes 524320 | tf_op jit(solution)/shard_map/ppermute | solution.py:567
  14.0 0.0 copy-done
  14.0 1.3 %shard_map.52 = (f32[2,4,2,80,128]{4,3,2,1,0:T(8,128)S(1)}, f32[2,4,2,80,128]{4,3,2,1,0:T(8,128)S(1)}, f32[2,5,2,80,128]{4,3,2,1,0:T(8,128)S(1)}, f32[2,3,2,80,1...) custom-call(f32[2,4,64,256]{3,2,1,0:T(8,128)S(1)} %collective-permute-done.1.of_chip, ...), custom_call_target="tpu_custom_call" | custom-call | flops 5898240 | bytes 8437760 | tf_op jit(solution)/shard_map/pallas_call | solution.py:546
  15.3 1.7 %collective-permute-done.m_chip = f32[3,2,64,128]{3,2,1,0:T(8,128)S(1)} collective-permute-done((f32[3,2,64,128]{3,2,1,0:T(8,128)S(1)}, f32[3,2,64,128]{3,2,1,0:T(8,128)S(1)}, u32[]{:S(2)}, u32[]{:S(2)}) %collective-permute-start) | collective-permute-done | bytes 196640 | tf_op jit(solution)/shard_map/ppermute | solution.py:567
  17.0 1.2 %shard_map.53 = (f32[3,2,64,128]{3,2,1,0:T(8,128)S(1)}, f32[2,2,64,128]{3,2,1,0:T(8,128)S(1)}, f32[2,2,64,128]{3,2,1,0:T(8,128)S(1)}, f32[2,2,64,128]{3,2,1,0:T(...) custom-call(f32[3,2,64,128]{3,2,1,0:T(8,128)S(1)} %collective-permut, ...), custom_call_target="tpu_custom_call" | custom-call | flops 5898240 | bytes 11014144 | tf_op jit(solution)/shard_map/pallas_call | solution.py:546
  18.2 3.8 %collective-permute-start.5 = (f32[2,3,2,72,128]{4,3,2,1,0:T(8,128)S(1)}, f32[2,3,2,72,128]{4,3,2,1,0:T(8,128)S(1)}, u32[]{:S(2)}, u32[]{:S(2)}) collective-permute-start(f32[2,3,2,72,128]{4,3,2,1,0:T(8,128)S(1)} %get-tuple-element.71), channel_id=1, source_target_pairs={{0,1},{1,0},{2,3},{3,2},{4,5},{5,4},{6,7},{7,6},{8,9},{9,8},{10,11... | collective-permute-start | bytes 1327112 | tf_op jit(solution)/shard_map/ppermute | solution.py:566
  22.0 4.8 %collective-permute-start.4 = (f32[2,3,2,64,128]{4,3,2,1,0:T(8,128)S(1)}, f32[2,3,2,64,128]{4,3,2,1,0:T(8,128)S(1)}, u32[]{:S(2)}, u32[]{:S(2)}) collective-permute-start(f32[2,3,2,64,128]{4,3,2,1,0:T(8,128)S(1)} %get-tuple-element.62), channel_id=1, source_target_pairs={{0,15},{1,2},{2,1},{3,4},{4,3},{5,6},{6,5},{7,8},{8,7},{9,10},{10,... | collective-permute-start | bytes 1179656 | tf_op jit(solution)/shard_map/ppermute | solution.py:567
  26.7 0.0 collective-permute-done.5.of_core
  26.8 1.5 %collective-permute-start.8 = (f32[8,128]{1,0:T(8,128)S(1)}, f32[8,128]{1,0:T(8,128)S(1)}, u32[]{:S(2)}, u32[]{:S(2)}) collective-permute-start(f32[8,128]{1,0:T(8,128)S(1)} %fusion.share_in), channel_id=1, source_target_pairs={{0,16},{1,13},{2,14},{3,19},{4,20},{5,9},{6,10},{7,23},{8,24},{9,5... | collective-permute-start | bytes 12296 | tf_op jit(solution)/shard_map/ppermute | solution.py:629
  28.2 0.5 %collective-permute-start.6 = (f32[8,128]{1,0:T(8,128)S(1)}, f32[8,128]{1,0:T(8,128)S(1)}, u32[]{:S(2)}, u32[]{:S(2)}) collective-permute-start(f32[8,128]{1,0:T(8,128)S(1)} %fusion.share_in), channel_id=1, source_target_pairs={{0,16},{1,9},{2,10},{3,19},{4,20},{5,13},{6,14},{7,23},{8,24},{9,1... | collective-permute-start | bytes 12296 | tf_op jit(solution)/shard_map/ppermute | solution.py:629
  28.8 1.5 %collective-permute-start.7 = (f32[8,128]{1,0:T(8,128)S(1)}, f32[8,128]{1,0:T(8,128)S(1)}, u32[]{:S(2)}, u32[]{:S(2)}) collective-permute-start(f32[8,128]{1,0:T(8,128)S(1)} %fusion.share_in), channel_id=1, source_target_pairs={{0,16},{1,5},{2,6},{3,19},{4,20},{5,1},{6,2},{7,23},{8,24},{9,13},... | collective-permute-start | bytes 12296 | tf_op jit(solution)/shard_map/ppermute | solution.py:629
  30.3 1.9 %shard_map.54 = (f32[2,5,2,80,128]{4,3,2,1,0:T(8,128)S(1)}, f32[2,1,2,80,128]{4,3,2,1,0:T(8,128)S(1)}, f32[2,3,2,80,128]{4,3,2,1,0:T(8,128)S(1)}, f32[2,3,2,64,1...) custom-call(f32[2,3,2,72,128]{4,3,2,1,0:T(8,128)S(1)} %collective-pe, ...), custom_call_target="tpu_custom_call" | custom-call | flops 7864320 | bytes 10903552 | tf_op jit(solution)/shard_map/pallas_call | solution.py:546
  32.2 0.0 collective-permute-done.8
  32.2 0.0 collective-permute-done.6
  32.2 0.2 collective-permute-done.7
  32.4 0.0 collective-permute-start.9
  32.4 1.3 %collective-permute-start.10 = (f32[8,128]{1,0:T(8,128)S(1)}, f32[8,128]{1,0:T(8,128)S(1)}, u32[]{:S(2)}, u32[]{:S(2)}) collective-permute-start(f32[8,128]{1,0:T(8,128)S(1)} %add_add_fusion.share_in), channel_id=1, source_target_pairs={{0,2},{1,3},{2,0},{3,1},{4,6},{5,7},{6,4},{7,5},{8,10},{9,11},{10,... | collective-permute-start | bytes 12296 | tf_op jit(solution)/shard_map/ppermute | solution.py:653
  33.7 0.6 %collective-permute-start.11 = (f32[8,128]{1,0:T(8,128)S(1)}, f32[8,128]{1,0:T(8,128)S(1)}, u32[]{:S(2)}, u32[]{:S(2)}) collective-permute-start(f32[8,128]{1,0:T(8,128)S(1)} %add_add_fusion.share_in), channel_id=1, source_target_pairs={{0,3},{1,2},{2,1},{3,0},{4,7},{5,6},{6,5},{7,4},{8,11},{9,10},{10,... | collective-permute-start | bytes 12296 | tf_op jit(solution)/shard_map/ppermute | solution.py:653
  34.3 0.0 collective-permute-done.4.of_chip
  34.3 1.6 %shard_map.55 = (f32[4,64,256]{2,1,0:T(8,128)}, f32[8,128]{1,0:T(8,128)S(1)}) custom-call(f32[2,3,2,64,128]{4,3,2,1,0:T(8,128)S(1)} %collective-permute-done.4.of_chip, f32[6,2,64,128]{3,2,1,0:T(8,128)S(1)} %get-tuple-element.50.mx.mx_a, f32[6,2,64,128]{3,2,1,0:T(8,128)S(1)} %get-tuple-element.51.my.my_a, ...), custom_call_target="tpu_custom_call" | custom-call | flops 5898240 | bytes 9150464 | tf_op jit(solution)/shard_map/pallas_call | solution.py:546
  35.8 0.0 collective-permute-done.9.other_core
  35.8 0.2 collective-permute-done.10.across
  36.1 0.6 %collective-permute-done.11.other_across = f32[8,128]{1,0:T(8,128)S(1)} collective-permute-done((f32[8,128]{1,0:T(8,128)S(1)}, f32[8,128]{1,0:T(8,128)S(1)}, u32[]{:S(2)}, u32[]{:S(2)}) %collective-permute-start.11) | collective-permute-done | bytes 4128 | tf_op jit(solution)/shard_map/ppermute | solution.py:653
  36.7 0.6 %shard_map.56 = f32[1]{0:T(128)} custom-call(f32[8,128]{1,0:T(8,128)S(1)} %get-tuple-element.85.core, f32[8,128]{1,0:T(8,128)S(1)} %collective-permute-done.9.other_core, f32[8,128]{1,0:T(8,128)S(1)} %collective-permute-done.10.across, f32[8,128]{1,0:T(8,128)S(1)} %collective-permute-done.11.other_across), custom_call_target="tpu_custom_call" | custom-call | flops 1 | bytes 16388 | tf_op jit(solution)/shard_map/pallas_call | solution.py:546
  (2 shorter events, 0.0 us)
Async XLA Ops:
  0.6 9.8 %collective-permute-start.2 = (f32[2,4,64,256]{3,2,1,0:T(8,128)}, f32[2,4,64,256]{3,2,1,0:T(8,128)S(1)}, u32[]{:S(2)}, u32[]{:S(2)}) collective-permute-start(f32[2,4,64,256]{3,2,1,0:T(8,128)} %initial.1), channel_id=1, source_target_pairs={{0,1},{1,0},{2,3},{3,2},{4,5},{5,4},{6,7},{7,6},{8,9},{9,8},{10,11... | collective-permute-start | bytes 1572872 | tf_op jit(solution)/shard_map/ppermute | solution.py:566
  1.1 12.8 %collective-permute-start.1 = (f32[2,4,64,256]{3,2,1,0:T(8,128)}, f32[2,4,64,256]{3,2,1,0:T(8,128)S(1)}, u32[]{:S(2)}, u32[]{:S(2)}) collective-permute-start(f32[2,4,64,256]{3,2,1,0:T(8,128)} %initial.1), channel_id=1, source_target_pairs={{0,15},{1,2},{2,1},{3,4},{4,3},{5,6},{6,5},{7,8},{8,7},{9,10},{10,... | collective-permute-start | bytes 1572872 | tf_op jit(solution)/shard_map/ppermute | solution.py:567
  6.8 1.1 %copy-start.1 = (f32[2,4,64,256]{3,2,1,0:T(8,128)S(1)}, f32[2,4,64,256]{3,2,1,0:T(8,128)}, u32[]{:S(2)}) copy-start(f32[2,4,64,256]{3,2,1,0:T(8,128)} %initial.1) | copy-start | bytes 1572868
  7.9 0.9 %copy-start.2 = (f32[4,64,256]{2,1,0:T(8,128)S(1)}, f32[4,64,256]{2,1,0:T(8,128)}, u32[]{:S(2)}) copy-start(f32[4,64,256]{2,1,0:T(8,128)} %mobility.1) | copy-start | bytes 786436
  8.9 1.5 %collective-permute-start.3 = (f32[3,2,64,128]{3,2,1,0:T(8,128)S(1)}, f32[3,2,64,128]{3,2,1,0:T(8,128)S(1)}, u32[]{:S(2)}, u32[]{:S(2)}) collective-permute-start(f32[3,2,64,128]{3,2,1,0:T(8,128)S(1)} %get-tuple-element.47), channel_id=1, source_target_pairs={{0,1},{1,0},{2,3},{3,2},{4,5},{5,4},{6,7},{7,6},{8,9},{9,8},{10,11... | collective-permute-start | bytes 589832 | tf_op jit(solution)/shard_map/ppermute | solution.py:566
  9.0 8.0 %collective-permute-start = (f32[3,2,64,128]{3,2,1,0:T(8,128)S(1)}, f32[3,2,64,128]{3,2,1,0:T(8,128)S(1)}, u32[]{:S(2)}, u32[]{:S(2)}) collective-permute-start(f32[3,2,64,128]{3,2,1,0:T(8,128)S(1)} %get-tuple-element.44), channel_id=1, source_target_pairs={{0,15},{1,2},{2,1},{3,4},{4,3},{5,6},{6,5},{7,8},{8,7},{9,10},{10,... | collective-permute-start | bytes 589832 | tf_op jit(solution)/shard_map/ppermute | solution.py:567
  10.4 3.6 %copy-start = (f32[2,4,64,256]{3,2,1,0:T(8,128)S(1)}, f32[2,4,64,256]{3,2,1,0:T(8,128)}, u32[]{:S(2)}) copy-start(f32[2,4,64,256]{3,2,1,0:T(8,128)} %observed.3) | copy-start | bytes 1572868
  18.2 8.6 %collective-permute-start.5 = (f32[2,3,2,72,128]{4,3,2,1,0:T(8,128)S(1)}, f32[2,3,2,72,128]{4,3,2,1,0:T(8,128)S(1)}, u32[]{:S(2)}, u32[]{:S(2)}) collective-permute-start(f32[2,3,2,72,128]{4,3,2,1,0:T(8,128)S(1)} %get-tuple-element.71), channel_id=1, source_target_pairs={{0,1},{1,0},{2,3},{3,2},{4,5},{5,4},{6,7},{7,6},{8,9},{9,8},{10,11... | collective-permute-start | bytes 1327112 | tf_op jit(solution)/shard_map/ppermute | solution.py:566
  22.0 12.3 %collective-permute-start.4 = (f32[2,3,2,64,128]{4,3,2,1,0:T(8,128)S(1)}, f32[2,3,2,64,128]{4,3,2,1,0:T(8,128)S(1)}, u32[]{:S(2)}, u32[]{:S(2)}) collective-permute-start(f32[2,3,2,64,128]{4,3,2,1,0:T(8,128)S(1)} %get-tuple-element.62), channel_id=1, source_target_pairs={{0,15},{1,2},{2,1},{3,4},{4,3},{5,6},{6,5},{7,8},{8,7},{9,10},{10,... | collective-permute-start | bytes 1179656 | tf_op jit(solution)/shard_map/ppermute | solution.py:567
  26.8 5.5 %collective-permute-start.8 = (f32[8,128]{1,0:T(8,128)S(1)}, f32[8,128]{1,0:T(8,128)S(1)}, u32[]{:S(2)}, u32[]{:S(2)}) collective-permute-start(f32[8,128]{1,0:T(8,128)S(1)} %fusion.share_in), channel_id=1, source_target_pairs={{0,16},{1,13},{2,14},{3,19},{4,20},{5,9},{6,10},{7,23},{8,24},{9,5... | collective-permute-start | bytes 12296 | tf_op jit(solution)/shard_map/ppermute | solution.py:629
  28.2 4.0 %collective-permute-start.6 = (f32[8,128]{1,0:T(8,128)S(1)}, f32[8,128]{1,0:T(8,128)S(1)}, u32[]{:S(2)}, u32[]{:S(2)}) collective-permute-start(f32[8,128]{1,0:T(8,128)S(1)} %fusion.share_in), channel_id=1, source_target_pairs={{0,16},{1,9},{2,10},{3,19},{4,20},{5,13},{6,14},{7,23},{8,24},{9,1... | collective-permute-start | bytes 12296 | tf_op jit(solution)/shard_map/ppermute | solution.py:629
  28.8 3.6 %collective-permute-start.7 = (f32[8,128]{1,0:T(8,128)S(1)}, f32[8,128]{1,0:T(8,128)S(1)}, u32[]{:S(2)}, u32[]{:S(2)}) collective-permute-start(f32[8,128]{1,0:T(8,128)S(1)} %fusion.share_in), channel_id=1, source_target_pairs={{0,16},{1,5},{2,6},{3,19},{4,20},{5,1},{6,2},{7,23},{8,24},{9,13},... | collective-permute-start | bytes 12296 | tf_op jit(solution)/shard_map/ppermute | solution.py:629
  32.4 3.4 %collective-permute-start.9 = (f32[8,128]{1,0:T(8,128)S(1)}, f32[8,128]{1,0:T(8,128)S(1)}, u32[]{:S(2)}, u32[]{:S(2)}) collective-permute-start(f32[8,128]{1,0:T(8,128)S(1)} %add_add_fusion.share_in), channel_id=1, source_target_pairs={{0,1},{1,0},{2,3},{3,2},{4,5},{5,4},{6,7},{7,6},{8,9},{9,8},{10,11... | collective-permute-start | bytes 12296 | tf_op jit(solution)/shard_map/ppermute | solution.py:653
  32.4 3.7 %collective-permute-start.10 = (f32[8,128]{1,0:T(8,128)S(1)}, f32[8,128]{1,0:T(8,128)S(1)}, u32[]{:S(2)}, u32[]{:S(2)}) collective-permute-start(f32[8,128]{1,0:T(8,128)S(1)} %add_add_fusion.share_in), channel_id=1, source_target_pairs={{0,2},{1,3},{2,0},{3,1},{4,6},{5,7},{6,4},{7,5},{8,10},{9,11},{10,... | collective-permute-start | bytes 12296 | tf_op jit(solution)/shard_map/ppermute | solution.py:653
  33.7 3.0 %collective-permute-start.11 = (f32[8,128]{1,0:T(8,128)S(1)}, f32[8,128]{1,0:T(8,128)S(1)}, u32[]{:S(2)}, u32[]{:S(2)}) collective-permute-start(f32[8,128]{1,0:T(8,128)S(1)} %add_add_fusion.share_in), channel_id=1, source_target_pairs={{0,3},{1,2},{2,1},{3,0},{4,7},{5,6},{6,5},{7,4},{8,11},{9,10},{10,... | collective-permute-start | bytes 12296 | tf_op jit(solution)/shard_map/ppermute | solution.py:653

commit v24 on v21

--- a/solution.py
+++ b/solution.py
@@ -537,7 +537,7 @@
     return (at ^ (at >> 1)) & 1
 
 
-def misfit_kernel(core, other_core, across, other_across, misfit):
+def misfit_kernel(core, other_across, across, other_core, misfit):
     misfit[0] = ((core[...] + other_core[...]) + (across[...] + other_across[...]))[0, 0]
 
 
@@ -650,7 +650,7 @@
         share = share + sum(fars)
         fars = hops(share, bits)
     share = share + sum(fars)
-    fars = [lax.ppermute(share, "gx", [(at, at ^ apart) for at in range(count)]) for apart in (1, 2, 3)]
+    fars = [lax.ppermute(share, "gx", [(at, at ^ apart) for at in range(count)]) for apart in (3, 2, 1)]
     result, share = call(
         late_kernel,
         ((n, ny, nz), (ROWS, LANES)),

time: 37.5 us -> 36.9 us (0.984)
  waiting for transfers between devices: 6.21 us -> 5.6 us
    ppermute x3, waiting for transfers between devices: 0.83 us -> 0.21 us  [on_device(): lax.ppermute(share, 'gx', [(at, at ^ apart) for at in range(count)])]
  transfers between devices with their start and end apart: 12 -> 12, of which waited for: 6 -> 5; matrix products, arithmetic and copies ran while one was open for 0% -> 0% of each run, Pallas kernels for 15% -> 16%
where the time goes in v24:
time: 36.9 us; the launch traced here: 36.7 us
  starting transfers between devices  20.8 us (56%)
  Pallas kernels  7.53 us (20%)
  waiting for transfers between devices  5.6 us (15%)
  local copies, waits for them, and re-layouts  2.03 us (6%)
  between operations  0.7 us (2%)
    ppermute x3, starting transfers between devices, neighbours(): return (lax.ppermute(to_chip, 'gx', over_chips), of_core)  11.1 us
    pallas_call x7, Pallas kernels, call(): pl.pallas_call(kernel, out_shape=tuple((jax.ShapeDtypeStruct(o, jnp.float...  7.53 us
    ppermute x3, waiting for transfers between devices, neighbours(): return (lax.ppermute(to_chip, 'gx', over_chips), of_core)  4.44 us
    ppermute x3, starting transfers between devices, neighbours(): of_core = lax.ppermute(to_core, 'gx', over_cores)  4.37 us
    ppermute x3, starting transfers between devices, hop(): return lax.ppermute(value, ('group', 'gx'), pairs)  3.52 us
    unnamed x6, local copies, waits for them, and re-layouts  2.03 us
    ppermute x3, starting transfers between devices, on_device(): lax.ppermute(share, 'gx', [(at, at ^ apart) for at in range(count)])  1.86 us
    ppermute x3, waiting for transfers between devices, neighbours(): of_core = lax.ppermute(to_core, 'gx', over_cores)  0.83 us
  transfers between devices with their start and end apart: 12, of which 5 were waited for; matrix products, arithmetic and copies ran while one was open for 0% of the time, Pallas kernels for 16%

profile of v24, /device:TPU:0, one launch (start us, length us, event | category | flops | bytes accessed | tf_op | source)
XLA Modules:
  0.0 36.7 jit_solution(7625527098827507912)
XLA Ops:
  0.6 0.5 %collective-permute-start.2 = (f32[2,4,64,256]{3,2,1,0:T(8,128)}, f32[2,4,64,256]{3,2,1,0:T(8,128)S(1)}, u32[]{:S(2)}, u32[]{:S(2)}) collective-permute-start(f32[2,4,64,256]{3,2,1,0:T(8,128)} %initial.1), channel_id=1, source_target_pairs={{0,1},{1,0},{2,3},{3,2},{4,5},{5,4},{6,7},{7,6},{8,9},{9,8},{10,11... | collective-permute-start | bytes 1572872 | tf_op jit(solution)/shard_map/ppermute | solution.py:566
  1.1 5.7 %collective-permute-start.1 = (f32[2,4,64,256]{3,2,1,0:T(8,128)}, f32[2,4,64,256]{3,2,1,0:T(8,128)S(1)}, u32[]{:S(2)}, u32[]{:S(2)}) collective-permute-start(f32[2,4,64,256]{3,2,1,0:T(8,128)} %initial.1), channel_id=1, source_target_pairs={{0,15},{1,2},{2,1},{3,4},{4,3},{5,6},{6,5},{7,8},{8,7},{9,10},{10,... | collective-permute-start | bytes 1572872 | tf_op jit(solution)/shard_map/ppermute | solution.py:567
  6.8 0.0 copy-start.1
  6.8 1.1 %copy-done.1 = f32[2,4,64,256]{3,2,1,0:T(8,128)S(1)} copy-done((f32[2,4,64,256]{3,2,1,0:T(8,128)S(1)}, f32[2,4,64,256]{3,2,1,0:T(8,128)}, u32[]{:S(2)}) %copy-start.1) | copy-done | bytes 524312
  7.9 0.0 copy-start.2
  7.9 0.9 %copy-done.2 = f32[4,64,256]{2,1,0:T(8,128)S(1)} copy-done((f32[4,64,256]{2,1,0:T(8,128)S(1)}, f32[4,64,256]{2,1,0:T(8,128)}, u32[]{:S(2)}) %copy-start.2) | copy-done | bytes 262168
  8.8 0.1 shard_map.50
  8.9 0.1 collective-permute-start.3
  9.0 0.6 %collective-permute-start = (f32[3,2,64,128]{3,2,1,0:T(8,128)S(1)}, f32[3,2,64,128]{3,2,1,0:T(8,128)S(1)}, u32[]{:S(2)}, u32[]{:S(2)}) collective-permute-start(f32[3,2,64,128]{3,2,1,0:T(8,128)S(1)} %get-tuple-element.44), channel_id=1, source_target_pairs={{0,15},{1,2},{2,1},{3,4},{4,3},{5,6},{6,5},{7,8},{8,7},{9,10},{10,... | collective-permute-start | bytes 589832 | tf_op jit(solution)/shard_map/ppermute | solution.py:567
  9.6 0.8 %collective-permute-done.3.m_core = f32[3,2,64,128]{3,2,1,0:T(8,128)S(1)} collective-permute-done((f32[3,2,64,128]{3,2,1,0:T(8,128)S(1)}, f32[3,2,64,128]{3,2,1,0:T(8,128)S(1)}, u32[]{:S(2)}, u32[]{:S(2)}) %collective-permute-start.3) | collective-permute-done | bytes 196640 | tf_op jit(solution)/shard_map/ppermute | solution.py:566
  10.5 0.0 collective-permute-done.2.of_core
  10.5 0.0 copy-start
  10.5 0.7 %shard_map.51 = (f32[2,4,2,80,128]{4,3,2,1,0:T(8,128)S(1)}, f32[2,6,2,80,128]{4,3,2,1,0:T(8,128)S(1)}, f32[6,2,64,128]{3,2,1,0:T(8,128)S(1)}, f32[6,2,64,128]{3,...) custom-call(f32[2,4,64,256]{3,2,1,0:T(8,128)S(1)} %collective-permut, ...), custom_call_target="tpu_custom_call" | custom-call | flops 3932160 | bytes 5636096 | tf_op jit(solution)/shard_map/pallas_call | solution.py:546
  11.2 2.8 %collective-permute-done.1.of_chip = f32[2,4,64,256]{3,2,1,0:T(8,128)S(1)} collective-permute-done((f32[2,4,64,256]{3,2,1,0:T(8,128)}, f32[2,4,64,256]{3,2,1,0:T(8,128)S(1)}, u32[]{:S(2)}, u32[]{:S(2)}) %collective-permute-start.1) | collective-permute-done | bytes 524320 | tf_op jit(solution)/shard_map/ppermute | solution.py:567
  14.0 0.0 copy-done
  14.0 1.3 %shard_map.52 = (f32[2,4,2,80,128]{4,3,2,1,0:T(8,128)S(1)}, f32[2,4,2,80,128]{4,3,2,1,0:T(8,128)S(1)}, f32[2,5,2,80,128]{4,3,2,1,0:T(8,128)S(1)}, f32[2,3,2,80,1...) custom-call(f32[2,4,64,256]{3,2,1,0:T(8,128)S(1)} %collective-permute-done.1.of_chip, ...), custom_call_target="tpu_custom_call" | custom-call | flops 5898240 | bytes 8425472 | tf_op jit(solution)/shard_map/pallas_call | solution.py:546
  15.4 1.6 %collective-permute-done.m_chip = f32[3,2,64,128]{3,2,1,0:T(8,128)S(1)} collective-permute-done((f32[3,2,64,128]{3,2,1,0:T(8,128)S(1)}, f32[3,2,64,128]{3,2,1,0:T(8,128)S(1)}, u32[]{:S(2)}, u32[]{:S(2)}) %collective-permute-start) | collective-permute-done | bytes 196640 | tf_op jit(solution)/shard_map/ppermute | solution.py:567
  17.0 1.2 %shard_map.53 = (f32[3,2,64,128]{3,2,1,0:T(8,128)S(1)}, f32[2,2,64,128]{3,2,1,0:T(8,128)S(1)}, f32[2,2,64,128]{3,2,1,0:T(8,128)S(1)}, f32[2,2,64,128]{3,2,1,0:T(...) custom-call(f32[3,2,64,128]{3,2,1,0:T(8,128)S(1)} %collective-permut, ...), custom_call_target="tpu_custom_call" | custom-call | flops 5898240 | bytes 11001856 | tf_op jit(solution)/shard_map/pallas_call | solution.py:546
  18.2 3.8 %collective-permute-start.5 = (f32[2,3,2,72,128]{4,3,2,1,0:T(8,128)S(1)}, f32[2,3,2,72,128]{4,3,2,1,0:T(8,128)S(1)}, u32[]{:S(2)}, u32[]{:S(2)}) collective-permute-start(f32[2,3,2,72,128]{4,3,2,1,0:T(8,128)S(1)} %get-tuple-element.71), channel_id=1, source_target_pairs={{0,1},{1,0},{2,3},{3,2},{4,5},{5,4},{6,7},{7,6},{8,9},{9,8},{10,11... | collective-permute-start | bytes 1327112 | tf_op jit(solution)/shard_map/ppermute | solution.py:566
  22.0 4.8 %collective-permute-start.4 = (f32[2,3,2,64,128]{4,3,2,1,0:T(8,128)S(1)}, f32[2,3,2,64,128]{4,3,2,1,0:T(8,128)S(1)}, u32[]{:S(2)}, u32[]{:S(2)}) collective-permute-start(f32[2,3,2,64,128]{4,3,2,1,0:T(8,128)S(1)} %get-tuple-element.62), channel_id=1, source_target_pairs={{0,15},{1,2},{2,1},{3,4},{4,3},{5,6},{6,5},{7,8},{8,7},{9,10},{10,... | collective-permute-start | bytes 1179656 | tf_op jit(solution)/shard_map/ppermute | solution.py:567
  26.8 0.0 collective-permute-done.5.of_core
  26.8 1.5 %collective-permute-start.8 = (f32[8,128]{1,0:T(8,128)S(1)}, f32[8,128]{1,0:T(8,128)S(1)}, u32[]{:S(2)}, u32[]{:S(2)}) collective-permute-start(f32[8,128]{1,0:T(8,128)S(1)} %fusion.share_in), channel_id=1, source_target_pairs={{0,16},{1,13},{2,14},{3,19},{4,20},{5,9},{6,10},{7,23},{8,24},{9,5... | collective-permute-start | bytes 12296 | tf_op jit(solution)/shard_map/ppermute | solution.py:629
  28.3 0.5 %collective-permute-start.6 = (f32[8,128]{1,0:T(8,128)S(1)}, f32[8,128]{1,0:T(8,128)S(1)}, u32[]{:S(2)}, u32[]{:S(2)}) collective-permute-start(f32[8,128]{1,0:T(8,128)S(1)} %fusion.share_in), channel_id=1, source_target_pairs={{0,16},{1,9},{2,10},{3,19},{4,20},{5,13},{6,14},{7,23},{8,24},{9,1... | collective-permute-start | bytes 12296 | tf_op jit(solution)/shard_map/ppermute | solution.py:629
  28.8 1.5 %collective-permute-start.7 = (f32[8,128]{1,0:T(8,128)S(1)}, f32[8,128]{1,0:T(8,128)S(1)}, u32[]{:S(2)}, u32[]{:S(2)}) collective-permute-start(f32[8,128]{1,0:T(8,128)S(1)} %fusion.share_in), channel_id=1, source_target_pairs={{0,16},{1,5},{2,6},{3,19},{4,20},{5,1},{6,2},{7,23},{8,24},{9,13},... | collective-permute-start | bytes 12296 | tf_op jit(solution)/shard_map/ppermute | solution.py:629
  30.3 2.0 %shard_map.54 = (f32[2,5,2,80,128]{4,3,2,1,0:T(8,128)S(1)}, f32[2,1,2,80,128]{4,3,2,1,0:T(8,128)S(1)}, f32[2,3,2,80,128]{4,3,2,1,0:T(8,128)S(1)}, f32[2,3,2,64,1...) custom-call(f32[2,3,2,72,128]{4,3,2,1,0:T(8,128)S(1)} %collective-pe, ...), custom_call_target="tpu_custom_call" | custom-call | flops 7864320 | bytes 10903552 | tf_op jit(solution)/shard_map/pallas_call | solution.py:546
  32.3 0.0 collective-permute-done.8
  32.3 0.0 collective-permute-done.6
  32.3 0.1 collective-permute-done.7
  32.4 0.0 collective-permute-start.9
  32.4 1.3 %collective-permute-start.10 = (f32[8,128]{1,0:T(8,128)S(1)}, f32[8,128]{1,0:T(8,128)S(1)}, u32[]{:S(2)}, u32[]{:S(2)}) collective-permute-start(f32[8,128]{1,0:T(8,128)S(1)} %add_add_fusion.share_in), channel_id=1, source_target_pairs={{0,2},{1,3},{2,0},{3,1},{4,6},{5,7},{6,4},{7,5},{8,10},{9,11},{10,... | collective-permute-start | bytes 12296 | tf_op jit(solution)/shard_map/ppermute | solution.py:653
  33.7 0.6 %collective-permute-start.11 = (f32[8,128]{1,0:T(8,128)S(1)}, f32[8,128]{1,0:T(8,128)S(1)}, u32[]{:S(2)}, u32[]{:S(2)}) collective-permute-start(f32[8,128]{1,0:T(8,128)S(1)} %add_add_fusion.share_in), channel_id=1, source_target_pairs={{0,1},{1,0},{2,3},{3,2},{4,5},{5,4},{6,7},{7,6},{8,9},{9,8},{10,11... | collective-permute-start | bytes 12296 | tf_op jit(solution)/shard_map/ppermute | solution.py:653
  34.3 0.0 collective-permute-done.4.of_chip
  34.3 1.6 %shard_map.55 = (f32[4,64,256]{2,1,0:T(8,128)}, f32[8,128]{1,0:T(8,128)S(1)}) custom-call(f32[2,3,2,64,128]{4,3,2,1,0:T(8,128)S(1)} %collective-permute-done.4.of_chip, f32[6,2,64,128]{3,2,1,0:T(8,128)S(1)} %get-tuple-element.50.mx.mx_a, f32[6,2,64,128]{3,2,1,0:T(8,128)S(1)} %get-tuple-element.51.my.my_a, ...), custom_call_target="tpu_custom_call" | custom-call | flops 5898240 | bytes 9150464 | tf_op jit(solution)/shard_map/pallas_call | solution.py:546
  35.9 0.0 collective-permute-done.9.other_across
  35.9 0.2 collective-permute-done.10.across
  36.1 0.0 collective-permute-done.11.other_core
  36.1 0.6 %shard_map.56 = f32[1]{0:T(128)} custom-call(f32[8,128]{1,0:T(8,128)S(1)} %get-tuple-element.85.core, f32[8,128]{1,0:T(8,128)S(1)} %collective-permute-done.9.other_across, f32[8,128]{1,0:T(8,128)S(1)} %collective-permute-done.10.across, f32[8,128]{1,0:T(8,128)S(1)} %collective-permute-done.11.other_core), custom_call_target="tpu_custom_call" | custom-call | flops 1 | bytes 16388 | tf_op jit(solution)/shard_map/pallas_call | solution.py:546
  (2 shorter events, 0.0 us)
Async XLA Ops:
  0.6 9.8 %collective-permute-start.2 = (f32[2,4,64,256]{3,2,1,0:T(8,128)}, f32[2,4,64,256]{3,2,1,0:T(8,128)S(1)}, u32[]{:S(2)}, u32[]{:S(2)}) collective-permute-start(f32[2,4,64,256]{3,2,1,0:T(8,128)} %initial.1), channel_id=1, source_target_pairs={{0,1},{1,0},{2,3},{3,2},{4,5},{5,4},{6,7},{7,6},{8,9},{9,8},{10,11... | collective-permute-start | bytes 1572872 | tf_op jit(solution)/shard_map/ppermute | solution.py:566
  1.1 12.8 %collective-permute-start.1 = (f32[2,4,64,256]{3,2,1,0:T(8,128)}, f32[2,4,64,256]{3,2,1,0:T(8,128)S(1)}, u32[]{:S(2)}, u32[]{:S(2)}) collective-permute-start(f32[2,4,64,256]{3,2,1,0:T(8,128)} %initial.1), channel_id=1, source_target_pairs={{0,15},{1,2},{2,1},{3,4},{4,3},{5,6},{6,5},{7,8},{8,7},{9,10},{10,... | collective-permute-start | bytes 1572872 | tf_op jit(solution)/shard_map/ppermute | solution.py:567
  6.8 1.1 %copy-start.1 = (f32[2,4,64,256]{3,2,1,0:T(8,128)S(1)}, f32[2,4,64,256]{3,2,1,0:T(8,128)}, u32[]{:S(2)}) copy-start(f32[2,4,64,256]{3,2,1,0:T(8,128)} %initial.1) | copy-start | bytes 1572868
  7.9 0.9 %copy-start.2 = (f32[4,64,256]{2,1,0:T(8,128)S(1)}, f32[4,64,256]{2,1,0:T(8,128)}, u32[]{:S(2)}) copy-start(f32[4,64,256]{2,1,0:T(8,128)} %mobility.1) | copy-start | bytes 786436
  8.9 1.5 %collective-permute-start.3 = (f32[3,2,64,128]{3,2,1,0:T(8,128)S(1)}, f32[3,2,64,128]{3,2,1,0:T(8,128)S(1)}, u32[]{:S(2)}, u32[]{:S(2)}) collective-permute-start(f32[3,2,64,128]{3,2,1,0:T(8,128)S(1)} %get-tuple-element.47), channel_id=1, source_target_pairs={{0,1},{1,0},{2,3},{3,2},{4,5},{5,4},{6,7},{7,6},{8,9},{9,8},{10,11... | collective-permute-start | bytes 589832 | tf_op jit(solution)/shard_map/ppermute | solution.py:566
  9.0 8.0 %collective-permute-start = (f32[3,2,64,128]{3,2,1,0:T(8,128)S(1)}, f32[3,2,64,128]{3,2,1,0:T(8,128)S(1)}, u32[]{:S(2)}, u32[]{:S(2)}) collective-permute-start(f32[3,2,64,128]{3,2,1,0:T(8,128)S(1)} %get-tuple-element.44), channel_id=1, source_target_pairs={{0,15},{1,2},{2,1},{3,4},{4,3},{5,6},{6,5},{7,8},{8,7},{9,10},{10,... | collective-permute-start | bytes 589832 | tf_op jit(solution)/shard_map/ppermute | solution.py:567
  10.5 3.5 %copy-start = (f32[2,4,64,256]{3,2,1,0:T(8,128)S(1)}, f32[2,4,64,256]{3,2,1,0:T(8,128)}, u32[]{:S(2)}) copy-start(f32[2,4,64,256]{3,2,1,0:T(8,128)} %observed.3) | copy-start | bytes 1572868
  18.2 8.6 %collective-permute-start.5 = (f32[2,3,2,72,128]{4,3,2,1,0:T(8,128)S(1)}, f32[2,3,2,72,128]{4,3,2,1,0:T(8,128)S(1)}, u32[]{:S(2)}, u32[]{:S(2)}) collective-permute-start(f32[2,3,2,72,128]{4,3,2,1,0:T(8,128)S(1)} %get-tuple-element.71), channel_id=1, source_target_pairs={{0,1},{1,0},{2,3},{3,2},{4,5},{5,4},{6,7},{7,6},{8,9},{9,8},{10,11... | collective-permute-start | bytes 1327112 | tf_op jit(solution)/shard_map/ppermute | solution.py:566
  22.0 12.3 %collective-permute-start.4 = (f32[2,3,2,64,128]{4,3,2,1,0:T(8,128)S(1)}, f32[2,3,2,64,128]{4,3,2,1,0:T(8,128)S(1)}, u32[]{:S(2)}, u32[]{:S(2)}) collective-permute-start(f32[2,3,2,64,128]{4,3,2,1,0:T(8,128)S(1)} %get-tuple-element.62), channel_id=1, source_target_pairs={{0,15},{1,2},{2,1},{3,4},{4,3},{5,6},{6,5},{7,8},{8,7},{9,10},{10,... | collective-permute-start | bytes 1179656 | tf_op jit(solution)/shard_map/ppermute | solution.py:567
  26.8 5.5 %collective-permute-start.8 = (f32[8,128]{1,0:T(8,128)S(1)}, f32[8,128]{1,0:T(8,128)S(1)}, u32[]{:S(2)}, u32[]{:S(2)}) collective-permute-start(f32[8,128]{1,0:T(8,128)S(1)} %fusion.share_in), channel_id=1, source_target_pairs={{0,16},{1,13},{2,14},{3,19},{4,20},{5,9},{6,10},{7,23},{8,24},{9,5... | collective-permute-start | bytes 12296 | tf_op jit(solution)/shard_map/ppermute | solution.py:629
  28.3 4.0 %collective-permute-start.6 = (f32[8,128]{1,0:T(8,128)S(1)}, f32[8,128]{1,0:T(8,128)S(1)}, u32[]{:S(2)}, u32[]{:S(2)}) collective-permute-start(f32[8,128]{1,0:T(8,128)S(1)} %fusion.share_in), channel_id=1, source_target_pairs={{0,16},{1,9},{2,10},{3,19},{4,20},{5,13},{6,14},{7,23},{8,24},{9,1... | collective-permute-start | bytes 12296 | tf_op jit(solution)/shard_map/ppermute | solution.py:629
  28.8 3.6 %collective-permute-start.7 = (f32[8,128]{1,0:T(8,128)S(1)}, f32[8,128]{1,0:T(8,128)S(1)}, u32[]{:S(2)}, u32[]{:S(2)}) collective-permute-start(f32[8,128]{1,0:T(8,128)S(1)} %fusion.share_in), channel_id=1, source_target_pairs={{0,16},{1,5},{2,6},{3,19},{4,20},{5,1},{6,2},{7,23},{8,24},{9,13},... | collective-permute-start | bytes 12296 | tf_op jit(solution)/shard_map/ppermute | solution.py:629
  32.4 3.5 %collective-permute-start.9 = (f32[8,128]{1,0:T(8,128)S(1)}, f32[8,128]{1,0:T(8,128)S(1)}, u32[]{:S(2)}, u32[]{:S(2)}) collective-permute-start(f32[8,128]{1,0:T(8,128)S(1)} %add_add_fusion.share_in), channel_id=1, source_target_pairs={{0,3},{1,2},{2,1},{3,0},{4,7},{5,6},{6,5},{7,4},{8,11},{9,10},{10,... | collective-permute-start | bytes 12296 | tf_op jit(solution)/shard_map/ppermute | solution.py:653
  32.4 3.7 %collective-permute-start.10 = (f32[8,128]{1,0:T(8,128)S(1)}, f32[8,128]{1,0:T(8,128)S(1)}, u32[]{:S(2)}, u32[]{:S(2)}) collective-permute-start(f32[8,128]{1,0:T(8,128)S(1)} %add_add_fusion.share_in), channel_id=1, source_target_pairs={{0,2},{1,3},{2,0},{3,1},{4,6},{5,7},{6,4},{7,5},{8,10},{9,11},{10,... | collective-permute-start | bytes 12296 | tf_op jit(solution)/shard_map/ppermute | solution.py:653
  33.7 2.4 %collective-permute-start.11 = (f32[8,128]{1,0:T(8,128)S(1)}, f32[8,128]{1,0:T(8,128)S(1)}, u32[]{:S(2)}, u32[]{:S(2)}) collective-permute-start(f32[8,128]{1,0:T(8,128)S(1)} %add_add_fusion.share_in), channel_id=1, source_target_pairs={{0,1},{1,0},{2,3},{3,2},{4,5},{5,4},{6,7},{7,6},{8,9},{9,8},{10,11... | collective-permute-start | bytes 12296 | tf_op jit(solution)/shard_map/ppermute | solution.py:653
